TPU v7x, 32 devices: a whole 2x2x4 slice. The times are simulated.
32 devices in a mesh: batch: 8 (over z, y), proto: 4 (over x, core).
Axes of the slice: x: 2, y: 2, z: 4, core: 2. Of those that a mesh axis runs over, the one named last changes fastest.
Arguments:
- embeddings: bfloat16 [8192, 1024], P('batch'), may hold values from -6 to 6
- pairing: int32 [8192], P('batch'), may hold values from 0 to 1023, as said below
- w_in: bfloat16 [1024, 512], replicated, may hold values from -0.1875 to 0.1875
- w_out: bfloat16 [512, 128], replicated, may hold values from -0.25 to 0.25
- prototypes: bfloat16 [32768, 128], P('proto'), may hold values from -1.8 to 1.8
Outputs:
- grad_in: float32 [1024, 512], replicated
- grad_out: float32 [512, 128], replicated
- grad_proto: float32 [32768, 128], P('proto')
Inputs may be any that keep to these rules, and one draw needn't show every extreme that they name: Within every aligned block of 1024 rows the views come in pairs: pairing[pairing[i]] = i and pairing[i] != i, both counted within the block.
All inputs are finite; a program needn't handle non-finite values.
Results may differ from a plain program's by a relative error of at most 0.007.
Values may be sent and summed in bfloat16 or wider, within the bound.
No kernel may reach another device: no remote copies, remote signals or barrier semaphores. Data moves between devices by JAX's collectives and lax.ppermute only.
A program may use at most 64 MiB of HBM per device.

v0:
```python
import jax
import jax.numpy as jnp
from jax import lax
from jax.sharding import PartitionSpec as P

ITERS = 3


norm_eps = 1e-06
code_temp = 0.05
pred_temp = 0.1
loss_scale = 64.0


def head_forward(rows_in, w_in, w_out):
    pre_act = jnp.dot(rows_in, w_in, preferred_element_type=jnp.float32)
    hidden = jax.nn.gelu(pre_act).astype(jnp.bfloat16)
    raw_out = jnp.dot(hidden, w_out, preferred_element_type=jnp.float32)
    inv_norm = lax.rsqrt(jnp.sum(raw_out * raw_out, axis=1, keepdims=True) + norm_eps)
    return (pre_act, hidden, raw_out, inv_norm, (raw_out * inv_norm).astype(jnp.bfloat16))


def head_backward(rows_in, w_out, pre_act, hidden, raw_out, inv_norm, view_grad):
    along = jnp.sum(raw_out * view_grad, axis=1, keepdims=True)
    d_raw = (inv_norm * view_grad - raw_out * (inv_norm * inv_norm * inv_norm) * along).astype(
        jnp.bfloat16
    )
    grad_out = lax.dot_general(
        hidden, d_raw, (((0,), (0,)), ((), ())), preferred_element_type=jnp.float32
    )
    d_hidden = lax.dot_general(
        d_raw, w_out, (((1,), (1,)), ((), ())), preferred_element_type=jnp.float32
    )
    _, pullback = jax.vjp(jax.nn.gelu, pre_act)
    d_pre = pullback(d_hidden)[0].astype(jnp.bfloat16)
    grad_in = lax.dot_general(
        rows_in, d_pre, (((0,), (0,)), ((), ())), preferred_element_type=jnp.float32
    )
    return (grad_in, grad_out)


def unit_rows(prototypes):
    proto_f = prototypes.astype(jnp.float32)
    proto_inv = lax.rsqrt(jnp.sum(proto_f * proto_f, axis=1, keepdims=True) + norm_eps)
    return (proto_f, proto_inv, (proto_f * proto_inv).astype(jnp.bfloat16))


def scores_of(rows_in, unit):
    return lax.dot_general(
        rows_in, unit, (((1,), (1,)), ((), ())), preferred_element_type=jnp.float32
    )


def body(embeddings, pairing, w_in, w_out, prototypes):
    proto_f, proto_inv, unit = unit_rows(prototypes)
    width = unit.shape[0]
    depth = unit.shape[1]
    block_cols = min(1024, width)
    count = width // block_cols
    unit_blocks = unit.reshape(count, block_cols, depth)
    rows = embeddings.shape[0]
    pre_act, hidden, raw_out, inv_norm, views = head_forward(embeddings, w_in, w_out)
    mates = views[pairing]
    row_scale = jnp.ones((rows,), jnp.float32)
    col_scale = jnp.ones((width,), jnp.float32)
    totals = jnp.ones((rows,), jnp.float32)
    for sweep in range(ITERS):

        def one_block(block):
            return jnp.sum(
                row_scale[:, None] * jnp.exp(scores_of(views, block) / code_temp), axis=0
            )

        column_partial_value = lax.map(one_block, unit_blocks).reshape(width)
        col_scale = 1.0 / lax.psum(column_partial_value, "batch")
        with_totals = sweep == 0
        row_scale_blocks = col_scale.reshape(count, block_cols)
        lines = 2 if with_totals else 1

        def add(running, pair):
            block, scale = pair
            scores = scores_of(views, block)
            found = jnp.sum(jnp.exp(scores / code_temp) * scale[None, :], axis=1)
            if with_totals:
                found = jnp.stack([found, jnp.sum(jnp.exp(scores / pred_temp), axis=1)])
            else:
                found = found[None, :]
            return (running + found, None)

        partial_value, _ = lax.scan(
            add, jnp.zeros((lines, rows), jnp.float32), (unit_blocks, row_scale_blocks)
        )
        summed = lax.psum(partial_value, "proto")
        row_scale = 1.0 / summed[0]
        if sweep == 0:
            totals = summed[1]
    mate_scale = row_scale[pairing]
    scale_blocks = col_scale.reshape(count, block_cols)

    def finish(running, pair):
        block, scale = pair
        scores = scores_of(views, block)
        mate_scores = scores_of(mates, block)
        predicted = jnp.exp(scores / pred_temp) / totals[:, None]
        codes = mate_scale[:, None] * jnp.exp(mate_scores / code_temp) * scale[None, :]
        d_scores = ((predicted - codes) * (loss_scale / pred_temp)).astype(jnp.bfloat16)
        running = running + jnp.dot(d_scores, block, preferred_element_type=jnp.float32)
        unit_part = lax.dot_general(
            d_scores, views, (((0,), (0,)), ((), ())), preferred_element_type=jnp.float32
        )
        return (running, unit_part)

    view_partial, unit_parts = lax.scan(
        finish, jnp.zeros((rows, depth), jnp.float32), (unit_blocks, scale_blocks)
    )
    view_grad = lax.psum(view_partial, "proto")
    unit_grad = unit_parts.reshape(width, depth)
    along = jnp.sum(proto_f * unit_grad, axis=1, keepdims=True)
    proto_part = proto_inv * unit_grad - proto_f * (proto_inv * proto_inv * proto_inv) * along
    grad_in, grad_out = head_backward(
        embeddings, w_out, pre_act, hidden, raw_out, inv_norm, view_grad
    )
    grad_proto, grad_in, grad_out = lax.psum((proto_part, grad_in, grad_out), "batch")
    return (grad_in, grad_out, grad_proto)


def solution(mesh):
    return jax.shard_map(
        body,
        mesh=mesh,
        in_specs=(P("batch", None), P("batch"), P(), P(), P("proto", None)),
        out_specs=(P(), P(), P("proto", None)),
        check_vma=False,
    )
```

profile of v0, /device:TPU:0, one launch (start us, length us, event | category | flops | bytes accessed | tf_op | source)
XLA Modules:
  0.0 607.9 jit_solution(7380517019745069113)
XLA Ops:
  8.8 4.1 multiply_convert_fusion.1
  15.8 2.9 fusion.32
  21.0 14.5 %while.76 = (s32[]{:T(128)}, f32[8,1024]{1,0:T(8,128)S(1)}, bf16[8,1024,128]{2,1,0:T(8,128)(2,1)}, bf16[1024,128]{1,0:T(8,128)(2,1)S(1)}, s32[]{:T(128)}, /*index=5*/s32[]{:T(128)}) while((s32[]{:T(128)}, f32[8,1024]{1,0:T(8,128)S(1)}, bf16[8,1024,128]{2,1,0:T(8,128)(2,1)}, bf16[1024,128]{1,0:T(8,128)(2,1)S(1)}, s32[]{:T(128)}, ...), condition=%wide.region_4.5_spmd, body=%wide.region_2.4_spmd.sunk | while | flops 270531584 | bytes 537161 | solution.py:74
  36.1 39.5 %psum.70 = f32[8192]{0:T(1024)S(1)} all-reduce(f32[8192]{0:T(1024)} %bitcast.157), channel_id=1, replica_groups=mesh['batch'=8,'proto'=4] {'batch'}, use_global_device_ids=true, to_apply=%region_5.6 | all-reduce | flops 8192 | bytes 65536 | tf_op jit(solution)/shard_map/psum | solution.py:75
  77.0 19.4 %while.79 = (s32[]{:T(128)}, f32[2,1024]{1,0:T(2,128)S(1)}, bf16[8,1024,128]{2,1,0:T(8,128)(2,1)}, bf16[1024,128]{1,0:T(8,128)(2,1)S(1)}, f32[8,1024]{1,0:T(8,128)S(1)}, /*index=5*/s32[]{:T(128)}, s32[]{:T(128)}) while((s32[]{:T(128)}, f32[2,1024]{1,0:T(2,128)S(1)}, bf16[8,1024,128]{2,1,0:T(8,128)(2,1)}, ...), condition=%wide.region_9.10_spmd.clone, body=%wide.region_6.9_spmd.clone.sunk | while | flops 273682432 | bytes 569947 | solution.py:90
  77.1 2.4 multiply_reduce_fusion.14
  79.5 2.4 multiply_reduce_fusion.14
  81.9 2.4 multiply_reduce_fusion.14
  84.3 2.4 multiply_reduce_fusion.14
  86.8 2.4 multiply_reduce_fusion.14
  89.2 2.4 multiply_reduce_fusion.14
  91.6 2.4 multiply_reduce_fusion.14
  94.1 2.4 multiply_reduce_fusion.14
  96.5 5.8 psum.71
  102.3 15.6 %while.77 = (s32[]{:T(128)}, f32[8,1024]{1,0:T(8,128)S(1)}, f32[1024]{0:T(1024)S(1)}, bf16[8,1024,128]{2,1,0:T(8,128)(2,1)}, bf16[1024,128]{1,0:T(8,128)(2,1)S(1)}, /*index=5*/s32[]{:T(128)}, s32[]{:T(128)}) while((s32[]{:T(128)}, f32[8,1024]{1,0:T(8,128)S(1)}, f32[1024]{0:T(1024)S(1)}, bf16[8,1024,128]{2,1,0:T(8,128)(2,1)}, ...), condition=%wide.region_13.14_spmd, body=%wide.region_11.13_spmd.sunk | while | flops 271580160 | bytes 541265 | solution.py:74
  118.5 33.6 %psum.72 = f32[8192]{0:T(1024)S(1)} all-reduce(f32[8192]{0:T(1024)} %bitcast.158), channel_id=1, replica_groups=mesh['batch'=8,'proto'=4] {'batch'}, use_global_device_ids=true, to_apply=%region_14.15 | all-reduce | flops 8192 | bytes 65536 | tf_op jit(solution)/shard_map/psum | solution.py:75
  153.5 15.0 %while.80 = (s32[]{:T(128)}, f32[1,1024]{1,0:T(1,128)S(1)}, bf16[8,1024,128]{2,1,0:T(8,128)(2,1)}, bf16[1024,128]{1,0:T(8,128)(2,1)S(1)}, f32[8,1024]{1,0:T(8,128)S(1)}, /*index=5*/s32[]{:T(128)}, s32[]{:T(128)}) while((s32[]{:T(128)}, f32[1,1024]{1,0:T(1,128)S(1)}, bf16[8,1024,128]{2,1,0:T(8,128)(2,1)}, ...), condition=%wide.region_17.18_spmd.clone, body=%wide.region_15.17_spmd.clone.sunk | while | flops 271582208 | bytes 553563 | solution.py:90
  168.5 5.7 psum.73
  174.2 15.6 %while.78 = (s32[]{:T(128)}, f32[8,1024]{1,0:T(8,128)S(1)}, f32[1024]{0:T(1024)S(1)}, bf16[8,1024,128]{2,1,0:T(8,128)(2,1)}, bf16[1024,128]{1,0:T(8,128)(2,1)S(1)}, /*index=5*/s32[]{:T(128)}, s32[]{:T(128)}) while((s32[]{:T(128)}, f32[8,1024]{1,0:T(8,128)S(1)}, f32[1024]{0:T(1024)S(1)}, bf16[8,1024,128]{2,1,0:T(8,128)(2,1)}, ...), condition=%wide.region_21.22_spmd, body=%wide.region_19.21_spmd.sunk | while | flops 271580160 | bytes 541265 | solution.py:74
  189.9 33.0 %psum.74 = f32[8192]{0:T(1024)S(1)} all-reduce(f32[8192]{0:T(1024)S(1)} %bitcast.159), channel_id=1, replica_groups=mesh['batch'=8,'proto'=4] {'batch'}, use_global_device_ids=true, to_apply=%region_22.23 | all-reduce | flops 8192 | bytes 65536 | tf_op jit(solution)/shard_map/psum | solution.py:75
  223.0 15.0 %while.81 = (s32[]{:T(128)}, f32[1,1024]{1,0:T(1,128)S(1)}, bf16[8,1024,128]{2,1,0:T(8,128)(2,1)}, bf16[1024,128]{1,0:T(8,128)(2,1)S(1)}, f32[8,1024]{1,0:T(8,128)S(1)}, /*index=5*/s32[]{:T(128)}, s32[]{:T(128)}) while((s32[]{:T(128)}, f32[1,1024]{1,0:T(1,128)S(1)}, bf16[8,1024,128]{2,1,0:T(8,128)(2,1)}, ...), condition=%wide.region_25.26_spmd.clone, body=%wide.region_23.25_spmd.clone.sunk | while | flops 271582208 | bytes 553563 | solution.py:90
  238.0 5.7 psum.75
  243.7 4.3 gather_fusion.1
  248.0 4.5 gather_fusion
  252.6 77.5 %while.82 = (s32[]{:T(128)}, f32[1024,128]{1,0:T(8,128)S(1)}, f32[8,1024,128]{2,1,0:T(8,128)}, bf16[8,1024,128]{2,1,0:T(8,128)(2,1)}, bf16[1024,128]{1,0:T(8,128...) while((s32[]{:T(128)}, f32[1024,128]{1,0:T(8,128)S(1)}, ...), condition=%wide.region_28.29_spmd.clone, body=%wide.region_27.28_spmd.clone.sunk | while | flops 1082392576 | bytes 27285680 | solution.py:113
  254.3 2.7 multiply_convert_fusion.4
  259.8 2.4 convolution_add_fusion.2
  264.0 2.7 multiply_convert_fusion.4
  269.5 2.4 convolution_add_fusion.2
  273.7 2.7 multiply_convert_fusion.4
  279.2 2.4 convolution_add_fusion.2
  283.4 2.7 multiply_convert_fusion.4
  288.9 2.4 convolution_add_fusion.2
  293.1 2.7 multiply_convert_fusion.4
  298.6 2.4 convolution_add_fusion.2
  302.8 2.7 multiply_convert_fusion.4
  308.3 2.4 convolution_add_fusion.2
  312.5 2.7 multiply_convert_fusion.4
  318.0 2.4 convolution_add_fusion.2
  322.2 2.7 multiply_convert_fusion.4
  327.7 2.4 convolution_add_fusion.2
  331.2 4.1 fusion.36
  335.3 9.9 %fusion.35 = f32[8192,128]{1,0:T(8,128)} fusion(bf16[8192,128]{1,0:T(8,128)(2,1)S(1)} %copy-done.3, f32[8,1024,128]{2,1,0:T(8,128)} %get-tuple-element.215, f32[8192]{0:T(1024)S(1)} %fusion.36, f32[8192]{0:T(1024)S(1)} %get-tuple-element.463, f32[8192]{0:T(1024)S(1)} %get-tuple-element.464), kind=kLoop, calls=%fused_computation.58 | loop fusion | flops 5242880 | bytes 10584064 | tf_op jit(solution)/shard_map/sub | solution.py:119
  345.2 17.0 %all-reduce.4.cloned.1.call-done = f32[1024,128]{0,1:T(8,128)} async-done(((f32[1024,128]{0,1:T(8,128)}), f32[1024,128]{0,1:T(8,128)}) %all-reduce.4.cloned.1.call-update) | async-done | bytes 524304 | tf_op jit(solution)/shard_map/psum | solution.py:116
  365.7 5.5 convolution_bitcast_fusion.1
  371.2 221.7 %all-reduce.6.cloned.1.call-done = (f32[1024,512]{0,1:T(8,128)}, f32[512,128]{1,0:T(8,128)}, f32[8192,128]{1,0:T(8,128)}) async-done(((f32[1024,512]{0,1:T(8,128)}, f32[512,128]{1,0:T(8,128)}, f32[8192,128]{1,0:T(8,128)}), (f32[1024,512]{0,1:T(8,128)}, f32[512,128]{1,0:T(8,128)}, f32[8192,128]{1,0:T(8,128)})) %all-reduce.6.cloned.1.call-update) | async-done | bytes 6553616 | tf_op jit(solution)/shard_map/psum | solution.py:123
  592.9 2.9 copy.27
  596.6 4.5 copy.91
  (222 shorter events, 127.0 us)
Async XLA Ops:
  7.2 1.6 copy-start
  7.2 355.0 %all-reduce.4.cloned.1.call-start = ((), (), s32[]{:S(2)}) async-start(), calls=%async_computation | async-start | bytes 1048576 | tf_op jit(solution)/shard_map/psum | solution.py:116
  8.8 4.1 copy-start.8
  12.9 1.0 copy-start.4
  15.7 2.9 copy-start.2
  223.0 20.7 %copy-start.10 = (s32[1024]{0:T(1024)S(1)}, s32[1024]{0:T(1024)}, u32[]{:S(2)}) copy-start(s32[1024]{0:T(1024)} %param.20) | copy-start | bytes 12292
  252.6 1.7 copy-start.6
  257.0 1.3 copy-start.1
  262.3 1.7 copy-start.6
  266.7 1.3 copy-start.1
  272.0 1.7 copy-start.6
  276.4 1.3 copy-start.1
  281.6 1.7 copy-start.6
  286.1 1.3 copy-start.1
  291.3 1.7 copy-start.6
  295.8 1.3 copy-start.1
  301.0 1.7 copy-start.6
  305.5 1.3 copy-start.1
  310.7 1.7 copy-start.6
  315.2 1.3 copy-start.1
  320.4 1.7 copy-start.6
  324.9 1.3 copy-start.1
  331.1 261.8 %all-reduce.6.cloned.1.call-start = ((), (), s32[]{:S(2)}) async-start(), calls=%async_computation.1 | async-start | bytes 13107200 | tf_op jit(solution)/shard_map/psum | solution.py:123
  331.2 4.1 copy-start.3
  345.2 20.5 %copy-start.9 = (bf16[512,128]{1,0:T(8,128)(2,1)S(1)}, bf16[512,128]{1,0:T(8,128)(2,1)}, u32[]{:S(2)}) copy-start(bf16[512,128]{1,0:T(8,128)(2,1)} %param.22) | copy-start | bytes 393220
  362.2 2.3 copy-start.5
  592.9 2.9 copy-start.7
Sparse Core Ops, SparseCore 0:
  331.3 30.8 all-reduce.3
  371.4 221.5 all-reduce.5
where the time goes:
time: 611 us; the launch traced here: 608 us
  waiting for transfers between devices  239 us (39%)
  matrix products  168 us (27%)
  blocking collectives  123 us (20%)
  local copies, waits for them, and re-layouts  37.1 us (6%)
  other arithmetic  24 us (4%)
  between operations  14.3 us (2%)
    psum x1, waiting for transfers between devices, body(): lax.psum((proto_part, grad_in, grad_out), 'batch')  222 us
    dot_general x64, matrix products, scores_of(): lax.dot_general(rows_in, unit, (((1,), (1,)), ((), ())), preferred_elemen...  126 us
    psum x3, blocking collectives, body(): col_scale = 1.0 / lax.psum(column_partial_value, 'batch')  106 us
    dot_general x8, matrix products, finish(): jnp.dot(d_scores, block, preferred_element_type=jnp.float32)  19.4 us
    psum x3, blocking collectives, body(): summed = lax.psum(partial_value, 'proto')  17.1 us
    psum x1, waiting for transfers between devices, body(): view_grad = lax.psum(view_partial, 'proto')  17 us
    unnamed x25, local copies, waits for them, and re-layouts  12.5 us
  transfers between devices with their start and end apart: 2, of which 2 were waited for; matrix products, arithmetic and copies ran while one was open for 2% of the time, Pallas kernels for 0%

commit v1 on v0

v1 whole, which is shorter than its diff:
```python
import functools
import math

import jax
import jax.numpy as jnp
from jax import lax
from jax.experimental import pallas as pl
from jax.experimental.pallas import tpu as pltpu
from jax.sharding import PartitionSpec as P

ITERS = 3
norm_eps = 1e-06
code_temp = 0.05
pred_temp = 0.1
loss_scale = 64.0
GRAD_SCALE = loss_scale / pred_temp
EXP2_SCALE = math.log2(math.e) / pred_temp
GELU_K = math.sqrt(2.0 / math.pi)
GELU_A = 0.044715

f32 = jnp.float32
bf16 = jnp.bfloat16
NN = (((1,), (0,)), ((), ()))
NT = (((1,), (1,)), ((), ()))
TN = (((0,), (0,)), ((), ()))
VMEM_LIMIT = 56 * 1024 * 1024


def dot(a, b, dims=NN):
    return lax.dot_general(a, b, dims, preferred_element_type=f32)


def params(*semantics):
    return pltpu.CompilerParams(
        dimension_semantics=semantics or None, vmem_limit_bytes=VMEM_LIMIT
    )


def split_rows(vec):
    hi = vec.astype(bf16)
    lo = (vec - hi.astype(f32)).astype(bf16)
    n = vec.shape[1]
    row = lax.broadcasted_iota(jnp.int32, (8, n), 0)
    hi8 = jnp.broadcast_to(hi.astype(f32), (8, n))
    lo8 = jnp.broadcast_to(lo.astype(f32), (8, n))
    return jnp.where(row == 0, hi8, jnp.where(row == 1, lo8, 0.0)).astype(bf16)


def to_column(vec):
    n = vec.shape[1]
    return jnp.broadcast_to(vec, (8, n)).T[:, :1]


def swap_lanes(x):
    half = x.shape[1] // 2
    return jnp.concatenate([x[:, half:], x[:, :half]], axis=1)


def swap_rows(x):
    half = x.shape[0] // 2
    return jnp.concatenate([x[half:], x[:half]], axis=0)


def full(shape):
    return pl.BlockSpec(shape, lambda *_: (0,) * len(shape))


def head_kernel(emb, pairing, w_in, w_out, pre, hid, raw, views, views_t, pos, scratch):
    step = pl.program_id(0)
    rows = emb.shape[0]
    pre_act = dot(emb[...], w_in[...])
    pre[...] = pre_act
    t = jnp.tanh(GELU_K * (pre_act + GELU_A * (pre_act * pre_act * pre_act)))
    hidden = (0.5 * pre_act * (1.0 + t)).astype(bf16)
    hid[...] = hidden
    raw_out = dot(hidden, w_out[...])
    raw[...] = raw_out
    inv = lax.rsqrt(jnp.sum(raw_out * raw_out, axis=1, keepdims=True) + norm_eps)
    scratch[pl.ds(pl.multiple_of(step * rows, rows), rows), :] = (raw_out * inv).astype(bf16)

    @pl.when(step == pl.num_programs(0) - 1)
    def _():
        mate = pairing[...]
        n = mate.shape[1]
        lane = lax.broadcasted_iota(jnp.int32, (1, n), 1)
        first = lane < mate
        low = jnp.minimum(lane, mate)
        sub = lax.broadcasted_iota(jnp.int32, (n, n), 0)
        before = jnp.where(sub < low, 1.0, 0.0).astype(bf16)
        first8 = jnp.broadcast_to(jnp.where(first, 1.0, 0.0), (8, n)).astype(bf16)
        rank = dot(first8, before)[:1].astype(jnp.int32)
        place = jnp.where(first, rank, rank + n // 2)
        pos[...] = place
        move = jnp.where(sub == place, 1.0, 0.0).astype(bf16)
        ordered = dot(move, scratch[...])
        views[...] = ordered.astype(bf16)
        views_t[...] = ordered.T.astype(bf16)


def head(embeddings, pairing, w_in, w_out):
    rows, wide = embeddings.shape
    hidden = w_in.shape[1]
    depth = w_out.shape[1]
    steps = 4
    block = rows // steps
    return pl.pallas_call(
        head_kernel,
        grid=(steps,),
        in_specs=[
            pl.BlockSpec((block, wide), lambda i: (i, 0)),
            full((1, rows)),
            full((wide, hidden)),
            full((hidden, depth)),
        ],
        out_specs=[
            pl.BlockSpec((block, hidden), lambda i: (i, 0)),
            pl.BlockSpec((block, hidden), lambda i: (i, 0)),
            pl.BlockSpec((block, depth), lambda i: (i, 0)),
            full((rows, depth)),
            full((depth, rows)),
            full((1, rows)),
        ],
        out_shape=[
            jax.ShapeDtypeStruct((rows, hidden), f32),
            jax.ShapeDtypeStruct((rows, hidden), bf16),
            jax.ShapeDtypeStruct((rows, depth), f32),
            jax.ShapeDtypeStruct((rows, depth), bf16),
            jax.ShapeDtypeStruct((depth, rows), bf16),
            jax.ShapeDtypeStruct((1, rows), jnp.int32),
        ],
        scratch_shapes=[pltpu.VMEM((rows, depth), bf16)],
        compiler_params=params("arbitrary"),
        name="head",
    )(embeddings, pairing.reshape(1, rows), w_in, w_out)


def unit_of(protos):
    proto_f = protos.astype(f32)
    inv = lax.rsqrt(jnp.sum(proto_f * proto_f, axis=1, keepdims=True) + norm_eps)
    return proto_f, inv, proto_f * inv


def first_kernel(chunk, views, protos, expo, unit_t, col, tot, along, tot_acc, along_acc):
    step = pl.program_id(0)
    rows, depth = views.shape

    @pl.when(step == 0)
    def _():
        tot_acc[...] = jnp.zeros_like(tot_acc)
        along_acc[...] = jnp.zeros_like(along_acc)

    _, _, unit = unit_of(protos[...])
    unit16 = unit.astype(bf16)
    unit_tr = unit.T.astype(bf16)
    unit_t[...] = unit_tr
    width = unit.shape[0]
    running = jnp.zeros((8, width), f32)
    for start in range(0, rows, chunk):
        part = pl.ds(start, chunk)
        scores = dot(views[part, :], unit_tr)
        soft = jnp.exp2(scores * EXP2_SCALE)
        hard = soft * soft
        expo[part, :] = hard.astype(bf16)
        running = running + jnp.sum(hard.reshape(chunk // 8, 8, width), axis=0)
        lanes = soft[:, :128]
        for k in range(1, width // 128):
            lanes = lanes + soft[:, k * 128 : (k + 1) * 128]
        tot_acc[part, :] += lanes
        along_acc[part, :] += dot(soft.astype(bf16), unit16)
    col[...] = jnp.sum(running, axis=0, keepdims=True)

    @pl.when(step == pl.num_programs(0) - 1)
    def _():
        tot[...] = jnp.sum(tot_acc[...].T, axis=0, keepdims=True)
        along[...] = along_acc[...]


def first_pass(views, protos):
    rows, depth = views.shape
    width = protos.shape[0]
    block = min(512, width)
    chunk = min(256, rows)
    return pl.pallas_call(
        functools.partial(first_kernel, chunk),
        grid=(width // block,),
        in_specs=[full((rows, depth)), pl.BlockSpec((block, depth), lambda j: (j, 0))],
        out_specs=[
            pl.BlockSpec((rows, block), lambda j: (0, j)),
            pl.BlockSpec((depth, block), lambda j: (0, j)),
            pl.BlockSpec((1, block), lambda j: (0, j)),
            full((1, rows)),
            full((rows, depth)),
        ],
        out_shape=[
            jax.ShapeDtypeStruct((rows, width), bf16),
            jax.ShapeDtypeStruct((depth, width), bf16),
            jax.ShapeDtypeStruct((1, width), f32),
            jax.ShapeDtypeStruct((1, rows), f32),
            jax.ShapeDtypeStruct((rows, depth), f32),
        ],
        scratch_shapes=[pltpu.VMEM((rows, 128), f32), pltpu.VMEM((rows, depth), f32)],
        compiler_params=params("arbitrary"),
        name="first_pass",
    )(views, protos)


def rowsum_kernel(count, last, *refs):
    expo = refs[0]
    parts = refs[1 : 1 + count]
    if last:
        unit_t, scale, out, code, acc = refs[1 + count :]
    else:
        scale, out, acc = refs[1 + count :]
    step = pl.program_id(0)

    @pl.when(step == 0)
    def _():
        acc[...] = jnp.zeros_like(acc)

    total = parts[0][...]
    for other in parts[1:]:
        total = total + other[...]
    inverse = 1.0 / total
    scale[...] = inverse
    weights = split_rows(inverse)
    if last:
        scaled = (unit_t[...].astype(f32) * inverse).astype(bf16)
        pad = jnp.zeros((128 - 8, weights.shape[1]), bf16)
        weights = jnp.concatenate([scaled, weights, pad], axis=0)
    acc[...] += dot(expo[...], weights, NT)

    @pl.when(step == pl.num_programs(0) - 1)
    def _():
        depth = acc.shape[1] - 128 if last else 0
        sums = acc[:, depth:] if last else acc[...]
        sums = sums.T
        out[...] = sums[0:1] + sums[1:2]
        if last:
            code[...] = acc[:, :depth]


def rowsum(expo, parts, unit_t=None):
    rows, width = expo.shape
    block = min(1024, width)
    last = unit_t is not None
    vec = pl.BlockSpec((1, block), lambda j: (0, j))
    in_specs = [pl.BlockSpec((rows, block), lambda j: (0, j))] + [vec] * len(parts)
    out_specs = [vec, full((1, rows))]
    out_shape = [jax.ShapeDtypeStruct((1, width), f32), jax.ShapeDtypeStruct((1, rows), f32)]
    operands = [expo, *parts]
    lanes = 8
    if last:
        depth = unit_t.shape[0]
        in_specs.append(pl.BlockSpec((depth, block), lambda j: (0, j)))
        operands.append(unit_t)
        out_specs.append(full((rows, depth)))
        out_shape.append(jax.ShapeDtypeStruct((rows, depth), f32))
        lanes = depth + 128
    return pl.pallas_call(
        functools.partial(rowsum_kernel, len(parts), last),
        grid=(width // block,),
        in_specs=in_specs,
        out_specs=out_specs,
        out_shape=out_shape,
        scratch_shapes=[pltpu.VMEM((rows, lanes), f32)],
        compiler_params=params("arbitrary"),
        name="rowsum_last" if last else "rowsum",
    )(*operands)


def colsum_kernel(expo, total, out):
    weights = split_rows(1.0 / total[...])
    sums = dot(weights, expo[...])
    out[...] = sums[0:1] + sums[1:2]


def colsum(expo, total):
    rows, width = expo.shape
    block = min(1024, width)
    return pl.pallas_call(
        colsum_kernel,
        grid=(width // block,),
        in_specs=[pl.BlockSpec((rows, block), lambda j: (0, j)), full((1, rows))],
        out_specs=pl.BlockSpec((1, block), lambda j: (0, j)),
        out_shape=jax.ShapeDtypeStruct((1, width), f32),
        compiler_params=params("arbitrary"),
        name="colsum",
    )(expo, total)


def proto_first_kernel(count, *refs):
    protos = refs[0]
    views = refs[1 : 1 + count]
    totals = refs[1 + count : 1 + 2 * count]
    expo, grad, weights = refs[1 + 2 * count :]
    rows = views[0].shape[1]

    @pl.when(pl.program_id(0) == 0)
    def _():
        for k in range(count):
            scale = GRAD_SCALE / totals[k][...]
            weights[:, k * rows : (k + 1) * rows] = (views[k][...].astype(f32) * scale).astype(bf16)

    _, _, unit = unit_of(protos[...])
    unit16 = unit.astype(bf16)
    running = jnp.zeros(grad.shape, f32)
    for k in range(count):
        part = pl.ds(k * rows, rows)
        soft = jnp.exp2(dot(unit16, views[k][...]) * EXP2_SCALE)
        expo[:, part] = (soft * soft).astype(bf16)
        running = running + dot(soft.astype(bf16), weights[:, part], NT)
    grad[...] = running


def proto_first(protos, views_t, totals):
    width, depth = protos.shape
    count = len(views_t)
    rows = views_t[0].shape[1]
    block = min(256, width)
    return pl.pallas_call(
        functools.partial(proto_first_kernel, count),
        grid=(width // block,),
        in_specs=[pl.BlockSpec((block, depth), lambda j: (j, 0))]
        + [full((depth, rows))] * count
        + [full((1, rows))] * count,
        out_specs=[
            pl.BlockSpec((block, count * rows), lambda j: (j, 0)),
            pl.BlockSpec((block, depth), lambda j: (j, 0)),
        ],
        out_shape=[
            jax.ShapeDtypeStruct((width, count * rows), bf16),
            jax.ShapeDtypeStruct((width, depth), f32),
        ],
        scratch_shapes=[pltpu.VMEM((depth, count * rows), bf16)],
        compiler_params=params("arbitrary"),
        name="proto_first",
    )(protos, *views_t, *totals)


def proto_last_kernel(count, *refs):
    expo, grad, scale, protos = refs[:4]
    views = refs[4 : 4 + count]
    totals = refs[4 + count : 4 + 2 * count]
    out, weights = refs[4 + 2 * count :]
    rows = views[0].shape[1]

    @pl.when(pl.program_id(0) == 0)
    def _():
        for k in range(count):
            mates = swap_lanes(views[k][...])
            weights[:, k * rows : (k + 1) * rows] = (
                mates.astype(f32) * (GRAD_SCALE / totals[k][...])
            ).astype(bf16)

    unit_grad = grad[...] - to_column(scale[...]) * dot(expo[...], weights[...], NT)
    proto_f, inv, _ = unit_of(protos[...])
    inner = jnp.sum(proto_f * unit_grad, axis=1, keepdims=True)
    out[...] = (inv * unit_grad - proto_f * (inv * inv * inv) * inner).astype(bf16)


def proto_last(expo, grad, scale, protos, views_t, totals):
    width, depth = protos.shape
    count = len(views_t)
    rows = views_t[0].shape[1]
    block = min(256, width)
    return pl.pallas_call(
        functools.partial(proto_last_kernel, count),
        grid=(width // block,),
        in_specs=[
            pl.BlockSpec((block, count * rows), lambda j: (j, 0)),
            pl.BlockSpec((block, depth), lambda j: (j, 0)),
            pl.BlockSpec((1, block), lambda j: (0, j)),
            pl.BlockSpec((block, depth), lambda j: (j, 0)),
        ]
        + [full((depth, rows))] * count
        + [full((1, rows))] * count,
        out_specs=pl.BlockSpec((block, depth), lambda j: (j, 0)),
        out_shape=jax.ShapeDtypeStruct((width, depth), bf16),
        scratch_shapes=[pltpu.VMEM((depth, count * rows), bf16)],
        compiler_params=params("arbitrary"),
        name="proto_last",
    )(expo, grad, scale, protos, *views_t, *totals)


def view_grad_kernel(along, code, tot, total, out):
    soft = along[...] * to_column(GRAD_SCALE / tot[...])
    hard = swap_rows(code[...] * to_column(GRAD_SCALE / total[...]))
    out[...] = (soft - hard).astype(out.dtype)


def view_grad_part(along, code, tot, total):
    return pl.pallas_call(
        view_grad_kernel,
        out_shape=jax.ShapeDtypeStruct(along.shape, bf16),
        compiler_params=params(),
        name="view_grad",
    )(along, code, tot, total)


def backward_kernel(count, grad_a, grad_b, pos, raw, hid, pre, emb, hid_part, w_out, g_in, g_out):
    total = grad_a[...].astype(f32) + grad_b[...].astype(f32)
    n, depth = raw.shape
    place = jnp.broadcast_to(pos[...].astype(f32), (8, n)).T[:, :1].astype(jnp.int32)
    lane = lax.broadcasted_iota(jnp.int32, (n, n), 1)
    move = jnp.where(lane == place, 1.0, 0.0).astype(bf16)
    hi = total.astype(bf16)
    lo = (total - hi.astype(f32)).astype(bf16)
    moved = dot(move, jnp.concatenate([hi, lo], axis=1))
    grad = moved[:, :depth] + moved[:, depth:]
    raw_out = raw[...]
    inv = lax.rsqrt(jnp.sum(raw_out * raw_out, axis=1, keepdims=True) + norm_eps)
    inner = jnp.sum(raw_out * grad, axis=1, keepdims=True)
    d_raw = (inv * grad - raw_out * (inv * inv * inv) * inner).astype(bf16)
    g_out[...] = dot(hid_part[...], d_raw, TN)
    d_hidden = dot(d_raw, w_out[...], NT)
    v = pre[...]
    t = jnp.tanh(GELU_K * (v + GELU_A * (v * v * v)))
    slope = 0.5 * (1.0 + t) + (0.5 * GELU_K) * v * (1.0 - t * t) * (1.0 + (3.0 * GELU_A) * (v * v))
    d_pre = (slope * d_hidden).astype(bf16)
    g_in[...] = dot(emb[...], d_pre, TN)


def backward(grad_a, grad_b, pos, raw, hid, pre, emb, hid_part, w_out):
    return pl.pallas_call(
        functools.partial(backward_kernel, 1),
        out_shape=[
            jax.ShapeDtypeStruct((emb.shape[1], pre.shape[1]), f32),
            jax.ShapeDtypeStruct((hid_part.shape[1], raw.shape[1]), f32),
        ],
        compiler_params=params(),
        name="backward",
    )(grad_a, grad_b, pos, raw, hid, pre, emb, hid_part, w_out)


def body(nb, npr, embeddings, pairing, w_in, w_out, prototypes):
    b = lax.axis_index("batch")
    p = lax.axis_index("proto")
    rows, wide = embeddings.shape
    width, depth = prototypes.shape
    hidden_n = w_in.shape[1]
    own = width // nb

    def shifted(x, s):
        return lax.ppermute(x, "batch", [(i, (i + s) % nb) for i in range(nb)])

    def everyone(x):
        return [x] + [shifted(x, s) for s in range(1, nb)]

    pre, hid, raw, views, views_t, pos = head(embeddings, pairing, w_in, w_out)
    views_all = everyone(views_t)
    expo, unit_t, col, tot, along = first_pass(views, prototypes)
    protos_own = lax.dynamic_slice_in_dim(prototypes, b * own, own, 0)

    scale, row = rowsum(expo, everyone(col))
    summed = lax.psum(jnp.concatenate([row, tot], axis=0), "proto")
    total, tot = summed[:1], summed[1:]
    expo_own, grad_own = proto_first(protos_own, views_all, everyone(tot))
    for sweep in range(1, ITERS):
        col = colsum(expo, total)
        if sweep < ITERS - 1:
            scale, row = rowsum(expo, everyone(col))
        else:
            scale, row, code = rowsum(expo, everyone(col), unit_t)
        total = lax.psum(row, "proto")

    scale_own = lax.dynamic_slice_in_dim(scale, b * own, own, 1)
    proto_part = proto_last(
        expo_own, grad_own, scale_own, protos_own, views_all, everyone(total)
    )
    grad_proto = lax.all_gather(proto_part, "batch", axis=0, tiled=True).astype(f32)

    part = view_grad_part(along, code, tot, total)
    step = 1
    other = jnp.zeros_like(part)
    while step < npr:
        other = lax.ppermute(part, "proto", [(i, i ^ step) for i in range(npr)])
        if step * 2 < npr:
            part = (part.astype(f32) + other.astype(f32)).astype(bf16)
        step *= 2
    emb_part = lax.dynamic_slice_in_dim(embeddings, p * (wide // npr), wide // npr, 1)
    hid_part = lax.dynamic_slice_in_dim(hid, p * (hidden_n // npr), hidden_n // npr, 1)
    g_in, g_out = backward(part, other, pos, raw, hid, pre, emb_part, hid_part, w_out)
    both = jnp.concatenate([g_in.reshape(nb, -1), g_out.reshape(nb, -1)], axis=1)
    both = lax.psum_scatter(both, "batch", scatter_dimension=0, tiled=True).astype(bf16)
    both = lax.all_gather(both, ("proto", "batch"), axis=0, tiled=True)
    cut = g_in.size // nb
    grad_in = both[:, :cut].astype(f32).reshape(wide, hidden_n)
    grad_out = both[:, cut:].astype(f32).reshape(hidden_n, depth)
    return (grad_in, grad_out, grad_proto)


def solution(mesh):
    return jax.shard_map(
        functools.partial(body, mesh.shape["batch"], mesh.shape["proto"]),
        mesh=mesh,
        in_specs=(P("batch", None), P("batch"), P(), P(), P("proto", None)),
        out_specs=(P(), P(), P("proto", None)),
        check_vma=False,
    )
```

time: 611 us -> 378 us (0.62)
  matrix products: 168 us -> 0 us
  waiting for transfers between devices: 239 us -> 75.7 us
  Pallas kernels: 0 us -> 121 us
  starting transfers between devices: 0.08 us -> 77.3 us
  blocking collectives: 123 us -> 63.2 us
  other arithmetic: 24 us -> 5.78 us
  local copies, waits for them, and re-layouts: 37.1 us -> 19.3 us
    psum x2 -> x0, waiting for transfers between devices: 239 us -> none  [the longest x1 222 us: body(): lax.psum((proto_part, grad_in, grad_out), 'batch')]
    dot_general x84 -> x0, matrix products: 168 us -> none  [the longest x64 126 us: scores_of(): lax.dot_general(rows_in, unit, (((1,), (1,)), ((), ())), preferred_elemen...]
    pallas_call x0 -> x11, Pallas kernels: none -> 121 us  [the longest x3 34.8 us: rowsum(): pl.pallas_call(functools.partial(rowsum_kernel, len(parts), last), grid=(...]
    psum x6 -> x3, blocking collectives: 123 us -> 18.4 us  [the longest x2 12.7 us: body(): total = lax.psum(row, 'proto')]
    ppermute x0 -> x44, starting transfers between devices: none -> 77.3 us  [the longest x42 75.1 us: shifted(): return lax.ppermute(x, 'batch', [(i, (i + s) % nb) for i in range(nb)])]
    all_gather x0 -> x2, waiting for transfers between devices: none -> 44.9 us  [the longest x1 44.9 us: body(): lax.all_gather(proto_part, 'batch', axis=0, tiled=True).astype(f32)]
    unnamed x0 -> x1, blocking collectives: none -> 44.8 us
    ppermute x0 -> x44, waiting for transfers between devices: none -> 30.8 us  [the longest x42 26.7 us: shifted(): return lax.ppermute(x, 'batch', [(i, (i + s) % nb) for i in range(nb)])]
  transfers between devices with their start and end apart: 2 -> 46, of which waited for: 2 -> 16; matrix products, arithmetic and copies ran while one was open for 2% -> 3% of each run, Pallas kernels for 0% -> 7%
where the time goes in v1:
time: 378 us; the launch traced here: 377 us
  Pallas kernels  121 us (32%)
  starting transfers between devices  77.3 us (20%)
  waiting for transfers between devices  75.7 us (20%)
  blocking collectives  63.2 us (17%)
  local copies, waits for them, and re-layouts  19.3 us (5%)
  between operations  14.6 us (4%)
  other arithmetic  5.78 us (2%)
    ppermute x42, starting transfers between devices, shifted(): return lax.ppermute(x, 'batch', [(i, (i + s) % nb) for i in range(nb)])  75.1 us
    all_gather x1, waiting for transfers between devices, body(): lax.all_gather(proto_part, 'batch', axis=0, tiled=True).astype(f32)  44.9 us
    unnamed x1, blocking collectives  44.8 us
    pallas_call x3, Pallas kernels, rowsum(): pl.pallas_call(functools.partial(rowsum_kernel, len(parts), last), grid=(...  34.8 us
    ppermute x42, waiting for transfers between devices, shifted(): return lax.ppermute(x, 'batch', [(i, (i + s) % nb) for i in range(nb)])  26.7 us
    pallas_call x1, Pallas kernels, first_pass(): pl.pallas_call(functools.partial(first_kernel, chunk), grid=(width // blo...  25 us
    pallas_call x2, Pallas kernels, colsum(): pl.pallas_call(colsum_kernel, grid=(width // block,), in_specs=[pl.BlockS...  19.3 us
    pallas_call x1, Pallas kernels, proto_first(): pl.pallas_call(functools.partial(proto_first_kernel, count), grid=(width...  15.1 us
  transfers between devices with their start and end apart: 46, of which 16 were waited for; matrix products, arithmetic and copies ran while one was open for 3% of the time, Pallas kernels for 7%

profile of v1, /device:TPU:0, one launch (start us, length us, event | category | flops | bytes accessed | tf_op | source)
XLA Modules:
  0.0 377.1 jit_solution(2752304249431715529)
XLA Ops:
  7.2 7.4 %head.1 = (f32[1024,512]{1,0:T(8,128)}, bf16[1024,512]{1,0:T(8,128)(2,1)}, f32[1024,128]{1,0:T(8,128)}, bf16[1024,128]{1,0:T(8,128)(2,1)}, bf16[128,1024]{1,0:T(8,128)(2,1)}, /*index=5*/s32[1,1024]{1,0:T(1,128)}) custom-call(bf16[1024,1024]{1,0:T(8,128)(2,1)} %emb.1, s32[1,1024]{1,0:T(1,128)} %bitcast.9, bf16[1024,512]{1,0:T(8,128)(2,1)} %w_in.1, ...), custom_call_target="tpu_custom_call" | custom-call | tf_op jit(solution)/shard_map/head/pallas_call | solution.py:106
  14.6 25.0 %first_pass.1 = (bf16[1024,8192]{1,0:T(8,128)(2,1)}, bf16[128,8192]{1,0:T(8,128)(2,1)}, f32[1,8192]{1,0:T(1,128)}, f32[1,1024]{1,0:T(1,128)}, f32[1024,128]{1,0:T(8,128)}) custom-call(bf16[1024,128]{1,0:T(8,128)(2,1)} %get-tuple-element.23.views, bf16[8192,128]{1,0:T(8,128)(2,1)} %protos.1), custom_call_target="tpu_custom_call" | custom-call | tf_op jit(solution)/shard_map/first_pass/pallas_call | solution.py:183
  39.6 3.0 collective-permute-start
  44.2 2.5 collective-permute-start.2
  48.0 2.6 collective-permute-start.4
  56.7 11.4 %rowsum.2 = (f32[1,8192]{1,0:T(1,128)}, f32[1,1024]{1,0:T(1,128)}) custom-call(bf16[1024,8192]{1,0:T(8,128)(2,1)} %get-tuple-element.25.refs_0_.expo, f32[1,8192]{1,0:T(1,128)} %get-tuple-element.26.refs_1_, f32[1,8192]{1,0:T(1,128)} %copy-done.13, f32[1,8192]{1,0:T(1,128)} %copy-done.16, f32[1,8192]{1,0:T(1,128)} %copy-done.19, f32[1,8192]{1,0:T(1,128)} %copy-done.22, ...), custom_call_target="tpu_custom_call" | custom-call | tf_op jit(solution)/shard_map/rowsum/pallas_call | solution.py:259
  68.8 5.8 %psum.21 = f32[2,1024]{1,0:T(2,128)S(1)} all-reduce(f32[2,1024]{1,0:T(2,128)S(1)} %pad_maximum_fusion.1), channel_id=1, replica_groups=mesh['batch'=8,'proto'=4] {'proto'}, use_global_device_ids=true, to_apply=%region_0.0 | all-reduce | flops 2048 | bytes 16384 | tf_op jit(solution)/shard_map/psum | solution.py:455
  75.2 9.7 %colsum.2.refs_1_ = f32[1,8192]{1,0:T(1,128)} custom-call(bf16[1024,8192]{1,0:T(8,128)(2,1)} %get-tuple-element.25.refs_0_.expo, f32[1,1024]{1,0:T(1,128)} %get-tuple-element.44.total), custom_call_target="tpu_custom_call" | custom-call | tf_op jit(solution)/shard_map/colsum/pallas_call | solution.py:280
  86.5 2.2 collective-permute-start.9
  88.7 2.1 collective-permute-start.10
  90.8 3.1 collective-permute-start.11
  96.1 1.9 collective-permute-done.12.refs_7_
  99.2 11.4 %rowsum.3 = (f32[1,8192]{1,0:T(1,128)}, f32[1,1024]{1,0:T(1,128)}) custom-call(bf16[1024,8192]{1,0:T(8,128)(2,1)} %get-tuple-element.25.refs_0_.expo, f32[1,8192]{1,0:T(1,128)} %colsum.2.refs_1_, f32[1,8192]{1,0:T(1,128)} %copy-done.14, f32[1,8192]{1,0:T(1,128)} %copy-done.17, f32[1,8192]{1,0:T(1,128)} %copy-done.20, f32[1,8192]{1,0:T(1,128)} %copy-done.23, ...), custom_call_target="tpu_custom_call" | custom-call | tf_op jit(solution)/shard_map/rowsum/pallas_call | solution.py:259
  110.6 6.2 %psum.22.total = f32[1,1024]{1,0:T(1,128)} all-reduce(f32[1,1024]{1,0:T(1,128)} %get-tuple-element.29), channel_id=1, replica_groups=mesh['batch'=8,'proto'=4] {'proto'}, use_global_device_ids=true, to_apply=%region_1.0 | all-reduce | flops 1024 | bytes 8192 | tf_op jit(solution)/shard_map/psum | solution.py:464
  116.9 9.7 %colsum.3.refs_1_ = f32[1,8192]{1,0:T(1,128)} custom-call(bf16[1024,8192]{1,0:T(8,128)(2,1)} %get-tuple-element.25.refs_0_.expo, f32[1,1024]{1,0:T(1,128)} %psum.22.total), custom_call_target="tpu_custom_call" | custom-call | tf_op jit(solution)/shard_map/colsum/pallas_call | solution.py:280
  127.8 1.8 collective-permute-start.15
  130.7 2.6 collective-permute-start.17
  133.3 1.9 collective-permute-start.18
  135.8 2.0 collective-permute-start.20
  140.5 11.9 %rowsum_last.1 = (f32[1,8192]{1,0:T(1,128)}, f32[1,1024]{1,0:T(1,128)}, f32[1024,128]{1,0:T(8,128)}) custom-call(bf16[1024,8192]{1,0:T(8,128)(2,1)} %get-tuple-element.25.refs_0_.expo, f32[1,8192]{1,0:T(1,128)} %colsum.3.refs_1_, f32[1,8192]{1,0:T(1,128)} %copy-done.12, f32[1,8192]{1,0:T(1,128)} %copy-done.15, f32[1,8192]{1,0:T(1,128)} %copy-done.18, ...), custom_call_target="tpu_custom_call" | custom-call | tf_op jit(solution)/shard_map/rowsum_last/pallas_call | solution.py:259
  152.4 6.4 %psum.23.total.refs_12_ = f32[1,1024]{1,0:T(1,128)} all-reduce(f32[1,1024]{1,0:T(1,128)} %get-tuple-element.32), channel_id=1, replica_groups=mesh['batch'=8,'proto'=4] {'proto'}, use_global_device_ids=true, to_apply=%region_2.0 | all-reduce | flops 1024 | bytes 8192 | tf_op jit(solution)/shard_map/psum | solution.py:464
  158.9 2.6 view_grad.1
  161.5 1.6 collective-permute-done.21
  164.2 2.0 collective-permute-start.22
  166.9 1.7 constant_dynamic-slice_fusion.2.hid_part
  168.6 1.9 constant_dynamic-slice_fusion.3.emb
  170.4 2.4 collective-permute-done.22.grad_b
  173.6 6.5 %backward.1 = (f32[256,512]{1,0:T(8,128)}, f32[128,128]{1,0:T(8,128)}) custom-call(bf16[1024,128]{1,0:T(8,128)(2,1)} %copy-done.8, bf16[1024,128]{1,0:T(8,128)(2,1)} %copy-done.9, s32[1,1024]{1,0:T(1,128)} %get-tuple-element.33.pos, f32[1024,128]{1,0:T(8,128)} %get-tuple-element.34.raw, bf16[1024,512]{1,0:T(8,128)(2,1)} %get-tuple-element.35.hid, ...), custom_call_target="tpu_custom_call" | custom-call | tf_op jit(solution)/shard_map/backward/pallas_call | solution.py:424
  182.2 44.8 %all-reduce.2 = bf16[8,18432]{1,0:T(8,128)(2,1)S(1)} all-reduce(f32[8,18432]{1,0:T(8,128)S(1)} %pad_maximum_fusion), channel_id=2, replica_groups=mesh['batch'=8,'proto'=4] {'batch'}, use_global_device_ids=true, to_apply=%region_3.0.clone | all-reduce | flops 147456 | bytes 884736
  229.9 1.6 collective-permute-start.31
  231.5 2.9 collective-permute-start.32
  234.3 6.3 %collective-permute-done.30.refs_10_ = f32[1,1024]{1,0:T(1,128)S(1)} collective-permute-done((f32[1,1024]{1,0:T(1,128)S(1)}, f32[1,1024]{1,0:T(1,128)S(1)}, u32[]{:S(2)}, u32[]{:S(2)}) %collective-permute-start.30) | collective-permute-done | bytes 4128 | tf_op jit(solution)/shard_map/ppermute | solution.py:444
  240.8 2.4 collective-permute-start.35
  243.1 3.5 collective-permute-done.33.refs_13_
  246.7 3.1 collective-permute-start.37
  249.7 3.5 collective-permute-start.38
  255.3 2.9 collective-permute-start.27
  260.7 1.7 constant_dynamic-slice_fusion.1.refs_0_.refs_3_
  262.4 8.1 %collective-permute-done.25.refs_4_.refs_7_ = bf16[128,1024]{1,0:T(8,128)(2,1)S(1)} collective-permute-done((bf16[128,1024]{1,0:T(8,128)(2,1)S(1)}, bf16[128,1024]{1,0:T(8,128)(2,1)S(1)}, u32[]{:S(2)}, u32[]{:S(2)}) %collective-permute-start.25) | collective-permute-done | bytes 262176 | tf_op jit(solution)/shard_map/ppermute | solution.py:444
  270.4 2.7 collective-permute-start.39
  273.5 4.7 %collective-permute-start.41 = (f32[1,1024]{1,0:T(1,128)S(1)}, f32[1,1024]{1,0:T(1,128)S(1)}, u32[]{:S(2)}, u32[]{:S(2)}) collective-permute-start(f32[1,1024]{1,0:T(1,128)S(1)} %copy-done.11), channel_id=1, source_target_pairs={{0,20},{4,24},{8,28},{12,0},{16,4},{20,8},{24,12},{28,16},{1,21},{... | collective-permute-start | bytes 12296 | tf_op jit(solution)/shard_map/ppermute | solution.py:444
  278.1 6.8 %collective-permute-start.42 = (f32[1,1024]{1,0:T(1,128)S(1)}, f32[1,1024]{1,0:T(1,128)S(1)}, u32[]{:S(2)}, u32[]{:S(2)}) collective-permute-start(f32[1,1024]{1,0:T(1,128)S(1)} %copy-done.11), channel_id=1, source_target_pairs={{0,24},{4,28},{8,0},{12,4},{16,8},{20,12},{24,16},{28,20},{1,25},{... | collective-permute-start | bytes 12296 | tf_op jit(solution)/shard_map/ppermute | solution.py:444
  284.9 4.1 %collective-permute-start.43 = (f32[1,1024]{1,0:T(1,128)S(1)}, f32[1,1024]{1,0:T(1,128)S(1)}, u32[]{:S(2)}, u32[]{:S(2)}) collective-permute-start(f32[1,1024]{1,0:T(1,128)S(1)} %copy-done.11), channel_id=1, source_target_pairs={{0,28},{4,0},{8,4},{12,8},{16,12},{20,16},{24,20},{28,24},{1,29},{... | collective-permute-start | bytes 12296 | tf_op jit(solution)/shard_map/ppermute | solution.py:444
  290.3 15.1 %proto_first.1 = (bf16[1024,8192]{1,0:T(8,128)(2,1)}, f32[1024,128]{1,0:T(8,128)}) custom-call(bf16[1024,128]{1,0:T(8,128)(2,1)} %constant_dynamic-slice_fusion.1.refs_0_.refs_3_, bf16[128,1024]{1,0:T(8,128)(2,1)} %get-tuple-element.39.refs_1_.refs_4_, bf16[128,1024]{1,0:T(8,128)(2,1)} %copy-done.1, bf16[128,1024]{1,0:T(8,128)(2,1)} %copy-done.2, ...), custom_call_target="tpu_custom_call" | custom-call | tf_op jit(solution)/shard_map/proto_first/pallas_call | solution.py:320
  306.1 10.5 %proto_last.1 = bf16[1024,128]{1,0:T(8,128)(2,1)} custom-call(bf16[1024,8192]{1,0:T(8,128)(2,1)} %get-tuple-element.40.refs_0_, f32[1024,128]{1,0:T(8,128)} %get-tuple-element.41.refs_1_, f32[1,1024]{1,0:T(1,128)} %constant_dynamic-slice_fusion.refs_2_, bf16[1024,128]{1,0:T(8,128)(2,1)} %constant_dynamic-slice_fusion.1.refs_0_.refs_3_, ...), custom_call_target="tpu_custom_call" | custom-call | tf_op jit(solution)/shard_map/proto_last/pallas_call | solution.py:366
  316.7 2.4 copy.10
  321.5 44.9 %all-gather.4.cloned.1.call-done = bf16[8192,128]{1,0:T(8,128)(2,1)} async-done(((bf16[1024,128]{1,0:T(8,128)(2,1)}), bf16[8192,128]{1,0:T(8,128)(2,1)}) %all-gather.4.cloned.1.call-update) | async-done | bytes 2097168 | tf_op jit(solution)/shard_map/all_gather | solution.py:470
  366.4 3.9 %convert_element_type.21 = f32[8192,128]{1,0:T(8,128)} convert(bf16[8192,128]{1,0:T(8,128)(2,1)} %all-gather.4.cloned.1.call-done) | non-fusion elementwise | flops 1048576 | bytes 6291456 | tf_op jit(solution)/shard_map/convert_element_type | solution.py:470
  (177 shorter events, 37.6 us)
Async XLA Ops:
  7.2 309.5 %all-gather.6.cloned.1.call-start = ((), (), s32[]{:S(2)}) async-start(), calls=%async_computation.1 | async-start | bytes 2433024 | tf_op jit(solution)/shard_map/all_gather | solution.py:485
  39.6 11.0 %collective-permute-start = (f32[1,8192]{1,0:T(1,128)}, f32[1,8192]{1,0:T(1,128)S(1)}, u32[]{:S(2)}, u32[]{:S(2)}) collective-permute-start(f32[1,8192]{1,0:T(1,128)} %get-tuple-element.26.refs_1_), channel_id=1, source_target_pairs={{0,4},{4,8},{8,12},{12,16},{16,20},{20,24},{24,28},{28,0},{1,5},{5... | collective-permute-start | bytes 98312 | tf_op jit(solution)/shard_map/ppermute | solution.py:444
  42.6 9.3 %collective-permute-start.1 = (f32[1,8192]{1,0:T(1,128)}, f32[1,8192]{1,0:T(1,128)S(1)}, u32[]{:S(2)}, u32[]{:S(2)}) collective-permute-start(f32[1,8192]{1,0:T(1,128)} %get-tuple-element.26.refs_1_), channel_id=1, source_target_pairs={{0,8},{4,12},{8,16},{12,20},{16,24},{20,28},{24,0},{28,4},{1,9},{5... | collective-permute-start | bytes 98312 | tf_op jit(solution)/shard_map/ppermute | solution.py:444
  44.2 9.1 %collective-permute-start.2 = (f32[1,8192]{1,0:T(1,128)}, f32[1,8192]{1,0:T(1,128)S(1)}, u32[]{:S(2)}, u32[]{:S(2)}) collective-permute-start(f32[1,8192]{1,0:T(1,128)} %get-tuple-element.26.refs_1_), channel_id=1, source_target_pairs={{0,12},{4,16},{8,20},{12,24},{16,28},{20,0},{24,4},{28,8},{1,13},{... | collective-permute-start | bytes 98312 | tf_op jit(solution)/shard_map/ppermute | solution.py:444
  46.7 6.7 %collective-permute-start.3 = (f32[1,8192]{1,0:T(1,128)}, f32[1,8192]{1,0:T(1,128)S(1)}, u32[]{:S(2)}, u32[]{:S(2)}) collective-permute-start(f32[1,8192]{1,0:T(1,128)} %get-tuple-element.26.refs_1_), channel_id=1, source_target_pairs={{0,16},{4,20},{8,24},{12,28},{16,0},{20,4},{24,8},{28,12},{1,17},{... | collective-permute-start | bytes 98312 | tf_op jit(solution)/shard_map/ppermute | solution.py:444
  48.0 5.4 %collective-permute-start.4 = (f32[1,8192]{1,0:T(1,128)}, f32[1,8192]{1,0:T(1,128)S(1)}, u32[]{:S(2)}, u32[]{:S(2)}) collective-permute-start(f32[1,8192]{1,0:T(1,128)} %get-tuple-element.26.refs_1_), channel_id=1, source_target_pairs={{0,20},{4,24},{8,28},{12,0},{16,4},{20,8},{24,12},{28,16},{1,21},{... | collective-permute-start | bytes 98312 | tf_op jit(solution)/shard_map/ppermute | solution.py:444
  50.6 4.1 %collective-permute-start.5 = (f32[1,8192]{1,0:T(1,128)}, f32[1,8192]{1,0:T(1,128)S(1)}, u32[]{:S(2)}, u32[]{:S(2)}) collective-permute-start(f32[1,8192]{1,0:T(1,128)} %get-tuple-element.26.refs_1_), channel_id=1, source_target_pairs={{0,24},{4,28},{8,0},{12,4},{16,8},{20,12},{24,16},{28,20},{1,25},{... | collective-permute-start | bytes 98312 | tf_op jit(solution)/shard_map/ppermute | solution.py:444
  52.0 4.1 %collective-permute-start.6 = (f32[1,8192]{1,0:T(1,128)}, f32[1,8192]{1,0:T(1,128)S(1)}, u32[]{:S(2)}, u32[]{:S(2)}) collective-permute-start(f32[1,8192]{1,0:T(1,128)} %get-tuple-element.26.refs_1_), channel_id=1, source_target_pairs={{0,28},{4,0},{8,4},{12,8},{16,12},{20,16},{24,20},{28,24},{1,29},{... | collective-permute-start | bytes 98312 | tf_op jit(solution)/shard_map/ppermute | solution.py:444
  84.8 9.0 %collective-permute-start.7 = (f32[1,8192]{1,0:T(1,128)}, f32[1,8192]{1,0:T(1,128)S(1)}, u32[]{:S(2)}, u32[]{:S(2)}) collective-permute-start(f32[1,8192]{1,0:T(1,128)} %colsum.2.refs_1_), channel_id=1, source_target_pairs={{0,4},{4,8},{8,12},{12,16},{16,20},{20,24},{24,28},{28,0},{1,5},{5... | collective-permute-start | bytes 98312 | tf_op jit(solution)/shard_map/ppermute | solution.py:444
  86.3 7.7 %collective-permute-start.8 = (f32[1,8192]{1,0:T(1,128)}, f32[1,8192]{1,0:T(1,128)S(1)}, u32[]{:S(2)}, u32[]{:S(2)}) collective-permute-start(f32[1,8192]{1,0:T(1,128)} %colsum.2.refs_1_), channel_id=1, source_target_pairs={{0,8},{4,12},{8,16},{12,20},{16,24},{20,28},{24,0},{28,4},{1,9},{5... | collective-permute-start | bytes 98312 | tf_op jit(solution)/shard_map/ppermute | solution.py:444
  86.5 8.9 %collective-permute-start.9 = (f32[1,8192]{1,0:T(1,128)}, f32[1,8192]{1,0:T(1,128)S(1)}, u32[]{:S(2)}, u32[]{:S(2)}) collective-permute-start(f32[1,8192]{1,0:T(1,128)} %colsum.2.refs_1_), channel_id=1, source_target_pairs={{0,12},{4,16},{8,20},{12,24},{16,28},{20,0},{24,4},{28,8},{1,13},{... | collective-permute-start | bytes 98312 | tf_op jit(solution)/shard_map/ppermute | solution.py:444
  88.7 6.7 %collective-permute-start.10 = (f32[1,8192]{1,0:T(1,128)}, f32[1,8192]{1,0:T(1,128)S(1)}, u32[]{:S(2)}, u32[]{:S(2)}) collective-permute-start(f32[1,8192]{1,0:T(1,128)} %colsum.2.refs_1_), channel_id=1, source_target_pairs={{0,16},{4,20},{8,24},{12,28},{16,0},{20,4},{24,8},{28,12},{1,17},{... | collective-permute-start | bytes 98312 | tf_op jit(solution)/shard_map/ppermute | solution.py:444
  90.8 5.4 %collective-permute-start.11 = (f32[1,8192]{1,0:T(1,128)}, f32[1,8192]{1,0:T(1,128)S(1)}, u32[]{:S(2)}, u32[]{:S(2)}) collective-permute-start(f32[1,8192]{1,0:T(1,128)} %colsum.2.refs_1_), channel_id=1, source_target_pairs={{0,20},{4,24},{8,28},{12,0},{16,4},{20,8},{24,12},{28,16},{1,21},{... | collective-permute-start | bytes 98312 | tf_op jit(solution)/shard_map/ppermute | solution.py:444
  93.9 4.1 %collective-permute-start.12 = (f32[1,8192]{1,0:T(1,128)}, f32[1,8192]{1,0:T(1,128)S(1)}, u32[]{:S(2)}, u32[]{:S(2)}) collective-permute-start(f32[1,8192]{1,0:T(1,128)} %colsum.2.refs_1_), channel_id=1, source_target_pairs={{0,24},{4,28},{8,0},{12,4},{16,8},{20,12},{24,16},{28,20},{1,25},{... | collective-permute-start | bytes 98312 | tf_op jit(solution)/shard_map/ppermute | solution.py:444
  94.0 4.1 %collective-permute-start.13 = (f32[1,8192]{1,0:T(1,128)}, f32[1,8192]{1,0:T(1,128)S(1)}, u32[]{:S(2)}, u32[]{:S(2)}) collective-permute-start(f32[1,8192]{1,0:T(1,128)} %colsum.2.refs_1_), channel_id=1, source_target_pairs={{0,28},{4,0},{8,4},{12,8},{16,12},{20,16},{24,20},{28,24},{1,29},{... | collective-permute-start | bytes 98312 | tf_op jit(solution)/shard_map/ppermute | solution.py:444
  126.5 8.6 %collective-permute-start.14 = (f32[1,8192]{1,0:T(1,128)}, f32[1,8192]{1,0:T(1,128)S(1)}, u32[]{:S(2)}, u32[]{:S(2)}) collective-permute-start(f32[1,8192]{1,0:T(1,128)} %colsum.3.refs_1_), channel_id=1, source_target_pairs={{0,4},{4,8},{8,12},{12,16},{16,20},{20,24},{24,28},{28,0},{1,5},{5... | collective-permute-start | bytes 98312 | tf_op jit(solution)/shard_map/ppermute | solution.py:444
  127.8 8.0 %collective-permute-start.15 = (f32[1,8192]{1,0:T(1,128)}, f32[1,8192]{1,0:T(1,128)S(1)}, u32[]{:S(2)}, u32[]{:S(2)}) collective-permute-start(f32[1,8192]{1,0:T(1,128)} %colsum.3.refs_1_), channel_id=1, source_target_pairs={{0,8},{4,12},{8,16},{12,20},{16,24},{20,28},{24,0},{28,4},{1,9},{5... | collective-permute-start | bytes 98312 | tf_op jit(solution)/shard_map/ppermute | solution.py:444
  129.6 8.3 %collective-permute-start.16 = (f32[1,8192]{1,0:T(1,128)}, f32[1,8192]{1,0:T(1,128)S(1)}, u32[]{:S(2)}, u32[]{:S(2)}) collective-permute-start(f32[1,8192]{1,0:T(1,128)} %colsum.3.refs_1_), channel_id=1, source_target_pairs={{0,12},{4,16},{8,20},{12,24},{16,28},{20,0},{24,4},{28,8},{1,13},{... | collective-permute-start | bytes 98312 | tf_op jit(solution)/shard_map/ppermute | solution.py:444
  130.7 7.1 %collective-permute-start.17 = (f32[1,8192]{1,0:T(1,128)}, f32[1,8192]{1,0:T(1,128)S(1)}, u32[]{:S(2)}, u32[]{:S(2)}) collective-permute-start(f32[1,8192]{1,0:T(1,128)} %colsum.3.refs_1_), channel_id=1, source_target_pairs={{0,16},{4,20},{8,24},{12,28},{16,0},{20,4},{24,8},{28,12},{1,17},{... | collective-permute-start | bytes 98312 | tf_op jit(solution)/shard_map/ppermute | solution.py:444
  133.3 5.0 %collective-permute-start.18 = (f32[1,8192]{1,0:T(1,128)}, f32[1,8192]{1,0:T(1,128)S(1)}, u32[]{:S(2)}, u32[]{:S(2)}) collective-permute-start(f32[1,8192]{1,0:T(1,128)} %colsum.3.refs_1_), channel_id=1, source_target_pairs={{0,20},{4,24},{8,28},{12,0},{16,4},{20,8},{24,12},{28,16},{1,21},{... | collective-permute-start | bytes 98312 | tf_op jit(solution)/shard_map/ppermute | solution.py:444
  135.2 4.1 %collective-permute-start.19 = (f32[1,8192]{1,0:T(1,128)}, f32[1,8192]{1,0:T(1,128)S(1)}, u32[]{:S(2)}, u32[]{:S(2)}) collective-permute-start(f32[1,8192]{1,0:T(1,128)} %colsum.3.refs_1_), channel_id=1, source_target_pairs={{0,24},{4,28},{8,0},{12,4},{16,8},{20,12},{24,16},{28,20},{1,25},{... | collective-permute-start | bytes 98312 | tf_op jit(solution)/shard_map/ppermute | solution.py:444
  135.8 4.1 %collective-permute-start.20 = (f32[1,8192]{1,0:T(1,128)}, f32[1,8192]{1,0:T(1,128)S(1)}, u32[]{:S(2)}, u32[]{:S(2)}) collective-permute-start(f32[1,8192]{1,0:T(1,128)} %colsum.3.refs_1_), channel_id=1, source_target_pairs={{0,28},{4,0},{8,4},{12,8},{16,12},{20,16},{24,20},{28,24},{1,29},{... | collective-permute-start | bytes 98312 | tf_op jit(solution)/shard_map/ppermute | solution.py:444
  161.4 1.7 collective-permute-start.21
  164.2 8.6 %collective-permute-start.22 = (bf16[1024,128]{1,0:T(8,128)(2,1)S(1)}, bf16[1024,128]{1,0:T(8,128)(2,1)S(1)}, u32[]{:S(2)}, u32[]{:S(2)}) collective-permute-start(bf16[1024,128]{1,0:T(8,128)(2,1)S(1)} %add_convert_fusion.grad_a), channel_id=1, source_target_pairs={{0,2},{1,3},{2,0},{3,1},{4,6},{5,7},{6,4},{7,5},{8,10},{9,11},{10,... | collective-permute-start | bytes 786440 | tf_op jit(solution)/shard_map/ppermute | solution.py:476
  180.1 66.6 %copy-start.11 = (f32[1,1024]{1,0:T(1,128)S(1)}, f32[1,1024]{1,0:T(1,128)}, u32[]{:S(2)}) copy-start(f32[1,1024]{1,0:T(1,128)} %psum.23.total.refs_12_) | copy-start | bytes 12292
  228.3 138.1 %all-gather.4.cloned.1.call-start = ((), (), s32[]{:S(2)}) async-start(), calls=%async_computation | async-start | bytes 2359296 | tf_op jit(solution)/shard_map/all_gather | solution.py:470
  228.4 29.8 %collective-permute-start.23 = (bf16[128,1024]{1,0:T(8,128)(2,1)S(1)}, bf16[128,1024]{1,0:T(8,128)(2,1)S(1)}, u32[]{:S(2)}, u32[]{:S(2)}) collective-permute-start(bf16[128,1024]{1,0:T(8,128)(2,1)S(1)} %copy-done), channel_id=1, source_target_pairs={{0,4},{4,8},{8,12},{12,16},{16,20},{20,24},{24,28},{28,0},{1,5},{5... | collective-permute-start | bytes 786440 | tf_op jit(solution)/shard_map/ppermute | solution.py:444
  228.4 31.1 %collective-permute-start.24 = (bf16[128,1024]{1,0:T(8,128)(2,1)S(1)}, bf16[128,1024]{1,0:T(8,128)(2,1)S(1)}, u32[]{:S(2)}, u32[]{:S(2)}) collective-permute-start(bf16[128,1024]{1,0:T(8,128)(2,1)S(1)} %copy-done), channel_id=1, source_target_pairs={{0,8},{4,12},{8,16},{12,20},{16,24},{20,28},{24,0},{28,4},{1,9},{5... | collective-permute-start | bytes 786440 | tf_op jit(solution)/shard_map/ppermute | solution.py:444
  228.5 12.2 %collective-permute-start.30 = (f32[1,1024]{1,0:T(1,128)S(1)}, f32[1,1024]{1,0:T(1,128)S(1)}, u32[]{:S(2)}, u32[]{:S(2)}) collective-permute-start(f32[1,1024]{1,0:T(1,128)S(1)} %copy-done.10), channel_id=1, source_target_pairs={{0,4},{4,8},{8,12},{12,16},{16,20},{20,24},{24,28},{28,0},{1,5},{5... | collective-permute-start | bytes 12296 | tf_op jit(solution)/shard_map/ppermute | solution.py:444
  229.9 10.8 %collective-permute-start.31 = (f32[1,1024]{1,0:T(1,128)S(1)}, f32[1,1024]{1,0:T(1,128)S(1)}, u32[]{:S(2)}, u32[]{:S(2)}) collective-permute-start(f32[1,1024]{1,0:T(1,128)S(1)} %copy-done.10), channel_id=1, source_target_pairs={{0,8},{4,12},{8,16},{12,20},{16,24},{20,28},{24,0},{28,4},{1,9},{5... | collective-permute-start | bytes 12296 | tf_op jit(solution)/shard_map/ppermute | solution.py:444
  231.5 9.3 %collective-permute-start.32 = (f32[1,1024]{1,0:T(1,128)S(1)}, f32[1,1024]{1,0:T(1,128)S(1)}, u32[]{:S(2)}, u32[]{:S(2)}) collective-permute-start(f32[1,1024]{1,0:T(1,128)S(1)} %copy-done.10), channel_id=1, source_target_pairs={{0,12},{4,16},{8,20},{12,24},{16,28},{20,0},{24,4},{28,8},{1,13},{... | collective-permute-start | bytes 12296 | tf_op jit(solution)/shard_map/ppermute | solution.py:444
  240.7 6.0 %collective-permute-start.33 = (f32[1,1024]{1,0:T(1,128)S(1)}, f32[1,1024]{1,0:T(1,128)S(1)}, u32[]{:S(2)}, u32[]{:S(2)}) collective-permute-start(f32[1,1024]{1,0:T(1,128)S(1)} %copy-done.10), channel_id=1, source_target_pairs={{0,16},{4,20},{8,24},{12,28},{16,0},{20,4},{24,8},{28,12},{1,17},{... | collective-permute-start | bytes 12296 | tf_op jit(solution)/shard_map/ppermute | solution.py:444
  240.7 6.0 %collective-permute-start.34 = (f32[1,1024]{1,0:T(1,128)S(1)}, f32[1,1024]{1,0:T(1,128)S(1)}, u32[]{:S(2)}, u32[]{:S(2)}) collective-permute-start(f32[1,1024]{1,0:T(1,128)S(1)} %copy-done.10), channel_id=1, source_target_pairs={{0,20},{4,24},{8,28},{12,0},{16,4},{20,8},{24,12},{28,16},{1,21},{... | collective-permute-start | bytes 12296 | tf_op jit(solution)/shard_map/ppermute | solution.py:444
  240.8 9.0 %collective-permute-start.35 = (f32[1,1024]{1,0:T(1,128)S(1)}, f32[1,1024]{1,0:T(1,128)S(1)}, u32[]{:S(2)}, u32[]{:S(2)}) collective-permute-start(f32[1,1024]{1,0:T(1,128)S(1)} %copy-done.10), channel_id=1, source_target_pairs={{0,24},{4,28},{8,0},{12,4},{16,8},{20,12},{24,16},{28,20},{1,25},{... | collective-permute-start | bytes 12296 | tf_op jit(solution)/shard_map/ppermute | solution.py:444
  246.6 6.6 %collective-permute-start.36 = (f32[1,1024]{1,0:T(1,128)S(1)}, f32[1,1024]{1,0:T(1,128)S(1)}, u32[]{:S(2)}, u32[]{:S(2)}) collective-permute-start(f32[1,1024]{1,0:T(1,128)S(1)} %copy-done.10), channel_id=1, source_target_pairs={{0,28},{4,0},{8,4},{12,8},{16,12},{20,16},{24,20},{28,24},{1,29},{... | collective-permute-start | bytes 12296 | tf_op jit(solution)/shard_map/ppermute | solution.py:444
  246.7 7.6 %collective-permute-start.37 = (f32[1,1024]{1,0:T(1,128)S(1)}, f32[1,1024]{1,0:T(1,128)S(1)}, u32[]{:S(2)}, u32[]{:S(2)}) collective-permute-start(f32[1,1024]{1,0:T(1,128)S(1)} %copy-done.11), channel_id=1, source_target_pairs={{0,4},{4,8},{8,12},{12,16},{16,20},{20,24},{24,28},{28,0},{1,5},{5... | collective-permute-start | bytes 12296 | tf_op jit(solution)/shard_map/ppermute | solution.py:444
  249.7 5.5 %collective-permute-start.38 = (f32[1,1024]{1,0:T(1,128)S(1)}, f32[1,1024]{1,0:T(1,128)S(1)}, u32[]{:S(2)}, u32[]{:S(2)}) collective-permute-start(f32[1,1024]{1,0:T(1,128)S(1)} %copy-done.11), channel_id=1, source_target_pairs={{0,8},{4,12},{8,16},{12,20},{16,24},{20,28},{24,0},{28,4},{1,9},{5... | collective-permute-start | bytes 12296 | tf_op jit(solution)/shard_map/ppermute | solution.py:444
  253.3 17.2 %collective-permute-start.25 = (bf16[128,1024]{1,0:T(8,128)(2,1)S(1)}, bf16[128,1024]{1,0:T(8,128)(2,1)S(1)}, u32[]{:S(2)}, u32[]{:S(2)}) collective-permute-start(bf16[128,1024]{1,0:T(8,128)(2,1)S(1)} %copy-done), channel_id=1, source_target_pairs={{0,12},{4,16},{8,20},{12,24},{16,28},{20,0},{24,4},{28,8},{1,13},{... | collective-permute-start | bytes 786440 | tf_op jit(solution)/shard_map/ppermute | solution.py:444
  254.3 51.3 %copy-start.41 = (f32[1,1024]{1,0:T(1,128)}, f32[1,1024]{1,0:T(1,128)S(1)}, u32[]{:S(2)}) copy-start(f32[1,1024]{1,0:T(1,128)S(1)} %collective-permute-done.37.refs_13_) | copy-start | bytes 12292
  254.3 19.2 %collective-permute-start.26 = (bf16[128,1024]{1,0:T(8,128)(2,1)S(1)}, bf16[128,1024]{1,0:T(8,128)(2,1)S(1)}, u32[]{:S(2)}, u32[]{:S(2)}) collective-permute-start(bf16[128,1024]{1,0:T(8,128)(2,1)S(1)} %copy-done), channel_id=1, source_target_pairs={{0,16},{4,20},{8,24},{12,28},{16,0},{20,4},{24,8},{28,12},{1,17},{... | collective-permute-start | bytes 786440 | tf_op jit(solution)/shard_map/ppermute | solution.py:444
  255.3 18.2 %collective-permute-start.27 = (bf16[128,1024]{1,0:T(8,128)(2,1)S(1)}, bf16[128,1024]{1,0:T(8,128)(2,1)S(1)}, u32[]{:S(2)}, u32[]{:S(2)}) collective-permute-start(bf16[128,1024]{1,0:T(8,128)(2,1)S(1)} %copy-done), channel_id=1, source_target_pairs={{0,20},{4,24},{8,28},{12,0},{16,4},{20,8},{24,12},{28,16},{1,21},{... | collective-permute-start | bytes 786440 | tf_op jit(solution)/shard_map/ppermute | solution.py:444
  258.2 20.0 %collective-permute-start.28 = (bf16[128,1024]{1,0:T(8,128)(2,1)S(1)}, bf16[128,1024]{1,0:T(8,128)(2,1)S(1)}, u32[]{:S(2)}, u32[]{:S(2)}) collective-permute-start(bf16[128,1024]{1,0:T(8,128)(2,1)S(1)} %copy-done), channel_id=1, source_target_pairs={{0,24},{4,28},{8,0},{12,4},{16,8},{20,12},{24,16},{28,20},{1,25},{... | collective-permute-start | bytes 786440 | tf_op jit(solution)/shard_map/ppermute | solution.py:444
  259.5 25.4 %collective-permute-start.29 = (bf16[128,1024]{1,0:T(8,128)(2,1)S(1)}, bf16[128,1024]{1,0:T(8,128)(2,1)S(1)}, u32[]{:S(2)}, u32[]{:S(2)}) collective-permute-start(bf16[128,1024]{1,0:T(8,128)(2,1)S(1)} %copy-done), channel_id=1, source_target_pairs={{0,28},{4,0},{8,4},{12,8},{16,12},{20,16},{24,20},{28,24},{1,29},{... | collective-permute-start | bytes 786440 | tf_op jit(solution)/shard_map/ppermute | solution.py:444
  270.4 35.0 %collective-permute-start.39 = (f32[1,1024]{1,0:T(1,128)S(1)}, f32[1,1024]{1,0:T(1,128)S(1)}, u32[]{:S(2)}, u32[]{:S(2)}) collective-permute-start(f32[1,1024]{1,0:T(1,128)S(1)} %copy-done.11), channel_id=1, source_target_pairs={{0,12},{4,16},{8,20},{12,24},{16,28},{20,0},{24,4},{28,8},{1,13},{... | collective-permute-start | bytes 12296 | tf_op jit(solution)/shard_map/ppermute | solution.py:444
  273.4 32.0 %collective-permute-start.40 = (f32[1,1024]{1,0:T(1,128)S(1)}, f32[1,1024]{1,0:T(1,128)S(1)}, u32[]{:S(2)}, u32[]{:S(2)}) collective-permute-start(f32[1,1024]{1,0:T(1,128)S(1)} %copy-done.11), channel_id=1, source_target_pairs={{0,16},{4,20},{8,24},{12,28},{16,0},{20,4},{24,8},{28,12},{1,17},{... | collective-permute-start | bytes 12296 | tf_op jit(solution)/shard_map/ppermute | solution.py:444
  273.5 32.0 %collective-permute-start.41 = (f32[1,1024]{1,0:T(1,128)S(1)}, f32[1,1024]{1,0:T(1,128)S(1)}, u32[]{:S(2)}, u32[]{:S(2)}) collective-permute-start(f32[1,1024]{1,0:T(1,128)S(1)} %copy-done.11), channel_id=1, source_target_pairs={{0,20},{4,24},{8,28},{12,0},{16,4},{20,8},{24,12},{28,16},{1,21},{... | collective-permute-start | bytes 12296 | tf_op jit(solution)/shard_map/ppermute | solution.py:444
  278.1 27.3 %collective-permute-start.42 = (f32[1,1024]{1,0:T(1,128)S(1)}, f32[1,1024]{1,0:T(1,128)S(1)}, u32[]{:S(2)}, u32[]{:S(2)}) collective-permute-start(f32[1,1024]{1,0:T(1,128)S(1)} %copy-done.11), channel_id=1, source_target_pairs={{0,24},{4,28},{8,0},{12,4},{16,8},{20,12},{24,16},{28,20},{1,25},{... | collective-permute-start | bytes 12296 | tf_op jit(solution)/shard_map/ppermute | solution.py:444
  284.9 20.6 %collective-permute-start.43 = (f32[1,1024]{1,0:T(1,128)S(1)}, f32[1,1024]{1,0:T(1,128)S(1)}, u32[]{:S(2)}, u32[]{:S(2)}) collective-permute-start(f32[1,1024]{1,0:T(1,128)S(1)} %copy-done.11), channel_id=1, source_target_pairs={{0,28},{4,0},{8,4},{12,8},{16,12},{20,16},{24,20},{28,24},{1,29},{... | collective-permute-start | bytes 12296 | tf_op jit(solution)/shard_map/ppermute | solution.py:444
  (47 other events, 684.7 us)
Sparse Core Ops, SparseCore 0:
  228.4 77.9 all-gather.5
  316.8 49.5 all-gather.3

commit v2 on v1

v2 whole, which is shorter than its diff:
```python
import functools
import math

import jax
import jax.numpy as jnp
from jax import lax
from jax.experimental import pallas as pl
from jax.experimental.pallas import tpu as pltpu
from jax.sharding import PartitionSpec as P

ITERS = 3
norm_eps = 1e-06
code_temp = 0.05
pred_temp = 0.1
loss_scale = 64.0
GRAD_SCALE = loss_scale / pred_temp
EXP2_SCALE = math.log2(math.e) / pred_temp
GELU_K = math.sqrt(2.0 / math.pi)
GELU_A = 0.044715

f32 = jnp.float32
bf16 = jnp.bfloat16
NN = (((1,), (0,)), ((), ()))
NT = (((1,), (1,)), ((), ()))
TN = (((0,), (0,)), ((), ()))
VMEM_LIMIT = 20 * 1024 * 1024


def dot(a, b, dims=NN):
    return lax.dot_general(a, b, dims, preferred_element_type=f32)


def params(*semantics):
    return pltpu.CompilerParams(
        dimension_semantics=semantics or None, vmem_limit_bytes=VMEM_LIMIT
    )


def to_column(vec):
    n = vec.shape[1]
    return jnp.broadcast_to(vec, (8, n)).T[:, :1]


def swap_lanes(x):
    half = x.shape[1] // 2
    return jnp.concatenate([x[:, half:], x[:, :half]], axis=1)


def swap_rows(x):
    half = x.shape[0] // 2
    return jnp.concatenate([x[half:], x[:half]], axis=0)


def full(shape):
    return pl.BlockSpec(shape, lambda *_: (0,) * len(shape))


def head_kernel(emb, pairing, w_in, w_out, pre, hid, raw, views, views_t, pos, scratch):
    step = pl.program_id(0)
    rows = emb.shape[0]
    pre_act = dot(emb[...], w_in[...])
    pre[...] = pre_act
    t = jnp.tanh(GELU_K * (pre_act + GELU_A * (pre_act * pre_act * pre_act)))
    hidden = (0.5 * pre_act * (1.0 + t)).astype(bf16)
    hid[...] = hidden
    raw_out = dot(hidden, w_out[...])
    raw[...] = raw_out
    inv = lax.rsqrt(jnp.sum(raw_out * raw_out, axis=1, keepdims=True) + norm_eps)
    scratch[pl.ds(pl.multiple_of(step * rows, rows), rows), :] = (raw_out * inv).astype(bf16)

    @pl.when(step == pl.num_programs(0) - 1)
    def _():
        mate = pairing[...]
        n = mate.shape[1]
        lane = lax.broadcasted_iota(jnp.int32, (1, n), 1)
        first = lane < mate
        low = jnp.minimum(lane, mate)
        sub = lax.broadcasted_iota(jnp.int32, (n, n), 0)
        before = jnp.where(sub < low, 1.0, 0.0).astype(bf16)
        first8 = jnp.broadcast_to(jnp.where(first, 1.0, 0.0), (8, n)).astype(bf16)
        rank = dot(first8, before)[:1].astype(jnp.int32)
        place = jnp.where(first, rank, rank + n // 2)
        pos[...] = place
        move = jnp.where(sub == place, 1.0, 0.0).astype(bf16)
        ordered = dot(move, scratch[...])
        views[...] = ordered.astype(bf16)
        views_t[...] = ordered.T.astype(bf16)


def head(embeddings, pairing, w_in, w_out):
    rows, wide = embeddings.shape
    hidden = w_in.shape[1]
    depth = w_out.shape[1]
    steps = 4
    block = rows // steps
    return pl.pallas_call(
        head_kernel,
        grid=(steps,),
        in_specs=[
            pl.BlockSpec((block, wide), lambda i: (i, 0)),
            full((1, rows)),
            full((wide, hidden)),
            full((hidden, depth)),
        ],
        out_specs=[
            pl.BlockSpec((block, hidden), lambda i: (i, 0)),
            pl.BlockSpec((block, hidden), lambda i: (i, 0)),
            pl.BlockSpec((block, depth), lambda i: (i, 0)),
            full((rows, depth)),
            full((depth, rows)),
            full((1, rows)),
        ],
        out_shape=[
            jax.ShapeDtypeStruct((rows, hidden), f32),
            jax.ShapeDtypeStruct((rows, hidden), bf16),
            jax.ShapeDtypeStruct((rows, depth), f32),
            jax.ShapeDtypeStruct((rows, depth), bf16),
            jax.ShapeDtypeStruct((depth, rows), bf16),
            jax.ShapeDtypeStruct((1, rows), jnp.int32),
        ],
        scratch_shapes=[pltpu.VMEM((rows, depth), bf16)],
        compiler_params=params("arbitrary"),
        name="head",
    )(embeddings, pairing.reshape(1, rows), w_in, w_out)


def unit_of(protos):
    proto_f = protos.astype(f32)
    inv = lax.rsqrt(jnp.sum(proto_f * proto_f, axis=1, keepdims=True) + norm_eps)
    return proto_f, inv, proto_f * inv


def in_vmem(x):
    return pltpu.with_memory_space_constraint(x, pltpu.VMEM)


WHOLE = pl.BlockSpec(memory_space=pltpu.VMEM)


def exp_pair(scores):
    soft = jnp.exp2(scores * EXP2_SCALE)
    return soft, soft * soft


def first_kernel(block, chunk, views, protos, expo, unit_t, col, tot, tot_acc):
    rows, depth = views.shape
    width = protos.shape[0]
    tot_acc[...] = jnp.zeros_like(tot_acc)

    def one(j, carry):
        here = pl.ds(pl.multiple_of(j * block, block), block)
        _, _, unit = unit_of(protos[here, :])
        unit_tr = unit.T.astype(bf16)
        unit_t[:, here] = unit_tr
        running = jnp.zeros((8, block), f32)
        for start in range(0, rows, chunk):
            part = pl.ds(start, chunk)
            soft, hard = exp_pair(dot(views[part, :], unit_tr))
            expo[part, here] = hard.astype(bf16)
            running = running + jnp.sum(hard.reshape(chunk // 8, 8, block), axis=0)
            lanes = soft[:, :128]
            for k in range(1, block // 128):
                lanes = lanes + soft[:, k * 128 : (k + 1) * 128]
            tot_acc[part, :] += lanes
        col[:, here] = jnp.sum(running, axis=0, keepdims=True)
        return carry

    lax.fori_loop(0, width // block, one, 0)
    tot[...] = jnp.sum(tot_acc[...].T, axis=0, keepdims=True)


def first_pass(views, protos):
    rows, depth = views.shape
    width = protos.shape[0]
    block = min(256, width)
    chunk = min(256, rows)
    return pl.pallas_call(
        functools.partial(first_kernel, block, chunk),
        in_specs=[WHOLE] * 2,
        out_specs=[WHOLE] * 4,
        out_shape=[
            pltpu.VMEM((rows, width), bf16),
            jax.ShapeDtypeStruct((depth, width), bf16),
            jax.ShapeDtypeStruct((1, width), f32),
            jax.ShapeDtypeStruct((1, rows), f32),
        ],
        scratch_shapes=[pltpu.VMEM((rows, 128), f32)],
        compiler_params=params(),
        name="first_pass",
    )(views, protos)


def rowsum_kernel(count, expo, *refs):
    parts = refs[:count]
    scale, out, spread, acc = refs[count:]
    rows, width = expo.shape
    total = jnp.sum(parts[0][...], axis=0, keepdims=True)
    for other in parts[1:]:
        total = total + other[...]
    inverse = 1.0 / total
    scale[...] = inverse
    spread[...] = jnp.broadcast_to(inverse, spread.shape).astype(bf16)
    tall = 64

    def one(i, carry):
        here = pl.ds(pl.multiple_of(i * tall, tall), tall)
        running = jnp.zeros((tall, 128), f32)
        for k in range(width // 128):
            lanes = slice(k * 128, (k + 1) * 128)
            weight = jnp.concatenate([spread[:, lanes]] * (tall // 16), axis=0)
            running = running + (expo[here, lanes] * weight).astype(f32)
        acc[here, :] = running
        return carry

    lax.fori_loop(0, rows // tall, one, 0)
    out[...] = jnp.sum(acc[...].T, axis=0, keepdims=True)


def rowsum(expo, parts):
    rows, width = expo.shape
    return pl.pallas_call(
        functools.partial(rowsum_kernel, len(parts)),
        in_specs=[WHOLE] * (1 + len(parts)),
        out_specs=[WHOLE] * 2,
        out_shape=[
            jax.ShapeDtypeStruct((1, width), f32),
            jax.ShapeDtypeStruct((1, rows), f32),
        ],
        scratch_shapes=[pltpu.VMEM((16, width), bf16), pltpu.VMEM((rows, 128), f32)],
        compiler_params=params(),
        name="rowsum",
    )(in_vmem(expo), *parts)


def colsum_kernel(count, expo, *refs):
    parts = refs[:count]
    out, spread = refs[count:]
    rows, width = expo.shape
    total = jnp.sum(parts[0][...], axis=0, keepdims=True)
    for other in parts[1:]:
        total = total + other[...]
    spread[...] = jnp.broadcast_to(1.0 / total, (128, rows)).T.astype(bf16)
    block = min(512, width)

    def one(j, carry):
        here = pl.ds(pl.multiple_of(j * block, block), block)
        running = jnp.zeros((16, block), f32)
        for i in range(rows // 16):
            part = slice(i * 16, (i + 1) * 16)
            weight = jnp.concatenate([spread[part, :]] * (block // 128), axis=1)
            running = running + (expo[part, here] * weight).astype(f32)
        out[:, here] = jnp.sum(running, axis=0, keepdims=True)
        return carry

    lax.fori_loop(0, width // block, one, 0)


def colsum(expo, parts):
    rows, width = expo.shape
    return pl.pallas_call(
        functools.partial(colsum_kernel, len(parts)),
        in_specs=[WHOLE] * (1 + len(parts)),
        out_specs=WHOLE,
        out_shape=jax.ShapeDtypeStruct((1, width), f32),
        scratch_shapes=[pltpu.VMEM((rows, 128), bf16)],
        compiler_params=params(),
        name="colsum",
    )(in_vmem(expo), *parts)


def proto_first_kernel(block, protos, views, totals, expo, grad, weights):
    count, depth, rows = views.shape
    for k in range(count):
        scale = GRAD_SCALE / totals[k]
        weights[:, k * rows : (k + 1) * rows] = (views[k].astype(f32) * scale).astype(bf16)

    def one(j, carry):
        here = pl.ds(pl.multiple_of(j * block, block), block)
        _, _, unit = unit_of(protos[here, :])
        unit16 = unit.astype(bf16)
        running = jnp.zeros((block, depth), f32)
        for k in range(count):
            part = slice(k * rows, (k + 1) * rows)
            soft, hard = exp_pair(dot(unit16, views[k]))
            expo[here, part] = hard.astype(bf16)
            running = running + dot(soft.astype(bf16), weights[:, part], NT)
        grad[here, :] = running
        return carry

    lax.fori_loop(0, protos.shape[0] // block, one, 0)


def proto_first(protos, views, totals):
    width, depth = protos.shape
    count, _, rows = views.shape
    block = min(256, width)
    return pl.pallas_call(
        functools.partial(proto_first_kernel, block),
        in_specs=[WHOLE] * 3,
        out_specs=[WHOLE] * 2,
        out_shape=[
            pltpu.VMEM((width, count * rows), bf16),
            jax.ShapeDtypeStruct((width, depth), f32),
        ],
        scratch_shapes=[pltpu.VMEM((depth, count * rows), bf16)],
        compiler_params=params(),
        name="proto_first",
    )(protos, views, totals)


def proto_last_kernel(block, expo, grad, scale, protos, views, totals, out, weights):
    count, depth, rows = views.shape
    for k in range(count):
        mates = swap_lanes(views[k])
        weights[:, k * rows : (k + 1) * rows] = (
            mates.astype(f32) * (GRAD_SCALE / totals[k])
        ).astype(bf16)

    def one(j, carry):
        here = pl.ds(pl.multiple_of(j * block, block), block)
        code = dot(expo[here, :], weights[...], NT)
        unit_grad = grad[here, :] - to_column(scale[:, here]) * code
        proto_f, inv, _ = unit_of(protos[here, :])
        inner = jnp.sum(proto_f * unit_grad, axis=1, keepdims=True)
        out[here, :] = (inv * unit_grad - proto_f * (inv * inv * inv) * inner).astype(bf16)
        return carry

    lax.fori_loop(0, protos.shape[0] // block, one, 0)


def proto_last(expo, grad, scale, protos, views, totals):
    width, depth = protos.shape
    count, _, rows = views.shape
    block = min(256, width)
    return pl.pallas_call(
        functools.partial(proto_last_kernel, block),
        in_specs=[WHOLE] * 6,
        out_specs=WHOLE,
        out_shape=jax.ShapeDtypeStruct((width, depth), bf16),
        scratch_shapes=[pltpu.VMEM((depth, count * rows), bf16)],
        compiler_params=params(),
        name="proto_last",
    )(in_vmem(expo), grad, scale, protos, views, totals)


def view_grad_kernel(block, views, unit_t, expo, scale, tot, total, out, soft_acc, hard_acc):
    rows, depth = views.shape
    width = expo.shape[1]
    soft_acc[...] = jnp.zeros_like(soft_acc)
    hard_acc[...] = jnp.zeros_like(hard_acc)

    def one(j, carry):
        here = pl.ds(pl.multiple_of(j * block, block), block)
        unit = unit_t[:, here]
        scaled = (unit.astype(f32) * scale[:, here]).astype(bf16)
        soft = jnp.exp2(dot(views[...], unit) * EXP2_SCALE).astype(bf16)
        soft_acc[...] += dot(soft, unit, NT)
        hard_acc[...] += dot(expo[:, here], scaled, NT)
        return carry

    lax.fori_loop(0, width // block, one, 0)
    soft = soft_acc[...] * to_column(GRAD_SCALE / tot[...])
    hard = swap_rows(hard_acc[...] * to_column(GRAD_SCALE / total[...]))
    out[...] = (soft - hard).astype(out.dtype)


def view_grad_part(views, unit_t, expo, scale, tot, total):
    rows, depth = views.shape
    block = min(512, expo.shape[1])
    return pl.pallas_call(
        functools.partial(view_grad_kernel, block),
        in_specs=[WHOLE] * 6,
        out_specs=WHOLE,
        out_shape=jax.ShapeDtypeStruct((rows, depth), bf16),
        scratch_shapes=[pltpu.VMEM((rows, depth), f32)] * 2,
        compiler_params=params(),
        name="view_grad",
    )(views, unit_t, in_vmem(expo), scale, tot, total)


def backward_kernel(grad_a, grad_b, pos, raw, pre, emb, hid_part, w_out, out):
    total = grad_a[...].astype(f32) + grad_b[...].astype(f32)
    n, depth = raw.shape
    place = jnp.broadcast_to(pos[...].astype(f32), (8, n)).T[:, :1].astype(jnp.int32)
    lane = lax.broadcasted_iota(jnp.int32, (n, n), 1)
    move = jnp.where(lane == place, 1.0, 0.0).astype(bf16)
    hi = total.astype(bf16)
    lo = (total - hi.astype(f32)).astype(bf16)
    moved = dot(move, jnp.concatenate([hi, lo], axis=1))
    grad = moved[:, :depth] + moved[:, depth:]
    raw_out = raw[...]
    inv = lax.rsqrt(jnp.sum(raw_out * raw_out, axis=1, keepdims=True) + norm_eps)
    inner = jnp.sum(raw_out * grad, axis=1, keepdims=True)
    d_raw = (inv * grad - raw_out * (inv * inv * inv) * inner).astype(bf16)
    g_out = dot(hid_part[...], d_raw, TN)
    d_hidden = dot(d_raw, w_out[...], NT)
    v = pre[...]
    t = jnp.tanh(GELU_K * (v + GELU_A * (v * v * v)))
    slope = 0.5 * (1.0 + t) + (0.5 * GELU_K) * v * (1.0 - t * t) * (1.0 + (3.0 * GELU_A) * (v * v))
    d_pre = (slope * d_hidden).astype(bf16)
    g_in = dot(emb[...], d_pre, TN)
    count = out.shape[0]
    tall, wide = g_in.shape[0] // count, g_in.shape[1]
    for k in range(count):
        for q in range(wide // 128):
            out[k, q * tall : (q + 1) * tall, :] = g_in[
                k * tall : (k + 1) * tall, q * 128 : (q + 1) * 128
            ]
        base, short = tall * (wide // 128), g_out.shape[0] // count
        out[k, base : base + short, :] = g_out[k * short : (k + 1) * short]


def backward(nb, grad_a, grad_b, pos, raw, pre, emb, hid_part, w_out):
    lines = (emb.shape[1] * pre.shape[1] + hid_part.shape[1] * raw.shape[1]) // (nb * 128)
    return pl.pallas_call(
        backward_kernel,
        in_specs=[WHOLE] * 8,
        out_specs=WHOLE,
        out_shape=jax.ShapeDtypeStruct((nb, lines, 128), f32),
        compiler_params=params(),
        name="backward",
    )(grad_a, grad_b, pos, raw, pre, emb, hid_part, w_out)


def unpack_kernel(both, g_in, g_out):
    count = both.shape[0]
    tall, wide = g_in.shape[0] // count, g_in.shape[1]
    base, short = tall * (wide // 128), g_out.shape[0] // count
    for k in range(count):
        x = both[k].astype(f32)
        for q in range(wide // 128):
            g_in[k * tall : (k + 1) * tall, q * 128 : (q + 1) * 128] = x[
                q * tall : (q + 1) * tall
            ]
        g_out[k * short : (k + 1) * short, :] = x[base : base + short]


def unpack(both, shape_in, shape_out):
    return pl.pallas_call(
        unpack_kernel,
        in_specs=[WHOLE],
        out_specs=[WHOLE] * 2,
        out_shape=[jax.ShapeDtypeStruct(shape_in, f32), jax.ShapeDtypeStruct(shape_out, f32)],
        compiler_params=params(),
        name="unpack",
    )(both)


def body(nb, npr, embeddings, pairing, w_in, w_out, prototypes):
    b = lax.axis_index("batch")
    p = lax.axis_index("proto")
    rows, wide = embeddings.shape
    width, depth = prototypes.shape
    hidden_n = w_in.shape[1]
    own = width // nb

    def doubled(x, axis, size):
        step = 1
        while step < size:
            other = lax.ppermute(x, axis, [(i, i ^ step) for i in range(size)])
            if step * 2 == size:
                return [x, other]
            x = x + other
            step *= 2
        return [x]

    def spread_all(x, axis, size):
        wide_x = jnp.broadcast_to(x, (size,) + x.shape[1:])
        return [lax.all_to_all(wide_x, axis, 0, 0, tiled=True)]

    def gathered(x, axis, size):
        return [lax.all_gather(x, axis, axis=0, tiled=True)]

    pre, hid, raw, views, views_t, pos = head(embeddings, pairing, w_in, w_out)
    views_all = lax.all_gather(views_t, "batch", axis=0)
    expo, unit_t, col, tot = first_pass(views, prototypes)
    protos_own = lax.dynamic_slice_in_dim(prototypes, b * own, own, 0)
    emb_part = lax.dynamic_slice_in_dim(embeddings, p * (wide // npr), wide // npr, 1)
    hid_part = lax.dynamic_slice_in_dim(hid, p * (hidden_n // npr), hidden_n // npr, 1)

    scale, row = rowsum(expo, doubled(col, "batch", nb))
    both = lax.psum(jnp.concatenate([row, tot], axis=0), "proto")
    totals, tot = [both[:1]], both[1:]
    tot_all = lax.all_gather(tot, "batch", axis=0)
    col = colsum(expo, totals)
    scale, row = rowsum(expo, spread_all(col, "batch", nb))
    totals = doubled(row, "proto", npr)
    col = colsum(expo, totals)
    scale, row = rowsum(expo, gathered(col, "batch", nb))
    total = jnp.sum(gathered(row, "proto", npr)[0], axis=0, keepdims=True)
    total_all = lax.all_gather(total, "batch", axis=0)

    expo_own, grad_own = proto_first(protos_own, views_all, tot_all)
    scale_own = lax.dynamic_slice_in_dim(scale, b * own, own, 1)
    proto_part = proto_last(expo_own, grad_own, scale_own, protos_own, views_all, total_all)
    grad_proto = lax.all_gather(proto_part, "batch", axis=0, tiled=True)

    part = view_grad_part(views, unit_t, expo, scale, tot, total)
    step = 1
    other = jnp.zeros_like(part)
    while step < npr:
        other = lax.ppermute(part, "proto", [(i, i ^ step) for i in range(npr)])
        if step * 2 < npr:
            part = (part.astype(f32) + other.astype(f32)).astype(bf16)
        step *= 2
    both = backward(nb, part, other, pos, raw, pre, emb_part, hid_part, w_out)
    both = lax.all_to_all(both.astype(bf16), "batch", 0, 0, tiled=True)
    both = jnp.sum(both.astype(f32), axis=0, keepdims=True).astype(bf16)
    both = lax.all_gather(both, ("proto", "batch"), axis=0, tiled=True)
    grad_in, grad_out = unpack(both, (wide, hidden_n), (hidden_n, depth))
    return (grad_in, grad_out, grad_proto.astype(f32))


def solution(mesh):
    return jax.shard_map(
        functools.partial(body, mesh.shape["batch"], mesh.shape["proto"]),
        mesh=mesh,
        in_specs=(P("batch", None), P("batch"), P(), P(), P("proto", None)),
        out_specs=(P(), P(), P("proto", None)),
        check_vma=False,
    )
```

time: 378 us -> 334 us (0.88)
  blocking collectives: 63.2 us -> 133 us
  starting transfers between devices: 77.3 us -> 11.8 us
  Pallas kernels: 121 us -> 81.2 us
  waiting for transfers between devices: 75.7 us -> 60.4 us
  local copies, waits for them, and re-layouts: 19.3 us -> 28.2 us
    all_gather x0 -> x4, blocking collectives: none -> 97.1 us  [the longest x2 36 us: gathered(): return [lax.all_gather(x, axis, axis=0, tiled=True)]]
    ppermute x42 -> x5, starting transfers between devices: 75.1 us -> 9.71 us  [doubled(): other = lax.ppermute(x, axis, [(i, i ^ step) for i in range(size)])]
    unnamed x1 -> x0, blocking collectives: 44.8 us -> none
    pallas_call x10 -> x11, Pallas kernels: 114 us -> 76.3 us  [the longest x1 17.2 us: first_pass(): pl.pallas_call(functools.partial(first_kernel, block, chunk), in_specs=[W...]
    all_to_all x0 -> x2, blocking collectives: none -> 28.6 us  [the longest x1 15.1 us: spread_all(): return [lax.all_to_all(wide_x, axis, 0, 0, tiled=True)]]
    unnamed x101 -> x35, local copies, waits for them, and re-layouts: 7.93 us -> 26 us
    ppermute x42 -> x5, waiting for transfers between devices: 26.7 us -> 9.16 us  [doubled(): other = lax.ppermute(x, axis, [(i, i ^ step) for i in range(size)])]
    psum x3 -> x1, blocking collectives: 18.4 us -> 7.05 us  [body(): both = lax.psum(jnp.concatenate([row, tot], axis=0), 'proto')]
  transfers between devices with their start and end apart: 46 -> 10, of which waited for: 16 -> 8; matrix products, arithmetic and copies ran while one was open for 3% -> 1% of each run, Pallas kernels for 7% -> 23%
where the time goes in v2:
time: 334 us; the launch traced here: 333 us
  blocking collectives  133 us (40%)
  Pallas kernels  81.2 us (24%)
  waiting for transfers between devices  60.4 us (18%)
  local copies, waits for them, and re-layouts  28.2 us (8%)
  between operations  13.9 us (4%)
  starting transfers between devices  11.8 us (4%)
  other arithmetic  4.76 us (1%)
    all_gather x1, waiting for transfers between devices, body(): grad_proto = lax.all_gather(proto_part, 'batch', axis=0, tiled=True)  45 us
    all_gather x2, blocking collectives, gathered(): return [lax.all_gather(x, axis, axis=0, tiled=True)]  36 us
    all_gather x1, blocking collectives, body(): total_all = lax.all_gather(total, 'batch', axis=0)  30.7 us
    all_gather x1, blocking collectives, body(): tot_all = lax.all_gather(tot, 'batch', axis=0)  30.4 us
    unnamed x35, local copies, waits for them, and re-layouts  26 us
    pallas_call x1, Pallas kernels, first_pass(): pl.pallas_call(functools.partial(first_kernel, block, chunk), in_specs=[W...  17.2 us
    pallas_call x1, Pallas kernels, view_grad_part(): pl.pallas_call(functools.partial(view_grad_kernel, block), in_specs=[WHOL...  16.2 us
    all_to_all x1, blocking collectives, spread_all(): return [lax.all_to_all(wide_x, axis, 0, 0, tiled=True)]  15.1 us
  transfers between devices with their start and end apart: 10, of which 8 were waited for; matrix products, arithmetic and copies ran while one was open for 1% of the time, Pallas kernels for 23%

profile of v2, /device:TPU:0, one launch (start us, length us, event | category | flops | bytes accessed | tf_op | source)
XLA Modules:
  0.0 333.0 jit_solution(15694764039847841454)
XLA Ops:
  7.2 1.6 copy-done.4
  8.8 1.2 copy-done.11
  10.0 0.9 copy-done.12
  10.9 0.7 copy-done.15
  11.6 4.9 %head.1 = (f32[1024,512]{1,0:T(8,128)S(1)}, bf16[1024,512]{1,0:T(8,128)(2,1)S(1)}, f32[1024,128]{1,0:T(8,128)S(1)}, bf16[1024,128]{1,0:T(8,128)(2,1)S(1)}, bf16[...) custom-call(bf16[1024,1024]{1,0:T(8,128)(2,1)S(1)} %copy-done.4, s32[1,1024]{1,0:T(1,128)S(1)} %bitcast.25, ...), custom_call_target="tpu_custom_call" | custom-call | tf_op jit(solution)/shard_map/head/pallas_call | solution.py:96
  16.5 1.3 copy-done.8
  17.8 1.0 copy-done.14
  18.9 17.2 %first_pass.1 = (bf16[1024,8192]{1,0:T(8,128)(2,1)S(1)}, bf16[128,8192]{1,0:T(8,128)(2,1)S(1)}, f32[1,8192]{1,0:T(1,128)S(1)}, f32[1,1024]{1,0:T(1,128)S(1)}) custom-call(bf16[1024,128]{1,0:T(8,128)(2,1)S(1)} %get-tuple-element.21.views, bf16[8192,128]{1,0:T(8,128)(2,1)S(1)} %copy-done.5), custom_call_target="tpu_custom_call" | custom-call | tf_op jit(solution)/shard_map/first_pass/pallas_call | solution.py:177
  36.1 1.3 copy-done.6
  37.4 3.0 collective-permute-start
  40.4 1.9 collective-permute-done
  42.3 2.1 collective-permute-start.1
  44.5 1.9 collective-permute-done.1
  46.4 3.1 collective-permute-start.2
  49.5 2.1 collective-permute-done.2.refs_1_
  51.6 4.8 %rowsum.3 = (f32[1,8192]{1,0:T(1,128)}, f32[1,1024]{1,0:T(1,128)S(1)}) custom-call(bf16[1024,8192]{1,0:T(8,128)(2,1)S(1)} %get-tuple-element.23.expo, f32[1,8192]{1,0:T(1,128)S(1)} %add.25.refs_0_, f32[1,8192]{1,0:T(1,128)S(1)} %collective-permute-done.2.refs_1_), custom_call_target="tpu_custom_call" | custom-call | tf_op jit(solution)/shard_map/rowsum/pallas_call | solution.py:221
  56.4 7.0 %psum.7 = f32[2,1024]{1,0:T(2,128)S(1)} all-reduce(f32[2,1024]{1,0:T(2,128)S(1)} %pad_maximum_fusion), channel_id=1, replica_groups=mesh['batch'=8,'proto'=4] {'proto'}, use_global_device_ids=true, to_apply=%region_0.0 | all-reduce | flops 2048 | bytes 16384 | tf_op jit(solution)/shard_map/psum | solution.py:482
  63.5 5.8 %copy-done.1 = bf16[1024,8192]{1,0:T(8,128)(2,1)S(1)} copy-done((bf16[1024,8192]{1,0:T(8,128)(2,1)S(1)}, bf16[1024,8192]{1,0:T(8,128)(2,1)}, u32[]{:S(2)}) %copy-start.1) | copy-done | bytes 16777240
  69.3 3.2 colsum.2
  72.6 15.1 %all_to_all.13 = f32[8,1,8192]{2,1,0:T(1,128)S(1)} all-to-all(f32[8,1,8192]{2,1,0:T(1,128)S(1)} %broadcast_in_dim.4), channel_id=1, replica_groups=mesh['batch'=8,'proto'=4] {'batch'}, dimensions={0} | all-to-all | bytes 524288 | tf_op jit(solution)/shard_map/all_to_all | solution.py:469
  87.9 4.5 %rowsum.4 = (f32[1,8192]{1,0:T(1,128)}, f32[1,1024]{1,0:T(1,128)S(1)}) custom-call(bf16[1024,8192]{1,0:T(8,128)(2,1)S(1)} %copy-done.1, f32[8,8192]{1,0:T(8,128)S(1)} %bitcast.19), custom_call_target="tpu_custom_call" | custom-call | tf_op jit(solution)/shard_map/rowsum/pallas_call | solution.py:221
  92.4 1.2 collective-permute-done.3
  93.6 1.5 collective-permute-start.4
  95.1 2.1 collective-permute-done.4.refs_1_
  97.2 3.2 colsum.3
  100.4 30.8 %all-gather.4 = f32[8,1,8192]{2,1,0:T(1,128)S(1)} all-gather(f32[1,1,8192]{2,1,0:T(1,128)S(1)} %bitcast.21), channel_id=1, replica_groups=mesh['batch'=8,'proto'=4] {'batch'}, dimensions={0}, use_global_device_ids=true | all-gather | bytes 294912 | tf_op jit(solution)/shard_map/all_gather | solution.py:472
  131.4 4.4 %rowsum.5 = (f32[1,8192]{1,0:T(1,128)S(1)}, f32[1,1024]{1,0:T(1,128)S(1)}) custom-call(bf16[1024,8192]{1,0:T(8,128)(2,1)S(1)} %copy-done.1, f32[8,8192]{1,0:T(8,128)S(1)} %bitcast.20), custom_call_target="tpu_custom_call" | custom-call | tf_op jit(solution)/shard_map/rowsum/pallas_call | solution.py:221
  135.8 5.2 %all-gather.5 = f32[4,1,1024]{2,1,0:T(1,128)S(1)} all-gather(f32[1,1,1024]{2,1,0:T(1,128)S(1)} %bitcast.26), channel_id=1, replica_groups=mesh['batch'=8,'proto'=4] {'proto'}, dimensions={0}, use_global_device_ids=true | all-gather | bytes 20480 | tf_op jit(solution)/shard_map/all_gather | solution.py:472
  141.0 5.8 %copy-done.2 = bf16[1024,8192]{1,0:T(8,128)(2,1)S(1)} copy-done((bf16[1024,8192]{1,0:T(8,128)(2,1)S(1)}, bf16[1024,8192]{1,0:T(8,128)(2,1)}, u32[]{:S(2)}) %copy-start.2) | copy-done | bytes 16777240
  146.8 1.6 copy-done.7
  148.3 16.2 %view_grad.1 = bf16[1024,128]{1,0:T(8,128)(2,1)S(1)} custom-call(bf16[1024,128]{1,0:T(8,128)(2,1)S(1)} %get-tuple-element.21.views, bf16[128,8192]{1,0:T(8,128)(2,1)S(1)} %copy-done.7, bf16[1024,8192]{1,0:T(8,128)(2,1)S(1)} %copy-done.2, f32[1,8192]{1,0:T(1,128)S(1)} %get-tuple-element.28.scale, f32[1,1024]{1,0:T(1,128)S(1)} %get-tuple-element.40.tot, ...), custom_call_target="tpu_custom_call" | custom-call | tf_op jit(solution)/shard_map/view_grad/pallas_call | solution.py:370
  164.9 1.2 collective-permute-done.5
  166.3 1.6 collective-permute-start.6
  167.8 1.0 constant_dynamic-slice_fusion.2.hid_part
  168.8 1.1 constant_dynamic-slice_fusion.3.emb
  169.9 5.0 %collective-permute-done.6.grad_b = bf16[1024,128]{1,0:T(8,128)(2,1)S(1)} collective-permute-done((bf16[1024,128]{1,0:T(8,128)(2,1)S(1)}, bf16[1024,128]{1,0:T(8,128)(2,1)S(1)}, u32[]{:S(2)}, u32[]{:S(2)}) %collective-permute-start.6) | collective-permute-done | bytes 262176 | tf_op jit(solution)/shard_map/ppermute | solution.py:502
  174.8 1.6 copy-done.9
  176.4 3.2 backward.1
  179.7 13.4 %all_to_all.14 = bf16[8,144,128]{2,1,0:T(8,128)(2,1)S(1)} all-to-all(bf16[8,144,128]{2,1,0:T(8,128)(2,1)S(1)} %convert_element_type.31), channel_id=1, replica_groups=mesh['batch'=8,'proto'=4] {'batch'}, dimensions={0} | all-to-all | bytes 589824 | tf_op jit(solution)/shard_map/all_to_all | solution.py:507
  194.0 30.4 %all-gather.6.totals = f32[8,1,1024]{2,1,0:T(1,128)S(1)} all-gather(f32[1,1,1024]{2,1,0:T(1,128)S(1)} %get-tuple-element.39), channel_id=4, replica_groups=mesh['batch'=8,'proto'=4] {'batch'}, dimensions={0}, use_global_device_ids=true | all-gather | bytes 36864 | tf_op jit(solution)/shard_map/all_gather | solution.py:484
  224.4 30.7 %all-gather.3 = f32[8192]{0:T(1024)S(1)} all-gather(f32[1024]{0:T(1024)S(1)} %reduce_sum.21), channel_id=5, replica_groups=mesh['batch'=8,'proto'=4] {'batch'}, dimensions={0}, use_global_device_ids=true | all-gather | bytes 36864 | tf_op jit(solution)/shard_map/all_gather | solution.py:491
  255.0 1.6 copy-done.3
  256.6 11.6 %proto_first.1 = (bf16[1024,8192]{1,0:T(8,128)(2,1)S(1)}, f32[1024,128]{1,0:T(8,128)S(1)}) custom-call(bf16[1024,128]{1,0:T(8,128)(2,1)S(1)} %constant_dynamic-slice_fusion.1.protos, bf16[8,128,1024]{2,1,0:T(8,128)(2,1)S(1)} %bitcast.16, f32[8,1,1024]{2,1,0:T(1,128)S(1)} %all-gather.6.totals), custom_call_target="tpu_custom_call" | custom-call | tf_op jit(solution)/shard_map/proto_first/pallas_call | solution.py:297
  268.3 6.4 %proto_last.1 = bf16[1024,128]{1,0:T(8,128)(2,1)} custom-call(bf16[1024,8192]{1,0:T(8,128)(2,1)S(1)} %get-tuple-element.37.expo, f32[1024,128]{1,0:T(8,128)S(1)} %get-tuple-element.38.grad, f32[1,1024]{1,0:T(1,128)S(1)} %constant_dynamic-slice_fusion.scale, bf16[1024,128]{1,0:T(8,128)(2,1)S(1)} %constant_dynamic-slice_fusion.1.protos, ...), custom_call_target="tpu_custom_call" | custom-call | tf_op jit(solution)/shard_map/proto_last/pallas_call | solution.py:335
  274.8 1.3 copy-done.10
  276.0 1.5 unpack.1
  277.6 45.0 %all-gather.11.cloned.1.call-done = bf16[8192,128]{1,0:T(8,128)(2,1)} async-done(((bf16[1024,128]{1,0:T(8,128)(2,1)}), bf16[8192,128]{1,0:T(8,128)(2,1)}) %all-gather.11.cloned.1.call-update) | async-done | bytes 2097168 | tf_op jit(solution)/shard_map/all_gather | solution.py:496
  322.6 3.9 %convert_element_type.33 = f32[8192,128]{1,0:T(8,128)} convert(bf16[8192,128]{1,0:T(8,128)(2,1)} %all-gather.11.cloned.1.call-done) | non-fusion elementwise | flops 1048576 | bytes 6291456 | tf_op jit(solution)/shard_map/convert_element_type | solution.py:511
  (43 shorter events, 2.0 us)
Async XLA Ops:
  7.2 247.9 %all-gather.15.cloned.1.call-start = ((), (), s32[]{:S(2)}) async-start(), calls=%async_computation.4 | async-start | bytes 2359296 | tf_op jit(solution)/shard_map/all_gather | solution.py:475
  7.2 1.6 copy-start.4
  8.8 1.2 copy-start.11
  10.0 0.9 copy-start.12
  10.9 0.7 copy-start.15
  11.6 7.3 %copy-start.5 = (bf16[8192,128]{1,0:T(8,128)(2,1)S(1)}, bf16[8192,128]{1,0:T(8,128)(2,1)}, u32[]{:S(2)}) copy-start(bf16[8192,128]{1,0:T(8,128)(2,1)} %protos.1) | copy-start | bytes 6291460
  16.5 1.3 copy-start.8
  17.8 1.0 copy-start.14
  18.8 255.9 %all-gather.13.cloned.1.call-start = ((), (), s32[]{:S(2)}) async-start(), calls=%async_computation.3 | async-start | bytes 1216512 | tf_op jit(solution)/shard_map/all_gather | solution.py:509
  36.1 1.3 copy-start.6
  37.4 19.0 %copy-start = (bf16[1024,8192]{1,0:T(8,128)(2,1)}, bf16[1024,8192]{1,0:T(8,128)(2,1)S(1)}, u32[]{:S(2)}) copy-start(bf16[1024,8192]{1,0:T(8,128)(2,1)S(1)} %get-tuple-element.23.expo) | copy-start | bytes 50331652
  37.4 4.9 %collective-permute-start = (f32[1,8192]{1,0:T(1,128)S(1)}, f32[1,8192]{1,0:T(1,128)S(1)}, u32[]{:S(2)}, u32[]{:S(2)}) collective-permute-start(f32[1,8192]{1,0:T(1,128)S(1)} %get-tuple-element.24), channel_id=1, source_target_pairs={{0,4},{4,0},{8,12},{12,8},{16,20},{20,16},{24,28},{28,24},{1,5},{5... | collective-permute-start | bytes 98312 | tf_op jit(solution)/shard_map/ppermute | solution.py:460
  42.3 4.0 %collective-permute-start.1 = (f32[1,8192]{1,0:T(1,128)S(1)}, f32[1,8192]{1,0:T(1,128)S(1)}, u32[]{:S(2)}, u32[]{:S(2)}) collective-permute-start(f32[1,8192]{1,0:T(1,128)S(1)} %add.24), channel_id=1, source_target_pairs={{0,8},{4,12},{8,0},{12,4},{16,24},{20,28},{24,16},{28,20},{1,9},{5... | collective-permute-start | bytes 98312 | tf_op jit(solution)/shard_map/ppermute | solution.py:460
  46.4 5.2 %collective-permute-start.2 = (f32[1,8192]{1,0:T(1,128)S(1)}, f32[1,8192]{1,0:T(1,128)S(1)}, u32[]{:S(2)}, u32[]{:S(2)}) collective-permute-start(f32[1,8192]{1,0:T(1,128)S(1)} %add.25.refs_0_), channel_id=1, source_target_pairs={{0,16},{4,20},{8,24},{12,28},{16,0},{20,4},{24,8},{28,12},{1,17},{... | collective-permute-start | bytes 98312 | tf_op jit(solution)/shard_map/ppermute | solution.py:460
  63.5 5.8 %copy-start.1 = (bf16[1024,8192]{1,0:T(8,128)(2,1)S(1)}, bf16[1024,8192]{1,0:T(8,128)(2,1)}, u32[]{:S(2)}) copy-start(bf16[1024,8192]{1,0:T(8,128)(2,1)} %copy-done) | copy-start | bytes 50331652
  92.4 1.2 collective-permute-start.3
  93.6 3.6 %collective-permute-start.4 = (f32[1,1024]{1,0:T(1,128)S(1)}, f32[1,1024]{1,0:T(1,128)S(1)}, u32[]{:S(2)}, u32[]{:S(2)}) collective-permute-start(f32[1,1024]{1,0:T(1,128)S(1)} %add.26.refs_0_), channel_id=1, source_target_pairs={{0,2},{1,3},{2,0},{3,1},{4,6},{5,7},{6,4},{7,5},{8,10},{9,11},{10,... | collective-permute-start | bytes 12296 | tf_op jit(solution)/shard_map/ppermute | solution.py:460
  141.0 5.8 %copy-start.2 = (bf16[1024,8192]{1,0:T(8,128)(2,1)S(1)}, bf16[1024,8192]{1,0:T(8,128)(2,1)}, u32[]{:S(2)}) copy-start(bf16[1024,8192]{1,0:T(8,128)(2,1)} %copy-done) | copy-start | bytes 50331652
  146.8 1.6 copy-start.7
  164.6 10.3 %copy-start.13 = (bf16[512,128]{1,0:T(8,128)(2,1)S(1)}, bf16[512,128]{1,0:T(8,128)(2,1)}, u32[]{:S(2)}) copy-start(bf16[512,128]{1,0:T(8,128)(2,1)} %w_out.3) | copy-start | bytes 393220
  164.6 1.6 collective-permute-start.5
  166.3 8.6 %collective-permute-start.6 = (bf16[1024,128]{1,0:T(8,128)(2,1)S(1)}, bf16[1024,128]{1,0:T(8,128)(2,1)S(1)}, u32[]{:S(2)}, u32[]{:S(2)}) collective-permute-start(bf16[1024,128]{1,0:T(8,128)(2,1)S(1)} %add_convert_fusion.grad_a), channel_id=1, source_target_pairs={{0,2},{1,3},{2,0},{3,1},{4,6},{5,7},{6,4},{7,5},{8,10},{9,11},{10,... | collective-permute-start | bytes 786440 | tf_op jit(solution)/shard_map/ppermute | solution.py:502
  174.8 1.6 copy-start.9
  193.9 128.7 %all-gather.11.cloned.1.call-start = ((), (), s32[]{:S(2)}) async-start(), calls=%async_computation.2 | async-start | bytes 2359296 | tf_op jit(solution)/shard_map/all_gather | solution.py:496
  255.0 1.6 copy-start.3
  274.7 1.3 copy-start.10
Sparse Core Ops, SparseCore 0:
  19.0 52.0 all-gather.14
  194.0 52.3 all-gather.12
  274.8 47.6 all-gather.10

commit v3 on v2

v3 whole, which is shorter than its diff:
```python
import functools
import math

import jax
import jax.numpy as jnp
from jax import lax
from jax.experimental import pallas as pl
from jax.experimental.pallas import tpu as pltpu
from jax.sharding import PartitionSpec as P

ITERS = 3
norm_eps = 1e-06
code_temp = 0.05
pred_temp = 0.1
loss_scale = 64.0
GRAD_SCALE = loss_scale / pred_temp
EXP2_SCALE = math.log2(math.e) / pred_temp
GELU_K = math.sqrt(2.0 / math.pi)
GELU_A = 0.044715

f32 = jnp.float32
bf16 = jnp.bfloat16
NN = (((1,), (0,)), ((), ()))
NT = (((1,), (1,)), ((), ()))
TN = (((0,), (0,)), ((), ()))
VMEM_LIMIT = 12 * 1024 * 1024


def dot(a, b, dims=NN):
    return lax.dot_general(a, b, dims, preferred_element_type=f32)


SMALL = pl.CostEstimate(flops=1000, bytes_accessed=1000, transcendentals=0)


def params(*semantics):
    return pltpu.CompilerParams(
        dimension_semantics=semantics or None, vmem_limit_bytes=VMEM_LIMIT
    )


def to_column(vec):
    n = vec.shape[1]
    return jnp.broadcast_to(vec, (8, n)).T[:, :1]


def swap_lanes(x):
    half = x.shape[1] // 2
    return jnp.concatenate([x[:, half:], x[:, :half]], axis=1)


def swap_rows(x):
    half = x.shape[0] // 2
    return jnp.concatenate([x[half:], x[:half]], axis=0)


def in_vmem(x):
    return pltpu.with_memory_space_constraint(x, pltpu.VMEM)


def in_hbm(x):
    return pltpu.with_memory_space_constraint(x, pltpu.HBM)


def full(shape):
    return pl.BlockSpec(shape, lambda *_: (0,) * len(shape))


def head_kernel(emb, pairing, w_in, w_out, pre, hid, raw, views, views_t, pos, scratch):
    step = pl.program_id(0)
    rows = emb.shape[0]
    pre_act = dot(emb[...], w_in[...])
    pre[...] = pre_act
    t = jnp.tanh(GELU_K * (pre_act + GELU_A * (pre_act * pre_act * pre_act)))
    hidden = (0.5 * pre_act * (1.0 + t)).astype(bf16)
    hid[...] = hidden
    raw_out = dot(hidden, w_out[...])
    raw[...] = raw_out
    inv = lax.rsqrt(jnp.sum(raw_out * raw_out, axis=1, keepdims=True) + norm_eps)
    scratch[pl.ds(pl.multiple_of(step * rows, rows), rows), :] = (raw_out * inv).astype(bf16)

    @pl.when(step == pl.num_programs(0) - 1)
    def _():
        mate = pairing[...]
        n = mate.shape[1]
        lane = lax.broadcasted_iota(jnp.int32, (1, n), 1)
        first = lane < mate
        low = jnp.minimum(lane, mate)
        sub = lax.broadcasted_iota(jnp.int32, (n, n), 0)
        before = jnp.where(sub < low, 1.0, 0.0).astype(bf16)
        first8 = jnp.broadcast_to(jnp.where(first, 1.0, 0.0), (8, n)).astype(bf16)
        rank = dot(first8, before)[:1].astype(jnp.int32)
        place = jnp.where(first, rank, rank + n // 2)
        pos[...] = place
        move = jnp.where(sub == place, 1.0, 0.0).astype(bf16)
        ordered = dot(move, scratch[...])
        views[...] = ordered.astype(bf16)
        views_t[...] = ordered.T.astype(bf16)


def head(embeddings, pairing, w_in, w_out):
    rows, wide = embeddings.shape
    hidden = w_in.shape[1]
    depth = w_out.shape[1]
    steps = 4
    block = rows // steps
    return pl.pallas_call(
        head_kernel,
        grid=(steps,),
        in_specs=[
            pl.BlockSpec((block, wide), lambda i: (i, 0)),
            full((1, rows)),
            full((wide, hidden)),
            full((hidden, depth)),
        ],
        out_specs=[
            pl.BlockSpec((block, hidden), lambda i: (i, 0)),
            pl.BlockSpec((block, hidden), lambda i: (i, 0)),
            pl.BlockSpec((block, depth), lambda i: (i, 0)),
            full((rows, depth)),
            full((depth, rows)),
            full((1, rows)),
        ],
        out_shape=[
            pltpu.HBM((rows, hidden), f32),
            pltpu.HBM((rows, hidden), bf16),
            pltpu.HBM((rows, depth), f32),
            jax.ShapeDtypeStruct((rows, depth), bf16),
            jax.ShapeDtypeStruct((depth, rows), bf16),
            jax.ShapeDtypeStruct((1, rows), jnp.int32),
        ],
        scratch_shapes=[pltpu.VMEM((rows, depth), bf16)],
        compiler_params=params("arbitrary"),
        name="head",
    )(in_hbm(embeddings), pairing.reshape(1, rows), in_hbm(w_in), in_hbm(w_out))


def unit_of(protos):
    proto_f = protos.astype(f32)
    inv = lax.rsqrt(jnp.sum(proto_f * proto_f, axis=1, keepdims=True) + norm_eps)
    return proto_f, inv, proto_f * inv


WHOLE = pl.BlockSpec(memory_space=pltpu.VMEM)


def scaled_pair(x, axis):
    wide = x.astype(f32) * EXP2_SCALE
    hi = wide.astype(bf16)
    lo = (wide - hi.astype(f32)).astype(bf16)
    return jnp.concatenate([hi, lo], axis=axis)


def first_kernel(block, chunk, tile, views, protos, expo, col, tot, pair, stage, tot_acc):
    rows, depth = views.shape
    width = protos.shape[0]
    tot_acc[...] = jnp.zeros_like(tot_acc)
    pair[...] = scaled_pair(views[...], 1)

    def one(j, carry):
        here = pl.ds(pl.multiple_of(j * block, block), block)
        _, _, unit = unit_of(protos[here, :])
        unit16 = unit.astype(bf16)
        twice = jnp.concatenate([unit16, unit16], axis=1)
        running = jnp.zeros((8, block), f32)
        for c in range(rows // chunk):
            stage[c % 2] = dot(pair[c * chunk : (c + 1) * chunk, :], twice, NT)
            for start in range(0, chunk, tile):
                part = slice(c * chunk + start, c * chunk + start + tile)
                soft = jnp.exp2(stage[c % 2, start : start + tile, :])
                hard = soft * soft
                expo[part, here] = hard.astype(bf16)
                lanes = soft[:, :128]
                for k in range(1, block // 128):
                    lanes = lanes + soft[:, k * 128 : (k + 1) * 128]
                tot_acc[part, :] += lanes
                for k in range(0, tile, 8):
                    running = running + hard[k : k + 8]
        col[:, here] = jnp.sum(running, axis=0, keepdims=True)
        return carry

    lax.fori_loop(0, width // block, one, 0)
    tot[...] = jnp.sum(tot_acc[...].T, axis=0, keepdims=True)


def first_pass(views, protos):
    rows, depth = views.shape
    width = protos.shape[0]
    block = min(512, width)
    chunk = min(256, rows)
    tile = min(32, chunk)
    return pl.pallas_call(
        functools.partial(first_kernel, block, chunk, tile),
        in_specs=[WHOLE] * 2,
        out_specs=[WHOLE] * 3,
        out_shape=[
            pltpu.VMEM((rows, width), bf16),
            jax.ShapeDtypeStruct((1, width), f32),
            jax.ShapeDtypeStruct((1, rows), f32),
        ],
        scratch_shapes=[
            pltpu.VMEM((rows, 2 * depth), bf16),
            pltpu.VMEM((2, chunk, block), f32),
            pltpu.VMEM((rows, 128), f32),
        ],
        compiler_params=params(),
        cost_estimate=SMALL,
        name="first_pass",
    )(views, protos)


def sum_parts(parts, width):
    if len(parts[0].shape) == 3:
        parts = [parts[0].at[k] for k in range(parts[0].shape[0])]
    total = parts[0][:, :width]
    for other in parts[1:]:
        total = total + other[:, :width]
    return total


def rowsum_kernel(count, expo, *refs):
    parts = refs[:count]
    scale, out, spread, acc = refs[count:]
    rows, width = expo.shape
    inverse = 1.0 / sum_parts(parts, width)
    scale[...] = inverse
    spread[...] = jnp.broadcast_to(inverse, spread.shape).astype(bf16)
    tall = 64

    def one(i, carry):
        here = pl.ds(pl.multiple_of(i * tall, tall), tall)
        running = jnp.zeros((tall, 128), f32)
        for k in range(width // 128):
            lanes = slice(k * 128, (k + 1) * 128)
            weight = jnp.concatenate([spread[:, lanes]] * (tall // 16), axis=0)
            running = running + (expo[here, lanes] * weight).astype(f32)
        acc[here, :] = running
        return carry

    lax.fori_loop(0, rows // tall, one, 0)
    out[...] = jnp.sum(acc[...].T, axis=0, keepdims=True)


def rowsum(expo, parts):
    rows, width = expo.shape
    return pl.pallas_call(
        functools.partial(rowsum_kernel, len(parts)),
        in_specs=[WHOLE] * (1 + len(parts)),
        out_specs=[WHOLE] * 2,
        out_shape=[
            jax.ShapeDtypeStruct((1, width), f32),
            jax.ShapeDtypeStruct((1, rows), f32),
        ],
        scratch_shapes=[pltpu.VMEM((16, width), bf16), pltpu.VMEM((rows, 128), f32)],
        compiler_params=params(),
        cost_estimate=SMALL,
        name="rowsum",
    )(in_vmem(expo), *parts)


def colsum_kernel(count, expo, *refs):
    parts = refs[:count]
    rest = refs[count:]
    out, spread = rest[-2:]
    rows, width = expo.shape
    inverse = 1.0 / sum_parts(parts, rows)
    spread[...] = jnp.broadcast_to(inverse, (128, rows)).T.astype(bf16)
    block = min(512, width)

    def one(j, carry):
        here = pl.ds(pl.multiple_of(j * block, block), block)
        running = jnp.zeros((16, block), f32)
        for i in range(rows // 16):
            part = slice(i * 16, (i + 1) * 16)
            weight = jnp.concatenate([spread[part, :]] * (block // 128), axis=1)
            running = running + (expo[part, here] * weight).astype(f32)
        total = jnp.sum(running, axis=0, keepdims=True)
        for k in range(out.shape[0]):
            out[k, :, here] = total
        return carry

    lax.fori_loop(0, width // block, one, 0)
    if len(rest) > 2:
        for k in range(out.shape[0]):
            out[k, :, width:] = rest[0][...]


def colsum(expo, parts, copies=1, behind=()):
    rows, width = expo.shape
    long = width + sum(x.shape[1] for x in behind)
    return pl.pallas_call(
        functools.partial(colsum_kernel, len(parts)),
        in_specs=[WHOLE] * (1 + len(parts) + len(behind)),
        out_specs=WHOLE,
        out_shape=jax.ShapeDtypeStruct((copies, 1, long), f32),
        scratch_shapes=[pltpu.VMEM((rows, 128), bf16)],
        compiler_params=params(),
        cost_estimate=SMALL,
        name="colsum",
    )(in_vmem(expo), *parts, *behind)


def proto_first_kernel(block, tile, base, protos, views, totals, expo, grad, weights, twice, stage, soft16):
    count, depth, rows = views.shape
    for k in range(count):
        total = totals[k, :, base : base + rows]
        here = slice(k * rows, (k + 1) * rows)
        weights[:, here] = (views[k].astype(f32) * (GRAD_SCALE / total)).astype(bf16)
        twice[:depth, here] = views[k]
        twice[depth:, here] = views[k]

    def one(j, carry):
        here = pl.ds(pl.multiple_of(j * block, block), block)
        _, _, unit = unit_of(protos[here, :])
        pair = scaled_pair(unit.astype(bf16), 1)
        running = jnp.zeros((block, depth), f32)
        for k in range(count):
            part = slice(k * rows, (k + 1) * rows)
            stage[k % 2] = dot(pair, twice[:, part])
            for start in range(0, block, tile):
                soft = jnp.exp2(stage[k % 2, start : start + tile, :])
                soft16[k % 2, start : start + tile, :] = soft.astype(bf16)
                expo[pl.ds(pl.multiple_of(j * block + start, tile), tile), part] = (
                    soft * soft
                ).astype(bf16)
            running = running + dot(soft16[k % 2], weights[:, part], NT)
        grad[here, :] = running
        return carry

    lax.fori_loop(0, protos.shape[0] // block, one, 0)


def proto_first(protos, views, totals, base):
    width, depth = protos.shape
    count, _, rows = views.shape
    block = min(256, width)
    tile = min(16, block)
    return pl.pallas_call(
        functools.partial(proto_first_kernel, block, tile, base),
        in_specs=[WHOLE] * 3,
        out_specs=[WHOLE] * 2,
        out_shape=[
            pltpu.VMEM((width, count * rows), bf16),
            jax.ShapeDtypeStruct((width, depth), f32),
        ],
        scratch_shapes=[
            pltpu.VMEM((depth, count * rows), bf16),
            pltpu.VMEM((2 * depth, count * rows), bf16),
            pltpu.VMEM((2, block, rows), f32),
            pltpu.VMEM((2, block, rows), bf16),
        ],
        compiler_params=params(),
        name="proto_first",
    )(protos, views, totals)


def proto_last_kernel(block, place, expo, grad, scale, protos, views, totals, out, weights):
    count, depth, rows = views.shape
    for k in range(count):
        mates = swap_lanes(views[k])
        weights[:, k * rows : (k + 1) * rows] = (
            mates.astype(f32) * (GRAD_SCALE / totals[place[0] ^ k])
        ).astype(bf16)

    def one(j, carry):
        here = pl.ds(pl.multiple_of(j * block, block), block)
        code = dot(expo[here, :], weights[...], NT)
        there = pl.ds(pl.multiple_of(place[0] * expo.shape[0] + j * block, block), block)
        unit_grad = grad[here, :] - to_column(scale[:, there]) * code
        proto_f, inv, _ = unit_of(protos[here, :])
        inner = jnp.sum(proto_f * unit_grad, axis=1, keepdims=True)
        out[here, :] = (inv * unit_grad - proto_f * (inv * inv * inv) * inner).astype(bf16)
        return carry

    lax.fori_loop(0, protos.shape[0] // block, one, 0)


def proto_last(place, expo, grad, scale, protos, views, totals):
    width, depth = protos.shape
    count, _, rows = views.shape
    block = min(256, width)
    return pl.pallas_call(
        functools.partial(proto_last_kernel, block),
        in_specs=[pl.BlockSpec(memory_space=pltpu.SMEM)] + [WHOLE] * 6,
        out_specs=WHOLE,
        out_shape=jax.ShapeDtypeStruct((width, depth), bf16),
        scratch_shapes=[pltpu.VMEM((depth, count * rows), bf16)],
        compiler_params=params(),
        name="proto_last",
    )(place, in_vmem(expo), grad, scale, protos, views, totals)


def view_grad_kernel(block, tile, views, protos, expo, scale, tot, total, out, *scratch):
    pair, stage, soft16, soft_acc, hard_acc = scratch
    rows, depth = views.shape
    width = expo.shape[1]
    pair[...] = scaled_pair(views[...], 1)
    soft_acc[...] = jnp.zeros_like(soft_acc)
    hard_acc[...] = jnp.zeros_like(hard_acc)

    def one(j, carry):
        here = pl.ds(pl.multiple_of(j * block, block), block)
        _, _, unit = unit_of(protos[here, :])
        unit16 = unit.astype(bf16)
        scaled = (unit16.astype(f32) * to_column(scale[:, here])).astype(bf16)
        stage[...] = dot(pair[...], jnp.concatenate([unit16, unit16], axis=1), NT)
        for start in range(0, rows, tile):
            part = slice(start, start + tile)
            soft16[part, :] = jnp.exp2(stage[part, :]).astype(bf16)
        soft_acc[...] += dot(soft16[...], unit16)
        hard_acc[...] += dot(expo[:, here], scaled)
        return carry

    lax.fori_loop(0, width // block, one, 0)
    soft = soft_acc[...] * to_column(GRAD_SCALE / tot[...])
    hard = swap_rows(hard_acc[...] * to_column(GRAD_SCALE / total[...]))
    out[...] = (soft - hard).astype(out.dtype)


def view_grad_part(views, protos, expo, scale, tot, total):
    rows, depth = views.shape
    block = min(512, expo.shape[1])
    return pl.pallas_call(
        functools.partial(view_grad_kernel, block, min(32, rows)),
        in_specs=[WHOLE] * 6,
        out_specs=WHOLE,
        out_shape=jax.ShapeDtypeStruct((rows, depth), bf16),
        scratch_shapes=[
            pltpu.VMEM((rows, 2 * depth), bf16),
            pltpu.VMEM((rows, block), f32),
            pltpu.VMEM((rows, block), bf16),
            pltpu.VMEM((rows, depth), f32),
            pltpu.VMEM((rows, depth), f32),
        ],
        compiler_params=params(),
        name="view_grad",
    )(views, protos, in_vmem(expo), scale, tot, total)


def backward_kernel(grad_a, grad_b, pos, raw, pre, emb, hid_part, w_out, out):
    total = grad_a[...].astype(f32) + grad_b[...].astype(f32)
    n, depth = raw.shape
    place = jnp.broadcast_to(pos[...].astype(f32), (8, n)).T[:, :1].astype(jnp.int32)
    lane = lax.broadcasted_iota(jnp.int32, (n, n), 1)
    move = jnp.where(lane == place, 1.0, 0.0).astype(bf16)
    hi = total.astype(bf16)
    lo = (total - hi.astype(f32)).astype(bf16)
    moved = dot(move, jnp.concatenate([hi, lo], axis=1))
    grad = moved[:, :depth] + moved[:, depth:]
    raw_out = raw[...]
    inv = lax.rsqrt(jnp.sum(raw_out * raw_out, axis=1, keepdims=True) + norm_eps)
    inner = jnp.sum(raw_out * grad, axis=1, keepdims=True)
    d_raw = (inv * grad - raw_out * (inv * inv * inv) * inner).astype(bf16)
    g_out = dot(hid_part[...], d_raw, TN)
    d_hidden = dot(d_raw, w_out[...], NT)
    v = pre[...]
    t = jnp.tanh(GELU_K * (v + GELU_A * (v * v * v)))
    slope = 0.5 * (1.0 + t) + (0.5 * GELU_K) * v * (1.0 - t * t) * (1.0 + (3.0 * GELU_A) * (v * v))
    d_pre = (slope * d_hidden).astype(bf16)
    g_in = dot(emb[...], d_pre, TN)
    count = out.shape[0]
    tall, wide = g_in.shape[0] // count, g_in.shape[1]
    for k in range(count):
        for q in range(wide // 128):
            out[k, q * tall : (q + 1) * tall, :] = g_in[
                k * tall : (k + 1) * tall, q * 128 : (q + 1) * 128
            ]
        base, short = tall * (wide // 128), g_out.shape[0] // count
        out[k, base : base + short, :] = g_out[k * short : (k + 1) * short]


def backward(nb, grad_a, grad_b, pos, raw, pre, emb, hid_part, w_out):
    lines = (emb.shape[1] * pre.shape[1] + hid_part.shape[1] * raw.shape[1]) // (nb * 128)
    return pl.pallas_call(
        backward_kernel,
        in_specs=[WHOLE] * 8,
        out_specs=WHOLE,
        out_shape=jax.ShapeDtypeStruct((nb, lines, 128), f32),
        compiler_params=params(),
        name="backward",
    )(grad_a, grad_b, pos, raw, pre, emb, hid_part, w_out)


def unpack_kernel(order, place, *refs):
    pieces, (g_in, g_out) = refs[:-2], refs[-2:]
    nb = pieces[0].shape[1]
    npr = len(order)
    tall, wide = g_in.shape[0] // (nb * npr), g_in.shape[1]
    base, short = tall * (wide // 128), g_out.shape[0] // (nb * npr)
    half = pieces[0].shape[0]
    for n, flip in enumerate(order):
        owner = place[0] ^ flip
        for k in range(nb):
            x = pieces[n // half][n % half, k].astype(f32)
            low = pl.multiple_of((owner * nb + k) * tall, tall)
            for q in range(wide // 128):
                g_in[pl.ds(low, tall), q * 128 : (q + 1) * 128] = x[q * tall : (q + 1) * tall]
            low = pl.multiple_of((owner * nb + k) * short, short)
            g_out[pl.ds(low, short), :] = x[base : base + short]


def unpack(order, place, pieces, shape_in, shape_out):
    return pl.pallas_call(
        functools.partial(unpack_kernel, order),
        in_specs=[pl.BlockSpec(memory_space=pltpu.SMEM)] + [WHOLE] * len(pieces),
        out_specs=[WHOLE] * 2,
        out_shape=[jax.ShapeDtypeStruct(shape_in, f32), jax.ShapeDtypeStruct(shape_out, f32)],
        compiler_params=params(),
        name="unpack",
    )(place, *pieces)


def body(nb, npr, embeddings, pairing, w_in, w_out, prototypes):
    b = lax.axis_index("batch")
    p = lax.axis_index("proto")
    rows, wide = embeddings.shape
    width, depth = prototypes.shape
    hidden_n = w_in.shape[1]
    own = width // nb

    def flipped(x, axis, size, step):
        return lax.ppermute(x, axis, [(i, i ^ step) for i in range(size)])

    def doubled(x, axis, size):
        step = 1
        while step * 2 < size:
            x = x + flipped(x, axis, size, step)
            step *= 2
        return [x, flipped(x, axis, size, step)] if size > 1 else [x]

    def shared(x):
        wide_x = jnp.broadcast_to(x, (nb,) + x.shape[1:])
        return lax.all_to_all(wide_x, "batch", 0, 0, tiled=True)

    pre, hid, raw, views, views_t, pos = head(embeddings, pairing, w_in, w_out)
    views_all = lax.all_gather(views_t, "batch", axis=0)
    protos_own = lax.dynamic_slice_in_dim(prototypes, b * own, own, 0)
    place = b.astype(jnp.int32).reshape(1)
    views, protos_own, place = lax.optimization_barrier((views, protos_own, place))
    expo, col, tot = first_pass(views, prototypes)

    scale, row = rowsum(expo, doubled(col, "batch", nb))
    first, second = doubled(jnp.concatenate([row, tot], axis=0), "proto", npr)
    both = first + second
    totals, tot = [both[:1]], both[1:]
    packed = lax.all_to_all(colsum(expo, totals, nb, [tot]), "batch", 0, 0, tiled=True)
    scale, row = rowsum(expo, [packed])
    col = colsum(expo, doubled(row, "proto", npr))
    col, views_all = lax.optimization_barrier((col, views_all))
    expo_own, grad_own = proto_first(protos_own, views_all, packed, width)
    scale, row = rowsum(expo, doubled(col[0], "batch", nb))
    first, second = doubled(row, "proto", npr)
    total = first + second
    total_all = total[None]
    step = 1
    while step < nb:
        total_all = jnp.concatenate([total_all, flipped(total_all, "batch", nb, step)], axis=0)
        step *= 2

    proto_part = proto_last(
        place, expo_own, grad_own, scale, protos_own, views_all, total_all)
    grad_proto = lax.all_gather(proto_part, "batch", axis=0, tiled=True)

    part = view_grad_part(views, prototypes, expo, scale, tot, total)
    step = 1
    while step * 2 < npr:
        other = flipped(part, "proto", npr, step)
        part = (part.astype(f32) + other.astype(f32)).astype(bf16)
        step *= 2
    other = flipped(part, "proto", npr, step)
    emb_part = lax.dynamic_slice_in_dim(embeddings, p * (wide // npr), wide // npr, 1)
    hid_part = lax.dynamic_slice_in_dim(hid, p * (hidden_n // npr), hidden_n // npr, 1)
    both = backward(nb, part, other, pos, raw, pre, emb_part, hid_part, w_out)
    both = lax.all_to_all(both.astype(bf16), "batch", 0, 0, tiled=True)
    both = jnp.sum(both.astype(f32), axis=0, keepdims=True).astype(bf16)
    piece = shared(both)[None]
    order = [0]
    step = npr // 2
    while step > 1:
        piece = jnp.concatenate([piece, flipped(piece, "proto", npr, step)], axis=0)
        order = order + [i ^ step for i in order]
        step //= 2
    pieces = [piece, flipped(piece, "proto", npr, 1)]
    order = order + [i ^ 1 for i in order]
    grad_in, grad_out = unpack(
        order, p.astype(jnp.int32).reshape(1), pieces, (wide, hidden_n), (hidden_n, depth)
    )
    return (grad_in, grad_out, grad_proto.astype(f32))


def solution(mesh):
    return jax.shard_map(
        functools.partial(body, mesh.shape["batch"], mesh.shape["proto"]),
        mesh=mesh,
        in_specs=(P("batch", None), P("batch"), P(), P(), P("proto", None)),
        out_specs=(P(), P(), P("proto", None)),
        check_vma=False,
    )
```

time: 334 us -> 233 us (0.70)
  blocking collectives: 133 us -> 50.2 us
  local copies, waits for them, and re-layouts: 28.2 us -> 14.5 us
  waiting for transfers between devices: 60.4 us -> 48 us
  starting transfers between devices: 11.8 us -> 19.6 us
    all_gather x4 -> x0, blocking collectives: 97.1 us -> none  [the longest x2 36 us: gathered(): return [lax.all_gather(x, axis, axis=0, tiled=True)]]
    all_gather x1, waiting for transfers between devices: 45 us -> 0.01 us  [body(): grad_proto = lax.all_gather(proto_part, 'batch', axis=0, tiled=True)]
    ppermute x7 -> x19, waiting for transfers between devices: 15.4 us -> 48 us  [flipped(): return lax.ppermute(x, axis, [(i, i ^ step) for i in range(size)])]
    all_to_all x1 -> x2, blocking collectives: 15.1 us -> 33 us  [the longest x1 19.6 us: body(): lax.all_to_all(colsum(expo, totals, nb, [tot]), 'batch', 0, 0, tiled=True)]
    unnamed x35 -> x18, local copies, waits for them, and re-layouts: 26 us -> 12.4 us
    ppermute x7 -> x19, starting transfers between devices: 11.6 us -> 19.6 us  [flipped(): return lax.ppermute(x, axis, [(i, i ^ step) for i in range(size)])]
    psum x1 -> x0, blocking collectives: 7.05 us -> none  [body(): both = lax.psum(jnp.concatenate([row, tot], axis=0), 'proto')]
    all_to_all x1, blocking collectives: 13.4 us -> 17.3 us  [body(): both = lax.all_to_all(both.astype(bf16), 'batch', 0, 0, tiled=True)]
  transfers between devices with their start and end apart: 10 -> 21, of which waited for: 8 -> 18; matrix products, arithmetic and copies ran while one was open for 1% -> 1% of each run, Pallas kernels for 23% -> 27%
where the time goes in v3:
time: 233 us
  Pallas kernels  81.9 us (35%)
  blocking collectives  50.2 us (22%)
  waiting for transfers between devices  48 us (21%)
  starting transfers between devices  19.6 us (8%)
  local copies, waits for them, and re-layouts  14.5 us (6%)
  between operations  14.3 us (6%)
  other arithmetic  4.35 us (2%)
    ppermute x19, waiting for transfers between devices, flipped(): return lax.ppermute(x, axis, [(i, i ^ step) for i in range(size)])  48 us
    all_to_all x1, blocking collectives, body(): lax.all_to_all(colsum(expo, totals, nb, [tot]), 'batch', 0, 0, tiled=True)  19.6 us
    ppermute x19, starting transfers between devices, flipped(): return lax.ppermute(x, axis, [(i, i ^ step) for i in range(size)])  19.6 us
    pallas_call x1, Pallas kernels, view_grad_part(): pl.pallas_call(functools.partial(view_grad_kernel, block, min(32, rows)),...  19.4 us
    all_to_all x1, blocking collectives, body(): both = lax.all_to_all(both.astype(bf16), 'batch', 0, 0, tiled=True)  17.3 us
    pallas_call x3, Pallas kernels, rowsum(): pl.pallas_call(functools.partial(rowsum_kernel, len(parts)), in_specs=[WH...  14.6 us
    all_to_all x1, blocking collectives, shared(): return lax.all_to_all(wide_x, 'batch', 0, 0, tiled=True)  13.4 us
    unnamed x18, local copies, waits for them, and re-layouts  12.4 us
  transfers between devices with their start and end apart: 21, of which 18 were waited for; matrix products, arithmetic and copies ran while one was open for 1% of the time, Pallas kernels for 27%

profile of v3, /device:TPU:0, one launch (start us, length us, event | category | flops | bytes accessed | tf_op | source)
XLA Modules:
  0.0 232.9 jit_solution(4893994827768782824)
XLA Ops:
  8.0 7.3 %head.1 = (f32[1024,512]{1,0:T(8,128)}, bf16[1024,512]{1,0:T(8,128)(2,1)}, f32[1024,128]{1,0:T(8,128)}, bf16[1024,128]{1,0:T(8,128)(2,1)S(1)}, bf16[128,1024]{1,0:T(8,128)(2,1)}, /*index=5*/s32[1,1024]{1,0:T(1,128)S(1)}) custom-call(bf16[1024,1024]{1,0:T(8,128)(2,1)} %emb.1, s32[1,1024]{1,0:T(1,128)S(1)} %bitcast.15, bf16[1024,512]{1,0:T(8,128)(2,1)} %w_in.1, ...), custom_call_target="tpu_custom_call" | custom-call | tf_op jit(solution)/shard_map/head/pallas_call | solution.py:107
  15.4 11.0 %first_pass.1 = (bf16[1024,8192]{1,0:T(8,128)(2,1)S(1)}, f32[1,8192]{1,0:T(1,128)S(1)}, f32[1,1024]{1,0:T(1,128)S(1)}) custom-call(bf16[1024,128]{1,0:T(8,128)(2,1)S(1)} %get-tuple-element.26.views, bf16[8192,128]{1,0:T(8,128)(2,1)S(1)} %copy-done.3), custom_call_target="tpu_custom_call" | custom-call | flops 1000 | bytes 1000 | tf_op jit(solution)/shard_map/first_pass/pallas_call | solution.py:192
  26.4 3.0 %collective-permute-start = (f32[1,8192]{1,0:T(1,128)S(1)}, f32[1,8192]{1,0:T(1,128)S(1)}, u32[]{:S(2)}, u32[]{:S(2)}) collective-permute-start(f32[1,8192]{1,0:T(1,128)S(1)} %get-tuple-element.28), channel_id=1, source_target_pairs={{0,4},{4,0},{8,12},{12,8},{16,20},{20,16},{24,28},{28,24},{1,5},{5... | collective-permute-start | bytes 98312 | tf_op jit(solution)/shard_map/ppermute | solution.py:522
  29.4 2.6 %collective-permute-done = f32[1,8192]{1,0:T(1,128)S(1)} collective-permute-done((f32[1,8192]{1,0:T(1,128)S(1)}, f32[1,8192]{1,0:T(1,128)S(1)}, u32[]{:S(2)}, u32[]{:S(2)}) %collective-permute-start) | collective-permute-done | bytes 32800 | tf_op jit(solution)/shard_map/ppermute | solution.py:522
  32.1 1.9 collective-permute-start.1
  33.9 3.2 %collective-permute-done.1 = f32[1,8192]{1,0:T(1,128)S(1)} collective-permute-done((f32[1,8192]{1,0:T(1,128)S(1)}, f32[1,8192]{1,0:T(1,128)S(1)}, u32[]{:S(2)}, u32[]{:S(2)}) %collective-permute-start.1) | collective-permute-done | bytes 32800 | tf_op jit(solution)/shard_map/ppermute | solution.py:522
  37.2 2.0 collective-permute-start.2
  39.2 2.8 %collective-permute-done.2.refs_1_ = f32[1,8192]{1,0:T(1,128)S(1)} collective-permute-done((f32[1,8192]{1,0:T(1,128)S(1)}, f32[1,8192]{1,0:T(1,128)S(1)}, u32[]{:S(2)}, u32[]{:S(2)}) %collective-permute-start.2) | collective-permute-done | bytes 32800 | tf_op jit(solution)/shard_map/ppermute | solution.py:522
  42.1 4.9 %rowsum.3 = (f32[1,8192]{1,0:T(1,128)}, f32[1,1024]{1,0:T(1,128)S(1)}) custom-call(bf16[1024,8192]{1,0:T(8,128)(2,1)S(1)} %get-tuple-element.27.expo, f32[1,8192]{1,0:T(1,128)S(1)} %add.41.refs_0_, f32[1,8192]{1,0:T(1,128)S(1)} %collective-permute-done.2.refs_1_), custom_call_target="tpu_custom_call" | custom-call | flops 1000 | bytes 1000 | tf_op jit(solution)/shard_map/rowsum/pallas_call | solution.py:246
  47.1 1.2 collective-permute-done.3
  48.3 1.9 collective-permute-start.4
  50.2 1.8 collective-permute-done.4
  52.0 3.3 %colsum.2 = f32[8,1,9216]{2,1,0:T(1,128)S(1)} custom-call(bf16[1024,8192]{1,0:T(8,128)(2,1)S(1)} %get-tuple-element.27.expo, f32[1,1024]{1,0:T(1,128)S(1)} %get-tuple-element.48.refs_0_, f32[1,1024]{1,0:T(1,128)S(1)} %get-tuple-element.47.refs_1_.tot), custom_call_target="tpu_custom_call" | custom-call | flops 1000 | bytes 1000 | tf_op jit(solution)/shard_map/colsum/pallas_call | solution.py:291
  55.4 19.6 %all_to_all.15.refs_0_.totals = f32[8,1,9216]{2,1,0:T(1,128)S(1)} all-to-all(f32[8,1,9216]{2,1,0:T(1,128)S(1)} %colsum.2), channel_id=1, replica_groups=mesh['batch'=8,'proto'=4] {'batch'}, dimensions={0} | all-to-all | bytes 589824 | tf_op jit(solution)/shard_map/all_to_all | solution.py:546
  75.0 5.0 %rowsum.4 = (f32[1,8192]{1,0:T(1,128)}, f32[1,1024]{1,0:T(1,128)S(1)}) custom-call(bf16[1024,8192]{1,0:T(8,128)(2,1)S(1)} %get-tuple-element.27.expo, f32[8,1,9216]{2,1,0:T(1,128)S(1)} %all_to_all.15.refs_0_.totals), custom_call_target="tpu_custom_call" | custom-call | flops 1000 | bytes 1000 | tf_op jit(solution)/shard_map/rowsum/pallas_call | solution.py:246
  79.9 1.2 collective-permute-done.5
  81.1 1.5 collective-permute-start.6
  82.6 2.1 collective-permute-done.6.refs_1_
  84.7 3.3 %colsum.3 = f32[1,1,8192]{2,1,0:T(1,128)S(1)} custom-call(bf16[1024,8192]{1,0:T(8,128)(2,1)S(1)} %get-tuple-element.27.expo, f32[1,1024]{1,0:T(1,128)S(1)} %add.44.refs_0_, f32[1,1024]{1,0:T(1,128)S(1)} %collective-permute-done.6.refs_1_), custom_call_target="tpu_custom_call" | custom-call | flops 1000 | bytes 1000 | tf_op jit(solution)/shard_map/colsum/pallas_call | solution.py:291
  88.1 1.5 collective-permute-start.7
  89.5 2.5 %collective-permute-done.7 = f32[1,8192]{1,0:T(1,128)S(1)} collective-permute-done((f32[1,8192]{1,0:T(1,128)S(1)}, f32[1,8192]{1,0:T(1,128)S(1)}, u32[]{:S(2)}, u32[]{:S(2)}) %collective-permute-start.7) | collective-permute-done | bytes 32800 | tf_op jit(solution)/shard_map/ppermute | solution.py:522
  92.7 3.4 %collective-permute-done.8 = f32[1,8192]{1,0:T(1,128)S(1)} collective-permute-done((f32[1,8192]{1,0:T(1,128)S(1)}, f32[1,8192]{1,0:T(1,128)S(1)}, u32[]{:S(2)}, u32[]{:S(2)}) %collective-permute-start.8) | collective-permute-done | bytes 32800 | tf_op jit(solution)/shard_map/ppermute | solution.py:522
  96.6 4.7 %collective-permute-done.9.refs_1_ = f32[1,8192]{1,0:T(1,128)S(1)} collective-permute-done((f32[1,8192]{1,0:T(1,128)S(1)}, f32[1,8192]{1,0:T(1,128)S(1)}, u32[]{:S(2)}, u32[]{:S(2)}) %collective-permute-start.9) | collective-permute-done | bytes 32800 | tf_op jit(solution)/shard_map/ppermute | solution.py:522
  101.3 5.8 %copy-done.1 = bf16[1024,8192]{1,0:T(8,128)(2,1)S(1)} copy-done((bf16[1024,8192]{1,0:T(8,128)(2,1)S(1)}, bf16[1024,8192]{1,0:T(8,128)(2,1)}, u32[]{:S(2)}) %copy-start.1) | copy-done | bytes 16777240
  107.1 4.7 %rowsum.5 = (f32[1,8192]{1,0:T(1,128)S(1)}, f32[1,1024]{1,0:T(1,128)S(1)}) custom-call(bf16[1024,8192]{1,0:T(8,128)(2,1)S(1)} %copy-done.1, f32[1,8192]{1,0:T(1,128)S(1)} %add.46.refs_0_, f32[1,8192]{1,0:T(1,128)S(1)} %collective-permute-done.9.refs_1_), custom_call_target="tpu_custom_call" | custom-call | flops 1000 | bytes 1000 | tf_op jit(solution)/shard_map/rowsum/pallas_call | solution.py:246
  111.8 1.2 collective-permute-done.10
  113.0 1.5 collective-permute-start.11
  114.5 2.1 collective-permute-done.11
  116.6 1.4 collective-permute-start.16
  118.0 2.2 collective-permute-done.16
  120.5 3.4 %collective-permute-done.17 = f32[2,1,1024]{2,1,0:T(1,128)S(1)} collective-permute-done((f32[2,1,1024]{2,1,0:T(1,128)S(1)}, f32[2,1,1024]{2,1,0:T(1,128)S(1)}, u32[]{:S(2)}, u32[]{:S(2)}) %collective-permute-start.17) | collective-permute-done | bytes 8224 | tf_op jit(solution)/shard_map/ppermute | solution.py:522
  124.1 11.7 %proto_first.1 = (bf16[1024,8192]{1,0:T(8,128)(2,1)S(1)}, f32[1024,128]{1,0:T(8,128)S(1)}) custom-call(bf16[1024,128]{1,0:T(8,128)(2,1)S(1)} %constant_dynamic-slice_fusion.2.protos, bf16[8,128,1024]{2,1,0:T(8,128)(2,1)S(1)} %bitcast.8, f32[8,1,9216]{2,1,0:T(1,128)S(1)} %all_to_all.15.refs_0_.totals), custom_call_target="tpu_custom_call" | custom-call | tf_op jit(solution)/shard_map/proto_first/pallas_call | solution.py:338
  135.9 6.5 %proto_last.1 = bf16[1024,128]{1,0:T(8,128)(2,1)} custom-call(s32[1]{0:T(128)} %bitcast.2.place, bf16[1024,8192]{1,0:T(8,128)(2,1)S(1)} %get-tuple-element.45.expo, f32[1024,128]{1,0:T(8,128)S(1)} %get-tuple-element.46.grad, f32[1,8192]{1,0:T(1,128)S(1)} %get-tuple-element.34.scale, bf16[1024,128]{1,0:T(8,128)(2,1)S(1)} %constant_dynamic-slice_fusion.2.protos, ...), custom_call_target="tpu_custom_call" | custom-call | tf_op jit(solution)/shard_map/proto_last/pallas_call | solution.py:382
  142.4 5.8 %copy-done.2 = bf16[1024,8192]{1,0:T(8,128)(2,1)S(1)} copy-done((bf16[1024,8192]{1,0:T(8,128)(2,1)S(1)}, bf16[1024,8192]{1,0:T(8,128)(2,1)}, u32[]{:S(2)}) %copy-start.2) | copy-done | bytes 16777240
  148.2 19.4 %view_grad.1 = bf16[1024,128]{1,0:T(8,128)(2,1)S(1)} custom-call(bf16[1024,128]{1,0:T(8,128)(2,1)S(1)} %get-tuple-element.26.views, bf16[8192,128]{1,0:T(8,128)(2,1)S(1)} %copy-done.3, bf16[1024,8192]{1,0:T(8,128)(2,1)S(1)} %copy-done.2, f32[1,8192]{1,0:T(1,128)S(1)} %get-tuple-element.34.scale, f32[1,1024]{1,0:T(1,128)S(1)} %get-tuple-element.47.refs_1_.tot, ...), custom_call_target="tpu_custom_call" | custom-call | tf_op jit(solution)/shard_map/view_grad/pallas_call | solution.py:423
  167.7 1.5 collective-permute-done.12
  169.3 1.6 collective-permute-start.13
  170.8 1.0 constant_dynamic-slice_fusion.hid_part
  171.8 1.1 constant_dynamic-slice_fusion.1.emb
  172.9 4.8 %collective-permute-done.13.grad_b = bf16[1024,128]{1,0:T(8,128)(2,1)S(1)} collective-permute-done((bf16[1024,128]{1,0:T(8,128)(2,1)S(1)}, bf16[1024,128]{1,0:T(8,128)(2,1)S(1)}, u32[]{:S(2)}, u32[]{:S(2)}) %collective-permute-start.13) | collective-permute-done | bytes 262176 | tf_op jit(solution)/shard_map/ppermute | solution.py:522
  177.7 3.3 %backward.1 = f32[8,144,128]{2,1,0:T(8,128)S(1)} custom-call(bf16[1024,128]{1,0:T(8,128)(2,1)S(1)} %add_convert_fusion.grad_a, bf16[1024,128]{1,0:T(8,128)(2,1)S(1)} %collective-permute-done.13.grad_b, s32[1,1024]{1,0:T(1,128)S(1)} %get-tuple-element.36.pos, f32[1024,128]{1,0:T(8,128)S(1)} %copy-done.6, f32[1024,512]{1,0:T(8,128)S(1)} %copy-done.5, ...), custom_call_target="tpu_custom_call" | custom-call | tf_op jit(solution)/shard_map/backward/pallas_call | solution.py:474
  181.1 17.3 %all_to_all.16 = bf16[8,144,128]{2,1,0:T(8,128)(2,1)S(1)} all-to-all(bf16[8,144,128]{2,1,0:T(8,128)(2,1)S(1)} %convert_element_type.25), channel_id=1, replica_groups=mesh['batch'=8,'proto'=4] {'batch'}, dimensions={0} | all-to-all | bytes 589824 | tf_op jit(solution)/shard_map/all_to_all | solution.py:574
  198.5 13.4 %all_to_all.17 = bf16[8,144,128]{2,1,0:T(8,128)(2,1)S(1)} all-to-all(bf16[8,144,128]{2,1,0:T(8,128)(2,1)S(1)} %broadcast_in_dim.12), channel_id=1, replica_groups=mesh['batch'=8,'proto'=4] {'batch'}, dimensions={0} | all-to-all | bytes 589824 | tf_op jit(solution)/shard_map/all_to_all | solution.py:533
  211.8 1.5 collective-permute-start.14
  213.3 5.3 %collective-permute-done.14 = bf16[1,8,144,128]{3,2,1,0:T(8,128)(2,1)S(1)} collective-permute-done((bf16[1,8,144,128]{3,2,1,0:T(8,128)(2,1)S(1)}, bf16[1,8,144,128]{3,2,1,0:T(8,128)(2,1)S(1)}, u32[]{:S(2)}, u32[]{:S(2)}) %collective-permute-start.14) | collective-permute-done | bytes 294944 | tf_op jit(solution)/shard_map/ppermute | solution.py:522
  218.7 2.0 collective-permute-done.15.refs_1_
  220.7 1.5 unpack.1
  222.2 3.9 %convert_element_type.26 = f32[8192,128]{1,0:T(8,128)} convert(bf16[8192,128]{1,0:T(8,128)(2,1)} %all-gather.4.cloned.1.call-done) | non-fusion elementwise | flops 1048576 | bytes 6291456 | tf_op jit(solution)/shard_map/convert_element_type | solution.py:588
  (52 shorter events, 3.4 us)
Async XLA Ops:
  7.2 8.2 %copy-start.3 = (bf16[8192,128]{1,0:T(8,128)(2,1)S(1)}, bf16[8192,128]{1,0:T(8,128)(2,1)}, u32[]{:S(2)}) copy-start(bf16[8192,128]{1,0:T(8,128)(2,1)} %protos.3) | copy-start | bytes 6291460
  7.2 80.9 %all-gather.6.cloned.1.call-start = ((), (), s32[]{:S(2)}) async-start(), calls=%async_computation.4 | async-start | bytes 2359296 | tf_op jit(solution)/shard_map/all_gather | solution.py:536
  7.2 0.8 copy-start.8
  15.3 206.9 %all-gather.4.cloned.1.call-start = ((), (), s32[]{:S(2)}) async-start(), calls=%async_computation.3 | async-start | bytes 2359296 | tf_op jit(solution)/shard_map/all_gather | solution.py:562
  26.4 58.3 %copy-start = (bf16[1024,8192]{1,0:T(8,128)(2,1)}, bf16[1024,8192]{1,0:T(8,128)(2,1)S(1)}, u32[]{:S(2)}) copy-start(bf16[1024,8192]{1,0:T(8,128)(2,1)S(1)} %get-tuple-element.27.expo) | copy-start | bytes 50331652
  26.4 5.6 %collective-permute-start = (f32[1,8192]{1,0:T(1,128)S(1)}, f32[1,8192]{1,0:T(1,128)S(1)}, u32[]{:S(2)}, u32[]{:S(2)}) collective-permute-start(f32[1,8192]{1,0:T(1,128)S(1)} %get-tuple-element.28), channel_id=1, source_target_pairs={{0,4},{4,0},{8,12},{12,8},{16,20},{20,16},{24,28},{28,24},{1,5},{5... | collective-permute-start | bytes 98312 | tf_op jit(solution)/shard_map/ppermute | solution.py:522
  32.1 5.1 %collective-permute-start.1 = (f32[1,8192]{1,0:T(1,128)S(1)}, f32[1,8192]{1,0:T(1,128)S(1)}, u32[]{:S(2)}, u32[]{:S(2)}) collective-permute-start(f32[1,8192]{1,0:T(1,128)S(1)} %add.40), channel_id=1, source_target_pairs={{0,8},{4,12},{8,0},{12,4},{16,24},{20,28},{24,16},{28,20},{1,9},{5... | collective-permute-start | bytes 98312 | tf_op jit(solution)/shard_map/ppermute | solution.py:522
  37.2 4.9 %collective-permute-start.2 = (f32[1,8192]{1,0:T(1,128)S(1)}, f32[1,8192]{1,0:T(1,128)S(1)}, u32[]{:S(2)}, u32[]{:S(2)}) collective-permute-start(f32[1,8192]{1,0:T(1,128)S(1)} %add.41.refs_0_), channel_id=1, source_target_pairs={{0,16},{4,20},{8,24},{12,28},{16,0},{20,4},{24,8},{28,12},{1,17},{... | collective-permute-start | bytes 98312 | tf_op jit(solution)/shard_map/ppermute | solution.py:522
  47.0 1.2 collective-permute-start.3
  48.3 3.7 %collective-permute-start.4 = (f32[2,1024]{1,0:T(2,128)S(1)}, f32[2,1024]{1,0:T(2,128)S(1)}, u32[]{:S(2)}, u32[]{:S(2)}) collective-permute-start(f32[2,1024]{1,0:T(2,128)S(1)} %fusion), channel_id=1, source_target_pairs={{0,2},{1,3},{2,0},{3,1},{4,6},{5,7},{6,4},{7,5},{8,10},{9,11},{10,... | collective-permute-start | bytes 24584 | tf_op jit(solution)/shard_map/ppermute | solution.py:522
  79.9 1.2 collective-permute-start.5
  81.1 3.6 %collective-permute-start.6 = (f32[1,1024]{1,0:T(1,128)S(1)}, f32[1,1024]{1,0:T(1,128)S(1)}, u32[]{:S(2)}, u32[]{:S(2)}) collective-permute-start(f32[1,1024]{1,0:T(1,128)S(1)} %add.44.refs_0_), channel_id=1, source_target_pairs={{0,2},{1,3},{2,0},{3,1},{4,6},{5,7},{6,4},{7,5},{8,10},{9,11},{10,... | collective-permute-start | bytes 12296 | tf_op jit(solution)/shard_map/ppermute | solution.py:522
  88.1 4.0 %collective-permute-start.7 = (f32[1,8192]{1,0:T(1,128)S(1)}, f32[1,8192]{1,0:T(1,128)S(1)}, u32[]{:S(2)}, u32[]{:S(2)}) collective-permute-start(f32[1,8192]{1,0:T(1,128)S(1)} %bitcast.10), channel_id=1, source_target_pairs={{0,4},{4,0},{8,12},{12,8},{16,20},{20,16},{24,28},{28,24},{1,5},{5... | collective-permute-start | bytes 98312 | tf_op jit(solution)/shard_map/ppermute | solution.py:522
  92.1 4.0 %collective-permute-start.8 = (f32[1,8192]{1,0:T(1,128)S(1)}, f32[1,8192]{1,0:T(1,128)S(1)}, u32[]{:S(2)}, u32[]{:S(2)}) collective-permute-start(f32[1,8192]{1,0:T(1,128)S(1)} %bitcast_add_fusion), channel_id=1, source_target_pairs={{0,8},{4,12},{8,0},{12,4},{16,24},{20,28},{24,16},{28,20},{1,9},{5... | collective-permute-start | bytes 98312 | tf_op jit(solution)/shard_map/ppermute | solution.py:522
  96.1 5.2 %collective-permute-start.9 = (f32[1,8192]{1,0:T(1,128)S(1)}, f32[1,8192]{1,0:T(1,128)S(1)}, u32[]{:S(2)}, u32[]{:S(2)}) collective-permute-start(f32[1,8192]{1,0:T(1,128)S(1)} %add.46.refs_0_), channel_id=1, source_target_pairs={{0,16},{4,20},{8,24},{12,28},{16,0},{20,4},{24,8},{28,12},{1,17},{... | collective-permute-start | bytes 98312 | tf_op jit(solution)/shard_map/ppermute | solution.py:522
  101.3 5.8 %copy-start.1 = (bf16[1024,8192]{1,0:T(8,128)(2,1)S(1)}, bf16[1024,8192]{1,0:T(8,128)(2,1)}, u32[]{:S(2)}) copy-start(bf16[1024,8192]{1,0:T(8,128)(2,1)} %copy-done) | copy-start | bytes 50331652
  107.1 17.1 %copy-start.4 = (bf16[1024,1024]{1,0:T(8,128)(2,1)S(1)}, bf16[1024,1024]{1,0:T(8,128)(2,1)}, u32[]{:S(2)}) copy-start(bf16[1024,1024]{1,0:T(8,128)(2,1)} %all-gather.6.cloned.1.call-done) | copy-start | bytes 6291460
  111.7 1.2 collective-permute-start.10
  113.0 3.6 %collective-permute-start.11 = (f32[1,1024]{1,0:T(1,128)S(1)}, f32[1,1024]{1,0:T(1,128)S(1)}, u32[]{:S(2)}, u32[]{:S(2)}) collective-permute-start(f32[1,1024]{1,0:T(1,128)S(1)} %add.47), channel_id=1, source_target_pairs={{0,2},{1,3},{2,0},{3,1},{4,6},{5,7},{6,4},{7,5},{8,10},{9,11},{10,... | collective-permute-start | bytes 12296 | tf_op jit(solution)/shard_map/ppermute | solution.py:522
  116.6 3.6 %collective-permute-start.16 = (f32[1,1,1024]{2,1,0:T(1,128)S(1)}, f32[1,1,1024]{2,1,0:T(1,128)S(1)}, u32[]{:S(2)}, u32[]{:S(2)}) collective-permute-start(f32[1,1,1024]{2,1,0:T(1,128)S(1)} %bitcast.11), channel_id=1, source_target_pairs={{0,4},{4,0},{8,12},{12,8},{16,20},{20,16},{24,28},{28,24},{1,5},{5... | collective-permute-start | bytes 12296 | tf_op jit(solution)/shard_map/ppermute | solution.py:522
  120.2 3.7 %collective-permute-start.17 = (f32[2,1,1024]{2,1,0:T(1,128)S(1)}, f32[2,1,1024]{2,1,0:T(1,128)S(1)}, u32[]{:S(2)}, u32[]{:S(2)}) collective-permute-start(f32[2,1,1024]{2,1,0:T(1,128)S(1)} %pad_maximum_fusion.4), channel_id=1, source_target_pairs={{0,8},{4,12},{8,0},{12,4},{16,24},{20,28},{24,16},{28,20},{1,9},{5... | collective-permute-start | bytes 24584 | tf_op jit(solution)/shard_map/ppermute | solution.py:522
  123.9 11.9 %collective-permute-start.18 = (f32[4,1,1024]{2,1,0:T(1,128)S(1)}, f32[4,1,1024]{2,1,0:T(1,128)S(1)}, u32[]{:S(2)}, u32[]{:S(2)}) collective-permute-start(f32[4,1,1024]{2,1,0:T(1,128)S(1)} %pad_maximum_fusion.2), channel_id=1, source_target_pairs={{0,16},{4,20},{8,24},{12,28},{16,0},{20,4},{24,8},{28,12},{1,17},{... | collective-permute-start | bytes 49160 | tf_op jit(solution)/shard_map/ppermute | solution.py:522
  142.4 5.8 %copy-start.2 = (bf16[1024,8192]{1,0:T(8,128)(2,1)S(1)}, bf16[1024,8192]{1,0:T(8,128)(2,1)}, u32[]{:S(2)}) copy-start(bf16[1024,8192]{1,0:T(8,128)(2,1)} %copy-done) | copy-start | bytes 50331652
  148.2 29.5 %copy-start.6 = (f32[1024,128]{1,0:T(8,128)S(1)}, f32[1024,128]{1,0:T(8,128)}, u32[]{:S(2)}) copy-start(f32[1024,128]{1,0:T(8,128)} %get-tuple-element.37.raw) | copy-start | bytes 1572868
  167.6 10.1 %copy-start.5 = (f32[1024,512]{1,0:T(8,128)S(1)}, f32[1024,512]{1,0:T(8,128)}, u32[]{:S(2)}) copy-start(f32[1024,512]{1,0:T(8,128)} %get-tuple-element.38.pre) | copy-start | bytes 6291460
  167.6 10.1 %copy-start.7 = (bf16[512,128]{1,0:T(8,128)(2,1)S(1)}, bf16[512,128]{1,0:T(8,128)(2,1)}, u32[]{:S(2)}) copy-start(bf16[512,128]{1,0:T(8,128)(2,1)} %w_out.3) | copy-start | bytes 393220
  167.6 1.6 collective-permute-start.12
  169.3 8.4 %collective-permute-start.13 = (bf16[1024,128]{1,0:T(8,128)(2,1)S(1)}, bf16[1024,128]{1,0:T(8,128)(2,1)S(1)}, u32[]{:S(2)}, u32[]{:S(2)}) collective-permute-start(bf16[1024,128]{1,0:T(8,128)(2,1)S(1)} %add_convert_fusion.grad_a), channel_id=1, source_target_pairs={{0,2},{1,3},{2,0},{3,1},{4,6},{5,7},{6,4},{7,5},{8,10},{9,11},{10,... | collective-permute-start | bytes 786440 | tf_op jit(solution)/shard_map/ppermute | solution.py:522
  211.8 6.7 %collective-permute-start.14 = (bf16[1,8,144,128]{3,2,1,0:T(8,128)(2,1)S(1)}, bf16[1,8,144,128]{3,2,1,0:T(8,128)(2,1)S(1)}, u32[]{:S(2)}, u32[]{:S(2)}) collective-permute-start(bf16[1,8,144,128]{3,2,1,0:T(8,128)(2,1)S(1)} %bitcast.16), channel_id=1, source_target_pairs={{0,2},{1,3},{2,0},{3,1},{4,6},{5,7},{6,4},{7,5},{8,10},{9,11},{10,... | collective-permute-start | bytes 884744 | tf_op jit(solution)/shard_map/ppermute | solution.py:522
  218.6 2.1 collective-permute-start.15
Sparse Core Ops, SparseCore 0:
  15.5 59.1 all-gather.5
  142.5 53.0 all-gather.3

commit v4 on v3

--- a/solution.py
+++ b/solution.py
@@ -218,6 +218,31 @@
     return total
 
 
+def add_fours(terms):
+    total = None
+    for k in range(0, len(terms), 4):
+        four = terms[k : k + 4]
+        while len(four) > 1:
+            four = [x + y for x, y in zip(four[::2], four[1::2])]
+        part = four[0].astype(f32)
+        total = part if total is None else total + part
+    return total
+
+
+def rowsum_tile(expo, here, spread, tall, width):
+    terms = []
+    total = None
+    for k in range(width // 128):
+        lanes = slice(k * 128, (k + 1) * 128)
+        weight = jnp.concatenate([spread[:, lanes]] * (tall // 16), axis=0)
+        terms.append(expo[here, lanes] * weight)
+        if len(terms) == 4 or k == width // 128 - 1:
+            part = add_fours(terms)
+            total = part if total is None else total + part
+            terms = []
+    return total
+
+
 def rowsum_kernel(count, expo, *refs):
     parts = refs[:count]
     scale, out, spread, acc = refs[count:]
@@ -229,12 +254,7 @@
 
     def one(i, carry):
         here = pl.ds(pl.multiple_of(i * tall, tall), tall)
-        running = jnp.zeros((tall, 128), f32)
-        for k in range(width // 128):
-            lanes = slice(k * 128, (k + 1) * 128)
-            weight = jnp.concatenate([spread[:, lanes]] * (tall // 16), axis=0)
-            running = running + (expo[here, lanes] * weight).astype(f32)
-        acc[here, :] = running
+        acc[here, :] = rowsum_tile(expo, here, spread, tall, width)
         return carry
 
     lax.fori_loop(0, rows // tall, one, 0)
@@ -256,6 +276,48 @@
         cost_estimate=SMALL,
         name="rowsum",
     )(in_vmem(expo), *parts)
+
+
+def rowsum_stream_kernel(count, expo, *refs):
+    parts = refs[:count]
+    scale, out, spread, acc = refs[count:]
+    block, width = expo.shape
+    step = pl.program_id(0)
+
+    @pl.when(step == 0)
+    def _():
+        inverse = 1.0 / sum_parts(parts, width)
+        scale[...] = inverse
+        spread[...] = jnp.broadcast_to(inverse, spread.shape).astype(bf16)
+
+    tall = 64
+    for i in range(block // tall):
+        here = pl.ds(pl.multiple_of(step * block + i * tall, tall), tall)
+        acc[here, :] = rowsum_tile(expo, slice(i * tall, (i + 1) * tall), spread, tall, width)
+
+    @pl.when(step == pl.num_programs(0) - 1)
+    def _():
+        out[...] = jnp.sum(acc[...].T, axis=0, keepdims=True)
+
+
+def rowsum_stream(expo, parts):
+    rows, width = expo.shape
+    block = min(128, rows)
+    return pl.pallas_call(
+        functools.partial(rowsum_stream_kernel, len(parts)),
+        grid=(rows // block,),
+        in_specs=[pl.BlockSpec((block, width), lambda i: (i, 0))]
+        + [full((1, width))] * len(parts),
+        out_specs=[full((1, width)), full((1, rows))],
+        out_shape=[
+            jax.ShapeDtypeStruct((1, width), f32),
+            jax.ShapeDtypeStruct((1, rows), f32),
+        ],
+        scratch_shapes=[pltpu.VMEM((16, width), bf16), pltpu.VMEM((rows, 128), f32)],
+        compiler_params=params("arbitrary"),
+        cost_estimate=SMALL,
+        name="rowsum_stream",
+    )(in_hbm(expo), *parts)
 
 
 def colsum_kernel(count, expo, *refs):
@@ -270,10 +332,13 @@
     def one(j, carry):
         here = pl.ds(pl.multiple_of(j * block, block), block)
         running = jnp.zeros((16, block), f32)
-        for i in range(rows // 16):
-            part = slice(i * 16, (i + 1) * 16)
-            weight = jnp.concatenate([spread[part, :]] * (block // 128), axis=1)
-            running = running + (expo[part, here] * weight).astype(f32)
+        for i in range(0, rows // 16, 4):
+            terms = []
+            for k in range(i, min(i + 4, rows // 16)):
+                part = slice(k * 16, (k + 1) * 16)
+                weight = jnp.concatenate([spread[part, :]] * (block // 128), axis=1)
+                terms.append(expo[part, here] * weight)
+            running = running + add_fours(terms)
         total = jnp.sum(running, axis=0, keepdims=True)
         for k in range(out.shape[0]):
             out[k, :, here] = total
@@ -300,141 +365,191 @@
     )(in_vmem(expo), *parts, *behind)
 
 
-def proto_first_kernel(block, tile, base, protos, views, totals, expo, grad, weights, twice, stage, soft16):
-    count, depth, rows = views.shape
-    for k in range(count):
-        total = totals[k, :, base : base + rows]
-        here = slice(k * rows, (k + 1) * rows)
-        weights[:, here] = (views[k].astype(f32) * (GRAD_SCALE / total)).astype(bf16)
-        twice[:depth, here] = views[k]
-        twice[depth:, here] = views[k]
-
-    def one(j, carry):
-        here = pl.ds(pl.multiple_of(j * block, block), block)
-        _, _, unit = unit_of(protos[here, :])
-        pair = scaled_pair(unit.astype(bf16), 1)
-        running = jnp.zeros((block, depth), f32)
-        for k in range(count):
-            part = slice(k * rows, (k + 1) * rows)
-            stage[k % 2] = dot(pair, twice[:, part])
-            for start in range(0, block, tile):
-                soft = jnp.exp2(stage[k % 2, start : start + tile, :])
-                soft16[k % 2, start : start + tile, :] = soft.astype(bf16)
-                expo[pl.ds(pl.multiple_of(j * block + start, tile), tile), part] = (
-                    soft * soft
-                ).astype(bf16)
-            running = running + dot(soft16[k % 2], weights[:, part], NT)
-        grad[here, :] = running
-        return carry
-
-    lax.fori_loop(0, protos.shape[0] // block, one, 0)
-
-
-def proto_first(protos, views, totals, base):
+def proto_first_kernel(chunk, tile, lead, place, protos, views, totals, expo, grad, *scratch):
+    weights, twice, pair, stage, soft16, acc = scratch
+    count = expo.shape[1] // views.shape[2]
+    _, depth, rows = views.shape
+    width = protos.shape[0]
+    _, _, unit = unit_of(protos[...])
+    pair[...] = scaled_pair(unit.astype(bf16), 1)
+    for n in range(count):
+        k = lead + n
+        weights[...] = (views[k].astype(f32) * (GRAD_SCALE / totals[place[0] ^ k])).astype(bf16)
+        twice[:depth, :] = views[k]
+        twice[depth:, :] = views[k]
+        for c in range(width // chunk):
+            stage[c % 2] = dot(pair[c * chunk : (c + 1) * chunk, :], twice[...])
+            for start in range(0, chunk, tile):
+                part = slice(c * chunk + start, c * chunk + start + tile)
+                soft = jnp.exp2(stage[c % 2, start : start + tile, :])
+                soft16[part, :] = soft.astype(bf16)
+                expo[part, n * rows : (n + 1) * rows] = (soft * soft).astype(bf16)
+        found = dot(soft16[...], weights[...], NT)
+        if n == 0:
+            acc[...] = found
+        else:
+            acc[...] += found
+    grad[...] = acc[...]
+
+
+def proto_first(place, protos, views, totals, lead, count):
     width, depth = protos.shape
-    count, _, rows = views.shape
-    block = min(256, width)
-    tile = min(16, block)
-    return pl.pallas_call(
-        functools.partial(proto_first_kernel, block, tile, base),
-        in_specs=[WHOLE] * 3,
+    rows = views.shape[2]
+    chunk = min(256, width)
+    tile = min(16, chunk)
+    return pl.pallas_call(
+        functools.partial(proto_first_kernel, chunk, tile, lead),
+        in_specs=[pl.BlockSpec(memory_space=pltpu.SMEM)] + [WHOLE] * 3,
         out_specs=[WHOLE] * 2,
         out_shape=[
             pltpu.VMEM((width, count * rows), bf16),
             jax.ShapeDtypeStruct((width, depth), f32),
         ],
         scratch_shapes=[
-            pltpu.VMEM((depth, count * rows), bf16),
-            pltpu.VMEM((2 * depth, count * rows), bf16),
-            pltpu.VMEM((2, block, rows), f32),
-            pltpu.VMEM((2, block, rows), bf16),
+            pltpu.VMEM((depth, rows), bf16),
+            pltpu.VMEM((2 * depth, rows), bf16),
+            pltpu.VMEM((width, 2 * depth), bf16),
+            pltpu.VMEM((2, chunk, rows), f32),
+            pltpu.VMEM((width, rows), bf16),
+            pltpu.VMEM((width, depth), f32),
         ],
         compiler_params=params(),
+        cost_estimate=SMALL,
         name="proto_first",
-    )(protos, views, totals)
-
-
-def proto_last_kernel(block, place, expo, grad, scale, protos, views, totals, out, weights):
+    )(place, protos, views, totals)
+
+
+def proto_last_kernel(groups, place, *refs):
+    expos, grads = refs[:groups], refs[groups : 2 * groups]
+    scale, protos, views, totals, out, weights, acc = refs[2 * groups :]
     count, depth, rows = views.shape
+    each = count // groups
     for k in range(count):
         mates = swap_lanes(views[k])
-        weights[:, k * rows : (k + 1) * rows] = (
-            mates.astype(f32) * (GRAD_SCALE / totals[place[0] ^ k])
-        ).astype(bf16)
-
-    def one(j, carry):
-        here = pl.ds(pl.multiple_of(j * block, block), block)
-        code = dot(expo[here, :], weights[...], NT)
-        there = pl.ds(pl.multiple_of(place[0] * expo.shape[0] + j * block, block), block)
-        unit_grad = grad[here, :] - to_column(scale[:, there]) * code
-        proto_f, inv, _ = unit_of(protos[here, :])
-        inner = jnp.sum(proto_f * unit_grad, axis=1, keepdims=True)
-        out[here, :] = (inv * unit_grad - proto_f * (inv * inv * inv) * inner).astype(bf16)
-        return carry
-
-    lax.fori_loop(0, protos.shape[0] // block, one, 0)
-
-
-def proto_last(place, expo, grad, scale, protos, views, totals):
+        weights[...] = (mates.astype(f32) * (GRAD_SCALE / totals[place[0] ^ k])).astype(bf16)
+        found = dot(expos[k // each][:, (k % each) * rows : (k % each + 1) * rows], weights[...], NT)
+        if k == 0:
+            acc[...] = found
+        else:
+            acc[...] += found
+    width = protos.shape[0]
+    there = pl.ds(pl.multiple_of(place[0] * width, width), width)
+    unit_grad = grads[0][...]
+    for other in grads[1:]:
+        unit_grad = unit_grad + other[...]
+    unit_grad = unit_grad - to_column(scale[:, there]) * acc[...]
+    proto_f, inv, _ = unit_of(protos[...])
+    inner = jnp.sum(proto_f * unit_grad, axis=1, keepdims=True)
+    out[...] = (inv * unit_grad - proto_f * (inv * inv * inv) * inner).astype(bf16)
+
+
+def proto_last(place, expos, grads, scale, protos, views, totals):
     width, depth = protos.shape
-    count, _, rows = views.shape
-    block = min(256, width)
-    return pl.pallas_call(
-        functools.partial(proto_last_kernel, block),
-        in_specs=[pl.BlockSpec(memory_space=pltpu.SMEM)] + [WHOLE] * 6,
+    rows = views.shape[2]
+    groups = len(expos)
+    return pl.pallas_call(
+        functools.partial(proto_last_kernel, groups),
+        in_specs=[pl.BlockSpec(memory_space=pltpu.SMEM)] + [WHOLE] * (2 * groups + 4),
         out_specs=WHOLE,
         out_shape=jax.ShapeDtypeStruct((width, depth), bf16),
-        scratch_shapes=[pltpu.VMEM((depth, count * rows), bf16)],
+        scratch_shapes=[pltpu.VMEM((depth, rows), bf16), pltpu.VMEM((width, depth), f32)],
         compiler_params=params(),
         name="proto_last",
-    )(place, in_vmem(expo), grad, scale, protos, views, totals)
-
-
-def view_grad_kernel(block, tile, views, protos, expo, scale, tot, total, out, *scratch):
-    pair, stage, soft16, soft_acc, hard_acc = scratch
+    )(place, *[in_vmem(x) for x in expos], *grads, scale, protos, views, totals)
+
+
+def view_soft_kernel(block, tile, lead, views, protos, out, pair, stage, soft16):
     rows, depth = views.shape
-    width = expo.shape[1]
     pair[...] = scaled_pair(views[...], 1)
-    soft_acc[...] = jnp.zeros_like(soft_acc)
-    hard_acc[...] = jnp.zeros_like(hard_acc)
+    out[...] = jnp.zeros_like(out)
+    chunk = stage.shape[1]
 
     def one(j, carry):
-        here = pl.ds(pl.multiple_of(j * block, block), block)
+        here = pl.ds(pl.multiple_of(lead + j * block, block), block)
         _, _, unit = unit_of(protos[here, :])
         unit16 = unit.astype(bf16)
-        scaled = (unit16.astype(f32) * to_column(scale[:, here])).astype(bf16)
-        stage[...] = dot(pair[...], jnp.concatenate([unit16, unit16], axis=1), NT)
-        for start in range(0, rows, tile):
-            part = slice(start, start + tile)
-            soft16[part, :] = jnp.exp2(stage[part, :]).astype(bf16)
-        soft_acc[...] += dot(soft16[...], unit16)
-        hard_acc[...] += dot(expo[:, here], scaled)
+        twice = jnp.concatenate([unit16, unit16], axis=1)
+        for c in range(rows // chunk):
+            stage[c % 2] = dot(pair[c * chunk : (c + 1) * chunk, :], twice, NT)
+            for start in range(0, chunk, tile):
+                part = slice(c * chunk + start, c * chunk + start + tile)
+                soft16[part, :] = jnp.exp2(stage[c % 2, start : start + tile, :]).astype(bf16)
+        out[...] += dot(soft16[...], unit16)
         return carry
 
-    lax.fori_loop(0, width // block, one, 0)
-    soft = soft_acc[...] * to_column(GRAD_SCALE / tot[...])
-    hard = swap_rows(hard_acc[...] * to_column(GRAD_SCALE / total[...]))
-    out[...] = (soft - hard).astype(out.dtype)
-
-
-def view_grad_part(views, protos, expo, scale, tot, total):
+    return one
+
+
+def view_soft_body(block, tile, lead, count, *refs):
+    lax.fori_loop(0, count // block, view_soft_kernel(block, tile, lead, *refs), 0)
+
+
+def view_soft(views, protos, lead, count):
     rows, depth = views.shape
-    block = min(512, expo.shape[1])
-    return pl.pallas_call(
-        functools.partial(view_grad_kernel, block, min(32, rows)),
-        in_specs=[WHOLE] * 6,
+    block = min(512, count)
+    chunk = min(256, rows)
+    return pl.pallas_call(
+        functools.partial(view_soft_body, block, min(32, chunk), lead, count),
+        in_specs=[WHOLE] * 2,
         out_specs=WHOLE,
-        out_shape=jax.ShapeDtypeStruct((rows, depth), bf16),
+        out_shape=jax.ShapeDtypeStruct((rows, depth), f32),
         scratch_shapes=[
             pltpu.VMEM((rows, 2 * depth), bf16),
-            pltpu.VMEM((rows, block), f32),
+            pltpu.VMEM((2, chunk, block), f32),
             pltpu.VMEM((rows, block), bf16),
-            pltpu.VMEM((rows, depth), f32),
-            pltpu.VMEM((rows, depth), f32),
         ],
         compiler_params=params(),
+        cost_estimate=SMALL,
+        name="view_soft",
+    )(views, protos)
+
+
+def view_grad_kernel(groups, protos, expo, scale, tot, total, *refs):
+    softs, (out, acc) = refs[:groups], refs[groups:]
+    step = pl.program_id(0)
+    _, _, unit = unit_of(protos[...])
+    scaled = (unit.astype(bf16).astype(f32) * to_column(scale[...])).astype(bf16)
+    found = dot(expo[...], scaled)
+
+    @pl.when(step == 0)
+    def _():
+        acc[...] = found
+
+    @pl.when(step > 0)
+    def _():
+        acc[...] += found
+
+    @pl.when(step == pl.num_programs(0) - 1)
+    def _():
+        soft = softs[0][...]
+        for other in softs[1:]:
+            soft = soft + other[...]
+        soft = soft * to_column(GRAD_SCALE / tot[...])
+        hard = swap_rows(acc[...] * to_column(GRAD_SCALE / total[...]))
+        out[...] = (soft - hard).astype(out.dtype)
+
+
+def view_grad_part(protos, expo, scale, tot, total, softs):
+    rows, width = expo.shape
+    depth = protos.shape[1]
+    block = min(1024, width)
+    return pl.pallas_call(
+        functools.partial(view_grad_kernel, len(softs)),
+        grid=(width // block,),
+        in_specs=[
+            pl.BlockSpec((block, depth), lambda j: (j, 0)),
+            pl.BlockSpec((rows, block), lambda j: (0, j)),
+            pl.BlockSpec((1, block), lambda j: (0, j)),
+            full((1, rows)),
+            full((1, rows)),
+        ]
+        + [full((rows, depth))] * len(softs),
+        out_specs=full((rows, depth)),
+        out_shape=jax.ShapeDtypeStruct((rows, depth), bf16),
+        scratch_shapes=[pltpu.VMEM((rows, depth), f32)],
+        compiler_params=params("arbitrary"),
         name="view_grad",
-    )(views, protos, in_vmem(expo), scale, tot, total)
+    )(protos, in_hbm(expo), scale, tot, total, *[in_hbm(x) for x in softs])
 
 
 def backward_kernel(grad_a, grad_b, pos, raw, pre, emb, hid_part, w_out, out):
@@ -510,6 +625,25 @@
     )(place, *pieces)
 
 
+def widen_kernel(x, out):
+    out[...] = x[...].astype(f32)
+
+
+def widen(x):
+    rows, depth = x.shape
+    block = min(1024, rows)
+    spec = pl.BlockSpec((block, depth), lambda i: (i, 0))
+    return pl.pallas_call(
+        widen_kernel,
+        grid=(rows // block,),
+        in_specs=[spec],
+        out_specs=spec,
+        out_shape=jax.ShapeDtypeStruct((rows, depth), f32),
+        compiler_params=params("arbitrary"),
+        name="widen",
+    )(in_hbm(x))
+
+
 def body(nb, npr, embeddings, pairing, w_in, w_out, prototypes):
     b = lax.axis_index("batch")
     p = lax.axis_index("proto")
@@ -521,12 +655,21 @@
     def flipped(x, axis, size, step):
         return lax.ppermute(x, axis, [(i, i ^ step) for i in range(size)])
 
-    def doubled(x, axis, size):
+    def exchange(x, axis, size, step, queue, results):
+        other = flipped(x, axis, size, step)
+        if queue:
+            work, operands = queue.pop(0)
+            operands, _ = lax.optimization_barrier((operands, x))
+            other, found = lax.optimization_barrier((other, work(*operands)))
+            results.append(found)
+        return other
+
+    def doubled(x, axis, size, queue=(), results=None):
         step = 1
         while step * 2 < size:
-            x = x + flipped(x, axis, size, step)
+            x = x + exchange(x, axis, size, step, queue, results)
             step *= 2
-        return [x, flipped(x, axis, size, step)] if size > 1 else [x]
+        return [x, exchange(x, axis, size, step, queue, results)]
 
     def shared(x):
         wide_x = jnp.broadcast_to(x, (nb,) + x.shape[1:])
@@ -539,29 +682,67 @@
     views, protos_own, place = lax.optimization_barrier((views, protos_own, place))
     expo, col, tot = first_pass(views, prototypes)
 
-    scale, row = rowsum(expo, doubled(col, "batch", nb))
-    first, second = doubled(jnp.concatenate([row, tot], axis=0), "proto", npr)
+    groups = 4
+    cols = width // groups
+    softs = []
+    queue = [
+        (functools.partial(view_soft, lead=k * cols, count=cols), (views, prototypes))
+        for k in range(groups)
+    ]
+    scale, row = rowsum(expo, doubled(col, "batch", nb, queue, softs))
+    first, second = doubled(jnp.concatenate([row, tot], axis=0), "proto", npr, queue, softs)
     both = first + second
     totals, tot = [both[:1]], both[1:]
-    packed = lax.all_to_all(colsum(expo, totals, nb, [tot]), "batch", 0, 0, tiled=True)
-    scale, row = rowsum(expo, [packed])
-    col = colsum(expo, doubled(row, "proto", npr))
+
+    col = colsum(expo, totals)[0]
+    tot_all = tot[None]
+    step = 1
+    while step < nb:
+        other = flipped(tot_all, "batch", nb, step)
+        part = flipped(col, "batch", nb, step)
+        other, part = lax.optimization_barrier((other, part))
+        tot_all = jnp.concatenate([tot_all, other], axis=0)
+        step *= 2
+        if step < nb:
+            col = col + part
+    scale, row = rowsum(expo, [col, part])
+    col = colsum(expo, doubled(row, "proto", npr, queue, softs))[0]
+    while queue:
+        work, operands = queue.pop(0)
+        softs.append(work(*operands))
+
     col, views_all = lax.optimization_barrier((col, views_all))
-    expo_own, grad_own = proto_first(protos_own, views_all, packed, width)
-    scale, row = rowsum(expo, doubled(col[0], "batch", nb))
-    first, second = doubled(row, "proto", npr)
+    each = nb // groups
+    owns = []
+    queue = [
+        (
+            functools.partial(proto_first, lead=k * each, count=each),
+            (place, protos_own, views_all, tot_all),
+        )
+        for k in range(groups)
+    ]
+    scale, row = rowsum_stream(expo, doubled(col, "batch", nb, queue, owns))
+    first, second = doubled(row, "proto", npr, queue, owns)
     total = first + second
     total_all = total[None]
     step = 1
     while step < nb:
-        total_all = jnp.concatenate([total_all, flipped(total_all, "batch", nb, step)], axis=0)
+        other = exchange(total_all, "batch", nb, step, queue, owns)
+        total_all = jnp.concatenate([total_all, other], axis=0)
         step *= 2
 
     proto_part = proto_last(
-        place, expo_own, grad_own, scale, protos_own, views_all, total_all)
+        place,
+        [x for x, _ in owns],
+        [x for _, x in owns],
+        scale,
+        protos_own,
+        views_all,
+        total_all,
+    )
     grad_proto = lax.all_gather(proto_part, "batch", axis=0, tiled=True)
 
-    part = view_grad_part(views, prototypes, expo, scale, tot, total)
+    part = view_grad_part(prototypes, expo, scale, tot, total, softs)
     step = 1
     while step * 2 < npr:
         other = flipped(part, "proto", npr, step)
@@ -585,7 +766,7 @@
     grad_in, grad_out = unpack(
         order, p.astype(jnp.int32).reshape(1), pieces, (wide, hidden_n), (hidden_n, depth)
     )
-    return (grad_in, grad_out, grad_proto.astype(f32))
+    return (grad_in, grad_out, widen(grad_proto))
 
 
 def solution(mesh):

time: 233 us -> 220 us (0.944)
  blocking collectives: 50.2 us -> 33.9 us
  Pallas kernels: 81.9 us -> 96.9 us
  starting transfers between devices: 19.6 us -> 30.2 us
  waiting for transfers between devices: 48 us -> 38.3 us
  local copies, waits for them, and re-layouts: 14.5 us -> 5.36 us
  other arithmetic: 4.35 us -> 0.6 us
    pallas_call x3 -> x12, Pallas kernels: 37.6 us -> 61.1 us  [the longest x4 13.9 us: view_soft(): pl.pallas_call(functools.partial(view_soft_body, block, min(32, chunk), l...]
    all_to_all x1 -> x0, blocking collectives: 19.6 us -> none  [body(): lax.all_to_all(colsum(expo, totals, nb, [tot]), 'batch', 0, 0, tiled=True)]
    ppermute x19 -> x25, starting transfers between devices: 19.6 us -> 30.1 us  [flipped(): return lax.ppermute(x, axis, [(i, i ^ step) for i in range(size)])]
    ppermute x19 -> x25, waiting for transfers between devices: 48 us -> 38.3 us  [flipped(): return lax.ppermute(x, axis, [(i, i ^ step) for i in range(size)])]
    unnamed x18 -> x24, local copies, waits for them, and re-layouts: 12.4 us -> 3.23 us
    pallas_call x3 -> x2, Pallas kernels: 14.6 us -> 8.08 us  [rowsum(): pl.pallas_call(functools.partial(rowsum_kernel, len(parts)), in_specs=[WH...]
    convert_element_type x1 -> x0, other arithmetic: 3.87 us -> none  [body(): return (grad_in, grad_out, grad_proto.astype(f32))]
    all_to_all x1, blocking collectives: 17.3 us -> 21 us  [body(): both = lax.all_to_all(both.astype(bf16), 'batch', 0, 0, tiled=True)]
  transfers between devices with their start and end apart: 21 -> 27, of which waited for: 18 -> 15; matrix products, arithmetic and copies ran while one was open for 1% -> 1% of each run, Pallas kernels for 27% -> 31%
where the time goes in v4:
time: 220 us
  Pallas kernels  96.9 us (44%)
  waiting for transfers between devices  38.3 us (17%)
  blocking collectives  33.9 us (15%)
  starting transfers between devices  30.2 us (14%)
  between operations  14.5 us (7%)
  local copies, waits for them, and re-layouts  5.36 us (2%)
    ppermute x25, waiting for transfers between devices, flipped(): return lax.ppermute(x, axis, [(i, i ^ step) for i in range(size)])  38.3 us
    ppermute x25, starting transfers between devices, flipped(): return lax.ppermute(x, axis, [(i, i ^ step) for i in range(size)])  30.1 us
    all_to_all x1, blocking collectives, body(): both = lax.all_to_all(both.astype(bf16), 'batch', 0, 0, tiled=True)  21 us
    pallas_call x4, Pallas kernels, view_soft(): pl.pallas_call(functools.partial(view_soft_body, block, min(32, chunk), l...  13.9 us
    pallas_call x1, Pallas kernels, view_grad_part(): pl.pallas_call(functools.partial(view_grad_kernel, len(softs)), grid=(wid...  13.4 us
    pallas_call x4, Pallas kernels, proto_first(): pl.pallas_call(functools.partial(proto_first_kernel, chunk, tile, lead),...  13 us
    all_to_all x1, blocking collectives, shared(): return lax.all_to_all(wide_x, 'batch', 0, 0, tiled=True)  12.9 us
    pallas_call x1, Pallas kernels, first_pass(): pl.pallas_call(functools.partial(first_kernel, block, chunk, tile), in_sp...  11 us
  transfers between devices with their start and end apart: 27, of which 15 were waited for; matrix products, arithmetic and copies ran while one was open for 1% of the time, Pallas kernels for 31%

profile of v4, /device:TPU:0, one launch (start us, length us, event | category | flops | bytes accessed | tf_op | source)
XLA Modules:
  0.0 219.7 jit_solution(2263333151630272171)
XLA Ops:
  8.0 7.3 %head.1 = (f32[1024,512]{1,0:T(8,128)}, bf16[1024,512]{1,0:T(8,128)(2,1)}, f32[1024,128]{1,0:T(8,128)}, bf16[1024,128]{1,0:T(8,128)(2,1)S(1)}, bf16[128,1024]{1,0:T(8,128)(2,1)}, /*index=5*/s32[1,1024]{1,0:T(1,128)S(1)}) custom-call(bf16[1024,1024]{1,0:T(8,128)(2,1)} %emb.1, s32[1,1024]{1,0:T(1,128)S(1)} %bitcast.23, bf16[1024,512]{1,0:T(8,128)(2,1)} %w_in.1, ...), custom_call_target="tpu_custom_call" | custom-call | tf_op jit(solution)/shard_map/head/pallas_call | solution.py:107
  15.4 11.0 %first_pass.1 = (bf16[1024,8192]{1,0:T(8,128)(2,1)S(1)}, f32[1,8192]{1,0:T(1,128)S(1)}, f32[1,1024]{1,0:T(1,128)S(1)}) custom-call(bf16[1024,128]{1,0:T(8,128)(2,1)S(1)} %get-tuple-element.96.views.refs_0_, bf16[8192,128]{1,0:T(8,128)(2,1)S(1)} %copy-done.1), custom_call_target="tpu_custom_call" | custom-call | flops 1000 | bytes 1000 | tf_op jit(solution)/shard_map/first_pass/pallas_call | solution.py:192
  26.4 3.0 %collective-permute-start = (f32[1,8192]{1,0:T(1,128)S(1)}, f32[1,8192]{1,0:T(1,128)S(1)}, u32[]{:S(2)}, u32[]{:S(2)}) collective-permute-start(f32[1,8192]{1,0:T(1,128)S(1)} %get-tuple-element.84), channel_id=1, source_target_pairs={{0,4},{4,0},{8,12},{12,8},{16,20},{20,16},{24,28},{28,24},{1,5},{5... | collective-permute-start | bytes 98312 | tf_op jit(solution)/shard_map/ppermute | solution.py:656
  29.4 3.5 %view_soft.4.refs_0_ = f32[1024,128]{1,0:T(8,128)S(1)} custom-call(bf16[1024,128]{1,0:T(8,128)(2,1)S(1)} %get-tuple-element.96.views.refs_0_, bf16[8192,128]{1,0:T(8,128)(2,1)S(1)} %copy-done.1), custom_call_target="tpu_custom_call" | custom-call | flops 1000 | bytes 1000 | tf_op jit(solution)/shard_map/view_soft/pallas_call | solution.py:491
  33.7 1.8 collective-permute-start.1
  35.5 3.5 %view_soft.5.refs_1_ = f32[1024,128]{1,0:T(8,128)S(1)} custom-call(bf16[1024,128]{1,0:T(8,128)(2,1)S(1)} %get-tuple-element.96.views.refs_0_, bf16[8192,128]{1,0:T(8,128)(2,1)S(1)} %copy-done.1), custom_call_target="tpu_custom_call" | custom-call | flops 1000 | bytes 1000 | tf_op jit(solution)/shard_map/view_soft/pallas_call | solution.py:491
  39.1 2.7 %collective-permute-start.2 = (f32[1,8192]{1,0:T(1,128)S(1)}, f32[1,8192]{1,0:T(1,128)S(1)}, u32[]{:S(2)}, u32[]{:S(2)}) collective-permute-start(f32[1,8192]{1,0:T(1,128)S(1)} %add.47.refs_0_), channel_id=1, source_target_pairs={{0,16},{4,20},{8,24},{12,28},{16,0},{20,4},{24,8},{28,12},{1,17},{... | collective-permute-start | bytes 98312 | tf_op jit(solution)/shard_map/ppermute | solution.py:656
  41.7 3.5 %view_soft.6.refs_2_ = f32[1024,128]{1,0:T(8,128)S(1)} custom-call(bf16[1024,128]{1,0:T(8,128)(2,1)S(1)} %get-tuple-element.96.views.refs_0_, bf16[8192,128]{1,0:T(8,128)(2,1)S(1)} %copy-done.1), custom_call_target="tpu_custom_call" | custom-call | flops 1000 | bytes 1000 | tf_op jit(solution)/shard_map/view_soft/pallas_call | solution.py:491
  45.2 4.0 %rowsum.2 = (f32[1,8192]{1,0:T(1,128)}, f32[1,1024]{1,0:T(1,128)S(1)}) custom-call(bf16[1024,8192]{1,0:T(8,128)(2,1)S(1)} %get-tuple-element.83.expo, f32[1,8192]{1,0:T(1,128)S(1)} %add.47.refs_0_, f32[1,8192]{1,0:T(1,128)S(1)} %collective-permute-done.2.refs_1_), custom_call_target="tpu_custom_call" | custom-call | flops 1000 | bytes 1000 | tf_op jit(solution)/shard_map/rowsum/pallas_call | solution.py:266
  49.4 3.5 %view_soft.7.refs_3_ = f32[1024,128]{1,0:T(8,128)S(1)} custom-call(bf16[1024,128]{1,0:T(8,128)(2,1)S(1)} %get-tuple-element.96.views.refs_0_, bf16[8192,128]{1,0:T(8,128)(2,1)S(1)} %copy-done.1), custom_call_target="tpu_custom_call" | custom-call | flops 1000 | bytes 1000 | tf_op jit(solution)/shard_map/view_soft/pallas_call | solution.py:491
  52.9 1.6 collective-permute-start.4
  54.5 2.2 collective-permute-done.4
  56.7 2.2 %colsum.2 = f32[1,1,8192]{2,1,0:T(1,128)S(1)} custom-call(bf16[1024,8192]{1,0:T(8,128)(2,1)S(1)} %get-tuple-element.83.expo, f32[1,1024]{1,0:T(1,128)S(1)} %get-tuple-element.161.refs_0_), custom_call_target="tpu_custom_call" | custom-call | flops 1000 | bytes 1000 | tf_op jit(solution)/shard_map/colsum/pallas_call | solution.py:356
  61.0 2.8 %collective-permute-done.5 = f32[1,1,1024]{2,1,0:T(1,128)S(1)} collective-permute-done((f32[1,1,1024]{2,1,0:T(1,128)S(1)}, f32[1,1,1024]{2,1,0:T(1,128)S(1)}, u32[]{:S(2)}, u32[]{:S(2)}) %collective-permute-start.5) | collective-permute-done | bytes 4128 | tf_op jit(solution)/shard_map/ppermute | solution.py:656
  64.4 1.6 collective-permute-start.7
  66.0 2.2 collective-permute-done.7
  68.2 1.6 collective-permute-start.10
  69.8 1.5 collective-permute-start.9
  71.3 3.2 %collective-permute-done.9 = f32[4,1,1024]{2,1,0:T(1,128)S(1)} collective-permute-done((f32[4,1,1024]{2,1,0:T(1,128)S(1)}, f32[4,1,1024]{2,1,0:T(1,128)S(1)}, u32[]{:S(2)}, u32[]{:S(2)}) %collective-permute-start.9) | collective-permute-done | bytes 16416 | tf_op jit(solution)/shard_map/ppermute | solution.py:656
  74.5 4.0 %rowsum.3 = (f32[1,8192]{1,0:T(1,128)}, f32[1,1024]{1,0:T(1,128)S(1)}) custom-call(bf16[1024,8192]{1,0:T(8,128)(2,1)S(1)} %get-tuple-element.83.expo, f32[1,8192]{1,0:T(1,128)S(1)} %add.51.refs_0_, f32[1,8192]{1,0:T(1,128)S(1)} %collective-permute-done.10.refs_1_), custom_call_target="tpu_custom_call" | custom-call | flops 1000 | bytes 1000 | tf_op jit(solution)/shard_map/rowsum/pallas_call | solution.py:266
  79.7 1.5 collective-permute-start.12
  81.1 2.1 collective-permute-done.12.refs_1_
  83.3 2.4 %colsum.3 = f32[1,1,8192]{2,1,0:T(1,128)S(1)} custom-call(bf16[1024,8192]{1,0:T(8,128)(2,1)S(1)} %get-tuple-element.83.expo, f32[1,1024]{1,0:T(1,128)S(1)} %add.52.refs_0_, f32[1,1024]{1,0:T(1,128)S(1)} %collective-permute-done.12.refs_1_), custom_call_target="tpu_custom_call" | custom-call | flops 1000 | bytes 1000 | tf_op jit(solution)/shard_map/colsum/pallas_call | solution.py:356
  86.6 1.6 copy-done.2
  88.2 3.3 %proto_first.4 = (bf16[1024,2048]{1,0:T(8,128)(2,1)S(1)}, f32[1024,128]{1,0:T(8,128)S(1)}) custom-call(s32[1]{0:T(128)} %bitcast.2.place, bf16[1024,128]{1,0:T(8,128)(2,1)S(1)} %constant_dynamic-slice_fusion.2.protos.refs_9_, bf16[8,128,1024]{2,1,0:T(8,128)(2,1)S(1)} %bitcast.11, f32[8,1,1024]{2,1,0:T(1,128)S(1)} %pad_maximum_fusion.1.totals), custom_call_target="tpu_custom_call" | custom-call | flops 1000 | bytes 1000 | tf_op jit(solution)/shard_map/proto_first/pallas_call | solution.py:400
  92.9 3.3 %proto_first.5 = (bf16[1024,2048]{1,0:T(8,128)(2,1)S(1)}, f32[1024,128]{1,0:T(8,128)S(1)}) custom-call(s32[1]{0:T(128)} %bitcast.2.place, bf16[1024,128]{1,0:T(8,128)(2,1)S(1)} %constant_dynamic-slice_fusion.2.protos.refs_9_, bf16[8,128,1024]{2,1,0:T(8,128)(2,1)S(1)} %bitcast.12, f32[8,1,1024]{2,1,0:T(1,128)S(1)} %pad_maximum_fusion.1.totals), custom_call_target="tpu_custom_call" | custom-call | flops 1000 | bytes 1000 | tf_op jit(solution)/shard_map/proto_first/pallas_call | solution.py:400
  96.2 1.9 collective-permute-start.15
  98.1 3.3 %proto_first.6 = (bf16[1024,2048]{1,0:T(8,128)(2,1)S(1)}, f32[1024,128]{1,0:T(8,128)S(1)}) custom-call(s32[1]{0:T(128)} %bitcast.2.place, bf16[1024,128]{1,0:T(8,128)(2,1)S(1)} %constant_dynamic-slice_fusion.2.protos.refs_9_, bf16[8,128,1024]{2,1,0:T(8,128)(2,1)S(1)} %bitcast.13, f32[8,1,1024]{2,1,0:T(1,128)S(1)} %pad_maximum_fusion.1.totals), custom_call_target="tpu_custom_call" | custom-call | flops 1000 | bytes 1000 | tf_op jit(solution)/shard_map/proto_first/pallas_call | solution.py:400
  101.5 9.3 %rowsum_stream.1 = (f32[1,8192]{1,0:T(1,128)S(1)}, f32[1,1024]{1,0:T(1,128)S(1)}) custom-call(bf16[1024,8192]{1,0:T(8,128)(2,1)} %copy-done, f32[1,8192]{1,0:T(1,128)S(1)} %add.54.refs_0_, f32[1,8192]{1,0:T(1,128)S(1)} %collective-permute-done.15.refs_1_), custom_call_target="tpu_custom_call" | custom-call | flops 1000 | bytes 1000 | tf_op jit(solution)/shard_map/rowsum_stream/pallas_call | solution.py:306
  110.9 3.3 %proto_first.7 = (bf16[1024,2048]{1,0:T(8,128)(2,1)S(1)}, f32[1024,128]{1,0:T(8,128)S(1)}) custom-call(s32[1]{0:T(128)} %bitcast.2.place, bf16[1024,128]{1,0:T(8,128)(2,1)S(1)} %constant_dynamic-slice_fusion.2.protos.refs_9_, bf16[8,128,1024]{2,1,0:T(8,128)(2,1)S(1)} %bitcast.14, f32[8,1,1024]{2,1,0:T(1,128)S(1)} %pad_maximum_fusion.1.totals), custom_call_target="tpu_custom_call" | custom-call | flops 1000 | bytes 1000 | tf_op jit(solution)/shard_map/proto_first/pallas_call | solution.py:400
  114.2 1.6 collective-permute-start.17
  115.7 2.1 collective-permute-done.17
  119.0 2.4 %collective-permute-done.22 = f32[1,1,1024]{2,1,0:T(1,128)S(1)} collective-permute-done((f32[1,1,1024]{2,1,0:T(1,128)S(1)}, f32[1,1,1024]{2,1,0:T(1,128)S(1)}, u32[]{:S(2)}, u32[]{:S(2)}) %collective-permute-start.22) | collective-permute-done | bytes 4128 | tf_op jit(solution)/shard_map/ppermute | solution.py:656
  122.1 3.1 %collective-permute-done.23 = f32[2,1,1024]{2,1,0:T(1,128)S(1)} collective-permute-done((f32[2,1,1024]{2,1,0:T(1,128)S(1)}, f32[2,1,1024]{2,1,0:T(1,128)S(1)}, u32[]{:S(2)}, u32[]{:S(2)}) %collective-permute-start.23) | collective-permute-done | bytes 8224 | tf_op jit(solution)/shard_map/ppermute | solution.py:656
  125.2 1.5 collective-permute-start.24
  126.7 3.3 %collective-permute-done.24 = f32[4,1,1024]{2,1,0:T(1,128)S(1)} collective-permute-done((f32[4,1,1024]{2,1,0:T(1,128)S(1)}, f32[4,1,1024]{2,1,0:T(1,128)S(1)}, u32[]{:S(2)}, u32[]{:S(2)}) %collective-permute-start.24) | collective-permute-done | bytes 16416 | tf_op jit(solution)/shard_map/ppermute | solution.py:656
  130.1 5.4 %proto_last.1 = bf16[1024,128]{1,0:T(8,128)(2,1)} custom-call(s32[1]{0:T(128)} %bitcast.2.place, bf16[1024,2048]{1,0:T(8,128)(2,1)S(1)} %get-tuple-element.151.refs_0_, bf16[1024,2048]{1,0:T(8,128)(2,1)S(1)} %get-tuple-element.152.refs_1_, bf16[1024,2048]{1,0:T(8,128)(2,1)S(1)} %get-tuple-element.153.refs_2_, ...), custom_call_target="tpu_custom_call" | custom-call | tf_op jit(solution)/shard_map/proto_last/pallas_call | solution.py:450
  135.6 13.4 %view_grad.1 = bf16[1024,128]{1,0:T(8,128)(2,1)S(1)} custom-call(bf16[8192,128]{1,0:T(8,128)(2,1)S(1)} %copy-done.1, bf16[1024,8192]{1,0:T(8,128)(2,1)} %copy-done, f32[1,8192]{1,0:T(1,128)S(1)} %get-tuple-element.132.scale.refs_8_, f32[1,1024]{1,0:T(1,128)S(1)} %get-tuple-element.159.tot, f32[1,1024]{1,0:T(1,128)S(1)} %add.56.total, f32[1024,128]{1,0:T(8,128)} %copy-done.4, ...), custom_call_target="tpu_custom_call" | custom-call | tf_op jit(solution)/shard_map/view_grad/pallas_call | solution.py:536
  149.1 1.5 collective-permute-done.18
  150.7 1.6 collective-permute-start.19
  154.4 4.7 %collective-permute-done.19.grad_b = bf16[1024,128]{1,0:T(8,128)(2,1)S(1)} collective-permute-done((bf16[1024,128]{1,0:T(8,128)(2,1)S(1)}, bf16[1024,128]{1,0:T(8,128)(2,1)S(1)}, u32[]{:S(2)}, u32[]{:S(2)}) %collective-permute-start.19) | collective-permute-done | bytes 262176 | tf_op jit(solution)/shard_map/ppermute | solution.py:656
  159.1 3.3 %backward.1 = f32[8,144,128]{2,1,0:T(8,128)S(1)} custom-call(bf16[1024,128]{1,0:T(8,128)(2,1)S(1)} %add_convert_fusion.grad_a, bf16[1024,128]{1,0:T(8,128)(2,1)S(1)} %collective-permute-done.19.grad_b, s32[1,1024]{1,0:T(1,128)S(1)} %get-tuple-element.145.pos, f32[1024,128]{1,0:T(8,128)S(1)} %copy-done.9, f32[1024,512]{1,0:T(8,128)S(1)} %copy-done.8, ...), custom_call_target="tpu_custom_call" | custom-call | tf_op jit(solution)/shard_map/backward/pallas_call | solution.py:589
  162.5 21.0 %all_to_all.10 = bf16[8,144,128]{2,1,0:T(8,128)(2,1)S(1)} all-to-all(bf16[8,144,128]{2,1,0:T(8,128)(2,1)S(1)} %convert_element_type.22), channel_id=1, replica_groups=mesh['batch'=8,'proto'=4] {'batch'}, dimensions={0} | all-to-all | bytes 589824 | tf_op jit(solution)/shard_map/all_to_all | solution.py:755
  183.6 12.9 %all_to_all.11 = bf16[8,144,128]{2,1,0:T(8,128)(2,1)S(1)} all-to-all(bf16[8,144,128]{2,1,0:T(8,128)(2,1)S(1)} %broadcast_in_dim.16), channel_id=1, replica_groups=mesh['batch'=8,'proto'=4] {'batch'}, dimensions={0} | all-to-all | bytes 589824 | tf_op jit(solution)/shard_map/all_to_all | solution.py:676
  197.9 5.3 %collective-permute-done.20 = bf16[1,8,144,128]{3,2,1,0:T(8,128)(2,1)S(1)} collective-permute-done((bf16[1,8,144,128]{3,2,1,0:T(8,128)(2,1)S(1)}, bf16[1,8,144,128]{3,2,1,0:T(8,128)(2,1)S(1)}, u32[]{:S(2)}, u32[]{:S(2)}) %collective-permute-start.20) | collective-permute-done | bytes 294944 | tf_op jit(solution)/shard_map/ppermute | solution.py:656
  203.4 2.0 collective-permute-done.21.refs_1_
  205.4 1.5 unpack.1
  206.9 6.0 %widen.1 = f32[8192,128]{1,0:T(8,128)} custom-call(bf16[8192,128]{1,0:T(8,128)(2,1)} %all-gather.4.cloned.1.call-done.x), custom_call_target="tpu_custom_call" | custom-call | tf_op jit(solution)/shard_map/widen/pallas_call | solution.py:636
  (81 shorter events, 14.2 us)
Async XLA Ops:
  7.2 8.2 %copy-start.1 = (bf16[8192,128]{1,0:T(8,128)(2,1)S(1)}, bf16[8192,128]{1,0:T(8,128)(2,1)}, u32[]{:S(2)}) copy-start(bf16[8192,128]{1,0:T(8,128)(2,1)} %protos.3) | copy-start | bytes 6291460
  7.2 78.5 %all-gather.6.cloned.1.call-start = ((), (), s32[]{:S(2)}) async-start(), calls=%async_computation.3 | async-start | bytes 2359296 | tf_op jit(solution)/shard_map/all_gather | solution.py:679
  7.2 0.8 copy-start.11
  15.3 191.6 %all-gather.4.cloned.1.call-start = ((), (), s32[]{:S(2)}) async-start(), calls=%async_computation.2 | async-start | bytes 2359296 | tf_op jit(solution)/shard_map/all_gather | solution.py:743
  26.4 56.9 %copy-start = (bf16[1024,8192]{1,0:T(8,128)(2,1)}, bf16[1024,8192]{1,0:T(8,128)(2,1)S(1)}, u32[]{:S(2)}) copy-start(bf16[1024,8192]{1,0:T(8,128)(2,1)S(1)} %get-tuple-element.83.expo) | copy-start | bytes 50331652
  26.4 7.3 %collective-permute-start = (f32[1,8192]{1,0:T(1,128)S(1)}, f32[1,8192]{1,0:T(1,128)S(1)}, u32[]{:S(2)}, u32[]{:S(2)}) collective-permute-start(f32[1,8192]{1,0:T(1,128)S(1)} %get-tuple-element.84), channel_id=1, source_target_pairs={{0,4},{4,0},{8,12},{12,8},{16,20},{20,16},{24,28},{28,24},{1,5},{5... | collective-permute-start | bytes 98312 | tf_op jit(solution)/shard_map/ppermute | solution.py:656
  32.9 0.8 copy-start.4
  33.7 5.3 %collective-permute-start.1 = (f32[1,8192]{1,0:T(1,128)S(1)}, f32[1,8192]{1,0:T(1,128)S(1)}, u32[]{:S(2)}, u32[]{:S(2)}) collective-permute-start(f32[1,8192]{1,0:T(1,128)S(1)} %add.46), channel_id=1, source_target_pairs={{0,8},{4,12},{8,0},{12,4},{16,24},{20,28},{24,16},{28,20},{1,9},{5... | collective-permute-start | bytes 98312 | tf_op jit(solution)/shard_map/ppermute | solution.py:656
  39.0 10.3 %copy-start.5 = (f32[1024,128]{1,0:T(8,128)}, f32[1024,128]{1,0:T(8,128)S(1)}, u32[]{:S(2)}) copy-start(f32[1024,128]{1,0:T(8,128)S(1)} %view_soft.5.refs_1_) | copy-start | bytes 1572868
  39.1 6.2 %collective-permute-start.2 = (f32[1,8192]{1,0:T(1,128)S(1)}, f32[1,8192]{1,0:T(1,128)S(1)}, u32[]{:S(2)}, u32[]{:S(2)}) collective-permute-start(f32[1,8192]{1,0:T(1,128)S(1)} %add.47.refs_0_), channel_id=1, source_target_pairs={{0,16},{4,20},{8,24},{12,28},{16,0},{20,4},{24,8},{28,12},{1,17},{... | collective-permute-start | bytes 98312 | tf_op jit(solution)/shard_map/ppermute | solution.py:656
  45.2 4.1 %copy-start.6 = (f32[1024,128]{1,0:T(8,128)}, f32[1024,128]{1,0:T(8,128)S(1)}, u32[]{:S(2)}) copy-start(f32[1024,128]{1,0:T(8,128)S(1)} %view_soft.6.refs_2_) | copy-start | bytes 1572868
  49.3 3.6 %collective-permute-start.3 = (f32[2,1024]{1,0:T(2,128)S(1)}, f32[2,1024]{1,0:T(2,128)S(1)}, u32[]{:S(2)}, u32[]{:S(2)}) collective-permute-start(f32[2,1024]{1,0:T(2,128)S(1)} %pad_maximum_fusion.5), channel_id=1, source_target_pairs={{0,1},{1,0},{2,3},{3,2},{4,5},{5,4},{6,7},{7,6},{8,9},{9,8},{10,11... | collective-permute-start | bytes 24584 | tf_op jit(solution)/shard_map/ppermute | solution.py:656
  52.9 6.0 %copy-start.7 = (f32[1024,128]{1,0:T(8,128)}, f32[1024,128]{1,0:T(8,128)S(1)}, u32[]{:S(2)}) copy-start(f32[1024,128]{1,0:T(8,128)S(1)} %view_soft.7.refs_3_) | copy-start | bytes 1572868
  52.9 3.7 %collective-permute-start.4 = (f32[2,1024]{1,0:T(2,128)S(1)}, f32[2,1024]{1,0:T(2,128)S(1)}, u32[]{:S(2)}, u32[]{:S(2)}) collective-permute-start(f32[2,1024]{1,0:T(2,128)S(1)} %fusion), channel_id=1, source_target_pairs={{0,2},{1,3},{2,0},{3,1},{4,6},{5,7},{6,4},{7,5},{8,10},{9,11},{10,... | collective-permute-start | bytes 24584 | tf_op jit(solution)/shard_map/ppermute | solution.py:656
  58.9 4.9 %collective-permute-start.6 = (f32[1,8192]{1,0:T(1,128)S(1)}, f32[1,8192]{1,0:T(1,128)S(1)}, u32[]{:S(2)}, u32[]{:S(2)}) collective-permute-start(f32[1,8192]{1,0:T(1,128)S(1)} %bitcast.18), channel_id=1, source_target_pairs={{0,4},{4,0},{8,12},{12,8},{16,20},{20,16},{24,28},{28,24},{1,5},{5... | collective-permute-start | bytes 98312 | tf_op jit(solution)/shard_map/ppermute | solution.py:656
  60.2 3.6 %collective-permute-start.5 = (f32[1,1,1024]{2,1,0:T(1,128)S(1)}, f32[1,1,1024]{2,1,0:T(1,128)S(1)}, u32[]{:S(2)}, u32[]{:S(2)}) collective-permute-start(f32[1,1,1024]{2,1,0:T(1,128)S(1)} %get-tuple-element.160), channel_id=1, source_target_pairs={{0,4},{4,0},{8,12},{12,8},{16,20},{20,16},{24,28},{28,24},{1,5},{5... | collective-permute-start | bytes 12296 | tf_op jit(solution)/shard_map/ppermute | solution.py:656
  63.8 4.3 %collective-permute-start.8 = (f32[1,8192]{1,0:T(1,128)S(1)}, f32[1,8192]{1,0:T(1,128)S(1)}, u32[]{:S(2)}, u32[]{:S(2)}) collective-permute-start(f32[1,8192]{1,0:T(1,128)S(1)} %bitcast_add_fusion), channel_id=1, source_target_pairs={{0,8},{4,12},{8,0},{12,4},{16,24},{20,28},{24,16},{28,20},{1,9},{5... | collective-permute-start | bytes 98312 | tf_op jit(solution)/shard_map/ppermute | solution.py:656
  64.4 3.7 %collective-permute-start.7 = (f32[2,1,1024]{2,1,0:T(1,128)S(1)}, f32[2,1,1024]{2,1,0:T(1,128)S(1)}, u32[]{:S(2)}, u32[]{:S(2)}) collective-permute-start(f32[2,1,1024]{2,1,0:T(1,128)S(1)} %pad_maximum_fusion.6), channel_id=1, source_target_pairs={{0,8},{4,12},{8,0},{12,4},{16,24},{20,28},{24,16},{28,20},{1,9},{5... | collective-permute-start | bytes 24584 | tf_op jit(solution)/shard_map/ppermute | solution.py:656
  68.2 6.3 %collective-permute-start.10 = (f32[1,8192]{1,0:T(1,128)S(1)}, f32[1,8192]{1,0:T(1,128)S(1)}, u32[]{:S(2)}, u32[]{:S(2)}) collective-permute-start(f32[1,8192]{1,0:T(1,128)S(1)} %add.51.refs_0_), channel_id=1, source_target_pairs={{0,16},{4,20},{8,24},{12,28},{16,0},{20,4},{24,8},{28,12},{1,17},{... | collective-permute-start | bytes 98312 | tf_op jit(solution)/shard_map/ppermute | solution.py:656
  69.8 4.7 %collective-permute-start.9 = (f32[4,1,1024]{2,1,0:T(1,128)S(1)}, f32[4,1,1024]{2,1,0:T(1,128)S(1)}, u32[]{:S(2)}, u32[]{:S(2)}) collective-permute-start(f32[4,1,1024]{2,1,0:T(1,128)S(1)} %pad_maximum_fusion.3), channel_id=1, source_target_pairs={{0,16},{4,20},{8,24},{12,28},{16,0},{20,4},{24,8},{28,12},{1,17},{... | collective-permute-start | bytes 49160 | tf_op jit(solution)/shard_map/ppermute | solution.py:656
  78.5 1.2 collective-permute-start.11
  79.7 3.6 %collective-permute-start.12 = (f32[1,1024]{1,0:T(1,128)S(1)}, f32[1,1024]{1,0:T(1,128)S(1)}, u32[]{:S(2)}, u32[]{:S(2)}) collective-permute-start(f32[1,1024]{1,0:T(1,128)S(1)} %add.52.refs_0_), channel_id=1, source_target_pairs={{0,2},{1,3},{2,0},{3,1},{4,6},{5,7},{6,4},{7,5},{8,10},{9,11},{10,... | collective-permute-start | bytes 12296 | tf_op jit(solution)/shard_map/ppermute | solution.py:656
  85.7 5.7 %collective-permute-start.13 = (f32[1,8192]{1,0:T(1,128)S(1)}, f32[1,8192]{1,0:T(1,128)S(1)}, u32[]{:S(2)}, u32[]{:S(2)}) collective-permute-start(f32[1,8192]{1,0:T(1,128)S(1)} %bitcast.16), channel_id=1, source_target_pairs={{0,4},{4,0},{8,12},{12,8},{16,20},{20,16},{24,28},{28,24},{1,5},{5... | collective-permute-start | bytes 98312 | tf_op jit(solution)/shard_map/ppermute | solution.py:656
  86.6 1.6 copy-start.2
  91.5 4.7 %collective-permute-start.14 = (f32[1,8192]{1,0:T(1,128)S(1)}, f32[1,8192]{1,0:T(1,128)S(1)}, u32[]{:S(2)}, u32[]{:S(2)}) collective-permute-start(f32[1,8192]{1,0:T(1,128)S(1)} %add.53), channel_id=1, source_target_pairs={{0,8},{4,12},{8,0},{12,4},{16,24},{20,28},{24,16},{28,20},{1,9},{5... | collective-permute-start | bytes 98312 | tf_op jit(solution)/shard_map/ppermute | solution.py:656
  96.2 5.2 %collective-permute-start.15 = (f32[1,8192]{1,0:T(1,128)S(1)}, f32[1,8192]{1,0:T(1,128)S(1)}, u32[]{:S(2)}, u32[]{:S(2)}) collective-permute-start(f32[1,8192]{1,0:T(1,128)S(1)} %add.54.refs_0_), channel_id=1, source_target_pairs={{0,16},{4,20},{8,24},{12,28},{16,0},{20,4},{24,8},{28,12},{1,17},{... | collective-permute-start | bytes 98312 | tf_op jit(solution)/shard_map/ppermute | solution.py:656
  110.8 19.3 %copy-start.3 = (bf16[1024,1024]{1,0:T(8,128)(2,1)S(1)}, bf16[1024,1024]{1,0:T(8,128)(2,1)}, u32[]{:S(2)}) copy-start(bf16[1024,1024]{1,0:T(8,128)(2,1)} %all-gather.6.cloned.1.call-done) | copy-start | bytes 6291460
  110.8 3.3 %collective-permute-start.16 = (f32[1,1024]{1,0:T(1,128)S(1)}, f32[1,1024]{1,0:T(1,128)S(1)}, u32[]{:S(2)}, u32[]{:S(2)}) collective-permute-start(f32[1,1024]{1,0:T(1,128)S(1)} %get-tuple-element.133), channel_id=1, source_target_pairs={{0,1},{1,0},{2,3},{3,2},{4,5},{5,4},{6,7},{7,6},{8,9},{9,8},{10,11... | collective-permute-start | bytes 12296 | tf_op jit(solution)/shard_map/ppermute | solution.py:656
  114.2 3.7 %collective-permute-start.17 = (f32[1,1024]{1,0:T(1,128)S(1)}, f32[1,1024]{1,0:T(1,128)S(1)}, u32[]{:S(2)}, u32[]{:S(2)}) collective-permute-start(f32[1,1024]{1,0:T(1,128)S(1)} %add.55), channel_id=1, source_target_pairs={{0,2},{1,3},{2,0},{3,1},{4,6},{5,7},{6,4},{7,5},{8,10},{9,11},{10,... | collective-permute-start | bytes 12296 | tf_op jit(solution)/shard_map/ppermute | solution.py:656
  117.9 3.6 %collective-permute-start.22 = (f32[1,1,1024]{2,1,0:T(1,128)S(1)}, f32[1,1,1024]{2,1,0:T(1,128)S(1)}, u32[]{:S(2)}, u32[]{:S(2)}) collective-permute-start(f32[1,1,1024]{2,1,0:T(1,128)S(1)} %bitcast.19), channel_id=1, source_target_pairs={{0,4},{4,0},{8,12},{12,8},{16,20},{20,16},{24,28},{28,24},{1,5},{5... | collective-permute-start | bytes 12296 | tf_op jit(solution)/shard_map/ppermute | solution.py:656
  121.5 3.7 %collective-permute-start.23 = (f32[2,1,1024]{2,1,0:T(1,128)S(1)}, f32[2,1,1024]{2,1,0:T(1,128)S(1)}, u32[]{:S(2)}, u32[]{:S(2)}) collective-permute-start(f32[2,1,1024]{2,1,0:T(1,128)S(1)} %pad_maximum_fusion.7), channel_id=1, source_target_pairs={{0,8},{4,12},{8,0},{12,4},{16,24},{20,28},{24,16},{28,20},{1,9},{5... | collective-permute-start | bytes 24584 | tf_op jit(solution)/shard_map/ppermute | solution.py:656
  125.2 4.9 %collective-permute-start.24 = (f32[4,1,1024]{2,1,0:T(1,128)S(1)}, f32[4,1,1024]{2,1,0:T(1,128)S(1)}, u32[]{:S(2)}, u32[]{:S(2)}) collective-permute-start(f32[4,1,1024]{2,1,0:T(1,128)S(1)} %pad_maximum_fusion.4), channel_id=1, source_target_pairs={{0,16},{4,20},{8,24},{12,28},{16,0},{20,4},{24,8},{28,12},{1,17},{... | collective-permute-start | bytes 49160 | tf_op jit(solution)/shard_map/ppermute | solution.py:656
  135.6 23.6 %copy-start.9 = (f32[1024,128]{1,0:T(8,128)S(1)}, f32[1024,128]{1,0:T(8,128)}, u32[]{:S(2)}) copy-start(f32[1024,128]{1,0:T(8,128)} %get-tuple-element.146.raw) | copy-start | bytes 1572868
  149.0 10.1 %copy-start.8 = (f32[1024,512]{1,0:T(8,128)S(1)}, f32[1024,512]{1,0:T(8,128)}, u32[]{:S(2)}) copy-start(f32[1024,512]{1,0:T(8,128)} %get-tuple-element.147.pre) | copy-start | bytes 6291460
  149.0 10.1 %copy-start.10 = (bf16[512,128]{1,0:T(8,128)(2,1)S(1)}, bf16[512,128]{1,0:T(8,128)(2,1)}, u32[]{:S(2)}) copy-start(bf16[512,128]{1,0:T(8,128)(2,1)} %w_out.3) | copy-start | bytes 393220
  149.0 1.6 collective-permute-start.18
  150.7 8.4 %collective-permute-start.19 = (bf16[1024,128]{1,0:T(8,128)(2,1)S(1)}, bf16[1024,128]{1,0:T(8,128)(2,1)S(1)}, u32[]{:S(2)}, u32[]{:S(2)}) collective-permute-start(bf16[1024,128]{1,0:T(8,128)(2,1)S(1)} %add_convert_fusion.grad_a), channel_id=1, source_target_pairs={{0,2},{1,3},{2,0},{3,1},{4,6},{5,7},{6,4},{7,5},{8,10},{9,11},{10,... | collective-permute-start | bytes 786440 | tf_op jit(solution)/shard_map/ppermute | solution.py:656
  196.5 6.7 %collective-permute-start.20 = (bf16[1,8,144,128]{3,2,1,0:T(8,128)(2,1)S(1)}, bf16[1,8,144,128]{3,2,1,0:T(8,128)(2,1)S(1)}, u32[]{:S(2)}, u32[]{:S(2)}) collective-permute-start(bf16[1,8,144,128]{3,2,1,0:T(8,128)(2,1)S(1)} %bitcast.24), channel_id=1, source_target_pairs={{0,2},{1,3},{2,0},{3,1},{4,6},{5,7},{6,4},{7,5},{8,10},{9,11},{10,... | collective-permute-start | bytes 884744 | tf_op jit(solution)/shard_map/ppermute | solution.py:656
  203.3 2.1 collective-permute-start.21
Sparse Core Ops, SparseCore 0:
  15.5 52.0 all-gather.5
  135.7 51.9 all-gather.3

commit v5 on v4

--- a/solution.py
+++ b/solution.py
@@ -278,46 +278,93 @@
     )(in_vmem(expo), *parts)
 
 
-def rowsum_stream_kernel(count, expo, *refs):
-    parts = refs[:count]
-    scale, out, spread, acc = refs[count:]
-    block, width = expo.shape
+def split_rows(vec):
+    hi = vec.astype(bf16).astype(f32)
+    n = vec.shape[1]
+    row = lax.broadcasted_iota(jnp.int32, (8, n), 0)
+    hi8 = jnp.broadcast_to(hi, (8, n))
+    lo8 = jnp.broadcast_to(vec - hi, (8, n))
+    return jnp.where(row == 0, hi8, jnp.where(row == 1, lo8, 0.0))
+
+
+def rowsum_last_kernel(pieces, count, *refs):
+    expos = refs[:pieces]
+    parts = refs[pieces : pieces + count]
+    unit_t, scale, out, code, acc = refs[pieces + count :]
     step = pl.program_id(0)
-
-    @pl.when(step == 0)
-    def _():
-        inverse = 1.0 / sum_parts(parts, width)
-        scale[...] = inverse
-        spread[...] = jnp.broadcast_to(inverse, spread.shape).astype(bf16)
-
-    tall = 64
-    for i in range(block // tall):
-        here = pl.ds(pl.multiple_of(step * block + i * tall, tall), tall)
-        acc[here, :] = rowsum_tile(expo, slice(i * tall, (i + 1) * tall), spread, tall, width)
+    depth, block = unit_t.shape
+    tall = expos[0].shape[0]
+    inverse = 1.0 / sum_parts(parts, block)
+    scale[...] = inverse
+    scaled = unit_t[...].astype(f32) * inverse
+    pad = jnp.zeros((depth - 8, block), f32)
+    weights = jnp.concatenate([scaled, split_rows(inverse), pad], axis=0).astype(bf16)
+    for k in range(pieces):
+        part = slice(k * tall, (k + 1) * tall)
+        found = dot(expos[k][...], weights, NT)
+
+        @pl.when(step == 0)
+        def _():
+            acc[part, :] = found
+
+        @pl.when(step > 0)
+        def _():
+            acc[part, :] += found
 
     @pl.when(step == pl.num_programs(0) - 1)
     def _():
-        out[...] = jnp.sum(acc[...].T, axis=0, keepdims=True)
-
-
-def rowsum_stream(expo, parts):
+        sums = acc[:, depth:].T
+        out[...] = sums[0:1] + sums[1:2]
+        code[...] = acc[:, :depth]
+
+
+def rowsum_last(expo, parts, unit_t):
     rows, width = expo.shape
-    block = min(128, rows)
-    return pl.pallas_call(
-        functools.partial(rowsum_stream_kernel, len(parts)),
-        grid=(rows // block,),
-        in_specs=[pl.BlockSpec((block, width), lambda i: (i, 0))]
-        + [full((1, width))] * len(parts),
-        out_specs=[full((1, width)), full((1, rows))],
+    depth = unit_t.shape[0]
+    block = min(1024, width)
+    pieces = 4
+    tall = rows // pieces
+    vec = pl.BlockSpec((1, block), lambda j: (0, j))
+    return pl.pallas_call(
+        functools.partial(rowsum_last_kernel, pieces, len(parts)),
+        grid=(width // block,),
+        in_specs=[pl.BlockSpec((tall, block), lambda j, k=k: (k, j)) for k in range(pieces)]
+        + [vec] * len(parts)
+        + [pl.BlockSpec((depth, block), lambda j: (0, j))],
+        out_specs=[vec, full((1, rows)), full((rows, depth))],
         out_shape=[
             jax.ShapeDtypeStruct((1, width), f32),
             jax.ShapeDtypeStruct((1, rows), f32),
-        ],
-        scratch_shapes=[pltpu.VMEM((16, width), bf16), pltpu.VMEM((rows, 128), f32)],
+            jax.ShapeDtypeStruct((rows, depth), f32),
+        ],
+        scratch_shapes=[pltpu.VMEM((rows, 2 * depth), f32)],
         compiler_params=params("arbitrary"),
         cost_estimate=SMALL,
-        name="rowsum_stream",
-    )(in_hbm(expo), *parts)
+        name="rowsum_last",
+    )(*[in_hbm(expo)] * pieces, *parts, in_hbm(unit_t))
+
+
+def unit_t_kernel(block, protos, out):
+    def one(j, carry):
+        here = pl.ds(pl.multiple_of(j * block, block), block)
+        _, _, unit = unit_of(protos[here, :])
+        out[:, here] = unit.astype(bf16).astype(f32).T.astype(bf16)
+        return carry
+
+    lax.fori_loop(0, protos.shape[0] // block, one, 0)
+
+
+def unit_transposed(protos):
+    width, depth = protos.shape
+    return pl.pallas_call(
+        functools.partial(unit_t_kernel, min(512, width)),
+        in_specs=[WHOLE],
+        out_specs=WHOLE,
+        out_shape=jax.ShapeDtypeStruct((depth, width), bf16),
+        compiler_params=params(),
+        cost_estimate=SMALL,
+        name="unit_t",
+    )(protos)
 
 
 def colsum_kernel(count, expo, *refs):
@@ -504,52 +551,26 @@
     )(views, protos)
 
 
-def view_grad_kernel(groups, protos, expo, scale, tot, total, *refs):
-    softs, (out, acc) = refs[:groups], refs[groups:]
-    step = pl.program_id(0)
-    _, _, unit = unit_of(protos[...])
-    scaled = (unit.astype(bf16).astype(f32) * to_column(scale[...])).astype(bf16)
-    found = dot(expo[...], scaled)
-
-    @pl.when(step == 0)
-    def _():
-        acc[...] = found
-
-    @pl.when(step > 0)
-    def _():
-        acc[...] += found
-
-    @pl.when(step == pl.num_programs(0) - 1)
-    def _():
-        soft = softs[0][...]
-        for other in softs[1:]:
-            soft = soft + other[...]
-        soft = soft * to_column(GRAD_SCALE / tot[...])
-        hard = swap_rows(acc[...] * to_column(GRAD_SCALE / total[...]))
-        out[...] = (soft - hard).astype(out.dtype)
-
-
-def view_grad_part(protos, expo, scale, tot, total, softs):
-    rows, width = expo.shape
-    depth = protos.shape[1]
-    block = min(1024, width)
-    return pl.pallas_call(
-        functools.partial(view_grad_kernel, len(softs)),
-        grid=(width // block,),
-        in_specs=[
-            pl.BlockSpec((block, depth), lambda j: (j, 0)),
-            pl.BlockSpec((rows, block), lambda j: (0, j)),
-            pl.BlockSpec((1, block), lambda j: (0, j)),
-            full((1, rows)),
-            full((1, rows)),
-        ]
-        + [full((rows, depth))] * len(softs),
-        out_specs=full((rows, depth)),
-        out_shape=jax.ShapeDtypeStruct((rows, depth), bf16),
-        scratch_shapes=[pltpu.VMEM((rows, depth), f32)],
-        compiler_params=params("arbitrary"),
+def view_grad_kernel(code, tot, total, *refs):
+    softs, out = refs[:-1], refs[-1]
+    soft = softs[0][...]
+    for other in softs[1:]:
+        soft = soft + other[...]
+    soft = soft * to_column(GRAD_SCALE / tot[...])
+    hard = swap_rows(code[...] * to_column(GRAD_SCALE / total[...]))
+    out[...] = (soft - hard).astype(out.dtype)
+
+
+def view_grad_part(code, tot, total, *softs):
+    return pl.pallas_call(
+        view_grad_kernel,
+        in_specs=[WHOLE] * (3 + len(softs)),
+        out_specs=WHOLE,
+        out_shape=jax.ShapeDtypeStruct(code.shape, bf16),
+        compiler_params=params(),
+        cost_estimate=SMALL,
         name="view_grad",
-    )(protos, in_hbm(expo), scale, tot, total, *[in_hbm(x) for x in softs])
+    )(code, tot, total, *softs)
 
 
 def backward_kernel(grad_a, grad_b, pos, raw, pre, emb, hid_part, w_out, out):
@@ -575,13 +596,23 @@
     g_in = dot(emb[...], d_pre, TN)
     count = out.shape[0]
     tall, wide = g_in.shape[0] // count, g_in.shape[1]
+    base, short = tall * (wide // 128), g_out.shape[0] // count
     for k in range(count):
+        n = mirrored(k, count)
         for q in range(wide // 128):
-            out[k, q * tall : (q + 1) * tall, :] = g_in[
+            out[n, q * tall : (q + 1) * tall, :] = g_in[
                 k * tall : (k + 1) * tall, q * 128 : (q + 1) * 128
             ]
-        base, short = tall * (wide // 128), g_out.shape[0] // count
-        out[k, base : base + short, :] = g_out[k * short : (k + 1) * short]
+        out[n, base : base + short, :] = g_out[k * short : (k + 1) * short]
+
+
+def mirrored(k, count):
+    found = 0
+    while count > 1:
+        found = found * 2 + k % 2
+        k //= 2
+        count //= 2
+    return found
 
 
 def backward(nb, grad_a, grad_b, pos, raw, pre, emb, hid_part, w_out):
@@ -596,52 +627,33 @@
     )(grad_a, grad_b, pos, raw, pre, emb, hid_part, w_out)
 
 
-def unpack_kernel(order, place, *refs):
+def unpack_kernel(order, order_b, place, *refs):
     pieces, (g_in, g_out) = refs[:-2], refs[-2:]
-    nb = pieces[0].shape[1]
+    nb = len(order_b)
     npr = len(order)
     tall, wide = g_in.shape[0] // (nb * npr), g_in.shape[1]
     base, short = tall * (wide // 128), g_out.shape[0] // (nb * npr)
     half = pieces[0].shape[0]
     for n, flip in enumerate(order):
-        owner = place[0] ^ flip
-        for k in range(nb):
+        for k, flip_b in enumerate(order_b):
+            owner = (place[0] ^ flip) * nb + (place[1] ^ flip_b)
             x = pieces[n // half][n % half, k].astype(f32)
-            low = pl.multiple_of((owner * nb + k) * tall, tall)
+            low = pl.multiple_of(owner * tall, tall)
             for q in range(wide // 128):
                 g_in[pl.ds(low, tall), q * 128 : (q + 1) * 128] = x[q * tall : (q + 1) * tall]
-            low = pl.multiple_of((owner * nb + k) * short, short)
+            low = pl.multiple_of(owner * short, short)
             g_out[pl.ds(low, short), :] = x[base : base + short]
 
 
-def unpack(order, place, pieces, shape_in, shape_out):
-    return pl.pallas_call(
-        functools.partial(unpack_kernel, order),
+def unpack(order, order_b, place, pieces, shape_in, shape_out):
+    return pl.pallas_call(
+        functools.partial(unpack_kernel, order, order_b),
         in_specs=[pl.BlockSpec(memory_space=pltpu.SMEM)] + [WHOLE] * len(pieces),
         out_specs=[WHOLE] * 2,
         out_shape=[jax.ShapeDtypeStruct(shape_in, f32), jax.ShapeDtypeStruct(shape_out, f32)],
         compiler_params=params(),
         name="unpack",
     )(place, *pieces)
-
-
-def widen_kernel(x, out):
-    out[...] = x[...].astype(f32)
-
-
-def widen(x):
-    rows, depth = x.shape
-    block = min(1024, rows)
-    spec = pl.BlockSpec((block, depth), lambda i: (i, 0))
-    return pl.pallas_call(
-        widen_kernel,
-        grid=(rows // block,),
-        in_specs=[spec],
-        out_specs=spec,
-        out_shape=jax.ShapeDtypeStruct((rows, depth), f32),
-        compiler_params=params("arbitrary"),
-        name="widen",
-    )(in_hbm(x))
 
 
 def body(nb, npr, embeddings, pairing, w_in, w_out, prototypes):
@@ -670,10 +682,6 @@
             x = x + exchange(x, axis, size, step, queue, results)
             step *= 2
         return [x, exchange(x, axis, size, step, queue, results)]
-
-    def shared(x):
-        wide_x = jnp.broadcast_to(x, (nb,) + x.shape[1:])
-        return lax.all_to_all(wide_x, "batch", 0, 0, tiled=True)
 
     pre, hid, raw, views, views_t, pos = head(embeddings, pairing, w_in, w_out)
     views_all = lax.all_gather(views_t, "batch", axis=0)
@@ -706,10 +714,9 @@
         if step < nb:
             col = col + part
     scale, row = rowsum(expo, [col, part])
-    col = colsum(expo, doubled(row, "proto", npr, queue, softs))[0]
-    while queue:
-        work, operands = queue.pop(0)
-        softs.append(work(*operands))
+    units = []
+    queue = [(unit_transposed, (prototypes,))]
+    col = colsum(expo, doubled(row, "proto", npr, queue, units))[0]
 
     col, views_all = lax.optimization_barrier((col, views_all))
     each = nb // groups
@@ -721,13 +728,21 @@
         )
         for k in range(groups)
     ]
-    scale, row = rowsum_stream(expo, doubled(col, "batch", nb, queue, owns))
+    scale, row, code = rowsum_last(expo, doubled(col, "batch", nb, queue, owns), units[0])
     first, second = doubled(row, "proto", npr, queue, owns)
     total = first + second
     total_all = total[None]
+    grads = []
+    queue = [(view_grad_part, (code, tot, total, *softs))]
     step = 1
+    turn = 1
     while step < nb:
-        other = exchange(total_all, "batch", nb, step, queue, owns)
+        other = exchange(total_all, "batch", nb, step, queue, grads)
+        if step > 1 and turn < npr:
+            if len(grads) > 1:
+                grads = [(grads[0].astype(f32) + grads[1].astype(f32)).astype(bf16)]
+            grads = [grads[0], flipped(grads[0], "proto", npr, turn)]
+            turn *= 2
         total_all = jnp.concatenate([total_all, other], axis=0)
         step *= 2
 
@@ -742,19 +757,29 @@
     )
     grad_proto = lax.all_gather(proto_part, "batch", axis=0, tiled=True)
 
-    part = view_grad_part(prototypes, expo, scale, tot, total, softs)
-    step = 1
-    while step * 2 < npr:
-        other = flipped(part, "proto", npr, step)
-        part = (part.astype(f32) + other.astype(f32)).astype(bf16)
-        step *= 2
-    other = flipped(part, "proto", npr, step)
+    while turn < npr:
+        if len(grads) > 1:
+            grads = [(grads[0].astype(f32) + grads[1].astype(f32)).astype(bf16)]
+        grads = [grads[0], flipped(grads[0], "proto", npr, turn)]
+        turn *= 2
     emb_part = lax.dynamic_slice_in_dim(embeddings, p * (wide // npr), wide // npr, 1)
     hid_part = lax.dynamic_slice_in_dim(hid, p * (hidden_n // npr), hidden_n // npr, 1)
-    both = backward(nb, part, other, pos, raw, pre, emb_part, hid_part, w_out)
-    both = lax.all_to_all(both.astype(bf16), "batch", 0, 0, tiled=True)
-    both = jnp.sum(both.astype(f32), axis=0, keepdims=True).astype(bf16)
-    piece = shared(both)[None]
+    both = backward(nb, *grads, pos, raw, pre, emb_part, hid_part, w_out)
+    step = 1
+    while step < nb:
+        half = both.shape[0] // 2
+        bit = (b // step) % 2
+        away = lax.dynamic_slice_in_dim(both, (1 - bit) * half, half, 0).astype(bf16)
+        kept = lax.dynamic_slice_in_dim(both, bit * half, half, 0)
+        both = kept + flipped(away, "batch", nb, step).astype(f32)
+        step *= 2
+    piece = both.astype(bf16)
+    order_b = [0]
+    while step > 1:
+        step //= 2
+        piece = jnp.concatenate([piece, flipped(piece, "batch", nb, step)], axis=0)
+        order_b = order_b + [i ^ step for i in order_b]
+    piece = piece[None]
     order = [0]
     step = npr // 2
     while step > 1:
@@ -763,10 +788,11 @@
         step //= 2
     pieces = [piece, flipped(piece, "proto", npr, 1)]
     order = order + [i ^ 1 for i in order]
+    places = jnp.stack([p, b]).astype(jnp.int32)
     grad_in, grad_out = unpack(
-        order, p.astype(jnp.int32).reshape(1), pieces, (wide, hidden_n), (hidden_n, depth)
+        order, order_b, places, pieces, (wide, hidden_n), (hidden_n, depth)
     )
-    return (grad_in, grad_out, widen(grad_proto))
+    return (grad_in, grad_out, grad_proto.astype(f32))
 
 
 def solution(mesh):

time: 220 us -> 215 us (0.977)
  blocking collectives: 33.9 us -> 0 us
  waiting for transfers between devices: 38.3 us -> 61.6 us
  Pallas kernels: 96.9 us -> 89.7 us
  starting transfers between devices: 30.2 us -> 35.7 us
  other arithmetic: 0.6 us -> 4.59 us
  local copies, waits for them, and re-layouts: 5.36 us -> 8.48 us
    all_to_all x2 -> x0, blocking collectives: 33.9 us -> none  [the longest x1 21 us: body(): both = lax.all_to_all(both.astype(bf16), 'batch', 0, 0, tiled=True)]
    ppermute x25 -> x31, waiting for transfers between devices: 38.3 us -> 61.5 us  [flipped(): return lax.ppermute(x, axis, [(i, i ^ step) for i in range(size)])]
    pallas_call x4, Pallas kernels: 30.3 us -> 23.1 us  [the longest x1 16.5 us: rowsum_last(): pl.pallas_call(functools.partial(rowsum_last_kernel, pieces, len(parts)),...]
    ppermute x25 -> x31, starting transfers between devices: 30.1 us -> 35.6 us  [flipped(): return lax.ppermute(x, axis, [(i, i ^ step) for i in range(size)])]
    convert_element_type x2 -> x3, other arithmetic: 0.11 us -> 3.96 us  [the longest x1 3.87 us: body(): return (grad_in, grad_out, grad_proto.astype(f32))]
    unnamed x24 -> x34, local copies, waits for them, and re-layouts: 3.23 us -> 6.33 us
  transfers between devices with their start and end apart: 27 -> 33, of which waited for: 15 -> 20; matrix products, arithmetic and copies ran while one was open for 1% -> 1% of each run, Pallas kernels for 31% -> 31%
where the time goes in v5:
time: 215 us
  Pallas kernels  89.7 us (42%)
  waiting for transfers between devices  61.6 us (29%)
  starting transfers between devices  35.7 us (17%)
  between operations  14.5 us (7%)
  local copies, waits for them, and re-layouts  8.48 us (4%)
  other arithmetic  4.59 us (2%)
    ppermute x31, waiting for transfers between devices, flipped(): return lax.ppermute(x, axis, [(i, i ^ step) for i in range(size)])  61.5 us
    ppermute x31, starting transfers between devices, flipped(): return lax.ppermute(x, axis, [(i, i ^ step) for i in range(size)])  35.6 us
    pallas_call x1, Pallas kernels, rowsum_last(): pl.pallas_call(functools.partial(rowsum_last_kernel, pieces, len(parts)),...  16.5 us
    pallas_call x4, Pallas kernels, view_soft(): pl.pallas_call(functools.partial(view_soft_body, block, min(32, chunk), l...  14 us
    pallas_call x4, Pallas kernels, proto_first(): pl.pallas_call(functools.partial(proto_first_kernel, chunk, tile, lead),...  13 us
    pallas_call x1, Pallas kernels, first_pass(): pl.pallas_call(functools.partial(first_kernel, block, chunk, tile), in_sp...  11 us
    pallas_call x2, Pallas kernels, rowsum(): pl.pallas_call(functools.partial(rowsum_kernel, len(parts)), in_specs=[WH...  8.11 us
    pallas_call x1, Pallas kernels, head(): pl.pallas_call(head_kernel, grid=(steps,), in_specs=[pl.BlockSpec((block,...  7.26 us
  transfers between devices with their start and end apart: 33, of which 20 were waited for; matrix products, arithmetic and copies ran while one was open for 1% of the time, Pallas kernels for 31%

profile of v5, /device:TPU:0, one launch (start us, length us, event | category | flops | bytes accessed | tf_op | source)
XLA Modules:
  0.0 214.6 jit_solution(18172827008180843220)
XLA Ops:
  8.0 7.3 %head.1 = (f32[1024,512]{1,0:T(8,128)}, bf16[1024,512]{1,0:T(8,128)(2,1)}, f32[1024,128]{1,0:T(8,128)}, bf16[1024,128]{1,0:T(8,128)(2,1)S(1)}, bf16[128,1024]{1,0:T(8,128)(2,1)}, /*index=5*/s32[1,1024]{1,0:T(1,128)S(1)}) custom-call(bf16[1024,1024]{1,0:T(8,128)(2,1)} %emb.1, s32[1,1024]{1,0:T(1,128)S(1)} %bitcast.24, bf16[1024,512]{1,0:T(8,128)(2,1)} %w_in.1, ...), custom_call_target="tpu_custom_call" | custom-call | tf_op jit(solution)/shard_map/head/pallas_call | solution.py:107
  15.4 11.0 %first_pass.1 = (bf16[1024,8192]{1,0:T(8,128)(2,1)S(1)}, f32[1,8192]{1,0:T(1,128)S(1)}, f32[1,1024]{1,0:T(1,128)S(1)}) custom-call(bf16[1024,128]{1,0:T(8,128)(2,1)S(1)} %get-tuple-element.109.views.refs_0_, bf16[8192,128]{1,0:T(8,128)(2,1)S(1)} %copy-done.1), custom_call_target="tpu_custom_call" | custom-call | flops 1000 | bytes 1000 | tf_op jit(solution)/shard_map/first_pass/pallas_call | solution.py:192
  26.4 3.0 %collective-permute-start = (f32[1,8192]{1,0:T(1,128)S(1)}, f32[1,8192]{1,0:T(1,128)S(1)}, u32[]{:S(2)}, u32[]{:S(2)}) collective-permute-start(f32[1,8192]{1,0:T(1,128)S(1)} %get-tuple-element.97), channel_id=1, source_target_pairs={{0,4},{4,0},{8,12},{12,8},{16,20},{20,16},{24,28},{28,24},{1,5},{5... | collective-permute-start | bytes 98312 | tf_op jit(solution)/shard_map/ppermute | solution.py:668
  29.4 3.5 %view_soft.4.refs_0_ = f32[1024,128]{1,0:T(8,128)S(1)} custom-call(bf16[1024,128]{1,0:T(8,128)(2,1)S(1)} %get-tuple-element.109.views.refs_0_, bf16[8192,128]{1,0:T(8,128)(2,1)S(1)} %copy-done.1), custom_call_target="tpu_custom_call" | custom-call | flops 1000 | bytes 1000 | tf_op jit(solution)/shard_map/view_soft/pallas_call | solution.py:538
  33.0 1.7 collective-permute-start.1
  34.7 3.5 %view_soft.5.refs_1_ = f32[1024,128]{1,0:T(8,128)S(1)} custom-call(bf16[1024,128]{1,0:T(8,128)(2,1)S(1)} %get-tuple-element.109.views.refs_0_, bf16[8192,128]{1,0:T(8,128)(2,1)S(1)} %copy-done.1), custom_call_target="tpu_custom_call" | custom-call | flops 1000 | bytes 1000 | tf_op jit(solution)/shard_map/view_soft/pallas_call | solution.py:538
  38.4 2.5 %collective-permute-start.2 = (f32[1,8192]{1,0:T(1,128)S(1)}, f32[1,8192]{1,0:T(1,128)S(1)}, u32[]{:S(2)}, u32[]{:S(2)}) collective-permute-start(f32[1,8192]{1,0:T(1,128)S(1)} %add.88.refs_0_), channel_id=1, source_target_pairs={{0,16},{4,20},{8,24},{12,28},{16,0},{20,4},{24,8},{28,12},{1,17},{... | collective-permute-start | bytes 98312 | tf_op jit(solution)/shard_map/ppermute | solution.py:668
  40.9 3.5 %view_soft.6.refs_2_ = f32[1024,128]{1,0:T(8,128)S(1)} custom-call(bf16[1024,128]{1,0:T(8,128)(2,1)S(1)} %get-tuple-element.109.views.refs_0_, bf16[8192,128]{1,0:T(8,128)(2,1)S(1)} %copy-done.1), custom_call_target="tpu_custom_call" | custom-call | flops 1000 | bytes 1000 | tf_op jit(solution)/shard_map/view_soft/pallas_call | solution.py:538
  44.4 4.1 %rowsum.2 = (f32[1,8192]{1,0:T(1,128)}, f32[1,1024]{1,0:T(1,128)S(1)}) custom-call(bf16[1024,8192]{1,0:T(8,128)(2,1)S(1)} %get-tuple-element.96.expo.refs_0_.refs_1_.refs_2_.refs_3_, f32[1,8192]{1,0:T(1,128)S(1)} %add.88.refs_0_, f32[1,8192]{1,0:T(1,128)S(1)} %collective-permute-done.2.refs_1_), custom_call_target="tpu_custom_call" | custom-call | flops 1000 | bytes 1000 | tf_op jit(solution)/shard_map/rowsum/pallas_call | solution.py:266
  48.6 3.5 %view_soft.7.refs_3_ = f32[1024,128]{1,0:T(8,128)S(1)} custom-call(bf16[1024,128]{1,0:T(8,128)(2,1)S(1)} %get-tuple-element.109.views.refs_0_, bf16[8192,128]{1,0:T(8,128)(2,1)S(1)} %copy-done.1), custom_call_target="tpu_custom_call" | custom-call | flops 1000 | bytes 1000 | tf_op jit(solution)/shard_map/view_soft/pallas_call | solution.py:538
  52.1 1.6 collective-permute-start.4
  53.7 2.2 %collective-permute-done.4 = f32[2,1024]{1,0:T(2,128)S(1)} collective-permute-done((f32[2,1024]{1,0:T(2,128)S(1)}, f32[2,1024]{1,0:T(2,128)S(1)}, u32[]{:S(2)}, u32[]{:S(2)}) %collective-permute-start.4) | collective-permute-done | bytes 8224 | tf_op jit(solution)/shard_map/ppermute | solution.py:668
  55.9 2.2 %colsum.2 = f32[1,1,8192]{2,1,0:T(1,128)S(1)} custom-call(bf16[1024,8192]{1,0:T(8,128)(2,1)S(1)} %get-tuple-element.96.expo.refs_0_.refs_1_.refs_2_.refs_3_, f32[1,1024]{1,0:T(1,128)S(1)} %get-tuple-element.187.refs_0_), custom_call_target="tpu_custom_call" | custom-call | flops 1000 | bytes 1000 | tf_op jit(solution)/shard_map/colsum/pallas_call | solution.py:403
  60.2 2.1 collective-permute-done.5
  62.3 1.7 collective-permute-start.8
  64.5 3.5 %collective-permute-done.7 = f32[2,1,1024]{2,1,0:T(1,128)S(1)} collective-permute-done((f32[2,1,1024]{2,1,0:T(1,128)S(1)}, f32[2,1,1024]{2,1,0:T(1,128)S(1)}, u32[]{:S(2)}, u32[]{:S(2)}) %collective-permute-start.7) | collective-permute-done | bytes 8224 | tf_op jit(solution)/shard_map/ppermute | solution.py:668
  69.5 1.6 collective-permute-start.9
  71.1 3.1 %collective-permute-done.9 = f32[4,1,1024]{2,1,0:T(1,128)S(1)} collective-permute-done((f32[4,1,1024]{2,1,0:T(1,128)S(1)}, f32[4,1,1024]{2,1,0:T(1,128)S(1)}, u32[]{:S(2)}, u32[]{:S(2)}) %collective-permute-start.9) | collective-permute-done | bytes 16416 | tf_op jit(solution)/shard_map/ppermute | solution.py:668
  74.2 4.1 %rowsum.3 = (f32[1,8192]{1,0:T(1,128)}, f32[1,1024]{1,0:T(1,128)S(1)}) custom-call(bf16[1024,8192]{1,0:T(8,128)(2,1)S(1)} %get-tuple-element.96.expo.refs_0_.refs_1_.refs_2_.refs_3_, f32[1,8192]{1,0:T(1,128)S(1)} %add.92.refs_0_, f32[1,8192]{1,0:T(1,128)S(1)} %collective-permute-done.10.refs_1_), custom_call_target="tpu_custom_call" | custom-call | flops 1000 | bytes 1000 | tf_op jit(solution)/shard_map/rowsum/pallas_call | solution.py:266
  78.3 3.8 %unit_t.1.refs_6_ = bf16[128,8192]{1,0:T(8,128)(2,1)S(1)} custom-call(bf16[8192,128]{1,0:T(8,128)(2,1)S(1)} %copy-done.1), custom_call_target="tpu_custom_call" | custom-call | flops 1000 | bytes 1000 | tf_op jit(solution)/shard_map/unit_t/pallas_call | solution.py:359
  83.4 1.6 collective-permute-start.12
  84.9 2.1 collective-permute-done.12.refs_1_
  87.0 2.4 %colsum.3 = f32[1,1,8192]{2,1,0:T(1,128)S(1)} custom-call(bf16[1024,8192]{1,0:T(8,128)(2,1)S(1)} %get-tuple-element.96.expo.refs_0_.refs_1_.refs_2_.refs_3_, f32[1,1024]{1,0:T(1,128)S(1)} %add.93.refs_0_, f32[1,1024]{1,0:T(1,128)S(1)} %collective-permute-done.12.refs_1_), custom_call_target="tpu_custom_call" | custom-call | flops 1000 | bytes 1000 | tf_op jit(solution)/shard_map/colsum/pallas_call | solution.py:403
  90.3 1.6 copy-done.2
  91.8 3.3 %proto_first.4 = (bf16[1024,2048]{1,0:T(8,128)(2,1)S(1)}, f32[1024,128]{1,0:T(8,128)S(1)}) custom-call(s32[1]{0:T(128)} %bitcast.1.place, bf16[1024,128]{1,0:T(8,128)(2,1)S(1)} %constant_dynamic-slice_fusion.2.protos.refs_9_, bf16[8,128,1024]{2,1,0:T(8,128)(2,1)S(1)} %bitcast.12, f32[8,1,1024]{2,1,0:T(1,128)S(1)} %pad_maximum_fusion.3.totals), custom_call_target="tpu_custom_call" | custom-call | flops 1000 | bytes 1000 | tf_op jit(solution)/shard_map/proto_first/pallas_call | solution.py:447
  96.7 3.3 %proto_first.5 = (bf16[1024,2048]{1,0:T(8,128)(2,1)S(1)}, f32[1024,128]{1,0:T(8,128)S(1)}) custom-call(s32[1]{0:T(128)} %bitcast.1.place, bf16[1024,128]{1,0:T(8,128)(2,1)S(1)} %constant_dynamic-slice_fusion.2.protos.refs_9_, bf16[8,128,1024]{2,1,0:T(8,128)(2,1)S(1)} %bitcast.13, f32[8,1,1024]{2,1,0:T(1,128)S(1)} %pad_maximum_fusion.3.totals), custom_call_target="tpu_custom_call" | custom-call | flops 1000 | bytes 1000 | tf_op jit(solution)/shard_map/proto_first/pallas_call | solution.py:447
  101.2 3.3 %proto_first.6 = (bf16[1024,2048]{1,0:T(8,128)(2,1)S(1)}, f32[1024,128]{1,0:T(8,128)S(1)}) custom-call(s32[1]{0:T(128)} %bitcast.1.place, bf16[1024,128]{1,0:T(8,128)(2,1)S(1)} %constant_dynamic-slice_fusion.2.protos.refs_9_, bf16[8,128,1024]{2,1,0:T(8,128)(2,1)S(1)} %bitcast.14, f32[8,1,1024]{2,1,0:T(1,128)S(1)} %pad_maximum_fusion.3.totals), custom_call_target="tpu_custom_call" | custom-call | flops 1000 | bytes 1000 | tf_op jit(solution)/shard_map/proto_first/pallas_call | solution.py:447
  105.2 16.5 %rowsum_last.1 = (f32[1,8192]{1,0:T(1,128)S(1)}, f32[1,1024]{1,0:T(1,128)S(1)}, f32[1024,128]{1,0:T(8,128)S(1)}) custom-call(bf16[1024,8192]{1,0:T(8,128)(2,1)} %copy-done, bf16[1024,8192]{1,0:T(8,128)(2,1)} %copy-done, bf16[1024,8192]{1,0:T(8,128)(2,1)} %copy-done, bf16[1024,8192]{1,0:T(8,128)(2,1)} %copy-done, f32[1,8192]{1,0:T(1,128)S(1)} %add.95.refs_4_, ...), custom_call_target="tpu_custom_call" | custom-call | flops 1000 | bytes 1000 | tf_op jit(solution)/shard_map/rowsum_last/pallas_call | solution.py:328
  121.9 3.3 %proto_first.7 = (bf16[1024,2048]{1,0:T(8,128)(2,1)S(1)}, f32[1024,128]{1,0:T(8,128)S(1)}) custom-call(s32[1]{0:T(128)} %bitcast.1.place, bf16[1024,128]{1,0:T(8,128)(2,1)S(1)} %constant_dynamic-slice_fusion.2.protos.refs_9_, bf16[8,128,1024]{2,1,0:T(8,128)(2,1)S(1)} %bitcast.15, f32[8,1,1024]{2,1,0:T(1,128)S(1)} %pad_maximum_fusion.3.totals), custom_call_target="tpu_custom_call" | custom-call | flops 1000 | bytes 1000 | tf_op jit(solution)/shard_map/proto_first/pallas_call | solution.py:447
  125.2 1.5 collective-permute-start.17
  126.7 2.1 collective-permute-done.17
  133.0 3.2 %collective-permute-done.29 = f32[2,1,1024]{2,1,0:T(1,128)S(1)} collective-permute-done((f32[2,1,1024]{2,1,0:T(1,128)S(1)}, f32[2,1,1024]{2,1,0:T(1,128)S(1)}, u32[]{:S(2)}, u32[]{:S(2)}) %collective-permute-start.29) | collective-permute-done | bytes 8224 | tf_op jit(solution)/shard_map/ppermute | solution.py:668
  137.3 3.7 %collective-permute-done.30 = f32[4,1,1024]{2,1,0:T(1,128)S(1)} collective-permute-done((f32[4,1,1024]{2,1,0:T(1,128)S(1)}, f32[4,1,1024]{2,1,0:T(1,128)S(1)}, u32[]{:S(2)}, u32[]{:S(2)}) %collective-permute-start.30) | collective-permute-done | bytes 16416 | tf_op jit(solution)/shard_map/ppermute | solution.py:668
  141.0 5.4 %proto_last.1 = bf16[1024,128]{1,0:T(8,128)(2,1)} custom-call(s32[1]{0:T(128)} %bitcast.1.place, bf16[1024,2048]{1,0:T(8,128)(2,1)S(1)} %get-tuple-element.175.refs_0_, bf16[1024,2048]{1,0:T(8,128)(2,1)S(1)} %get-tuple-element.176.refs_1_, bf16[1024,2048]{1,0:T(8,128)(2,1)S(1)} %get-tuple-element.177.refs_2_, ...), custom_call_target="tpu_custom_call" | custom-call | tf_op jit(solution)/shard_map/proto_last/pallas_call | solution.py:497
  150.1 2.9 %collective-permute-done.20.grad_b = bf16[1024,128]{1,0:T(8,128)(2,1)S(1)} collective-permute-done((bf16[1024,128]{1,0:T(8,128)(2,1)S(1)}, bf16[1024,128]{1,0:T(8,128)(2,1)S(1)}, u32[]{:S(2)}, u32[]{:S(2)}) %collective-permute-start.20) | collective-permute-done | bytes 262176 | tf_op jit(solution)/shard_map/ppermute | solution.py:668
  155.6 3.3 %backward.1 = f32[8,144,128]{2,1,0:T(8,128)S(1)} custom-call(bf16[1024,128]{1,0:T(8,128)(2,1)S(1)} %add_convert_fusion.grad_a, bf16[1024,128]{1,0:T(8,128)(2,1)S(1)} %copy-done.15, s32[1,1024]{1,0:T(1,128)S(1)} %get-tuple-element.169.pos, f32[1024,128]{1,0:T(8,128)S(1)} %copy-done.12, f32[1024,512]{1,0:T(8,128)S(1)} %copy-done.5, ...), custom_call_target="tpu_custom_call" | custom-call | tf_op jit(solution)/shard_map/backward/pallas_call | solution.py:620
  160.4 3.7 %collective-permute-done.21 = bf16[4,144,128]{2,1,0:T(8,128)(2,1)S(1)} collective-permute-done((bf16[4,144,128]{2,1,0:T(8,128)(2,1)S(1)}, bf16[4,144,128]{2,1,0:T(8,128)(2,1)S(1)}, u32[]{:S(2)}, u32[]{:S(2)}) %collective-permute-start.21) | collective-permute-done | bytes 147488 | tf_op jit(solution)/shard_map/ppermute | solution.py:668
  164.6 4.3 %collective-permute-done.22 = bf16[2,144,128]{2,1,0:T(8,128)(2,1)S(1)} collective-permute-done((bf16[2,144,128]{2,1,0:T(8,128)(2,1)S(1)}, bf16[2,144,128]{2,1,0:T(8,128)(2,1)S(1)}, u32[]{:S(2)}, u32[]{:S(2)}) %collective-permute-start.22) | collective-permute-done | bytes 73760 | tf_op jit(solution)/shard_map/ppermute | solution.py:668
  169.0 1.7 collective-permute-start.23
  170.7 4.2 %collective-permute-done.23 = bf16[1,144,128]{2,1,0:T(8,128)(2,1)S(1)} collective-permute-done((bf16[1,144,128]{2,1,0:T(8,128)(2,1)S(1)}, bf16[1,144,128]{2,1,0:T(8,128)(2,1)S(1)}, u32[]{:S(2)}, u32[]{:S(2)}) %collective-permute-start.23) | collective-permute-done | bytes 36896 | tf_op jit(solution)/shard_map/ppermute | solution.py:668
  175.7 5.7 %collective-permute-done.24 = bf16[1,144,128]{2,1,0:T(8,128)(2,1)S(1)} collective-permute-done((bf16[1,144,128]{2,1,0:T(8,128)(2,1)S(1)}, bf16[1,144,128]{2,1,0:T(8,128)(2,1)S(1)}, u32[]{:S(2)}, u32[]{:S(2)}) %collective-permute-start.24) | collective-permute-done | bytes 36896 | tf_op jit(solution)/shard_map/ppermute | solution.py:668
  181.5 6.1 %collective-permute-done.25 = bf16[2,144,128]{2,1,0:T(8,128)(2,1)S(1)} collective-permute-done((bf16[2,144,128]{2,1,0:T(8,128)(2,1)S(1)}, bf16[2,144,128]{2,1,0:T(8,128)(2,1)S(1)}, u32[]{:S(2)}, u32[]{:S(2)}) %collective-permute-start.25) | collective-permute-done | bytes 73760 | tf_op jit(solution)/shard_map/ppermute | solution.py:668
  187.6 2.1 collective-permute-start.26
  189.7 3.1 %collective-permute-done.26 = bf16[4,144,128]{2,1,0:T(8,128)(2,1)S(1)} collective-permute-done((bf16[4,144,128]{2,1,0:T(8,128)(2,1)S(1)}, bf16[4,144,128]{2,1,0:T(8,128)(2,1)S(1)}, u32[]{:S(2)}, u32[]{:S(2)}) %collective-permute-start.26) | collective-permute-done | bytes 147488 | tf_op jit(solution)/shard_map/ppermute | solution.py:668
  194.3 5.3 %collective-permute-done.27 = bf16[1,8,144,128]{3,2,1,0:T(8,128)(2,1)S(1)} collective-permute-done((bf16[1,8,144,128]{3,2,1,0:T(8,128)(2,1)S(1)}, bf16[1,8,144,128]{3,2,1,0:T(8,128)(2,1)S(1)}, u32[]{:S(2)}, u32[]{:S(2)}) %collective-permute-start.27) | collective-permute-done | bytes 294944 | tf_op jit(solution)/shard_map/ppermute | solution.py:668
  199.9 1.9 collective-permute-done.28.refs_1_
  201.8 2.1 unpack.1
  203.9 3.9 %convert_element_type.43 = f32[8192,128]{1,0:T(8,128)} convert(bf16[8192,128]{1,0:T(8,128)(2,1)} %all-gather.4.cloned.1.call-done) | non-fusion elementwise | flops 1048576 | bytes 6291456 | tf_op jit(solution)/shard_map/convert_element_type | solution.py:795
  (109 shorter events, 27.5 us)
Async XLA Ops:
  7.2 8.2 %copy-start.1 = (bf16[8192,128]{1,0:T(8,128)(2,1)S(1)}, bf16[8192,128]{1,0:T(8,128)(2,1)}, u32[]{:S(2)}) copy-start(bf16[8192,128]{1,0:T(8,128)(2,1)} %protos.2) | copy-start | bytes 6291460
  7.2 82.3 %all-gather.6.cloned.1.call-start = ((), (), s32[]{:S(2)}) async-start(), calls=%async_computation.1 | async-start | bytes 2359296 | tf_op jit(solution)/shard_map/all_gather | solution.py:687
  15.3 188.5 %all-gather.4.cloned.1.call-start = ((), (), s32[]{:S(2)}) async-start(), calls=%async_computation | async-start | bytes 2359296 | tf_op jit(solution)/shard_map/all_gather | solution.py:758
  26.4 60.6 %copy-start = (bf16[1024,8192]{1,0:T(8,128)(2,1)}, bf16[1024,8192]{1,0:T(8,128)(2,1)S(1)}, u32[]{:S(2)}) copy-start(bf16[1024,8192]{1,0:T(8,128)(2,1)S(1)} %get-tuple-element.96.expo.refs_0_.refs_1_.refs_2_.refs_3_) | copy-start | bytes 50331652
  26.4 6.5 %collective-permute-start = (f32[1,8192]{1,0:T(1,128)S(1)}, f32[1,8192]{1,0:T(1,128)S(1)}, u32[]{:S(2)}, u32[]{:S(2)}) collective-permute-start(f32[1,8192]{1,0:T(1,128)S(1)} %get-tuple-element.97), channel_id=1, source_target_pairs={{0,4},{4,0},{8,12},{12,8},{16,20},{20,16},{24,28},{28,24},{1,5},{5... | collective-permute-start | bytes 98312 | tf_op jit(solution)/shard_map/ppermute | solution.py:668
  33.0 5.4 %collective-permute-start.1 = (f32[1,8192]{1,0:T(1,128)S(1)}, f32[1,8192]{1,0:T(1,128)S(1)}, u32[]{:S(2)}, u32[]{:S(2)}) collective-permute-start(f32[1,8192]{1,0:T(1,128)S(1)} %add.87), channel_id=1, source_target_pairs={{0,8},{4,12},{8,0},{12,4},{16,24},{20,28},{24,16},{28,20},{1,9},{5... | collective-permute-start | bytes 98312 | tf_op jit(solution)/shard_map/ppermute | solution.py:668
  38.2 10.3 %copy-start.6 = (f32[1024,128]{1,0:T(8,128)}, f32[1024,128]{1,0:T(8,128)S(1)}, u32[]{:S(2)}) copy-start(f32[1024,128]{1,0:T(8,128)S(1)} %view_soft.5.refs_1_) | copy-start | bytes 1572868
  38.4 6.0 %collective-permute-start.2 = (f32[1,8192]{1,0:T(1,128)S(1)}, f32[1,8192]{1,0:T(1,128)S(1)}, u32[]{:S(2)}, u32[]{:S(2)}) collective-permute-start(f32[1,8192]{1,0:T(1,128)S(1)} %add.88.refs_0_), channel_id=1, source_target_pairs={{0,16},{4,20},{8,24},{12,28},{16,0},{20,4},{24,8},{28,12},{1,17},{... | collective-permute-start | bytes 98312 | tf_op jit(solution)/shard_map/ppermute | solution.py:668
  44.4 4.1 %copy-start.8 = (f32[1024,128]{1,0:T(8,128)}, f32[1024,128]{1,0:T(8,128)S(1)}, u32[]{:S(2)}) copy-start(f32[1024,128]{1,0:T(8,128)S(1)} %view_soft.6.refs_2_) | copy-start | bytes 1572868
  48.5 3.6 %collective-permute-start.3 = (f32[2,1024]{1,0:T(2,128)S(1)}, f32[2,1024]{1,0:T(2,128)S(1)}, u32[]{:S(2)}, u32[]{:S(2)}) collective-permute-start(f32[2,1024]{1,0:T(2,128)S(1)} %pad_maximum_fusion.7), channel_id=1, source_target_pairs={{0,1},{1,0},{2,3},{3,2},{4,5},{5,4},{6,7},{7,6},{8,9},{9,8},{10,11... | collective-permute-start | bytes 24584 | tf_op jit(solution)/shard_map/ppermute | solution.py:668
  52.1 6.0 %copy-start.10 = (f32[1024,128]{1,0:T(8,128)}, f32[1024,128]{1,0:T(8,128)S(1)}, u32[]{:S(2)}) copy-start(f32[1024,128]{1,0:T(8,128)S(1)} %view_soft.7.refs_3_) | copy-start | bytes 1572868
  52.1 3.7 %collective-permute-start.4 = (f32[2,1024]{1,0:T(2,128)S(1)}, f32[2,1024]{1,0:T(2,128)S(1)}, u32[]{:S(2)}, u32[]{:S(2)}) collective-permute-start(f32[2,1024]{1,0:T(2,128)S(1)} %fusion), channel_id=1, source_target_pairs={{0,2},{1,3},{2,0},{3,1},{4,6},{5,7},{6,4},{7,5},{8,10},{9,11},{10,... | collective-permute-start | bytes 24584 | tf_op jit(solution)/shard_map/ppermute | solution.py:668
  58.1 4.2 %collective-permute-start.6 = (f32[1,8192]{1,0:T(1,128)S(1)}, f32[1,8192]{1,0:T(1,128)S(1)}, u32[]{:S(2)}, u32[]{:S(2)}) collective-permute-start(f32[1,8192]{1,0:T(1,128)S(1)} %bitcast.19), channel_id=1, source_target_pairs={{0,4},{4,0},{8,12},{12,8},{16,20},{20,16},{24,28},{28,24},{1,5},{5... | collective-permute-start | bytes 98312 | tf_op jit(solution)/shard_map/ppermute | solution.py:668
  58.7 3.6 %collective-permute-start.5 = (f32[1,1,1024]{2,1,0:T(1,128)S(1)}, f32[1,1,1024]{2,1,0:T(1,128)S(1)}, u32[]{:S(2)}, u32[]{:S(2)}) collective-permute-start(f32[1,1,1024]{2,1,0:T(1,128)S(1)} %get-tuple-element.186), channel_id=1, source_target_pairs={{0,4},{4,0},{8,12},{12,8},{16,20},{20,16},{24,28},{28,24},{1,5},{5... | collective-permute-start | bytes 12296 | tf_op jit(solution)/shard_map/ppermute | solution.py:668
  62.3 5.6 %collective-permute-start.8 = (f32[1,8192]{1,0:T(1,128)S(1)}, f32[1,8192]{1,0:T(1,128)S(1)}, u32[]{:S(2)}, u32[]{:S(2)}) collective-permute-start(f32[1,8192]{1,0:T(1,128)S(1)} %bitcast_add_fusion), channel_id=1, source_target_pairs={{0,8},{4,12},{8,0},{12,4},{16,24},{20,28},{24,16},{28,20},{1,9},{5... | collective-permute-start | bytes 98312 | tf_op jit(solution)/shard_map/ppermute | solution.py:668
  64.0 3.9 %collective-permute-start.7 = (f32[2,1,1024]{2,1,0:T(1,128)S(1)}, f32[2,1,1024]{2,1,0:T(1,128)S(1)}, u32[]{:S(2)}, u32[]{:S(2)}) collective-permute-start(f32[2,1,1024]{2,1,0:T(1,128)S(1)} %pad_maximum_fusion.8), channel_id=1, source_target_pairs={{0,8},{4,12},{8,0},{12,4},{16,24},{20,28},{24,16},{28,20},{1,9},{5... | collective-permute-start | bytes 24584 | tf_op jit(solution)/shard_map/ppermute | solution.py:668
  68.0 6.2 %collective-permute-start.10 = (f32[1,8192]{1,0:T(1,128)S(1)}, f32[1,8192]{1,0:T(1,128)S(1)}, u32[]{:S(2)}, u32[]{:S(2)}) collective-permute-start(f32[1,8192]{1,0:T(1,128)S(1)} %add.92.refs_0_), channel_id=1, source_target_pairs={{0,16},{4,20},{8,24},{12,28},{16,0},{20,4},{24,8},{28,12},{1,17},{... | collective-permute-start | bytes 98312 | tf_op jit(solution)/shard_map/ppermute | solution.py:668
  69.5 4.7 %collective-permute-start.9 = (f32[4,1,1024]{2,1,0:T(1,128)S(1)}, f32[4,1,1024]{2,1,0:T(1,128)S(1)}, u32[]{:S(2)}, u32[]{:S(2)}) collective-permute-start(f32[4,1,1024]{2,1,0:T(1,128)S(1)} %pad_maximum_fusion.5), channel_id=1, source_target_pairs={{0,16},{4,20},{8,24},{12,28},{16,0},{20,4},{24,8},{28,12},{1,17},{... | collective-permute-start | bytes 49160 | tf_op jit(solution)/shard_map/ppermute | solution.py:668
  78.3 5.1 %collective-permute-start.11 = (f32[1,1024]{1,0:T(1,128)S(1)}, f32[1,1024]{1,0:T(1,128)S(1)}, u32[]{:S(2)}, u32[]{:S(2)}) collective-permute-start(f32[1,1024]{1,0:T(1,128)S(1)} %get-tuple-element.117), channel_id=1, source_target_pairs={{0,1},{1,0},{2,3},{3,2},{4,5},{5,4},{6,7},{7,6},{8,9},{9,8},{10,11... | collective-permute-start | bytes 12296 | tf_op jit(solution)/shard_map/ppermute | solution.py:668
  82.0 1.3 copy-start.4
  83.4 3.7 %collective-permute-start.12 = (f32[1,1024]{1,0:T(1,128)S(1)}, f32[1,1024]{1,0:T(1,128)S(1)}, u32[]{:S(2)}, u32[]{:S(2)}) collective-permute-start(f32[1,1024]{1,0:T(1,128)S(1)} %add.93.refs_0_), channel_id=1, source_target_pairs={{0,2},{1,3},{2,0},{3,1},{4,6},{5,7},{6,4},{7,5},{8,10},{9,11},{10,... | collective-permute-start | bytes 12296 | tf_op jit(solution)/shard_map/ppermute | solution.py:668
  89.5 5.6 %collective-permute-start.13 = (f32[1,8192]{1,0:T(1,128)S(1)}, f32[1,8192]{1,0:T(1,128)S(1)}, u32[]{:S(2)}, u32[]{:S(2)}) collective-permute-start(f32[1,8192]{1,0:T(1,128)S(1)} %bitcast.17), channel_id=1, source_target_pairs={{0,4},{4,0},{8,12},{12,8},{16,20},{20,16},{24,28},{28,24},{1,5},{5... | collective-permute-start | bytes 98312 | tf_op jit(solution)/shard_map/ppermute | solution.py:668
  90.2 1.6 copy-start.2
  95.2 4.8 %collective-permute-start.14 = (f32[1,8192]{1,0:T(1,128)S(1)}, f32[1,8192]{1,0:T(1,128)S(1)}, u32[]{:S(2)}, u32[]{:S(2)}) collective-permute-start(f32[1,8192]{1,0:T(1,128)S(1)} %add.94), channel_id=1, source_target_pairs={{0,8},{4,12},{8,0},{12,4},{16,24},{20,28},{24,16},{28,20},{1,9},{5... | collective-permute-start | bytes 98312 | tf_op jit(solution)/shard_map/ppermute | solution.py:668
  100.0 5.2 %collective-permute-start.15 = (f32[1,8192]{1,0:T(1,128)S(1)}, f32[1,8192]{1,0:T(1,128)S(1)}, u32[]{:S(2)}, u32[]{:S(2)}) collective-permute-start(f32[1,8192]{1,0:T(1,128)S(1)} %add.95.refs_4_), channel_id=1, source_target_pairs={{0,16},{4,20},{8,24},{12,28},{16,0},{20,4},{24,8},{28,12},{1,17},{... | collective-permute-start | bytes 98312 | tf_op jit(solution)/shard_map/ppermute | solution.py:668
  105.2 16.7 %copy-start.3 = (bf16[1024,1024]{1,0:T(8,128)(2,1)S(1)}, bf16[1024,1024]{1,0:T(8,128)(2,1)}, u32[]{:S(2)}) copy-start(bf16[1024,1024]{1,0:T(8,128)(2,1)} %all-gather.6.cloned.1.call-done) | copy-start | bytes 6291460
  121.8 8.6 %copy-start.7 = (f32[1024,128]{1,0:T(8,128)S(1)}, f32[1024,128]{1,0:T(8,128)}, u32[]{:S(2)}) copy-start(f32[1024,128]{1,0:T(8,128)} %copy-done.6) | copy-start | bytes 1572868
  121.8 8.6 %copy-start.9 = (f32[1024,128]{1,0:T(8,128)S(1)}, f32[1024,128]{1,0:T(8,128)}, u32[]{:S(2)}) copy-start(f32[1024,128]{1,0:T(8,128)} %copy-done.8) | copy-start | bytes 1572868
  121.8 8.6 %copy-start.11 = (f32[1024,128]{1,0:T(8,128)S(1)}, f32[1024,128]{1,0:T(8,128)}, u32[]{:S(2)}) copy-start(f32[1024,128]{1,0:T(8,128)} %copy-done.10) | copy-start | bytes 1572868
  121.8 3.4 %collective-permute-start.16 = (f32[1,1024]{1,0:T(1,128)S(1)}, f32[1,1024]{1,0:T(1,128)S(1)}, u32[]{:S(2)}, u32[]{:S(2)}) collective-permute-start(f32[1,1024]{1,0:T(1,128)S(1)} %get-tuple-element.148), channel_id=1, source_target_pairs={{0,1},{1,0},{2,3},{3,2},{4,5},{5,4},{6,7},{7,6},{8,9},{9,8},{10,11... | collective-permute-start | bytes 12296 | tf_op jit(solution)/shard_map/ppermute | solution.py:668
  125.2 3.7 %collective-permute-start.17 = (f32[1,1024]{1,0:T(1,128)S(1)}, f32[1,1024]{1,0:T(1,128)S(1)}, u32[]{:S(2)}, u32[]{:S(2)}) collective-permute-start(f32[1,1024]{1,0:T(1,128)S(1)} %add.96), channel_id=1, source_target_pairs={{0,2},{1,3},{2,0},{3,1},{4,6},{5,7},{6,4},{7,5},{8,10},{9,11},{10,... | collective-permute-start | bytes 12296 | tf_op jit(solution)/shard_map/ppermute | solution.py:668
  128.9 3.6 %collective-permute-start.18 = (f32[1,1,1024]{2,1,0:T(1,128)S(1)}, f32[1,1,1024]{2,1,0:T(1,128)S(1)}, u32[]{:S(2)}, u32[]{:S(2)}) collective-permute-start(f32[1,1,1024]{2,1,0:T(1,128)S(1)} %bitcast.20), channel_id=1, source_target_pairs={{0,4},{4,0},{8,12},{12,8},{16,20},{20,16},{24,28},{28,24},{1,5},{5... | collective-permute-start | bytes 12296 | tf_op jit(solution)/shard_map/ppermute | solution.py:668
  132.5 3.7 %collective-permute-start.29 = (f32[2,1,1024]{2,1,0:T(1,128)S(1)}, f32[2,1,1024]{2,1,0:T(1,128)S(1)}, u32[]{:S(2)}, u32[]{:S(2)}) collective-permute-start(f32[2,1,1024]{2,1,0:T(1,128)S(1)} %pad_maximum_fusion.9), channel_id=1, source_target_pairs={{0,8},{4,12},{8,0},{12,4},{16,24},{20,28},{24,16},{28,20},{1,9},{5... | collective-permute-start | bytes 24584 | tf_op jit(solution)/shard_map/ppermute | solution.py:668
  136.2 4.8 %collective-permute-start.30 = (f32[4,1,1024]{2,1,0:T(1,128)S(1)}, f32[4,1,1024]{2,1,0:T(1,128)S(1)}, u32[]{:S(2)}, u32[]{:S(2)}) collective-permute-start(f32[4,1,1024]{2,1,0:T(1,128)S(1)} %pad_maximum_fusion.6), channel_id=1, source_target_pairs={{0,16},{4,20},{8,24},{12,28},{16,0},{20,4},{24,8},{28,12},{1,17},{... | collective-permute-start | bytes 49160 | tf_op jit(solution)/shard_map/ppermute | solution.py:668
  137.3 9.1 %collective-permute-start.19 = (bf16[1024,128]{1,0:T(8,128)(2,1)S(1)}, bf16[1024,128]{1,0:T(8,128)(2,1)S(1)}, u32[]{:S(2)}, u32[]{:S(2)}) collective-permute-start(bf16[1024,128]{1,0:T(8,128)(2,1)S(1)} %view_grad.1), channel_id=1, source_target_pairs={{0,1},{1,0},{2,3},{3,2},{4,5},{5,4},{6,7},{7,6},{8,9},{9,8},{10,11... | collective-permute-start | bytes 786440 | tf_op jit(solution)/shard_map/ppermute | solution.py:668
  146.4 7.3 %copy-start.5 = (f32[1024,512]{1,0:T(8,128)S(1)}, f32[1024,512]{1,0:T(8,128)}, u32[]{:S(2)}) copy-start(f32[1024,512]{1,0:T(8,128)} %get-tuple-element.171.pre) | copy-start | bytes 6291460
  146.4 7.3 %copy-start.12 = (f32[1024,128]{1,0:T(8,128)S(1)}, f32[1024,128]{1,0:T(8,128)}, u32[]{:S(2)}) copy-start(f32[1024,128]{1,0:T(8,128)} %get-tuple-element.170.raw) | copy-start | bytes 1572868
  146.5 6.4 %collective-permute-start.20 = (bf16[1024,128]{1,0:T(8,128)(2,1)S(1)}, bf16[1024,128]{1,0:T(8,128)(2,1)S(1)}, u32[]{:S(2)}, u32[]{:S(2)}) collective-permute-start(bf16[1024,128]{1,0:T(8,128)(2,1)S(1)} %add_convert_fusion.grad_a), channel_id=1, source_target_pairs={{0,2},{1,3},{2,0},{3,1},{4,6},{5,7},{6,4},{7,5},{8,10},{9,11},{10,... | collective-permute-start | bytes 786440 | tf_op jit(solution)/shard_map/ppermute | solution.py:668
  153.7 0.9 copy-start.13
  154.6 0.9 copy-start.15
  158.9 5.2 %collective-permute-start.21 = (bf16[4,144,128]{2,1,0:T(8,128)(2,1)S(1)}, bf16[4,144,128]{2,1,0:T(8,128)(2,1)S(1)}, u32[]{:S(2)}, u32[]{:S(2)}) collective-permute-start(bf16[4,144,128]{2,1,0:T(8,128)(2,1)S(1)} %dynamic-slice_convert_fusion), channel_id=1, source_target_pairs={{0,4},{4,0},{8,12},{12,8},{16,20},{20,16},{24,28},{28,24},{1,5},{5... | collective-permute-start | bytes 442376 | tf_op jit(solution)/shard_map/ppermute | solution.py:668
  164.2 4.8 %collective-permute-start.22 = (bf16[2,144,128]{2,1,0:T(8,128)(2,1)S(1)}, bf16[2,144,128]{2,1,0:T(8,128)(2,1)S(1)}, u32[]{:S(2)}, u32[]{:S(2)}) collective-permute-start(bf16[2,144,128]{2,1,0:T(8,128)(2,1)S(1)} %dynamic-slice_convert_fusion.1), channel_id=1, source_target_pairs={{0,8},{4,12},{8,0},{12,4},{16,24},{20,28},{24,16},{28,20},{1,9},{5... | collective-permute-start | bytes 221192 | tf_op jit(solution)/shard_map/ppermute | solution.py:668
  169.0 5.8 %collective-permute-start.23 = (bf16[1,144,128]{2,1,0:T(8,128)(2,1)S(1)}, bf16[1,144,128]{2,1,0:T(8,128)(2,1)S(1)}, u32[]{:S(2)}, u32[]{:S(2)}) collective-permute-start(bf16[1,144,128]{2,1,0:T(8,128)(2,1)S(1)} %dynamic-slice_convert_fusion.2), channel_id=1, source_target_pairs={{0,16},{4,20},{8,24},{12,28},{16,0},{20,4},{24,8},{28,12},{1,17},{... | collective-permute-start | bytes 110600 | tf_op jit(solution)/shard_map/ppermute | solution.py:668
  174.8 6.5 %collective-permute-start.24 = (bf16[1,144,128]{2,1,0:T(8,128)(2,1)S(1)}, bf16[1,144,128]{2,1,0:T(8,128)(2,1)S(1)}, u32[]{:S(2)}, u32[]{:S(2)}) collective-permute-start(bf16[1,144,128]{2,1,0:T(8,128)(2,1)S(1)} %add_convert_fusion.1), channel_id=1, source_target_pairs={{0,16},{4,20},{8,24},{12,28},{16,0},{20,4},{24,8},{28,12},{1,17},{... | collective-permute-start | bytes 110600 | tf_op jit(solution)/shard_map/ppermute | solution.py:668
  181.4 6.2 %collective-permute-start.25 = (bf16[2,144,128]{2,1,0:T(8,128)(2,1)S(1)}, bf16[2,144,128]{2,1,0:T(8,128)(2,1)S(1)}, u32[]{:S(2)}, u32[]{:S(2)}) collective-permute-start(bf16[2,144,128]{2,1,0:T(8,128)(2,1)S(1)} %pad_maximum_fusion.2), channel_id=1, source_target_pairs={{0,8},{4,12},{8,0},{12,4},{16,24},{20,28},{24,16},{28,20},{1,9},{5... | collective-permute-start | bytes 221192 | tf_op jit(solution)/shard_map/ppermute | solution.py:668
  187.6 5.3 %collective-permute-start.26 = (bf16[4,144,128]{2,1,0:T(8,128)(2,1)S(1)}, bf16[4,144,128]{2,1,0:T(8,128)(2,1)S(1)}, u32[]{:S(2)}, u32[]{:S(2)}) collective-permute-start(bf16[4,144,128]{2,1,0:T(8,128)(2,1)S(1)} %pad_maximum_fusion.1), channel_id=1, source_target_pairs={{0,4},{4,0},{8,12},{12,8},{16,20},{20,16},{24,28},{28,24},{1,5},{5... | collective-permute-start | bytes 442376 | tf_op jit(solution)/shard_map/ppermute | solution.py:668
  192.9 6.8 %collective-permute-start.27 = (bf16[1,8,144,128]{3,2,1,0:T(8,128)(2,1)S(1)}, bf16[1,8,144,128]{3,2,1,0:T(8,128)(2,1)S(1)}, u32[]{:S(2)}, u32[]{:S(2)}) collective-permute-start(bf16[1,8,144,128]{3,2,1,0:T(8,128)(2,1)S(1)} %maximum_bitcast_fusion), channel_id=1, source_target_pairs={{0,2},{1,3},{2,0},{3,1},{4,6},{5,7},{6,4},{7,5},{8,10},{9,11},{10,... | collective-permute-start | bytes 884744 | tf_op jit(solution)/shard_map/ppermute | solution.py:668
  199.7 2.1 collective-permute-start.28
  (2 other events, 1.5 us)
Sparse Core Ops, SparseCore 0:
  15.5 53.5 all-gather.5
  146.6 51.0 all-gather.3

commit v6 on v5

--- a/solution.py
+++ b/solution.py
@@ -33,10 +33,8 @@
 SMALL = pl.CostEstimate(flops=1000, bytes_accessed=1000, transcendentals=0)
 
 
-def params(*semantics):
-    return pltpu.CompilerParams(
-        dimension_semantics=semantics or None, vmem_limit_bytes=VMEM_LIMIT
-    )
+def params(*semantics, limit=VMEM_LIMIT):
+    return pltpu.CompilerParams(dimension_semantics=semantics or None, vmem_limit_bytes=limit)
 
 
 def to_column(vec):
@@ -293,23 +291,20 @@
     unit_t, scale, out, code, acc = refs[pieces + count :]
     step = pl.program_id(0)
     depth, block = unit_t.shape
-    tall = expos[0].shape[0]
+    deep = expos[0].shape[1]
     inverse = 1.0 / sum_parts(parts, block)
     scale[...] = inverse
-    scaled = unit_t[...].astype(f32) * inverse
-    pad = jnp.zeros((depth - 8, block), f32)
-    weights = jnp.concatenate([scaled, split_rows(inverse), pad], axis=0).astype(bf16)
+
+    @pl.when(step == 0)
+    def _():
+        acc[...] = jnp.zeros_like(acc)
+
     for k in range(pieces):
-        part = slice(k * tall, (k + 1) * tall)
-        found = dot(expos[k][...], weights, NT)
-
-        @pl.when(step == 0)
-        def _():
-            acc[part, :] = found
-
-        @pl.when(step > 0)
-        def _():
-            acc[part, :] += found
+        here = slice(k * deep, (k + 1) * deep)
+        scaled = unit_t[:, here].astype(f32) * inverse[:, here]
+        pad = jnp.zeros((depth - 8, deep), f32)
+        weights = jnp.concatenate([scaled, split_rows(inverse[:, here]), pad], axis=0)
+        acc[...] += dot(expos[k][...], weights.astype(bf16), NT)
 
     @pl.when(step == pl.num_programs(0) - 1)
     def _():
@@ -321,14 +316,16 @@
 def rowsum_last(expo, parts, unit_t):
     rows, width = expo.shape
     depth = unit_t.shape[0]
-    block = min(1024, width)
+    block = min(2048, width)
     pieces = 4
-    tall = rows // pieces
+    deep = block // pieces
     vec = pl.BlockSpec((1, block), lambda j: (0, j))
     return pl.pallas_call(
         functools.partial(rowsum_last_kernel, pieces, len(parts)),
         grid=(width // block,),
-        in_specs=[pl.BlockSpec((tall, block), lambda j, k=k: (k, j)) for k in range(pieces)]
+        in_specs=[
+            pl.BlockSpec((rows, deep), lambda j, k=k: (0, j * pieces + k)) for k in range(pieces)
+        ]
         + [vec] * len(parts)
         + [pl.BlockSpec((depth, block), lambda j: (0, j))],
         out_specs=[vec, full((1, rows)), full((rows, depth))],
@@ -338,7 +335,7 @@
             jax.ShapeDtypeStruct((rows, depth), f32),
         ],
         scratch_shapes=[pltpu.VMEM((rows, 2 * depth), f32)],
-        compiler_params=params("arbitrary"),
+        compiler_params=params("arbitrary", limit=VMEM_LIMIT + 4 * 1024 * 1024),
         cost_estimate=SMALL,
         name="rowsum_last",
     )(*[in_hbm(expo)] * pieces, *parts, in_hbm(unit_t))
@@ -562,15 +559,17 @@
 
 
 def view_grad_part(code, tot, total, *softs):
+    operands = [code, tot, total, *softs]
     return pl.pallas_call(
         view_grad_kernel,
-        in_specs=[WHOLE] * (3 + len(softs)),
-        out_specs=WHOLE,
+        grid=(1,),
+        in_specs=[full(x.shape) for x in operands],
+        out_specs=full(code.shape),
         out_shape=jax.ShapeDtypeStruct(code.shape, bf16),
-        compiler_params=params(),
+        compiler_params=params("arbitrary"),
         cost_estimate=SMALL,
         name="view_grad",
-    )(code, tot, total, *softs)
+    )(code, tot, total, *[in_hbm(x) for x in softs])
 
 
 def backward_kernel(grad_a, grad_b, pos, raw, pre, emb, hid_part, w_out, out):
@@ -617,14 +616,16 @@
 
 def backward(nb, grad_a, grad_b, pos, raw, pre, emb, hid_part, w_out):
     lines = (emb.shape[1] * pre.shape[1] + hid_part.shape[1] * raw.shape[1]) // (nb * 128)
+    operands = [grad_a, grad_b, pos, raw, pre, emb, hid_part, w_out]
     return pl.pallas_call(
         backward_kernel,
-        in_specs=[WHOLE] * 8,
-        out_specs=WHOLE,
+        grid=(1,),
+        in_specs=[full(x.shape) for x in operands],
+        out_specs=full((nb, lines, 128)),
         out_shape=jax.ShapeDtypeStruct((nb, lines, 128), f32),
-        compiler_params=params(),
+        compiler_params=params("arbitrary"),
         name="backward",
-    )(grad_a, grad_b, pos, raw, pre, emb, hid_part, w_out)
+    )(grad_a, grad_b, pos, *[in_hbm(x) for x in operands[3:]])
 
 
 def unpack_kernel(order, order_b, place, *refs):
@@ -687,7 +688,11 @@
     views_all = lax.all_gather(views_t, "batch", axis=0)
     protos_own = lax.dynamic_slice_in_dim(prototypes, b * own, own, 0)
     place = b.astype(jnp.int32).reshape(1)
-    views, protos_own, place = lax.optimization_barrier((views, protos_own, place))
+    at_in = (p * (wide // npr)).astype(jnp.uint32)
+    at_out = (p * (hidden_n // npr)).astype(jnp.uint32)
+    views, protos_own, place, at_in, at_out = lax.optimization_barrier(
+        (views, protos_own, place, at_in, at_out)
+    )
     expo, col, tot = first_pass(views, prototypes)
 
     groups = 4
@@ -702,21 +707,29 @@
     both = first + second
     totals, tot = [both[:1]], both[1:]
 
+    def slices(embeddings, hid):
+        none = jnp.uint32(0)
+        return (
+            lax.dynamic_slice(embeddings, (none, at_in), (rows, wide // npr)),
+            lax.dynamic_slice(hid, (none, at_out), (rows, hidden_n // npr)),
+        )
+
+    taken = []
+    queue = [(unit_transposed, (prototypes,)), (slices, (embeddings, hid))]
     col = colsum(expo, totals)[0]
     tot_all = tot[None]
     step = 1
     while step < nb:
         other = flipped(tot_all, "batch", nb, step)
-        part = flipped(col, "batch", nb, step)
+        part = exchange(col, "batch", nb, step, queue, taken)
         other, part = lax.optimization_barrier((other, part))
         tot_all = jnp.concatenate([tot_all, other], axis=0)
         step *= 2
         if step < nb:
             col = col + part
+    unit_t, (emb_part, hid_part) = taken
     scale, row = rowsum(expo, [col, part])
-    units = []
-    queue = [(unit_transposed, (prototypes,))]
-    col = colsum(expo, doubled(row, "proto", npr, queue, units))[0]
+    col = colsum(expo, doubled(row, "proto", npr))[0]
 
     col, views_all = lax.optimization_barrier((col, views_all))
     each = nb // groups
@@ -728,7 +741,7 @@
         )
         for k in range(groups)
     ]
-    scale, row, code = rowsum_last(expo, doubled(col, "batch", nb, queue, owns), units[0])
+    scale, row, code = rowsum_last(expo, doubled(col, "batch", nb, queue, owns), unit_t)
     first, second = doubled(row, "proto", npr, queue, owns)
     total = first + second
     total_all = total[None]
@@ -738,32 +751,22 @@
     turn = 1
     while step < nb:
         other = exchange(total_all, "batch", nb, step, queue, grads)
-        if step > 1 and turn < npr:
-            if len(grads) > 1:
-                grads = [(grads[0].astype(f32) + grads[1].astype(f32)).astype(bf16)]
+        if len(grads) > 1:
+            grads = [(grads[0].astype(f32) + grads[1].astype(f32)).astype(bf16)]
+            other, grads[0] = lax.optimization_barrier((other, grads[0]))
+        if turn * 2 < npr:
             grads = [grads[0], flipped(grads[0], "proto", npr, turn)]
             turn *= 2
         total_all = jnp.concatenate([total_all, other], axis=0)
         step *= 2
 
-    proto_part = proto_last(
-        place,
-        [x for x, _ in owns],
-        [x for _, x in owns],
-        scale,
-        protos_own,
-        views_all,
-        total_all,
-    )
-    grad_proto = lax.all_gather(proto_part, "batch", axis=0, tiled=True)
-
-    while turn < npr:
-        if len(grads) > 1:
-            grads = [(grads[0].astype(f32) + grads[1].astype(f32)).astype(bf16)]
-        grads = [grads[0], flipped(grads[0], "proto", npr, turn)]
-        turn *= 2
-    emb_part = lax.dynamic_slice_in_dim(embeddings, p * (wide // npr), wide // npr, 1)
-    hid_part = lax.dynamic_slice_in_dim(hid, p * (hidden_n // npr), hidden_n // npr, 1)
+    if len(grads) > 1:
+        grads = [(grads[0].astype(f32) + grads[1].astype(f32)).astype(bf16)]
+    expos, parts = [x for x, _ in owns], [x for _, x in owns]
+    queue = [(proto_last, (place, expos, parts, scale, protos_own, views_all, total_all))]
+    found = []
+    grads = [grads[0], exchange(grads[0], "proto", npr, npr // 2, queue, found)]
+    grad_proto = lax.all_gather(found[0], "batch", axis=0, tiled=True)
     both = backward(nb, *grads, pos, raw, pre, emb_part, hid_part, w_out)
     step = 1
     while step < nb:

time: 215 us -> 204 us (0.949)
  starting transfers between devices: 35.7 us -> 31.5 us
  Pallas kernels: 89.7 us -> 86 us
    pallas_call x1, Pallas kernels: 16.5 us -> 9.45 us  [rowsum_last(): pl.pallas_call(functools.partial(rowsum_last_kernel, pieces, len(parts)),...]
    ppermute x31, starting transfers between devices: 35.6 us -> 31.5 us  [flipped(): return lax.ppermute(x, axis, [(i, i ^ step) for i in range(size)])]
    pallas_call x2, Pallas kernels: 4.01 us -> 7.39 us  [the longest x1 5.17 us: backward(): pl.pallas_call(backward_kernel, grid=(1,), in_specs=[full(x.shape) for x...]
    unnamed x34 -> x20, local copies, waits for them, and re-layouts: 6.33 us -> 3.23 us
  transfers between devices with their start and end apart: 33 -> 33, of which waited for: 20 -> 19; matrix products, arithmetic and copies ran while one was open for 1% -> 2% of each run, Pallas kernels for 31% -> 34%
where the time goes in v6:
time: 204 us
  Pallas kernels  86 us (42%)
  waiting for transfers between devices  60.1 us (29%)
  starting transfers between devices  31.5 us (15%)
  between operations  14.5 us (7%)
  local copies, waits for them, and re-layouts  7.39 us (4%)
  other arithmetic  4.59 us (2%)
    ppermute x31, waiting for transfers between devices, flipped(): return lax.ppermute(x, axis, [(i, i ^ step) for i in range(size)])  60 us
    ppermute x31, starting transfers between devices, flipped(): return lax.ppermute(x, axis, [(i, i ^ step) for i in range(size)])  31.5 us
    pallas_call x4, Pallas kernels, view_soft(): pl.pallas_call(functools.partial(view_soft_body, block, min(32, chunk), l...  13.9 us
    pallas_call x4, Pallas kernels, proto_first(): pl.pallas_call(functools.partial(proto_first_kernel, chunk, tile, lead),...  13 us
    pallas_call x1, Pallas kernels, first_pass(): pl.pallas_call(functools.partial(first_kernel, block, chunk, tile), in_sp...  11 us
    pallas_call x1, Pallas kernels, rowsum_last(): pl.pallas_call(functools.partial(rowsum_last_kernel, pieces, len(parts)),...  9.45 us
    pallas_call x2, Pallas kernels, rowsum(): pl.pallas_call(functools.partial(rowsum_kernel, len(parts)), in_specs=[WH...  8.1 us
    pallas_call x1, Pallas kernels, head(): pl.pallas_call(head_kernel, grid=(steps,), in_specs=[pl.BlockSpec((block,...  7.26 us
  transfers between devices with their start and end apart: 33, of which 19 were waited for; matrix products, arithmetic and copies ran while one was open for 2% of the time, Pallas kernels for 34%

profile of v6, /device:TPU:0, one launch (start us, length us, event | category | flops | bytes accessed | tf_op | source)
XLA Modules:
  0.0 204.1 jit_solution(16352592106066809854)
XLA Ops:
  8.0 7.3 %head.1 = (f32[1024,512]{1,0:T(8,128)}, bf16[1024,512]{1,0:T(8,128)(2,1)}, f32[1024,128]{1,0:T(8,128)}, bf16[1024,128]{1,0:T(8,128)(2,1)S(1)}, bf16[128,1024]{1,0:T(8,128)(2,1)}, /*index=5*/s32[1,1024]{1,0:T(1,128)S(1)}) custom-call(bf16[1024,1024]{1,0:T(8,128)(2,1)} %emb.1, s32[1,1024]{1,0:T(1,128)S(1)} %bitcast.24, bf16[1024,512]{1,0:T(8,128)(2,1)} %w_in.1, ...), custom_call_target="tpu_custom_call" | custom-call | tf_op jit(solution)/shard_map/head/pallas_call | solution.py:105
  15.4 11.0 %first_pass.1 = (bf16[1024,8192]{1,0:T(8,128)(2,1)S(1)}, f32[1,8192]{1,0:T(1,128)S(1)}, f32[1,1024]{1,0:T(1,128)S(1)}) custom-call(bf16[1024,128]{1,0:T(8,128)(2,1)S(1)} %get-tuple-element.133.views.refs_0_, bf16[8192,128]{1,0:T(8,128)(2,1)S(1)} %copy-done.1), custom_call_target="tpu_custom_call" | custom-call | flops 1000 | bytes 1000 | tf_op jit(solution)/shard_map/first_pass/pallas_call | solution.py:190
  26.5 3.0 %collective-permute-start = (f32[1,8192]{1,0:T(1,128)S(1)}, f32[1,8192]{1,0:T(1,128)S(1)}, u32[]{:S(2)}, u32[]{:S(2)}) collective-permute-start(f32[1,8192]{1,0:T(1,128)S(1)} %get-tuple-element.121), channel_id=1, source_target_pairs={{0,4},{4,0},{8,12},{12,8},{16,20},{20,16},{24,28},{28,24},{1,5},{5... | collective-permute-start | bytes 98312 | tf_op jit(solution)/shard_map/ppermute | solution.py:669
  29.5 3.5 %view_soft.4.refs_0_ = f32[1024,128]{1,0:T(8,128)S(1)} custom-call(bf16[1024,128]{1,0:T(8,128)(2,1)S(1)} %get-tuple-element.133.views.refs_0_, bf16[8192,128]{1,0:T(8,128)(2,1)S(1)} %copy-done.1), custom_call_target="tpu_custom_call" | custom-call | flops 1000 | bytes 1000 | tf_op jit(solution)/shard_map/view_soft/pallas_call | solution.py:535
  33.8 1.6 collective-permute-start.1
  35.5 3.5 %view_soft.5.refs_1_ = f32[1024,128]{1,0:T(8,128)S(1)} custom-call(bf16[1024,128]{1,0:T(8,128)(2,1)S(1)} %get-tuple-element.133.views.refs_0_, bf16[8192,128]{1,0:T(8,128)(2,1)S(1)} %copy-done.1), custom_call_target="tpu_custom_call" | custom-call | flops 1000 | bytes 1000 | tf_op jit(solution)/shard_map/view_soft/pallas_call | solution.py:535
  39.0 2.7 %collective-permute-start.2 = (f32[1,8192]{1,0:T(1,128)S(1)}, f32[1,8192]{1,0:T(1,128)S(1)}, u32[]{:S(2)}, u32[]{:S(2)}) collective-permute-start(f32[1,8192]{1,0:T(1,128)S(1)} %add.82.refs_0_), channel_id=1, source_target_pairs={{0,16},{4,20},{8,24},{12,28},{16,0},{20,4},{24,8},{28,12},{1,17},{... | collective-permute-start | bytes 98312 | tf_op jit(solution)/shard_map/ppermute | solution.py:669
  41.7 3.5 %view_soft.6.refs_2_ = f32[1024,128]{1,0:T(8,128)S(1)} custom-call(bf16[1024,128]{1,0:T(8,128)(2,1)S(1)} %get-tuple-element.133.views.refs_0_, bf16[8192,128]{1,0:T(8,128)(2,1)S(1)} %copy-done.1), custom_call_target="tpu_custom_call" | custom-call | flops 1000 | bytes 1000 | tf_op jit(solution)/shard_map/view_soft/pallas_call | solution.py:535
  45.2 4.1 %rowsum.2 = (f32[1,8192]{1,0:T(1,128)}, f32[1,1024]{1,0:T(1,128)S(1)}) custom-call(bf16[1024,8192]{1,0:T(8,128)(2,1)S(1)} %get-tuple-element.120.expo.refs_0_.refs_1_.refs_2_.refs_3_, f32[1,8192]{1,0:T(1,128)S(1)} %add.82.refs_0_, f32[1,8192]{1,0:T(1,128)S(1)} %collective-permute-done.2.refs_1_), custom_call_target="tpu_custom_call" | custom-call | flops 1000 | bytes 1000 | tf_op jit(solution)/shard_map/rowsum/pallas_call | solution.py:264
  49.3 3.5 %view_soft.7.refs_3_ = f32[1024,128]{1,0:T(8,128)S(1)} custom-call(bf16[1024,128]{1,0:T(8,128)(2,1)S(1)} %get-tuple-element.133.views.refs_0_, bf16[8192,128]{1,0:T(8,128)(2,1)S(1)} %copy-done.1), custom_call_target="tpu_custom_call" | custom-call | flops 1000 | bytes 1000 | tf_op jit(solution)/shard_map/view_soft/pallas_call | solution.py:535
  52.9 1.5 collective-permute-start.4
  54.4 2.2 %collective-permute-done.4 = f32[2,1024]{1,0:T(2,128)S(1)} collective-permute-done((f32[2,1024]{1,0:T(2,128)S(1)}, f32[2,1024]{1,0:T(2,128)S(1)}, u32[]{:S(2)}, u32[]{:S(2)}) %collective-permute-start.4) | collective-permute-done | bytes 8224 | tf_op jit(solution)/shard_map/ppermute | solution.py:669
  56.6 2.2 %colsum.2 = f32[1,1,8192]{2,1,0:T(1,128)S(1)} custom-call(bf16[1024,8192]{1,0:T(8,128)(2,1)S(1)} %get-tuple-element.120.expo.refs_0_.refs_1_.refs_2_.refs_3_, f32[1,1024]{1,0:T(1,128)S(1)} %get-tuple-element.235.refs_0_), custom_call_target="tpu_custom_call" | custom-call | flops 1000 | bytes 1000 | tf_op jit(solution)/shard_map/colsum/pallas_call | solution.py:400
  60.9 3.7 %unit_t.1.refs_6_ = bf16[128,8192]{1,0:T(8,128)(2,1)S(1)} custom-call(bf16[8192,128]{1,0:T(8,128)(2,1)S(1)} %copy-done.1), custom_call_target="tpu_custom_call" | custom-call | flops 1000 | bytes 1000 | tf_op jit(solution)/shard_map/unit_t/pallas_call | solution.py:356
  65.5 1.5 collective-permute-start.7
  66.9 2.2 %constant_dynamic-slice_fusion.2.emb = bf16[1024,256]{1,0:T(8,128)(2,1)} fusion(bf16[1024,1024]{1,0:T(8,128)(2,1)} %emb.1, u32[]{:T(128)S(6)} %convert_element_type.39), kind=kLoop, calls=%fused_computation.20 | loop fusion | bytes 1048580 | tf_op jit(solution)/shard_map/dynamic_slice | solution.py:713
  69.1 1.9 constant_dynamic-slice_fusion.1.hid_part
  72.4 1.7 collective-permute-start.9
  74.1 3.2 %collective-permute-done.9 = f32[4,1,1024]{2,1,0:T(1,128)S(1)} collective-permute-done((f32[4,1,1024]{2,1,0:T(1,128)S(1)}, f32[4,1,1024]{2,1,0:T(1,128)S(1)}, u32[]{:S(2)}, u32[]{:S(2)}) %collective-permute-start.9) | collective-permute-done | bytes 16416 | tf_op jit(solution)/shard_map/ppermute | solution.py:669
  77.3 4.0 %rowsum.3 = (f32[1,8192]{1,0:T(1,128)}, f32[1,1024]{1,0:T(1,128)S(1)}) custom-call(bf16[1024,8192]{1,0:T(8,128)(2,1)S(1)} %get-tuple-element.120.expo.refs_0_.refs_1_.refs_2_.refs_3_, f32[1,8192]{1,0:T(1,128)S(1)} %add.86.refs_0_, f32[1,8192]{1,0:T(1,128)S(1)} %collective-permute-done.10.refs_1_), custom_call_target="tpu_custom_call" | custom-call | flops 1000 | bytes 1000 | tf_op jit(solution)/shard_map/rowsum/pallas_call | solution.py:264
  83.9 2.3 %collective-permute-done.12.refs_1_ = f32[1,1024]{1,0:T(1,128)S(1)} collective-permute-done((f32[1,1024]{1,0:T(1,128)S(1)}, f32[1,1024]{1,0:T(1,128)S(1)}, u32[]{:S(2)}, u32[]{:S(2)}) %collective-permute-start.12) | collective-permute-done | bytes 4128 | tf_op jit(solution)/shard_map/ppermute | solution.py:669
  86.2 2.4 %colsum.3 = f32[1,1,8192]{2,1,0:T(1,128)S(1)} custom-call(bf16[1024,8192]{1,0:T(8,128)(2,1)S(1)} %get-tuple-element.120.expo.refs_0_.refs_1_.refs_2_.refs_3_, f32[1,1024]{1,0:T(1,128)S(1)} %add.87.refs_0_, f32[1,1024]{1,0:T(1,128)S(1)} %collective-permute-done.12.refs_1_), custom_call_target="tpu_custom_call" | custom-call | flops 1000 | bytes 1000 | tf_op jit(solution)/shard_map/colsum/pallas_call | solution.py:400
  89.9 1.6 copy-done.2
  91.5 3.3 %proto_first.4 = (bf16[1024,2048]{1,0:T(8,128)(2,1)S(1)}, f32[1024,128]{1,0:T(8,128)S(1)}) custom-call(s32[1]{0:T(128)} %bitcast.1.place, bf16[1024,128]{1,0:T(8,128)(2,1)S(1)} %constant_dynamic-slice_fusion.protos.refs_9_, bf16[8,128,1024]{2,1,0:T(8,128)(2,1)S(1)} %bitcast.12, f32[8,1,1024]{2,1,0:T(1,128)S(1)} %pad_maximum_fusion.3.totals), custom_call_target="tpu_custom_call" | custom-call | flops 1000 | bytes 1000 | tf_op jit(solution)/shard_map/proto_first/pallas_call | solution.py:444
  95.2 3.3 %proto_first.5 = (bf16[1024,2048]{1,0:T(8,128)(2,1)S(1)}, f32[1024,128]{1,0:T(8,128)S(1)}) custom-call(s32[1]{0:T(128)} %bitcast.1.place, bf16[1024,128]{1,0:T(8,128)(2,1)S(1)} %constant_dynamic-slice_fusion.protos.refs_9_, bf16[8,128,1024]{2,1,0:T(8,128)(2,1)S(1)} %bitcast.13, f32[8,1,1024]{2,1,0:T(1,128)S(1)} %pad_maximum_fusion.3.totals), custom_call_target="tpu_custom_call" | custom-call | flops 1000 | bytes 1000 | tf_op jit(solution)/shard_map/proto_first/pallas_call | solution.py:444
  98.8 1.6 collective-permute-start.15
  100.4 3.3 %proto_first.6 = (bf16[1024,2048]{1,0:T(8,128)(2,1)S(1)}, f32[1024,128]{1,0:T(8,128)S(1)}) custom-call(s32[1]{0:T(128)} %bitcast.1.place, bf16[1024,128]{1,0:T(8,128)(2,1)S(1)} %constant_dynamic-slice_fusion.protos.refs_9_, bf16[8,128,1024]{2,1,0:T(8,128)(2,1)S(1)} %bitcast.14, f32[8,1,1024]{2,1,0:T(1,128)S(1)} %pad_maximum_fusion.3.totals), custom_call_target="tpu_custom_call" | custom-call | flops 1000 | bytes 1000 | tf_op jit(solution)/shard_map/proto_first/pallas_call | solution.py:444
  103.7 9.5 %rowsum_last.1 = (f32[1,8192]{1,0:T(1,128)S(1)}, f32[1,1024]{1,0:T(1,128)S(1)}, f32[1024,128]{1,0:T(8,128)S(1)}) custom-call(bf16[1024,8192]{1,0:T(8,128)(2,1)} %copy-done, bf16[1024,8192]{1,0:T(8,128)(2,1)} %copy-done, bf16[1024,8192]{1,0:T(8,128)(2,1)} %copy-done, bf16[1024,8192]{1,0:T(8,128)(2,1)} %copy-done, f32[1,8192]{1,0:T(1,128)S(1)} %add.89.refs_4_, ...), custom_call_target="tpu_custom_call" | custom-call | flops 1000 | bytes 1000 | tf_op jit(solution)/shard_map/rowsum_last/pallas_call | solution.py:323
  113.2 3.3 %proto_first.7 = (bf16[1024,2048]{1,0:T(8,128)(2,1)S(1)}, f32[1024,128]{1,0:T(8,128)S(1)}) custom-call(s32[1]{0:T(128)} %bitcast.1.place, bf16[1024,128]{1,0:T(8,128)(2,1)S(1)} %constant_dynamic-slice_fusion.protos.refs_9_, bf16[8,128,1024]{2,1,0:T(8,128)(2,1)S(1)} %bitcast.15, f32[8,1,1024]{2,1,0:T(1,128)S(1)} %pad_maximum_fusion.3.totals), custom_call_target="tpu_custom_call" | custom-call | flops 1000 | bytes 1000 | tf_op jit(solution)/shard_map/proto_first/pallas_call | solution.py:444
  116.5 1.5 collective-permute-start.17
  118.0 2.2 %collective-permute-done.17 = f32[1,1024]{1,0:T(1,128)S(1)} collective-permute-done((f32[1,1024]{1,0:T(1,128)S(1)}, f32[1,1024]{1,0:T(1,128)S(1)}, u32[]{:S(2)}, u32[]{:S(2)}) %collective-permute-start.17) | collective-permute-done | bytes 4128 | tf_op jit(solution)/shard_map/ppermute | solution.py:669
  121.0 2.2 %view_grad.1 = bf16[1024,128]{1,0:T(8,128)(2,1)S(1)} custom-call(f32[1024,128]{1,0:T(8,128)S(1)} %get-tuple-element.191.code, f32[1,1024]{1,0:T(1,128)S(1)} %get-tuple-element.192.tot, f32[1,1024]{1,0:T(1,128)S(1)} %add.91.total, f32[1024,128]{1,0:T(8,128)} %copy-done.5, f32[1024,128]{1,0:T(8,128)} %copy-done.6, f32[1024,128]{1,0:T(8,128)} %copy-done.7, ...), custom_call_target="tpu_custom_call" | custom-call | flops 1000 | bytes 1000 | tf_op jit(solution)/shard_map/view_grad/pallas_call | solution.py:563
  125.4 2.1 %collective-permute-done.19 = f32[2,1,1024]{2,1,0:T(1,128)S(1)} collective-permute-done((f32[2,1,1024]{2,1,0:T(1,128)S(1)}, f32[2,1,1024]{2,1,0:T(1,128)S(1)}, u32[]{:S(2)}, u32[]{:S(2)}) %collective-permute-start.19) | collective-permute-done | bytes 8224 | tf_op jit(solution)/shard_map/ppermute | solution.py:669
  127.5 1.5 collective-permute-start.21
  129.0 1.6 collective-permute-start.22
  130.6 3.1 %collective-permute-done.22 = f32[4,1,1024]{2,1,0:T(1,128)S(1)} collective-permute-done((f32[4,1,1024]{2,1,0:T(1,128)S(1)}, f32[4,1,1024]{2,1,0:T(1,128)S(1)}, u32[]{:S(2)}, u32[]{:S(2)}) %collective-permute-start.22) | collective-permute-done | bytes 16416 | tf_op jit(solution)/shard_map/ppermute | solution.py:669
  133.8 5.4 %proto_last.1 = bf16[1024,128]{1,0:T(8,128)(2,1)} custom-call(s32[1]{0:T(128)} %bitcast.1.place, bf16[1024,2048]{1,0:T(8,128)(2,1)S(1)} %get-tuple-element.212.refs_0_, bf16[1024,2048]{1,0:T(8,128)(2,1)S(1)} %get-tuple-element.213.refs_1_, bf16[1024,2048]{1,0:T(8,128)(2,1)S(1)} %get-tuple-element.214.refs_2_, ...), custom_call_target="tpu_custom_call" | custom-call | tf_op jit(solution)/shard_map/proto_last/pallas_call | solution.py:494
  139.2 5.2 %backward.1 = f32[8,144,128]{2,1,0:T(8,128)S(1)} custom-call(bf16[1024,128]{1,0:T(8,128)(2,1)S(1)} %add_convert_fusion.grad_a, bf16[1024,128]{1,0:T(8,128)(2,1)S(1)} %collective-permute-done.21.grad_b, s32[1,1024]{1,0:T(1,128)S(1)} %get-tuple-element.225.pos, f32[1024,128]{1,0:T(8,128)} %get-tuple-element.226.raw, f32[1024,512]{1,0:T(8,128)} %get-tuple-element.227.pre, ...), custom_call_target="tpu_custom_call" | custom-call | tf_op jit(solution)/shard_map/backward/pallas_call | solution.py:620
  145.3 6.3 %collective-permute-done.23 = bf16[4,144,128]{2,1,0:T(8,128)(2,1)S(1)} collective-permute-done((bf16[4,144,128]{2,1,0:T(8,128)(2,1)S(1)}, bf16[4,144,128]{2,1,0:T(8,128)(2,1)S(1)}, u32[]{:S(2)}, u32[]{:S(2)}) %collective-permute-start.23) | collective-permute-done | bytes 147488 | tf_op jit(solution)/shard_map/ppermute | solution.py:669
  152.8 5.6 %collective-permute-done.24 = bf16[2,144,128]{2,1,0:T(8,128)(2,1)S(1)} collective-permute-done((bf16[2,144,128]{2,1,0:T(8,128)(2,1)S(1)}, bf16[2,144,128]{2,1,0:T(8,128)(2,1)S(1)}, u32[]{:S(2)}, u32[]{:S(2)}) %collective-permute-start.24) | collective-permute-done | bytes 73760 | tf_op jit(solution)/shard_map/ppermute | solution.py:669
  158.6 4.9 %collective-permute-done.25 = bf16[1,144,128]{2,1,0:T(8,128)(2,1)S(1)} collective-permute-done((bf16[1,144,128]{2,1,0:T(8,128)(2,1)S(1)}, bf16[1,144,128]{2,1,0:T(8,128)(2,1)S(1)}, u32[]{:S(2)}, u32[]{:S(2)}) %collective-permute-start.25) | collective-permute-done | bytes 36896 | tf_op jit(solution)/shard_map/ppermute | solution.py:669
  163.5 4.9 %collective-permute-done.26 = bf16[1,144,128]{2,1,0:T(8,128)(2,1)S(1)} collective-permute-done((bf16[1,144,128]{2,1,0:T(8,128)(2,1)S(1)}, bf16[1,144,128]{2,1,0:T(8,128)(2,1)S(1)}, u32[]{:S(2)}, u32[]{:S(2)}) %collective-permute-start.26) | collective-permute-done | bytes 36896 | tf_op jit(solution)/shard_map/ppermute | solution.py:669
  168.6 8.2 %collective-permute-done.27 = bf16[2,144,128]{2,1,0:T(8,128)(2,1)S(1)} collective-permute-done((bf16[2,144,128]{2,1,0:T(8,128)(2,1)S(1)}, bf16[2,144,128]{2,1,0:T(8,128)(2,1)S(1)}, u32[]{:S(2)}, u32[]{:S(2)}) %collective-permute-start.27) | collective-permute-done | bytes 73760 | tf_op jit(solution)/shard_map/ppermute | solution.py:669
  178.1 4.2 %collective-permute-done.28 = bf16[4,144,128]{2,1,0:T(8,128)(2,1)S(1)} collective-permute-done((bf16[4,144,128]{2,1,0:T(8,128)(2,1)S(1)}, bf16[4,144,128]{2,1,0:T(8,128)(2,1)S(1)}, u32[]{:S(2)}, u32[]{:S(2)}) %collective-permute-start.28) | collective-permute-done | bytes 147488 | tf_op jit(solution)/shard_map/ppermute | solution.py:669
  182.4 6.7 %collective-permute-done.29 = bf16[1,8,144,128]{3,2,1,0:T(8,128)(2,1)S(1)} collective-permute-done((bf16[1,8,144,128]{3,2,1,0:T(8,128)(2,1)S(1)}, bf16[1,8,144,128]{3,2,1,0:T(8,128)(2,1)S(1)}, u32[]{:S(2)}, u32[]{:S(2)}) %collective-permute-start.29) | collective-permute-done | bytes 294944 | tf_op jit(solution)/shard_map/ppermute | solution.py:669
  189.4 1.9 collective-permute-done.30.refs_1_
  191.3 2.1 %unpack.1 = (f32[1024,512]{1,0:T(8,128)}, f32[512,128]{1,0:T(8,128)}) custom-call(s32[2]{0:T(128)S(1)} %pad_add_fusion.place, bf16[2,8,144,128]{3,2,1,0:T(8,128)(2,1)S(1)} %pad_maximum_fusion.refs_0_, bf16[2,8,144,128]{3,2,1,0:T(8,128)(2,1)S(1)} %collective-permute-done.30.refs_1_), custom_call_target="tpu_custom_call" | custom-call | tf_op jit(solution)/shard_map/unpack/pallas_call | solution.py:650
  193.4 3.9 %convert_element_type.51 = f32[8192,128]{1,0:T(8,128)} convert(bf16[8192,128]{1,0:T(8,128)(2,1)} %all-gather.4.cloned.1.call-done) | non-fusion elementwise | flops 1048576 | bytes 6291456 | tf_op jit(solution)/shard_map/convert_element_type | solution.py:798
  (95 shorter events, 18.0 us)
Async XLA Ops:
  7.2 8.2 %copy-start.1 = (bf16[8192,128]{1,0:T(8,128)(2,1)S(1)}, bf16[8192,128]{1,0:T(8,128)(2,1)}, u32[]{:S(2)}) copy-start(bf16[8192,128]{1,0:T(8,128)(2,1)} %protos.2) | copy-start | bytes 6291460
  7.2 81.4 %all-gather.6.cloned.1.call-start = ((), (), s32[]{:S(2)}) async-start(), calls=%async_computation.1 | async-start | bytes 2359296 | tf_op jit(solution)/shard_map/all_gather | solution.py:688
  7.2 0.8 copy-start.9
  15.3 178.0 %all-gather.4.cloned.1.call-start = ((), (), s32[]{:S(2)}) async-start(), calls=%async_computation | async-start | bytes 2359296 | tf_op jit(solution)/shard_map/all_gather | solution.py:769
  26.4 59.7 %copy-start = (bf16[1024,8192]{1,0:T(8,128)(2,1)}, bf16[1024,8192]{1,0:T(8,128)(2,1)S(1)}, u32[]{:S(2)}) copy-start(bf16[1024,8192]{1,0:T(8,128)(2,1)S(1)} %get-tuple-element.120.expo.refs_0_.refs_1_.refs_2_.refs_3_) | copy-start | bytes 50331652
  26.5 7.3 %collective-permute-start = (f32[1,8192]{1,0:T(1,128)S(1)}, f32[1,8192]{1,0:T(1,128)S(1)}, u32[]{:S(2)}, u32[]{:S(2)}) collective-permute-start(f32[1,8192]{1,0:T(1,128)S(1)} %get-tuple-element.121), channel_id=1, source_target_pairs={{0,4},{4,0},{8,12},{12,8},{16,20},{20,16},{24,28},{28,24},{1,5},{5... | collective-permute-start | bytes 98312 | tf_op jit(solution)/shard_map/ppermute | solution.py:669
  33.0 0.8 copy-start.5
  33.8 5.1 %collective-permute-start.1 = (f32[1,8192]{1,0:T(1,128)S(1)}, f32[1,8192]{1,0:T(1,128)S(1)}, u32[]{:S(2)}, u32[]{:S(2)}) collective-permute-start(f32[1,8192]{1,0:T(1,128)S(1)} %add.81), channel_id=1, source_target_pairs={{0,8},{4,12},{8,0},{12,4},{16,24},{20,28},{24,16},{28,20},{1,9},{5... | collective-permute-start | bytes 98312 | tf_op jit(solution)/shard_map/ppermute | solution.py:669
  38.9 10.3 %copy-start.6 = (f32[1024,128]{1,0:T(8,128)}, f32[1024,128]{1,0:T(8,128)S(1)}, u32[]{:S(2)}) copy-start(f32[1024,128]{1,0:T(8,128)S(1)} %view_soft.5.refs_1_) | copy-start | bytes 1572868
  39.0 6.2 %collective-permute-start.2 = (f32[1,8192]{1,0:T(1,128)S(1)}, f32[1,8192]{1,0:T(1,128)S(1)}, u32[]{:S(2)}, u32[]{:S(2)}) collective-permute-start(f32[1,8192]{1,0:T(1,128)S(1)} %add.82.refs_0_), channel_id=1, source_target_pairs={{0,16},{4,20},{8,24},{12,28},{16,0},{20,4},{24,8},{28,12},{1,17},{... | collective-permute-start | bytes 98312 | tf_op jit(solution)/shard_map/ppermute | solution.py:669
  45.2 4.1 %copy-start.7 = (f32[1024,128]{1,0:T(8,128)}, f32[1024,128]{1,0:T(8,128)S(1)}, u32[]{:S(2)}) copy-start(f32[1024,128]{1,0:T(8,128)S(1)} %view_soft.6.refs_2_) | copy-start | bytes 1572868
  49.2 3.6 %collective-permute-start.3 = (f32[2,1024]{1,0:T(2,128)S(1)}, f32[2,1024]{1,0:T(2,128)S(1)}, u32[]{:S(2)}, u32[]{:S(2)}) collective-permute-start(f32[2,1024]{1,0:T(2,128)S(1)} %pad_maximum_fusion.7), channel_id=1, source_target_pairs={{0,1},{1,0},{2,3},{3,2},{4,5},{5,4},{6,7},{7,6},{8,9},{9,8},{10,11... | collective-permute-start | bytes 24584 | tf_op jit(solution)/shard_map/ppermute | solution.py:669
  52.8 6.0 %copy-start.8 = (f32[1024,128]{1,0:T(8,128)}, f32[1024,128]{1,0:T(8,128)S(1)}, u32[]{:S(2)}) copy-start(f32[1024,128]{1,0:T(8,128)S(1)} %view_soft.7.refs_3_) | copy-start | bytes 1572868
  52.9 3.7 %collective-permute-start.4 = (f32[2,1024]{1,0:T(2,128)S(1)}, f32[2,1024]{1,0:T(2,128)S(1)}, u32[]{:S(2)}, u32[]{:S(2)}) collective-permute-start(f32[2,1024]{1,0:T(2,128)S(1)} %fusion), channel_id=1, source_target_pairs={{0,2},{1,3},{2,0},{3,1},{4,6},{5,7},{6,4},{7,5},{8,10},{9,11},{10,... | collective-permute-start | bytes 24584 | tf_op jit(solution)/shard_map/ppermute | solution.py:669
  58.8 5.9 %collective-permute-start.6 = (f32[1,8192]{1,0:T(1,128)S(1)}, f32[1,8192]{1,0:T(1,128)S(1)}, u32[]{:S(2)}, u32[]{:S(2)}) collective-permute-start(f32[1,8192]{1,0:T(1,128)S(1)} %bitcast.19), channel_id=1, source_target_pairs={{0,4},{4,0},{8,12},{12,8},{16,20},{20,16},{24,28},{28,24},{1,5},{5... | collective-permute-start | bytes 98312 | tf_op jit(solution)/shard_map/ppermute | solution.py:669
  60.2 4.6 %collective-permute-start.5 = (f32[1,1,1024]{2,1,0:T(1,128)S(1)}, f32[1,1,1024]{2,1,0:T(1,128)S(1)}, u32[]{:S(2)}, u32[]{:S(2)}) collective-permute-start(f32[1,1,1024]{2,1,0:T(1,128)S(1)} %get-tuple-element.234), channel_id=1, source_target_pairs={{0,4},{4,0},{8,12},{12,8},{16,20},{20,16},{24,28},{28,24},{1,5},{5... | collective-permute-start | bytes 12296 | tf_op jit(solution)/shard_map/ppermute | solution.py:669
  64.7 16.7 %copy-start.4 = (bf16[128,8192]{1,0:T(8,128)(2,1)}, bf16[128,8192]{1,0:T(8,128)(2,1)S(1)}, u32[]{:S(2)}) copy-start(bf16[128,8192]{1,0:T(8,128)(2,1)S(1)} %unit_t.1.refs_6_) | copy-start | bytes 6291460
  64.8 6.2 %collective-permute-start.8 = (f32[1,8192]{1,0:T(1,128)S(1)}, f32[1,8192]{1,0:T(1,128)S(1)}, u32[]{:S(2)}, u32[]{:S(2)}) collective-permute-start(f32[1,8192]{1,0:T(1,128)S(1)} %bitcast_add_fusion), channel_id=1, source_target_pairs={{0,8},{4,12},{8,0},{12,4},{16,24},{20,28},{24,16},{28,20},{1,9},{5... | collective-permute-start | bytes 98312 | tf_op jit(solution)/shard_map/ppermute | solution.py:669
  65.5 5.5 %collective-permute-start.7 = (f32[2,1,1024]{2,1,0:T(1,128)S(1)}, f32[2,1,1024]{2,1,0:T(1,128)S(1)}, u32[]{:S(2)}, u32[]{:S(2)}) collective-permute-start(f32[2,1,1024]{2,1,0:T(1,128)S(1)} %pad_maximum_fusion.8), channel_id=1, source_target_pairs={{0,8},{4,12},{8,0},{12,4},{16,24},{20,28},{24,16},{28,20},{1,9},{5... | collective-permute-start | bytes 24584 | tf_op jit(solution)/shard_map/ppermute | solution.py:669
  71.0 6.3 %collective-permute-start.10 = (f32[1,8192]{1,0:T(1,128)S(1)}, f32[1,8192]{1,0:T(1,128)S(1)}, u32[]{:S(2)}, u32[]{:S(2)}) collective-permute-start(f32[1,8192]{1,0:T(1,128)S(1)} %add.86.refs_0_), channel_id=1, source_target_pairs={{0,16},{4,20},{8,24},{12,28},{16,0},{20,4},{24,8},{28,12},{1,17},{... | collective-permute-start | bytes 98312 | tf_op jit(solution)/shard_map/ppermute | solution.py:669
  72.4 4.9 %collective-permute-start.9 = (f32[4,1,1024]{2,1,0:T(1,128)S(1)}, f32[4,1,1024]{2,1,0:T(1,128)S(1)}, u32[]{:S(2)}, u32[]{:S(2)}) collective-permute-start(f32[4,1,1024]{2,1,0:T(1,128)S(1)} %pad_maximum_fusion.5), channel_id=1, source_target_pairs={{0,16},{4,20},{8,24},{12,28},{16,0},{20,4},{24,8},{28,12},{1,17},{... | collective-permute-start | bytes 49160 | tf_op jit(solution)/shard_map/ppermute | solution.py:669
  81.4 1.2 collective-permute-start.11
  82.5 3.6 %collective-permute-start.12 = (f32[1,1024]{1,0:T(1,128)S(1)}, f32[1,1024]{1,0:T(1,128)S(1)}, u32[]{:S(2)}, u32[]{:S(2)}) collective-permute-start(f32[1,1024]{1,0:T(1,128)S(1)} %add.87.refs_0_), channel_id=1, source_target_pairs={{0,2},{1,3},{2,0},{3,1},{4,6},{5,7},{6,4},{7,5},{8,10},{9,11},{10,... | collective-permute-start | bytes 12296 | tf_op jit(solution)/shard_map/ppermute | solution.py:669
  88.6 6.1 %collective-permute-start.13 = (f32[1,8192]{1,0:T(1,128)S(1)}, f32[1,8192]{1,0:T(1,128)S(1)}, u32[]{:S(2)}, u32[]{:S(2)}) collective-permute-start(f32[1,8192]{1,0:T(1,128)S(1)} %bitcast.17), channel_id=1, source_target_pairs={{0,4},{4,0},{8,12},{12,8},{16,20},{20,16},{24,28},{28,24},{1,5},{5... | collective-permute-start | bytes 98312 | tf_op jit(solution)/shard_map/ppermute | solution.py:669
  89.9 1.6 copy-start.2
  94.8 4.0 %collective-permute-start.14 = (f32[1,8192]{1,0:T(1,128)S(1)}, f32[1,8192]{1,0:T(1,128)S(1)}, u32[]{:S(2)}, u32[]{:S(2)}) collective-permute-start(f32[1,8192]{1,0:T(1,128)S(1)} %add.88), channel_id=1, source_target_pairs={{0,8},{4,12},{8,0},{12,4},{16,24},{20,28},{24,16},{28,20},{1,9},{5... | collective-permute-start | bytes 98312 | tf_op jit(solution)/shard_map/ppermute | solution.py:669
  98.8 4.9 %collective-permute-start.15 = (f32[1,8192]{1,0:T(1,128)S(1)}, f32[1,8192]{1,0:T(1,128)S(1)}, u32[]{:S(2)}, u32[]{:S(2)}) collective-permute-start(f32[1,8192]{1,0:T(1,128)S(1)} %add.89.refs_4_), channel_id=1, source_target_pairs={{0,16},{4,20},{8,24},{12,28},{16,0},{20,4},{24,8},{28,12},{1,17},{... | collective-permute-start | bytes 98312 | tf_op jit(solution)/shard_map/ppermute | solution.py:669
  103.7 9.5 %copy-start.3 = (bf16[1024,1024]{1,0:T(8,128)(2,1)S(1)}, bf16[1024,1024]{1,0:T(8,128)(2,1)}, u32[]{:S(2)}) copy-start(bf16[1024,1024]{1,0:T(8,128)(2,1)} %all-gather.6.cloned.1.call-done) | copy-start | bytes 6291460
  113.1 3.4 %collective-permute-start.16 = (f32[1,1024]{1,0:T(1,128)S(1)}, f32[1,1024]{1,0:T(1,128)S(1)}, u32[]{:S(2)}, u32[]{:S(2)}) collective-permute-start(f32[1,1024]{1,0:T(1,128)S(1)} %get-tuple-element.178), channel_id=1, source_target_pairs={{0,1},{1,0},{2,3},{3,2},{4,5},{5,4},{6,7},{7,6},{8,9},{9,8},{10,11... | collective-permute-start | bytes 12296 | tf_op jit(solution)/shard_map/ppermute | solution.py:669
  116.5 3.7 %collective-permute-start.17 = (f32[1,1024]{1,0:T(1,128)S(1)}, f32[1,1024]{1,0:T(1,128)S(1)}, u32[]{:S(2)}, u32[]{:S(2)}) collective-permute-start(f32[1,1024]{1,0:T(1,128)S(1)} %add.90), channel_id=1, source_target_pairs={{0,2},{1,3},{2,0},{3,1},{4,6},{5,7},{6,4},{7,5},{8,10},{9,11},{10,... | collective-permute-start | bytes 12296 | tf_op jit(solution)/shard_map/ppermute | solution.py:669
  120.2 3.6 %collective-permute-start.18 = (f32[1,1,1024]{2,1,0:T(1,128)S(1)}, f32[1,1,1024]{2,1,0:T(1,128)S(1)}, u32[]{:S(2)}, u32[]{:S(2)}) collective-permute-start(f32[1,1,1024]{2,1,0:T(1,128)S(1)} %bitcast.20), channel_id=1, source_target_pairs={{0,4},{4,0},{8,12},{12,8},{16,20},{20,16},{24,28},{28,24},{1,5},{5... | collective-permute-start | bytes 12296 | tf_op jit(solution)/shard_map/ppermute | solution.py:669
  123.8 1.5 collective-permute-start.20
  123.8 3.7 %collective-permute-start.19 = (f32[2,1,1024]{2,1,0:T(1,128)S(1)}, f32[2,1,1024]{2,1,0:T(1,128)S(1)}, u32[]{:S(2)}, u32[]{:S(2)}) collective-permute-start(f32[2,1,1024]{2,1,0:T(1,128)S(1)} %pad_maximum_fusion.9), channel_id=1, source_target_pairs={{0,8},{4,12},{8,0},{12,4},{16,24},{20,28},{24,16},{28,20},{1,9},{5... | collective-permute-start | bytes 24584 | tf_op jit(solution)/shard_map/ppermute | solution.py:669
  127.5 11.6 %collective-permute-start.21 = (bf16[1024,128]{1,0:T(8,128)(2,1)S(1)}, bf16[1024,128]{1,0:T(8,128)(2,1)S(1)}, u32[]{:S(2)}, u32[]{:S(2)}) collective-permute-start(bf16[1024,128]{1,0:T(8,128)(2,1)S(1)} %add_convert_fusion.grad_a), channel_id=1, source_target_pairs={{0,2},{1,3},{2,0},{3,1},{4,6},{5,7},{6,4},{7,5},{8,10},{9,11},{10,... | collective-permute-start | bytes 786440 | tf_op jit(solution)/shard_map/ppermute | solution.py:669
  129.0 4.7 %collective-permute-start.22 = (f32[4,1,1024]{2,1,0:T(1,128)S(1)}, f32[4,1,1024]{2,1,0:T(1,128)S(1)}, u32[]{:S(2)}, u32[]{:S(2)}) collective-permute-start(f32[4,1,1024]{2,1,0:T(1,128)S(1)} %pad_maximum_fusion.6), channel_id=1, source_target_pairs={{0,16},{4,20},{8,24},{12,28},{16,0},{20,4},{24,8},{28,12},{1,17},{... | collective-permute-start | bytes 49160 | tf_op jit(solution)/shard_map/ppermute | solution.py:669
  144.4 7.2 %collective-permute-start.23 = (bf16[4,144,128]{2,1,0:T(8,128)(2,1)S(1)}, bf16[4,144,128]{2,1,0:T(8,128)(2,1)S(1)}, u32[]{:S(2)}, u32[]{:S(2)}) collective-permute-start(bf16[4,144,128]{2,1,0:T(8,128)(2,1)S(1)} %dynamic-slice_convert_fusion), channel_id=1, source_target_pairs={{0,4},{4,0},{8,12},{12,8},{16,20},{20,16},{24,28},{28,24},{1,5},{5... | collective-permute-start | bytes 442376 | tf_op jit(solution)/shard_map/ppermute | solution.py:669
  151.6 6.8 %collective-permute-start.24 = (bf16[2,144,128]{2,1,0:T(8,128)(2,1)S(1)}, bf16[2,144,128]{2,1,0:T(8,128)(2,1)S(1)}, u32[]{:S(2)}, u32[]{:S(2)}) collective-permute-start(bf16[2,144,128]{2,1,0:T(8,128)(2,1)S(1)} %dynamic-slice_convert_fusion.1), channel_id=1, source_target_pairs={{0,8},{4,12},{8,0},{12,4},{16,24},{20,28},{24,16},{28,20},{1,9},{5... | collective-permute-start | bytes 221192 | tf_op jit(solution)/shard_map/ppermute | solution.py:669
  158.5 5.0 %collective-permute-start.25 = (bf16[1,144,128]{2,1,0:T(8,128)(2,1)S(1)}, bf16[1,144,128]{2,1,0:T(8,128)(2,1)S(1)}, u32[]{:S(2)}, u32[]{:S(2)}) collective-permute-start(bf16[1,144,128]{2,1,0:T(8,128)(2,1)S(1)} %dynamic-slice_convert_fusion.2), channel_id=1, source_target_pairs={{0,16},{4,20},{8,24},{12,28},{16,0},{20,4},{24,8},{28,12},{1,17},{... | collective-permute-start | bytes 110600 | tf_op jit(solution)/shard_map/ppermute | solution.py:669
  163.4 5.0 %collective-permute-start.26 = (bf16[1,144,128]{2,1,0:T(8,128)(2,1)S(1)}, bf16[1,144,128]{2,1,0:T(8,128)(2,1)S(1)}, u32[]{:S(2)}, u32[]{:S(2)}) collective-permute-start(bf16[1,144,128]{2,1,0:T(8,128)(2,1)S(1)} %add_convert_fusion.1), channel_id=1, source_target_pairs={{0,16},{4,20},{8,24},{12,28},{16,0},{20,4},{24,8},{28,12},{1,17},{... | collective-permute-start | bytes 110600 | tf_op jit(solution)/shard_map/ppermute | solution.py:669
  168.5 8.3 %collective-permute-start.27 = (bf16[2,144,128]{2,1,0:T(8,128)(2,1)S(1)}, bf16[2,144,128]{2,1,0:T(8,128)(2,1)S(1)}, u32[]{:S(2)}, u32[]{:S(2)}) collective-permute-start(bf16[2,144,128]{2,1,0:T(8,128)(2,1)S(1)} %pad_maximum_fusion.2), channel_id=1, source_target_pairs={{0,8},{4,12},{8,0},{12,4},{16,24},{20,28},{24,16},{28,20},{1,9},{5... | collective-permute-start | bytes 221192 | tf_op jit(solution)/shard_map/ppermute | solution.py:669
  176.8 5.5 %collective-permute-start.28 = (bf16[4,144,128]{2,1,0:T(8,128)(2,1)S(1)}, bf16[4,144,128]{2,1,0:T(8,128)(2,1)S(1)}, u32[]{:S(2)}, u32[]{:S(2)}) collective-permute-start(bf16[4,144,128]{2,1,0:T(8,128)(2,1)S(1)} %pad_maximum_fusion.1), channel_id=1, source_target_pairs={{0,4},{4,0},{8,12},{12,8},{16,20},{20,16},{24,28},{28,24},{1,5},{5... | collective-permute-start | bytes 442376 | tf_op jit(solution)/shard_map/ppermute | solution.py:669
  182.4 6.8 %collective-permute-start.29 = (bf16[1,8,144,128]{3,2,1,0:T(8,128)(2,1)S(1)}, bf16[1,8,144,128]{3,2,1,0:T(8,128)(2,1)S(1)}, u32[]{:S(2)}, u32[]{:S(2)}) collective-permute-start(bf16[1,8,144,128]{3,2,1,0:T(8,128)(2,1)S(1)} %maximum_bitcast_fusion), channel_id=1, source_target_pairs={{0,2},{1,3},{2,0},{3,1},{4,6},{5,7},{6,4},{7,5},{8,10},{9,11},{10,... | collective-permute-start | bytes 884744 | tf_op jit(solution)/shard_map/ppermute | solution.py:669
  189.2 2.1 %collective-permute-start.30 = (bf16[2,8,144,128]{3,2,1,0:T(8,128)(2,1)S(1)}, bf16[2,8,144,128]{3,2,1,0:T(8,128)(2,1)S(1)}, u32[]{:S(2)}, u32[]{:S(2)}) collective-permute-start(bf16[2,8,144,128]{3,2,1,0:T(8,128)(2,1)S(1)} %pad_maximum_fusion.refs_0_), channel_id=1, source_target_pairs={{0,1},{1,0},{2,3},{3,2},{4,5},{5,4},{6,7},{7,6},{8,9},{9,8},{10,11... | collective-permute-start | bytes 1769480 | tf_op jit(solution)/shard_map/ppermute | solution.py:669
Sparse Core Ops, SparseCore 0:
  15.5 52.4 all-gather.5
  139.3 49.7 all-gather.3

commit v7 on v6

--- a/solution.py
+++ b/solution.py
@@ -130,7 +130,7 @@
         scratch_shapes=[pltpu.VMEM((rows, depth), bf16)],
         compiler_params=params("arbitrary"),
         name="head",
-    )(in_hbm(embeddings), pairing.reshape(1, rows), in_hbm(w_in), in_hbm(w_out))
+    )(in_hbm(embeddings), in_hbm(pairing.reshape(1, rows)), in_hbm(w_in), in_hbm(w_out))
 
 
 def unit_of(protos):
@@ -341,27 +341,31 @@
     )(*[in_hbm(expo)] * pieces, *parts, in_hbm(unit_t))
 
 
-def unit_t_kernel(block, protos, out):
+def unit_t_kernel(block, lead, protos, *refs):
+    out = refs[-1]
+
     def one(j, carry):
-        here = pl.ds(pl.multiple_of(j * block, block), block)
+        here = pl.ds(pl.multiple_of(lead + j * block, block), block)
         _, _, unit = unit_of(protos[here, :])
         out[:, here] = unit.astype(bf16).astype(f32).T.astype(bf16)
         return carry
 
-    lax.fori_loop(0, protos.shape[0] // block, one, 0)
-
-
-def unit_transposed(protos):
+    lax.fori_loop(0, protos.shape[0] // 2 // block, one, 0)
+
+
+def unit_transposed(protos, *before):
     width, depth = protos.shape
-    return pl.pallas_call(
-        functools.partial(unit_t_kernel, min(512, width)),
-        in_specs=[WHOLE],
+    lead = width // 2 if before else 0
+    return pl.pallas_call(
+        functools.partial(unit_t_kernel, min(512, width // 2), lead),
+        in_specs=[WHOLE] * (1 + len(before)),
         out_specs=WHOLE,
         out_shape=jax.ShapeDtypeStruct((depth, width), bf16),
+        input_output_aliases={1: 0} if before else {},
         compiler_params=params(),
         cost_estimate=SMALL,
         name="unit_t",
-    )(protos)
+    )(protos, *before)
 
 
 def colsum_kernel(count, expo, *refs):
@@ -572,7 +576,7 @@
     )(code, tot, total, *[in_hbm(x) for x in softs])
 
 
-def backward_kernel(grad_a, grad_b, pos, raw, pre, emb, hid_part, w_out, out):
+def backward_kernel(share, turn, grad_a, grad_b, pos, raw, pre, emb, hid, w_out, out, g_all):
     total = grad_a[...].astype(f32) + grad_b[...].astype(f32)
     n, depth = raw.shape
     place = jnp.broadcast_to(pos[...].astype(f32), (8, n)).T[:, :1].astype(jnp.int32)
@@ -586,7 +590,7 @@
     inv = lax.rsqrt(jnp.sum(raw_out * raw_out, axis=1, keepdims=True) + norm_eps)
     inner = jnp.sum(raw_out * grad, axis=1, keepdims=True)
     d_raw = (inv * grad - raw_out * (inv * inv * inv) * inner).astype(bf16)
-    g_out = dot(hid_part[...], d_raw, TN)
+    g_all[...] = dot(hid[...], d_raw, TN)
     d_hidden = dot(d_raw, w_out[...], NT)
     v = pre[...]
     t = jnp.tanh(GELU_K * (v + GELU_A * (v * v * v)))
@@ -595,14 +599,15 @@
     g_in = dot(emb[...], d_pre, TN)
     count = out.shape[0]
     tall, wide = g_in.shape[0] // count, g_in.shape[1]
-    base, short = tall * (wide // 128), g_out.shape[0] // count
+    base, short = tall * (wide // 128), share // count
     for k in range(count):
         n = mirrored(k, count)
         for q in range(wide // 128):
             out[n, q * tall : (q + 1) * tall, :] = g_in[
                 k * tall : (k + 1) * tall, q * 128 : (q + 1) * 128
             ]
-        out[n, base : base + short, :] = g_out[k * short : (k + 1) * short]
+        low = pl.multiple_of(turn[0] * share + k * short, short)
+        out[n, base : base + short, :] = g_all[pl.ds(low, short), :]
 
 
 def mirrored(k, count):
@@ -614,18 +619,28 @@
     return found
 
 
-def backward(nb, grad_a, grad_b, pos, raw, pre, emb, hid_part, w_out):
-    lines = (emb.shape[1] * pre.shape[1] + hid_part.shape[1] * raw.shape[1]) // (nb * 128)
-    operands = [grad_a, grad_b, pos, raw, pre, emb, hid_part, w_out]
-    return pl.pallas_call(
-        backward_kernel,
-        grid=(1,),
-        in_specs=[full(x.shape) for x in operands],
-        out_specs=full((nb, lines, 128)),
+def backward(nb, npr, turn, grad_a, grad_b, pos, raw, pre, emb, hid, w_out):
+    rows, wide = emb.shape
+    hidden, depth = w_out.shape
+    part = wide // npr
+    share = hidden // npr
+    lines = (part * hidden + share * depth) // (nb * 128)
+    operands = [grad_a, grad_b, pos, raw, pre, emb, hid, w_out]
+    specs = [full(x.shape) for x in operands]
+    specs[5] = pl.BlockSpec((rows, part), lambda i, turn: (0, turn[0]))
+    return pl.pallas_call(
+        functools.partial(backward_kernel, share),
+        grid_spec=pltpu.PrefetchScalarGridSpec(
+            num_scalar_prefetch=1,
+            grid=(1,),
+            in_specs=specs,
+            out_specs=full((nb, lines, 128)),
+            scratch_shapes=[pltpu.VMEM((hidden, depth), f32)],
+        ),
         out_shape=jax.ShapeDtypeStruct((nb, lines, 128), f32),
         compiler_params=params("arbitrary"),
         name="backward",
-    )(grad_a, grad_b, pos, *[in_hbm(x) for x in operands[3:]])
+    )(turn, grad_a, grad_b, pos, *[in_hbm(x) for x in operands[3:]])
 
 
 def unpack_kernel(order, order_b, place, *refs):
@@ -657,6 +672,18 @@
     )(place, *pieces)
 
 
+def stages(size):
+    found, step = [[1]], 2
+    while step < size:
+        if step * 2 < size:
+            found.append([step, step * 2, step * 3])
+            step *= 4
+        else:
+            found.append([step])
+            step *= 2
+    return found
+
+
 def body(nb, npr, embeddings, pairing, w_in, w_out, prototypes):
     b = lax.axis_index("batch")
     p = lax.axis_index("proto")
@@ -670,7 +697,7 @@
 
     def exchange(x, axis, size, step, queue, results):
         other = flipped(x, axis, size, step)
-        if queue:
+        if queue and (axis == "batch" or step > 1):
             work, operands = queue.pop(0)
             operands, _ = lax.optimization_barrier((operands, x))
             other, found = lax.optimization_barrier((other, work(*operands)))
@@ -688,10 +715,9 @@
     views_all = lax.all_gather(views_t, "batch", axis=0)
     protos_own = lax.dynamic_slice_in_dim(prototypes, b * own, own, 0)
     place = b.astype(jnp.int32).reshape(1)
-    at_in = (p * (wide // npr)).astype(jnp.uint32)
-    at_out = (p * (hidden_n // npr)).astype(jnp.uint32)
-    views, protos_own, place, at_in, at_out = lax.optimization_barrier(
-        (views, protos_own, place, at_in, at_out)
+    turn_p = p.astype(jnp.int32).reshape(1)
+    views, protos_own, place, turn_p = lax.optimization_barrier(
+        (views, protos_own, place, turn_p)
     )
     expo, col, tot = first_pass(views, prototypes)
 
@@ -707,15 +733,11 @@
     both = first + second
     totals, tot = [both[:1]], both[1:]
 
-    def slices(embeddings, hid):
-        none = jnp.uint32(0)
-        return (
-            lax.dynamic_slice(embeddings, (none, at_in), (rows, wide // npr)),
-            lax.dynamic_slice(hid, (none, at_out), (rows, hidden_n // npr)),
-        )
+    def unit_half(protos):
+        return unit_transposed(protos, *taken)
 
     taken = []
-    queue = [(unit_transposed, (prototypes,)), (slices, (embeddings, hid))]
+    queue = [(unit_half, (prototypes,))] * 2
     col = colsum(expo, totals)[0]
     tot_all = tot[None]
     step = 1
@@ -727,7 +749,7 @@
         step *= 2
         if step < nb:
             col = col + part
-    unit_t, (emb_part, hid_part) = taken
+    unit_t = taken[-1]
     scale, row = rowsum(expo, [col, part])
     col = colsum(expo, doubled(row, "proto", npr))[0]
 
@@ -747,19 +769,22 @@
     total_all = total[None]
     grads = []
     queue = [(view_grad_part, (code, tot, total, *softs))]
-    step = 1
     turn = 1
-    while step < nb:
-        other = exchange(total_all, "batch", nb, step, queue, grads)
+    for steps in stages(nb):
+        others = [exchange(total_all, "batch", nb, step, queue, grads) for step in steps]
         if len(grads) > 1:
             grads = [(grads[0].astype(f32) + grads[1].astype(f32)).astype(bf16)]
-            other, grads[0] = lax.optimization_barrier((other, grads[0]))
+            others[0], grads[0] = lax.optimization_barrier((others[0], grads[0]))
         if turn * 2 < npr:
             grads = [grads[0], flipped(grads[0], "proto", npr, turn)]
             turn *= 2
-        total_all = jnp.concatenate([total_all, other], axis=0)
-        step *= 2
-
+        total_all = jnp.concatenate([total_all, *others], axis=0)
+
+    while turn * 2 < npr:
+        if len(grads) > 1:
+            grads = [(grads[0].astype(f32) + grads[1].astype(f32)).astype(bf16)]
+        grads = [grads[0], flipped(grads[0], "proto", npr, turn)]
+        turn *= 2
     if len(grads) > 1:
         grads = [(grads[0].astype(f32) + grads[1].astype(f32)).astype(bf16)]
     expos, parts = [x for x, _ in owns], [x for _, x in owns]
@@ -767,21 +792,25 @@
     found = []
     grads = [grads[0], exchange(grads[0], "proto", npr, npr // 2, queue, found)]
     grad_proto = lax.all_gather(found[0], "batch", axis=0, tiled=True)
-    both = backward(nb, *grads, pos, raw, pre, emb_part, hid_part, w_out)
-    step = 1
-    while step < nb:
-        half = both.shape[0] // 2
-        bit = (b // step) % 2
-        away = lax.dynamic_slice_in_dim(both, (1 - bit) * half, half, 0).astype(bf16)
-        kept = lax.dynamic_slice_in_dim(both, bit * half, half, 0)
-        both = kept + flipped(away, "batch", nb, step).astype(f32)
-        step *= 2
+    both = backward(nb, npr, turn_p, *grads, pos, raw, pre, embeddings, hid, w_out)
+    for steps in stages(nb):
+        count = len(steps) + 1
+        share = both.shape[0] // count
+        mine = (b // steps[0]) % 2
+        if count == 4:
+            mine = mine * 2 + (b // steps[1]) % 2
+        kept = lax.dynamic_slice_in_dim(both, mine * share, share, 0)
+        for flip, step in zip([1] if count == 2 else [2, 1, 3], steps):
+            away = lax.dynamic_slice_in_dim(both, (mine ^ flip) * share, share, 0)
+            kept = kept + flipped(away.astype(bf16), "batch", nb, step).astype(f32)
+        both = kept
     piece = both.astype(bf16)
     order_b = [0]
-    while step > 1:
-        step //= 2
-        piece = jnp.concatenate([piece, flipped(piece, "batch", nb, step)], axis=0)
-        order_b = order_b + [i ^ step for i in order_b]
+    for steps in reversed(stages(nb)):
+        piece = jnp.concatenate(
+            [piece, *[flipped(piece, "batch", nb, step) for step in steps]], axis=0
+        )
+        order_b = order_b + [i ^ step for step in steps for i in order_b]
     piece = piece[None]
     order = [0]
     step = npr // 2

time: 204 us -> 196 us (0.961)
  waiting for transfers between devices: 60.1 us -> 47.4 us
  starting transfers between devices: 31.5 us -> 40 us
  local copies, waits for them, and re-layouts: 7.39 us -> 2.61 us
    ppermute x31 -> x34, waiting for transfers between devices: 60 us -> 44.7 us  [flipped(): return lax.ppermute(x, axis, [(i, i ^ step) for i in range(size)])]
    ppermute x31 -> x34, starting transfers between devices: 31.5 us -> 39.9 us  [flipped(): return lax.ppermute(x, axis, [(i, i ^ step) for i in range(size)])]
    dynamic_slice x2 -> x0, local copies, waits for them, and re-layouts: 4.06 us -> none  [the longest x1 2.16 us: slices(): lax.dynamic_slice(embeddings, (none, at_in), (rows, wide // npr))]
    all_gather x1, waiting for transfers between devices: 0.01 us -> 2.59 us  [body(): grad_proto = lax.all_gather(found[0], 'batch', axis=0, tiled=True)]
    pallas_call x2 -> x3, Pallas kernels: 8.92 us -> 9.41 us  [the longest x1 5.67 us: backward(): pl.pallas_call(functools.partial(backward_kernel, share), grid_spec=pltpu...]
  transfers between devices with their start and end apart: 33 -> 36, of which waited for: 19 -> 20; matrix products, arithmetic and copies ran while one was open for 2% -> 0% of each run, Pallas kernels for 34% -> 36%
where the time goes in v7:
time: 196 us
  Pallas kernels  86.6 us (44%)
  waiting for transfers between devices  47.4 us (24%)
  starting transfers between devices  40 us (20%)
  between operations  14.5 us (7%)
  other arithmetic  4.5 us (2%)
  local copies, waits for them, and re-layouts  2.61 us (1%)
    ppermute x34, waiting for transfers between devices, flipped(): return lax.ppermute(x, axis, [(i, i ^ step) for i in range(size)])  44.7 us
    ppermute x34, starting transfers between devices, flipped(): return lax.ppermute(x, axis, [(i, i ^ step) for i in range(size)])  39.9 us
    pallas_call x4, Pallas kernels, view_soft(): pl.pallas_call(functools.partial(view_soft_body, block, min(32, chunk), l...  13.9 us
    pallas_call x4, Pallas kernels, proto_first(): pl.pallas_call(functools.partial(proto_first_kernel, chunk, tile, lead),...  13 us
    pallas_call x1, Pallas kernels, first_pass(): pl.pallas_call(functools.partial(first_kernel, block, chunk, tile), in_sp...  11 us
    pallas_call x1, Pallas kernels, rowsum_last(): pl.pallas_call(functools.partial(rowsum_last_kernel, pieces, len(parts)),...  9.46 us
    pallas_call x2, Pallas kernels, rowsum(): pl.pallas_call(functools.partial(rowsum_kernel, len(parts)), in_specs=[WH...  8.11 us
    pallas_call x1, Pallas kernels, head(): pl.pallas_call(head_kernel, grid=(steps,), in_specs=[pl.BlockSpec((block,...  7.41 us
  transfers between devices with their start and end apart: 36, of which 20 were waited for; matrix products, arithmetic and copies ran while one was open for 0% of the time, Pallas kernels for 36%

profile of v7, /device:TPU:0, one launch (start us, length us, event | category | flops | bytes accessed | tf_op | source)
XLA Modules:
  0.0 195.6 jit_solution(803051541329375747)
XLA Ops:
  7.2 7.4 %head.1 = (f32[1024,512]{1,0:T(8,128)}, bf16[1024,512]{1,0:T(8,128)(2,1)}, f32[1024,128]{1,0:T(8,128)}, bf16[1024,128]{1,0:T(8,128)(2,1)S(1)}, bf16[128,1024]{1,0:T(8,128)(2,1)}, /*index=5*/s32[1,1024]{1,0:T(1,128)S(1)}) custom-call(bf16[1024,1024]{1,0:T(8,128)(2,1)} %emb.3, s32[1,1024]{1,0:T(1,128)} %bitcast.24, bf16[1024,512]{1,0:T(8,128)(2,1)} %w_in.1, ...), custom_call_target="tpu_custom_call" | custom-call | tf_op jit(solution)/shard_map/head/pallas_call | solution.py:105
  14.8 11.0 %first_pass.1 = (bf16[1024,8192]{1,0:T(8,128)(2,1)S(1)}, f32[1,8192]{1,0:T(1,128)S(1)}, f32[1,1024]{1,0:T(1,128)S(1)}) custom-call(bf16[1024,128]{1,0:T(8,128)(2,1)S(1)} %get-tuple-element.131.views.refs_0_, bf16[8192,128]{1,0:T(8,128)(2,1)S(1)} %copy-done.1), custom_call_target="tpu_custom_call" | custom-call | flops 1000 | bytes 1000 | tf_op jit(solution)/shard_map/first_pass/pallas_call | solution.py:190
  25.8 3.0 %collective-permute-start = (f32[1,8192]{1,0:T(1,128)S(1)}, f32[1,8192]{1,0:T(1,128)S(1)}, u32[]{:S(2)}, u32[]{:S(2)}) collective-permute-start(f32[1,8192]{1,0:T(1,128)S(1)} %get-tuple-element.119), channel_id=1, source_target_pairs={{0,4},{4,0},{8,12},{12,8},{16,20},{20,16},{24,28},{28,24},{1,5},{5... | collective-permute-start | bytes 98312 | tf_op jit(solution)/shard_map/ppermute | solution.py:696
  28.8 3.5 %view_soft.4.refs_0_ = f32[1024,128]{1,0:T(8,128)S(1)} custom-call(bf16[1024,128]{1,0:T(8,128)(2,1)S(1)} %get-tuple-element.131.views.refs_0_, bf16[8192,128]{1,0:T(8,128)(2,1)S(1)} %copy-done.1), custom_call_target="tpu_custom_call" | custom-call | flops 1000 | bytes 1000 | tf_op jit(solution)/shard_map/view_soft/pallas_call | solution.py:539
  33.2 1.6 collective-permute-start.1
  34.8 3.5 %view_soft.5.refs_1_ = f32[1024,128]{1,0:T(8,128)S(1)} custom-call(bf16[1024,128]{1,0:T(8,128)(2,1)S(1)} %get-tuple-element.131.views.refs_0_, bf16[8192,128]{1,0:T(8,128)(2,1)S(1)} %copy-done.1), custom_call_target="tpu_custom_call" | custom-call | flops 1000 | bytes 1000 | tf_op jit(solution)/shard_map/view_soft/pallas_call | solution.py:539
  38.3 2.7 %collective-permute-start.2 = (f32[1,8192]{1,0:T(1,128)S(1)}, f32[1,8192]{1,0:T(1,128)S(1)}, u32[]{:S(2)}, u32[]{:S(2)}) collective-permute-start(f32[1,8192]{1,0:T(1,128)S(1)} %add.87.refs_0_), channel_id=1, source_target_pairs={{0,16},{4,20},{8,24},{12,28},{16,0},{20,4},{24,8},{28,12},{1,17},{... | collective-permute-start | bytes 98312 | tf_op jit(solution)/shard_map/ppermute | solution.py:696
  41.0 3.5 %view_soft.6.refs_2_ = f32[1024,128]{1,0:T(8,128)S(1)} custom-call(bf16[1024,128]{1,0:T(8,128)(2,1)S(1)} %get-tuple-element.131.views.refs_0_, bf16[8192,128]{1,0:T(8,128)(2,1)S(1)} %copy-done.1), custom_call_target="tpu_custom_call" | custom-call | flops 1000 | bytes 1000 | tf_op jit(solution)/shard_map/view_soft/pallas_call | solution.py:539
  44.5 4.1 %rowsum.2 = (f32[1,8192]{1,0:T(1,128)}, f32[1,1024]{1,0:T(1,128)S(1)}) custom-call(bf16[1024,8192]{1,0:T(8,128)(2,1)S(1)} %get-tuple-element.118.expo.refs_0_.refs_1_.refs_2_.refs_3_, f32[1,8192]{1,0:T(1,128)S(1)} %add.87.refs_0_, f32[1,8192]{1,0:T(1,128)S(1)} %collective-permute-done.2.refs_1_), custom_call_target="tpu_custom_call" | custom-call | flops 1000 | bytes 1000 | tf_op jit(solution)/shard_map/rowsum/pallas_call | solution.py:264
  49.8 1.5 collective-permute-start.4
  51.4 3.5 %view_soft.7.refs_3_ = f32[1024,128]{1,0:T(8,128)S(1)} custom-call(bf16[1024,128]{1,0:T(8,128)(2,1)S(1)} %get-tuple-element.131.views.refs_0_, bf16[8192,128]{1,0:T(8,128)(2,1)S(1)} %copy-done.1), custom_call_target="tpu_custom_call" | custom-call | flops 1000 | bytes 1000 | tf_op jit(solution)/shard_map/view_soft/pallas_call | solution.py:539
  54.9 2.2 %colsum.2 = f32[1,1,8192]{2,1,0:T(1,128)S(1)} custom-call(bf16[1024,8192]{1,0:T(8,128)(2,1)S(1)} %get-tuple-element.118.expo.refs_0_.refs_1_.refs_2_.refs_3_, f32[1,1024]{1,0:T(1,128)S(1)} %get-tuple-element.236.refs_0_), custom_call_target="tpu_custom_call" | custom-call | flops 1000 | bytes 1000 | tf_op jit(solution)/shard_map/colsum/pallas_call | solution.py:404
  59.2 1.9 unit_t.2.refs_0_
  62.7 1.6 collective-permute-start.7
  64.3 1.9 unit_t.3.refs_6_
  66.9 1.5 collective-permute-start.10
  68.5 1.5 collective-permute-start.9
  70.0 3.2 %collective-permute-done.9 = f32[4,1,1024]{2,1,0:T(1,128)S(1)} collective-permute-done((f32[4,1,1024]{2,1,0:T(1,128)S(1)}, f32[4,1,1024]{2,1,0:T(1,128)S(1)}, u32[]{:S(2)}, u32[]{:S(2)}) %collective-permute-start.9) | collective-permute-done | bytes 16416 | tf_op jit(solution)/shard_map/ppermute | solution.py:696
  73.2 4.1 %rowsum.3 = (f32[1,8192]{1,0:T(1,128)}, f32[1,1024]{1,0:T(1,128)S(1)}) custom-call(bf16[1024,8192]{1,0:T(8,128)(2,1)S(1)} %get-tuple-element.118.expo.refs_0_.refs_1_.refs_2_.refs_3_, f32[1,8192]{1,0:T(1,128)S(1)} %add.91.refs_0_, f32[1,8192]{1,0:T(1,128)S(1)} %collective-permute-done.10.refs_1_), custom_call_target="tpu_custom_call" | custom-call | flops 1000 | bytes 1000 | tf_op jit(solution)/shard_map/rowsum/pallas_call | solution.py:264
  78.9 3.1 %collective-permute-done.12.refs_1_ = f32[1,1024]{1,0:T(1,128)S(1)} collective-permute-done((f32[1,1024]{1,0:T(1,128)S(1)}, f32[1,1024]{1,0:T(1,128)S(1)}, u32[]{:S(2)}, u32[]{:S(2)}) %collective-permute-start.12) | collective-permute-done | bytes 4128 | tf_op jit(solution)/shard_map/ppermute | solution.py:696
  82.0 2.4 %colsum.3 = f32[1,1,8192]{2,1,0:T(1,128)S(1)} custom-call(bf16[1024,8192]{1,0:T(8,128)(2,1)S(1)} %get-tuple-element.118.expo.refs_0_.refs_1_.refs_2_.refs_3_, f32[1,1024]{1,0:T(1,128)S(1)} %add.92.refs_0_, f32[1,1024]{1,0:T(1,128)S(1)} %collective-permute-done.12.refs_1_), custom_call_target="tpu_custom_call" | custom-call | flops 1000 | bytes 1000 | tf_op jit(solution)/shard_map/colsum/pallas_call | solution.py:404
  85.3 1.6 copy-done.2
  86.9 3.3 %proto_first.4 = (bf16[1024,2048]{1,0:T(8,128)(2,1)S(1)}, f32[1024,128]{1,0:T(8,128)S(1)}) custom-call(s32[1]{0:T(128)} %bitcast.1.place, bf16[1024,128]{1,0:T(8,128)(2,1)S(1)} %constant_dynamic-slice_fusion.protos.refs_9_, bf16[8,128,1024]{2,1,0:T(8,128)(2,1)S(1)} %bitcast.12, f32[8,1,1024]{2,1,0:T(1,128)S(1)} %pad_maximum_fusion.2.totals), custom_call_target="tpu_custom_call" | custom-call | flops 1000 | bytes 1000 | tf_op jit(solution)/shard_map/proto_first/pallas_call | solution.py:448
  91.5 3.3 %proto_first.5 = (bf16[1024,2048]{1,0:T(8,128)(2,1)S(1)}, f32[1024,128]{1,0:T(8,128)S(1)}) custom-call(s32[1]{0:T(128)} %bitcast.1.place, bf16[1024,128]{1,0:T(8,128)(2,1)S(1)} %constant_dynamic-slice_fusion.protos.refs_9_, bf16[8,128,1024]{2,1,0:T(8,128)(2,1)S(1)} %bitcast.13, f32[8,1,1024]{2,1,0:T(1,128)S(1)} %pad_maximum_fusion.2.totals), custom_call_target="tpu_custom_call" | custom-call | flops 1000 | bytes 1000 | tf_op jit(solution)/shard_map/proto_first/pallas_call | solution.py:448
  96.2 3.3 %proto_first.6 = (bf16[1024,2048]{1,0:T(8,128)(2,1)S(1)}, f32[1024,128]{1,0:T(8,128)S(1)}) custom-call(s32[1]{0:T(128)} %bitcast.1.place, bf16[1024,128]{1,0:T(8,128)(2,1)S(1)} %constant_dynamic-slice_fusion.protos.refs_9_, bf16[8,128,1024]{2,1,0:T(8,128)(2,1)S(1)} %bitcast.14, f32[8,1,1024]{2,1,0:T(1,128)S(1)} %pad_maximum_fusion.2.totals), custom_call_target="tpu_custom_call" | custom-call | flops 1000 | bytes 1000 | tf_op jit(solution)/shard_map/proto_first/pallas_call | solution.py:448
  99.7 9.5 %rowsum_last.1 = (f32[1,8192]{1,0:T(1,128)S(1)}, f32[1,1024]{1,0:T(1,128)S(1)}, f32[1024,128]{1,0:T(8,128)S(1)}) custom-call(bf16[1024,8192]{1,0:T(8,128)(2,1)} %copy-done, bf16[1024,8192]{1,0:T(8,128)(2,1)} %copy-done, bf16[1024,8192]{1,0:T(8,128)(2,1)} %copy-done, bf16[1024,8192]{1,0:T(8,128)(2,1)} %copy-done, f32[1,8192]{1,0:T(1,128)S(1)} %add.94.refs_4_, ...), custom_call_target="tpu_custom_call" | custom-call | flops 1000 | bytes 1000 | tf_op jit(solution)/shard_map/rowsum_last/pallas_call | solution.py:323
  110.4 1.5 collective-permute-start.17
  111.9 3.3 %proto_first.7 = (bf16[1024,2048]{1,0:T(8,128)(2,1)S(1)}, f32[1024,128]{1,0:T(8,128)S(1)}) custom-call(s32[1]{0:T(128)} %bitcast.1.place, bf16[1024,128]{1,0:T(8,128)(2,1)S(1)} %constant_dynamic-slice_fusion.protos.refs_9_, bf16[8,128,1024]{2,1,0:T(8,128)(2,1)S(1)} %bitcast.15, f32[8,1,1024]{2,1,0:T(1,128)S(1)} %pad_maximum_fusion.2.totals), custom_call_target="tpu_custom_call" | custom-call | flops 1000 | bytes 1000 | tf_op jit(solution)/shard_map/proto_first/pallas_call | solution.py:448
  115.2 1.4 collective-permute-start.18
  116.6 2.2 %view_grad.1 = bf16[1024,128]{1,0:T(8,128)(2,1)S(1)} custom-call(f32[1024,128]{1,0:T(8,128)S(1)} %get-tuple-element.186.code, f32[1,1024]{1,0:T(1,128)S(1)} %get-tuple-element.187.tot, f32[1,1024]{1,0:T(1,128)S(1)} %get-tuple-element.188.total, f32[1024,128]{1,0:T(8,128)} %copy-done.5, f32[1024,128]{1,0:T(8,128)} %copy-done.6, f32[1024,128]{1,0:T(8,128)} %copy-done.7, ...), custom_call_target="tpu_custom_call" | custom-call | flops 1000 | bytes 1000 | tf_op jit(solution)/shard_map/view_grad/pallas_call | solution.py:567
  119.4 1.8 collective-permute-start.22
  121.2 2.2 %collective-permute-start.23 = (f32[2,1,1024]{2,1,0:T(1,128)S(1)}, f32[2,1,1024]{2,1,0:T(1,128)S(1)}, u32[]{:S(2)}, u32[]{:S(2)}) collective-permute-start(f32[2,1,1024]{2,1,0:T(1,128)S(1)} %pad_maximum_fusion.6), channel_id=1, source_target_pairs={{0,24},{4,28},{8,16},{12,20},{16,8},{20,12},{24,0},{28,4},{1,25},{... | collective-permute-start | bytes 24584 | tf_op jit(solution)/shard_map/ppermute | solution.py:696
  124.4 2.2 %collective-permute-done.23 = f32[2,1,1024]{2,1,0:T(1,128)S(1)} collective-permute-done((f32[2,1,1024]{2,1,0:T(1,128)S(1)}, f32[2,1,1024]{2,1,0:T(1,128)S(1)}, u32[]{:S(2)}, u32[]{:S(2)}) %collective-permute-start.23) | collective-permute-done | bytes 8224 | tf_op jit(solution)/shard_map/ppermute | solution.py:696
  126.6 5.4 %proto_last.1 = bf16[1024,128]{1,0:T(8,128)(2,1)} custom-call(s32[1]{0:T(128)} %bitcast.1.place, bf16[1024,2048]{1,0:T(8,128)(2,1)S(1)} %get-tuple-element.207.refs_0_, bf16[1024,2048]{1,0:T(8,128)(2,1)S(1)} %get-tuple-element.208.refs_1_, bf16[1024,2048]{1,0:T(8,128)(2,1)S(1)} %get-tuple-element.209.refs_2_, ...), custom_call_target="tpu_custom_call" | custom-call | tf_op jit(solution)/shard_map/proto_last/pallas_call | solution.py:498
  132.0 5.7 %backward.1 = f32[8,144,128]{2,1,0:T(8,128)S(1)} custom-call(s32[1]{0:T(128)} %bitcast.turn, bf16[1024,128]{1,0:T(8,128)(2,1)S(1)} %add_convert_fusion.grad_a, bf16[1024,128]{1,0:T(8,128)(2,1)S(1)} %collective-permute-done.21.grad_b, s32[1,1024]{1,0:T(1,128)S(1)} %get-tuple-element.220.pos, f32[1024,128]{1,0:T(8,128)} %get-tuple-element.221.raw, ...), custom_call_target="tpu_custom_call" | custom-call | tf_op jit(solution)/shard_map/backward/pallas_call | solution.py:631
  139.1 6.2 %collective-permute-done.24 = bf16[4,144,128]{2,1,0:T(8,128)(2,1)S(1)} collective-permute-done((bf16[4,144,128]{2,1,0:T(8,128)(2,1)S(1)}, bf16[4,144,128]{2,1,0:T(8,128)(2,1)S(1)}, u32[]{:S(2)}, u32[]{:S(2)}) %collective-permute-start.24) | collective-permute-done | bytes 147488 | tf_op jit(solution)/shard_map/ppermute | solution.py:696
  146.3 3.6 %collective-permute-start.27 = (bf16[1,144,128]{2,1,0:T(8,128)(2,1)S(1)}, bf16[1,144,128]{2,1,0:T(8,128)(2,1)S(1)}, u32[]{:S(2)}, u32[]{:S(2)}) collective-permute-start(bf16[1,144,128]{2,1,0:T(8,128)(2,1)S(1)} %get-tuple-element.232), channel_id=1, source_target_pairs={{0,24},{4,28},{8,16},{12,20},{16,8},{20,12},{24,0},{28,4},{1,25},{... | collective-permute-start | bytes 110600 | tf_op jit(solution)/shard_map/ppermute | solution.py:696
  151.3 2.9 %collective-permute-done.27 = bf16[1,144,128]{2,1,0:T(8,128)(2,1)S(1)} collective-permute-done((bf16[1,144,128]{2,1,0:T(8,128)(2,1)S(1)}, bf16[1,144,128]{2,1,0:T(8,128)(2,1)S(1)}, u32[]{:S(2)}, u32[]{:S(2)}) %collective-permute-start.27) | collective-permute-done | bytes 36896 | tf_op jit(solution)/shard_map/ppermute | solution.py:696
  155.4 1.7 collective-permute-start.29
  157.1 1.6 collective-permute-start.30
  158.7 1.6 collective-permute-done.29
  160.2 2.6 %collective-permute-done.30 = bf16[1,144,128]{2,1,0:T(8,128)(2,1)S(1)} collective-permute-done((bf16[1,144,128]{2,1,0:T(8,128)(2,1)S(1)}, bf16[1,144,128]{2,1,0:T(8,128)(2,1)S(1)}, u32[]{:S(2)}, u32[]{:S(2)}) %collective-permute-start.30) | collective-permute-done | bytes 36896 | tf_op jit(solution)/shard_map/ppermute | solution.py:696
  163.9 7.4 %collective-permute-done.31 = bf16[4,144,128]{2,1,0:T(8,128)(2,1)S(1)} collective-permute-done((bf16[4,144,128]{2,1,0:T(8,128)(2,1)S(1)}, bf16[4,144,128]{2,1,0:T(8,128)(2,1)S(1)}, u32[]{:S(2)}, u32[]{:S(2)}) %collective-permute-start.31) | collective-permute-done | bytes 147488 | tf_op jit(solution)/shard_map/ppermute | solution.py:696
  171.3 6.7 %collective-permute-done.32 = bf16[1,8,144,128]{3,2,1,0:T(8,128)(2,1)S(1)} collective-permute-done((bf16[1,8,144,128]{3,2,1,0:T(8,128)(2,1)S(1)}, bf16[1,8,144,128]{3,2,1,0:T(8,128)(2,1)S(1)}, u32[]{:S(2)}, u32[]{:S(2)}) %collective-permute-start.32) | collective-permute-done | bytes 294944 | tf_op jit(solution)/shard_map/ppermute | solution.py:696
  178.3 1.9 collective-permute-done.33.refs_1_
  180.2 2.1 %unpack.1 = (f32[1024,512]{1,0:T(8,128)}, f32[512,128]{1,0:T(8,128)}) custom-call(s32[2]{0:T(128)S(1)} %pad_add_fusion.place, bf16[2,8,144,128]{3,2,1,0:T(8,128)(2,1)S(1)} %pad_maximum_fusion.refs_0_, bf16[2,8,144,128]{3,2,1,0:T(8,128)(2,1)S(1)} %collective-permute-done.33.refs_1_), custom_call_target="tpu_custom_call" | custom-call | tf_op jit(solution)/shard_map/unpack/pallas_call | solution.py:665
  182.3 2.6 %all-gather.4.cloned.1.call-done = bf16[8192,128]{1,0:T(8,128)(2,1)} async-done(((bf16[1024,128]{1,0:T(8,128)(2,1)}), bf16[8192,128]{1,0:T(8,128)(2,1)}) %all-gather.4.cloned.1.call-update) | async-done | bytes 2097168 | tf_op jit(solution)/shard_map/all_gather | solution.py:794
  184.9 3.9 %convert_element_type.51 = f32[8192,128]{1,0:T(8,128)} convert(bf16[8192,128]{1,0:T(8,128)(2,1)} %all-gather.4.cloned.1.call-done) | non-fusion elementwise | flops 1048576 | bytes 6291456 | tf_op jit(solution)/shard_map/convert_element_type | solution.py:827
  (100 shorter events, 21.3 us)
Async XLA Ops:
  7.2 7.6 %copy-start.1 = (bf16[8192,128]{1,0:T(8,128)(2,1)S(1)}, bf16[8192,128]{1,0:T(8,128)(2,1)}, u32[]{:S(2)}) copy-start(bf16[8192,128]{1,0:T(8,128)(2,1)} %protos.3) | copy-start | bytes 6291460
  7.2 77.3 %all-gather.6.cloned.1.call-start = ((), (), s32[]{:S(2)}) async-start(), calls=%async_computation.1 | async-start | bytes 2359296 | tf_op jit(solution)/shard_map/all_gather | solution.py:715
  14.7 170.2 %all-gather.4.cloned.1.call-start = ((), (), s32[]{:S(2)}) async-start(), calls=%async_computation | async-start | bytes 2359296 | tf_op jit(solution)/shard_map/all_gather | solution.py:794
  25.8 56.2 %copy-start = (bf16[1024,8192]{1,0:T(8,128)(2,1)}, bf16[1024,8192]{1,0:T(8,128)(2,1)S(1)}, u32[]{:S(2)}) copy-start(bf16[1024,8192]{1,0:T(8,128)(2,1)S(1)} %get-tuple-element.118.expo.refs_0_.refs_1_.refs_2_.refs_3_) | copy-start | bytes 50331652
  25.8 7.4 %collective-permute-start = (f32[1,8192]{1,0:T(1,128)S(1)}, f32[1,8192]{1,0:T(1,128)S(1)}, u32[]{:S(2)}, u32[]{:S(2)}) collective-permute-start(f32[1,8192]{1,0:T(1,128)S(1)} %get-tuple-element.119), channel_id=1, source_target_pairs={{0,4},{4,0},{8,12},{12,8},{16,20},{20,16},{24,28},{28,24},{1,5},{5... | collective-permute-start | bytes 98312 | tf_op jit(solution)/shard_map/ppermute | solution.py:696
  32.3 0.8 copy-start.5
  33.2 5.1 %collective-permute-start.1 = (f32[1,8192]{1,0:T(1,128)S(1)}, f32[1,8192]{1,0:T(1,128)S(1)}, u32[]{:S(2)}, u32[]{:S(2)}) collective-permute-start(f32[1,8192]{1,0:T(1,128)S(1)} %add.86), channel_id=1, source_target_pairs={{0,8},{4,12},{8,0},{12,4},{16,24},{20,28},{24,16},{28,20},{1,9},{5... | collective-permute-start | bytes 98312 | tf_op jit(solution)/shard_map/ppermute | solution.py:696
  38.3 10.3 %copy-start.6 = (f32[1024,128]{1,0:T(8,128)}, f32[1024,128]{1,0:T(8,128)S(1)}, u32[]{:S(2)}) copy-start(f32[1024,128]{1,0:T(8,128)S(1)} %view_soft.5.refs_1_) | copy-start | bytes 1572868
  38.3 6.1 %collective-permute-start.2 = (f32[1,8192]{1,0:T(1,128)S(1)}, f32[1,8192]{1,0:T(1,128)S(1)}, u32[]{:S(2)}, u32[]{:S(2)}) collective-permute-start(f32[1,8192]{1,0:T(1,128)S(1)} %add.87.refs_0_), channel_id=1, source_target_pairs={{0,16},{4,20},{8,24},{12,28},{16,0},{20,4},{24,8},{28,12},{1,17},{... | collective-permute-start | bytes 98312 | tf_op jit(solution)/shard_map/ppermute | solution.py:696
  44.5 4.1 %copy-start.7 = (f32[1024,128]{1,0:T(8,128)}, f32[1024,128]{1,0:T(8,128)S(1)}, u32[]{:S(2)}) copy-start(f32[1024,128]{1,0:T(8,128)S(1)} %view_soft.6.refs_2_) | copy-start | bytes 1572868
  48.6 1.2 collective-permute-start.3
  49.8 5.0 %collective-permute-start.4 = (f32[2,1024]{1,0:T(2,128)S(1)}, f32[2,1024]{1,0:T(2,128)S(1)}, u32[]{:S(2)}, u32[]{:S(2)}) collective-permute-start(f32[2,1024]{1,0:T(2,128)S(1)} %fusion), channel_id=1, source_target_pairs={{0,2},{1,3},{2,0},{3,1},{4,6},{5,7},{6,4},{7,5},{8,10},{9,11},{10,... | collective-permute-start | bytes 24584 | tf_op jit(solution)/shard_map/ppermute | solution.py:696
  54.8 2.3 %copy-start.8 = (f32[1024,128]{1,0:T(8,128)}, f32[1024,128]{1,0:T(8,128)S(1)}, u32[]{:S(2)}) copy-start(f32[1024,128]{1,0:T(8,128)S(1)} %view_soft.7.refs_3_) | copy-start | bytes 1572868
  57.1 4.0 %collective-permute-start.6 = (f32[1,8192]{1,0:T(1,128)S(1)}, f32[1,8192]{1,0:T(1,128)S(1)}, u32[]{:S(2)}, u32[]{:S(2)}) collective-permute-start(f32[1,8192]{1,0:T(1,128)S(1)} %bitcast.19), channel_id=1, source_target_pairs={{0,4},{4,0},{8,12},{12,8},{16,20},{20,16},{24,28},{28,24},{1,5},{5... | collective-permute-start | bytes 98312 | tf_op jit(solution)/shard_map/ppermute | solution.py:696
  58.5 3.6 %collective-permute-start.5 = (f32[1,1,1024]{2,1,0:T(1,128)S(1)}, f32[1,1,1024]{2,1,0:T(1,128)S(1)}, u32[]{:S(2)}, u32[]{:S(2)}) collective-permute-start(f32[1,1,1024]{2,1,0:T(1,128)S(1)} %get-tuple-element.235), channel_id=1, source_target_pairs={{0,4},{4,0},{8,12},{12,8},{16,20},{20,16},{24,28},{28,24},{1,5},{5... | collective-permute-start | bytes 12296 | tf_op jit(solution)/shard_map/ppermute | solution.py:696
  62.1 4.6 %collective-permute-start.8 = (f32[1,8192]{1,0:T(1,128)S(1)}, f32[1,8192]{1,0:T(1,128)S(1)}, u32[]{:S(2)}, u32[]{:S(2)}) collective-permute-start(f32[1,8192]{1,0:T(1,128)S(1)} %bitcast_add_fusion), channel_id=1, source_target_pairs={{0,8},{4,12},{8,0},{12,4},{16,24},{20,28},{24,16},{28,20},{1,9},{5... | collective-permute-start | bytes 98312 | tf_op jit(solution)/shard_map/ppermute | solution.py:696
  62.7 4.2 %collective-permute-start.7 = (f32[2,1,1024]{2,1,0:T(1,128)S(1)}, f32[2,1,1024]{2,1,0:T(1,128)S(1)}, u32[]{:S(2)}, u32[]{:S(2)}) collective-permute-start(f32[2,1,1024]{2,1,0:T(1,128)S(1)} %pad_maximum_fusion.5), channel_id=1, source_target_pairs={{0,8},{4,12},{8,0},{12,4},{16,24},{20,28},{24,16},{28,20},{1,9},{5... | collective-permute-start | bytes 24584 | tf_op jit(solution)/shard_map/ppermute | solution.py:696
  66.2 11.1 %copy-start.4 = (bf16[128,8192]{1,0:T(8,128)(2,1)}, bf16[128,8192]{1,0:T(8,128)(2,1)S(1)}, u32[]{:S(2)}) copy-start(bf16[128,8192]{1,0:T(8,128)(2,1)S(1)} %unit_t.3.refs_6_) | copy-start | bytes 6291460
  66.9 6.2 %collective-permute-start.10 = (f32[1,8192]{1,0:T(1,128)S(1)}, f32[1,8192]{1,0:T(1,128)S(1)}, u32[]{:S(2)}, u32[]{:S(2)}) collective-permute-start(f32[1,8192]{1,0:T(1,128)S(1)} %add.91.refs_0_), channel_id=1, source_target_pairs={{0,16},{4,20},{8,24},{12,28},{16,0},{20,4},{24,8},{28,12},{1,17},{... | collective-permute-start | bytes 98312 | tf_op jit(solution)/shard_map/ppermute | solution.py:696
  68.5 4.7 %collective-permute-start.9 = (f32[4,1,1024]{2,1,0:T(1,128)S(1)}, f32[4,1,1024]{2,1,0:T(1,128)S(1)}, u32[]{:S(2)}, u32[]{:S(2)}) collective-permute-start(f32[4,1,1024]{2,1,0:T(1,128)S(1)} %pad_maximum_fusion.3), channel_id=1, source_target_pairs={{0,16},{4,20},{8,24},{12,28},{16,0},{20,4},{24,8},{28,12},{1,17},{... | collective-permute-start | bytes 49160 | tf_op jit(solution)/shard_map/ppermute | solution.py:696
  77.2 1.2 collective-permute-start.11
  78.4 3.6 %collective-permute-start.12 = (f32[1,1024]{1,0:T(1,128)S(1)}, f32[1,1024]{1,0:T(1,128)S(1)}, u32[]{:S(2)}, u32[]{:S(2)}) collective-permute-start(f32[1,1024]{1,0:T(1,128)S(1)} %add.92.refs_0_), channel_id=1, source_target_pairs={{0,2},{1,3},{2,0},{3,1},{4,6},{5,7},{6,4},{7,5},{8,10},{9,11},{10,... | collective-permute-start | bytes 12296 | tf_op jit(solution)/shard_map/ppermute | solution.py:696
  84.5 5.7 %collective-permute-start.13 = (f32[1,8192]{1,0:T(1,128)S(1)}, f32[1,8192]{1,0:T(1,128)S(1)}, u32[]{:S(2)}, u32[]{:S(2)}) collective-permute-start(f32[1,8192]{1,0:T(1,128)S(1)} %bitcast.17), channel_id=1, source_target_pairs={{0,4},{4,0},{8,12},{12,8},{16,20},{20,16},{24,28},{28,24},{1,5},{5... | collective-permute-start | bytes 98312 | tf_op jit(solution)/shard_map/ppermute | solution.py:696
  85.3 1.6 copy-start.2
  90.2 4.5 %collective-permute-start.14 = (f32[1,8192]{1,0:T(1,128)S(1)}, f32[1,8192]{1,0:T(1,128)S(1)}, u32[]{:S(2)}, u32[]{:S(2)}) collective-permute-start(f32[1,8192]{1,0:T(1,128)S(1)} %add.93), channel_id=1, source_target_pairs={{0,8},{4,12},{8,0},{12,4},{16,24},{20,28},{24,16},{28,20},{1,9},{5... | collective-permute-start | bytes 98312 | tf_op jit(solution)/shard_map/ppermute | solution.py:696
  94.8 4.9 %collective-permute-start.15 = (f32[1,8192]{1,0:T(1,128)S(1)}, f32[1,8192]{1,0:T(1,128)S(1)}, u32[]{:S(2)}, u32[]{:S(2)}) collective-permute-start(f32[1,8192]{1,0:T(1,128)S(1)} %add.94.refs_4_), channel_id=1, source_target_pairs={{0,16},{4,20},{8,24},{12,28},{16,0},{20,4},{24,8},{28,12},{1,17},{... | collective-permute-start | bytes 98312 | tf_op jit(solution)/shard_map/ppermute | solution.py:696
  99.7 12.2 %copy-start.3 = (bf16[1024,1024]{1,0:T(8,128)(2,1)S(1)}, bf16[1024,1024]{1,0:T(8,128)(2,1)}, u32[]{:S(2)}) copy-start(bf16[1024,1024]{1,0:T(8,128)(2,1)} %all-gather.6.cloned.1.call-done) | copy-start | bytes 6291460
  109.1 1.2 collective-permute-start.16
  110.4 4.8 %collective-permute-start.17 = (f32[1,1024]{1,0:T(1,128)S(1)}, f32[1,1024]{1,0:T(1,128)S(1)}, u32[]{:S(2)}, u32[]{:S(2)}) collective-permute-start(f32[1,1024]{1,0:T(1,128)S(1)} %add.95), channel_id=1, source_target_pairs={{0,2},{1,3},{2,0},{3,1},{4,6},{5,7},{6,4},{7,5},{8,10},{9,11},{10,... | collective-permute-start | bytes 12296 | tf_op jit(solution)/shard_map/ppermute | solution.py:696
  115.2 3.7 %collective-permute-start.18 = (f32[1,1,1024]{2,1,0:T(1,128)S(1)}, f32[1,1,1024]{2,1,0:T(1,128)S(1)}, u32[]{:S(2)}, u32[]{:S(2)}) collective-permute-start(f32[1,1,1024]{2,1,0:T(1,128)S(1)} %bitcast.20), channel_id=1, source_target_pairs={{0,4},{4,0},{8,12},{12,8},{16,20},{20,16},{24,28},{28,24},{1,5},{5... | collective-permute-start | bytes 12296 | tf_op jit(solution)/shard_map/ppermute | solution.py:696
  118.9 4.5 %collective-permute-start.20 = (bf16[1024,128]{1,0:T(8,128)(2,1)S(1)}, bf16[1024,128]{1,0:T(8,128)(2,1)S(1)}, u32[]{:S(2)}, u32[]{:S(2)}) collective-permute-start(bf16[1024,128]{1,0:T(8,128)(2,1)S(1)} %view_grad.1), channel_id=1, source_target_pairs={{0,1},{1,0},{2,3},{3,2},{4,5},{5,4},{6,7},{7,6},{8,9},{9,8},{10,11... | collective-permute-start | bytes 786440 | tf_op jit(solution)/shard_map/ppermute | solution.py:696
  118.9 4.5 %collective-permute-start.19 = (f32[2,1,1024]{2,1,0:T(1,128)S(1)}, f32[2,1,1024]{2,1,0:T(1,128)S(1)}, u32[]{:S(2)}, u32[]{:S(2)}) collective-permute-start(f32[2,1,1024]{2,1,0:T(1,128)S(1)} %pad_maximum_fusion.6), channel_id=1, source_target_pairs={{0,8},{4,12},{8,0},{12,4},{16,24},{20,28},{24,16},{28,20},{1,9},{5... | collective-permute-start | bytes 24584 | tf_op jit(solution)/shard_map/ppermute | solution.py:696
  119.4 5.0 %collective-permute-start.22 = (f32[2,1,1024]{2,1,0:T(1,128)S(1)}, f32[2,1,1024]{2,1,0:T(1,128)S(1)}, u32[]{:S(2)}, u32[]{:S(2)}) collective-permute-start(f32[2,1,1024]{2,1,0:T(1,128)S(1)} %pad_maximum_fusion.6), channel_id=1, source_target_pairs={{0,16},{4,20},{8,24},{12,28},{16,0},{20,4},{24,8},{28,12},{1,17},{... | collective-permute-start | bytes 24584 | tf_op jit(solution)/shard_map/ppermute | solution.py:696
  121.2 5.4 %collective-permute-start.23 = (f32[2,1,1024]{2,1,0:T(1,128)S(1)}, f32[2,1,1024]{2,1,0:T(1,128)S(1)}, u32[]{:S(2)}, u32[]{:S(2)}) collective-permute-start(f32[2,1,1024]{2,1,0:T(1,128)S(1)} %pad_maximum_fusion.6), channel_id=1, source_target_pairs={{0,24},{4,28},{8,16},{12,20},{16,8},{20,12},{24,0},{28,4},{1,25},{... | collective-permute-start | bytes 24584 | tf_op jit(solution)/shard_map/ppermute | solution.py:696
  123.5 8.5 %collective-permute-start.21 = (bf16[1024,128]{1,0:T(8,128)(2,1)S(1)}, bf16[1024,128]{1,0:T(8,128)(2,1)S(1)}, u32[]{:S(2)}, u32[]{:S(2)}) collective-permute-start(bf16[1024,128]{1,0:T(8,128)(2,1)S(1)} %add_convert_fusion.grad_a), channel_id=1, source_target_pairs={{0,2},{1,3},{2,0},{3,1},{4,6},{5,7},{6,4},{7,5},{8,10},{9,11},{10,... | collective-permute-start | bytes 786440 | tf_op jit(solution)/shard_map/ppermute | solution.py:696
  137.8 7.6 %collective-permute-start.24 = (bf16[4,144,128]{2,1,0:T(8,128)(2,1)S(1)}, bf16[4,144,128]{2,1,0:T(8,128)(2,1)S(1)}, u32[]{:S(2)}, u32[]{:S(2)}) collective-permute-start(bf16[4,144,128]{2,1,0:T(8,128)(2,1)S(1)} %dynamic-slice_convert_fusion), channel_id=1, source_target_pairs={{0,4},{4,0},{8,12},{12,8},{16,20},{20,16},{24,28},{28,24},{1,5},{5... | collective-permute-start | bytes 442376 | tf_op jit(solution)/shard_map/ppermute | solution.py:696
  145.4 5.1 %collective-permute-start.25 = (bf16[1,144,128]{2,1,0:T(8,128)(2,1)S(1)}, bf16[1,144,128]{2,1,0:T(8,128)(2,1)S(1)}, u32[]{:S(2)}, u32[]{:S(2)}) collective-permute-start(bf16[1,144,128]{2,1,0:T(8,128)(2,1)S(1)} %get-tuple-element.231), channel_id=1, source_target_pairs={{0,8},{4,12},{8,0},{12,4},{16,24},{20,28},{24,16},{28,20},{1,9},{5... | collective-permute-start | bytes 110600 | tf_op jit(solution)/shard_map/ppermute | solution.py:696
  145.5 5.8 %collective-permute-start.26 = (bf16[1,144,128]{2,1,0:T(8,128)(2,1)S(1)}, bf16[1,144,128]{2,1,0:T(8,128)(2,1)S(1)}, u32[]{:S(2)}, u32[]{:S(2)}) collective-permute-start(bf16[1,144,128]{2,1,0:T(8,128)(2,1)S(1)} %get-tuple-element.233), channel_id=1, source_target_pairs={{0,16},{4,20},{8,24},{12,28},{16,0},{20,4},{24,8},{28,12},{1,17},{... | collective-permute-start | bytes 110600 | tf_op jit(solution)/shard_map/ppermute | solution.py:696
  146.3 7.9 %collective-permute-start.27 = (bf16[1,144,128]{2,1,0:T(8,128)(2,1)S(1)}, bf16[1,144,128]{2,1,0:T(8,128)(2,1)S(1)}, u32[]{:S(2)}, u32[]{:S(2)}) collective-permute-start(bf16[1,144,128]{2,1,0:T(8,128)(2,1)S(1)} %get-tuple-element.232), channel_id=1, source_target_pairs={{0,24},{4,28},{8,16},{12,20},{16,8},{20,12},{24,0},{28,4},{1,25},{... | collective-permute-start | bytes 110600 | tf_op jit(solution)/shard_map/ppermute | solution.py:696
  154.2 4.5 %collective-permute-start.28 = (bf16[1,144,128]{2,1,0:T(8,128)(2,1)S(1)}, bf16[1,144,128]{2,1,0:T(8,128)(2,1)S(1)}, u32[]{:S(2)}, u32[]{:S(2)}) collective-permute-start(bf16[1,144,128]{2,1,0:T(8,128)(2,1)S(1)} %get-tuple-element.228), channel_id=1, source_target_pairs={{0,8},{4,12},{8,0},{12,4},{16,24},{20,28},{24,16},{28,20},{1,9},{5... | collective-permute-start | bytes 110600 | tf_op jit(solution)/shard_map/ppermute | solution.py:696
  155.4 4.9 %collective-permute-start.29 = (bf16[1,144,128]{2,1,0:T(8,128)(2,1)S(1)}, bf16[1,144,128]{2,1,0:T(8,128)(2,1)S(1)}, u32[]{:S(2)}, u32[]{:S(2)}) collective-permute-start(bf16[1,144,128]{2,1,0:T(8,128)(2,1)S(1)} %get-tuple-element.228), channel_id=1, source_target_pairs={{0,16},{4,20},{8,24},{12,28},{16,0},{20,4},{24,8},{28,12},{1,17},{... | collective-permute-start | bytes 110600 | tf_op jit(solution)/shard_map/ppermute | solution.py:696
  157.1 5.8 %collective-permute-start.30 = (bf16[1,144,128]{2,1,0:T(8,128)(2,1)S(1)}, bf16[1,144,128]{2,1,0:T(8,128)(2,1)S(1)}, u32[]{:S(2)}, u32[]{:S(2)}) collective-permute-start(bf16[1,144,128]{2,1,0:T(8,128)(2,1)S(1)} %get-tuple-element.228), channel_id=1, source_target_pairs={{0,24},{4,28},{8,16},{12,20},{16,8},{20,12},{24,0},{28,4},{1,25},{... | collective-permute-start | bytes 110600 | tf_op jit(solution)/shard_map/ppermute | solution.py:696
  162.9 8.3 %collective-permute-start.31 = (bf16[4,144,128]{2,1,0:T(8,128)(2,1)S(1)}, bf16[4,144,128]{2,1,0:T(8,128)(2,1)S(1)}, u32[]{:S(2)}, u32[]{:S(2)}) collective-permute-start(bf16[4,144,128]{2,1,0:T(8,128)(2,1)S(1)} %pad_maximum_fusion.1), channel_id=1, source_target_pairs={{0,4},{4,0},{8,12},{12,8},{16,20},{20,16},{24,28},{28,24},{1,5},{5... | collective-permute-start | bytes 442376 | tf_op jit(solution)/shard_map/ppermute | solution.py:696
  171.2 6.8 %collective-permute-start.32 = (bf16[1,8,144,128]{3,2,1,0:T(8,128)(2,1)S(1)}, bf16[1,8,144,128]{3,2,1,0:T(8,128)(2,1)S(1)}, u32[]{:S(2)}, u32[]{:S(2)}) collective-permute-start(bf16[1,8,144,128]{3,2,1,0:T(8,128)(2,1)S(1)} %bitcast.22), channel_id=1, source_target_pairs={{0,2},{1,3},{2,0},{3,1},{4,6},{5,7},{6,4},{7,5},{8,10},{9,11},{10,... | collective-permute-start | bytes 884744 | tf_op jit(solution)/shard_map/ppermute | solution.py:696
  178.1 2.1 %collective-permute-start.33 = (bf16[2,8,144,128]{3,2,1,0:T(8,128)(2,1)S(1)}, bf16[2,8,144,128]{3,2,1,0:T(8,128)(2,1)S(1)}, u32[]{:S(2)}, u32[]{:S(2)}) collective-permute-start(bf16[2,8,144,128]{3,2,1,0:T(8,128)(2,1)S(1)} %pad_maximum_fusion.refs_0_), channel_id=1, source_target_pairs={{0,1},{1,0},{2,3},{3,2},{4,5},{5,4},{6,7},{7,6},{8,9},{9,8},{10,11... | collective-permute-start | bytes 1769480 | tf_op jit(solution)/shard_map/ppermute | solution.py:696
Sparse Core Ops, SparseCore 0:
  14.8 52.7 all-gather.5
  132.2 52.6 all-gather.3

commit v8 on v7

--- a/solution.py
+++ b/solution.py
@@ -672,8 +672,8 @@
     )(place, *pieces)
 
 
-def stages(size):
-    found, step = [[1]], 2
+def stages(size, first=1):
+    found, step = ([[1]], 2) if first == 1 else ([], 1)
     while step < size:
         if step * 2 < size:
             found.append([step, step * 2, step * 3])
@@ -695,21 +695,23 @@
     def flipped(x, axis, size, step):
         return lax.ppermute(x, axis, [(i, i ^ step) for i in range(size)])
 
-    def exchange(x, axis, size, step, queue, results):
-        other = flipped(x, axis, size, step)
-        if queue and (axis == "batch" or step > 1):
-            work, operands = queue.pop(0)
-            operands, _ = lax.optimization_barrier((operands, x))
-            other, found = lax.optimization_barrier((other, work(*operands)))
+    def trade(x, axis, size, steps, queue=(), results=None):
+        others = [flipped(x, axis, size, step) for step in steps]
+        work = queue.pop(0) if queue else None
+        if work:
+            operands, _ = lax.optimization_barrier((work[1], x))
+            others, found = lax.optimization_barrier((others, work[0](*operands)))
             results.append(found)
-        return other
-
-    def doubled(x, axis, size, queue=(), results=None):
-        step = 1
-        while step * 2 < size:
-            x = x + exchange(x, axis, size, step, queue, results)
-            step *= 2
-        return [x, exchange(x, axis, size, step, queue, results)]
+        return others
+
+    def summed(x, axis, size, queue=(), results=None):
+        rounds = stages(size, 1 if axis == "batch" else 2)
+        for n, steps in enumerate(rounds):
+            others = trade(x, axis, size, steps, queue, results)
+            if n == len(rounds) - 1:
+                return [x, *others]
+            for other in others:
+                x = x + other
 
     pre, hid, raw, views, views_t, pos = head(embeddings, pairing, w_in, w_out)
     views_all = lax.all_gather(views_t, "batch", axis=0)
@@ -728,30 +730,35 @@
         (functools.partial(view_soft, lead=k * cols, count=cols), (views, prototypes))
         for k in range(groups)
     ]
-    scale, row = rowsum(expo, doubled(col, "batch", nb, queue, softs))
-    first, second = doubled(jnp.concatenate([row, tot], axis=0), "proto", npr, queue, softs)
-    both = first + second
+    scale, row = rowsum(expo, summed(col, "batch", nb, queue, softs))
+    rest = len(stages(npr, 2)) - 1
+    queue = [None] * rest + queue
+    both = sum(summed(jnp.concatenate([row, tot], axis=0), "proto", npr, queue, softs))
     totals, tot = [both[:1]], both[1:]
 
     def unit_half(protos):
         return unit_transposed(protos, *taken)
 
     taken = []
-    queue = [(unit_half, (prototypes,))] * 2
+    halves = [(unit_half, (prototypes,))] * 2
     col = colsum(expo, totals)[0]
     tot_all = tot[None]
-    step = 1
-    while step < nb:
-        other = flipped(tot_all, "batch", nb, step)
-        part = exchange(col, "batch", nb, step, queue, taken)
-        other, part = lax.optimization_barrier((other, part))
-        tot_all = jnp.concatenate([tot_all, other], axis=0)
-        step *= 2
-        if step < nb:
-            col = col + part
+    rounds = stages(nb)
+    for n, steps in enumerate(rounds):
+        others = [flipped(tot_all, "batch", nb, step) for step in steps]
+        if queue:
+            parts = trade(col, "batch", nb, steps, queue, softs)
+        else:
+            parts = trade(col, "batch", nb, steps, halves, taken)
+        others, parts = lax.optimization_barrier((others, parts))
+        tot_all = jnp.concatenate([tot_all, *others], axis=0)
+        if n < len(rounds) - 1:
+            for part in parts:
+                col = col + part
+    scale, row = rowsum(expo, [col, *parts])
+    halves = [None] * rest + halves
+    col = colsum(expo, summed(row, "proto", npr, halves, taken))[0]
     unit_t = taken[-1]
-    scale, row = rowsum(expo, [col, part])
-    col = colsum(expo, doubled(row, "proto", npr))[0]
 
     col, views_all = lax.optimization_barrier((col, views_all))
     each = nb // groups
@@ -763,15 +770,15 @@
         )
         for k in range(groups)
     ]
-    scale, row, code = rowsum_last(expo, doubled(col, "batch", nb, queue, owns), unit_t)
-    first, second = doubled(row, "proto", npr, queue, owns)
-    total = first + second
+    scale, row, code = rowsum_last(expo, summed(col, "batch", nb, queue, owns), unit_t)
+    queue = [None] * rest + queue
+    total = sum(summed(row, "proto", npr, queue, owns))
     total_all = total[None]
     grads = []
-    queue = [(view_grad_part, (code, tot, total, *softs))]
+    queue = [(view_grad_part, (code, tot, total, *softs))] + queue
     turn = 1
     for steps in stages(nb):
-        others = [exchange(total_all, "batch", nb, step, queue, grads) for step in steps]
+        others = trade(total_all, "batch", nb, steps, queue, grads if not grads else owns)
         if len(grads) > 1:
             grads = [(grads[0].astype(f32) + grads[1].astype(f32)).astype(bf16)]
             others[0], grads[0] = lax.optimization_barrier((others[0], grads[0]))
@@ -790,7 +797,7 @@
     expos, parts = [x for x, _ in owns], [x for _, x in owns]
     queue = [(proto_last, (place, expos, parts, scale, protos_own, views_all, total_all))]
     found = []
-    grads = [grads[0], exchange(grads[0], "proto", npr, npr // 2, queue, found)]
+    grads = [grads[0], *trade(grads[0], "proto", npr, [npr // 2], queue, found)]
     grad_proto = lax.all_gather(found[0], "batch", axis=0, tiled=True)
     both = backward(nb, npr, turn_p, *grads, pos, raw, pre, embeddings, hid, w_out)
     for steps in stages(nb):

time: 196 us -> 195 us (level)
  waiting for transfers between devices: 47.4 us -> 35.3 us
  starting transfers between devices: 40 us -> 50.4 us
    ppermute x34 -> x41, waiting for transfers between devices: 44.7 us -> 31.9 us  [flipped(): return lax.ppermute(x, axis, [(i, i ^ step) for i in range(size)])]
    ppermute x34 -> x41, starting transfers between devices: 39.9 us -> 50.4 us  [flipped(): return lax.ppermute(x, axis, [(i, i ^ step) for i in range(size)])]
  transfers between devices with their start and end apart: 36 -> 43, of which waited for: 20 -> 16; matrix products, arithmetic and copies ran while one was open for 0% -> 0% of each run, Pallas kernels for 36% -> 36%
where the time goes in v8:
time: 195 us
  Pallas kernels  87 us (45%)
  starting transfers between devices  50.4 us (26%)
  waiting for transfers between devices  35.3 us (18%)
  between operations  14.6 us (7%)
  other arithmetic  4.32 us (2%)
  local copies, waits for them, and re-layouts  3.14 us (2%)
    ppermute x41, starting transfers between devices, flipped(): return lax.ppermute(x, axis, [(i, i ^ step) for i in range(size)])  50.4 us
    ppermute x41, waiting for transfers between devices, flipped(): return lax.ppermute(x, axis, [(i, i ^ step) for i in range(size)])  31.9 us
    pallas_call x4, Pallas kernels, view_soft(): pl.pallas_call(functools.partial(view_soft_body, block, min(32, chunk), l...  14 us
    pallas_call x4, Pallas kernels, proto_first(): pl.pallas_call(functools.partial(proto_first_kernel, chunk, tile, lead),...  13 us
    pallas_call x1, Pallas kernels, first_pass(): pl.pallas_call(functools.partial(first_kernel, block, chunk, tile), in_sp...  11 us
    pallas_call x1, Pallas kernels, rowsum_last(): pl.pallas_call(functools.partial(rowsum_last_kernel, pieces, len(parts)),...  9.46 us
    pallas_call x2, Pallas kernels, rowsum(): pl.pallas_call(functools.partial(rowsum_kernel, len(parts)), in_specs=[WH...  8.11 us
    pallas_call x1, Pallas kernels, head(): pl.pallas_call(head_kernel, grid=(steps,), in_specs=[pl.BlockSpec((block,...  7.41 us
  transfers between devices with their start and end apart: 43, of which 16 were waited for; matrix products, arithmetic and copies ran while one was open for 0% of the time, Pallas kernels for 36%

profile of v8, /device:TPU:0, one launch (start us, length us, event | category | flops | bytes accessed | tf_op | source)
XLA Modules:
  0.0 194.7 jit_solution(5899090425784581778)
XLA Ops:
  7.2 7.4 %head.1 = (f32[1024,512]{1,0:T(8,128)}, bf16[1024,512]{1,0:T(8,128)(2,1)}, f32[1024,128]{1,0:T(8,128)}, bf16[1024,128]{1,0:T(8,128)(2,1)S(1)}, bf16[128,1024]{1,0:T(8,128)(2,1)}, /*index=5*/s32[1,1024]{1,0:T(1,128)S(1)}) custom-call(bf16[1024,1024]{1,0:T(8,128)(2,1)} %emb.3, s32[1,1024]{1,0:T(1,128)} %bitcast.25, bf16[1024,512]{1,0:T(8,128)(2,1)} %w_in.1, ...), custom_call_target="tpu_custom_call" | custom-call | tf_op jit(solution)/shard_map/head/pallas_call | solution.py:105
  14.8 11.0 %first_pass.1 = (bf16[1024,8192]{1,0:T(8,128)(2,1)S(1)}, f32[1,8192]{1,0:T(1,128)S(1)}, f32[1,1024]{1,0:T(1,128)S(1)}) custom-call(bf16[1024,128]{1,0:T(8,128)(2,1)S(1)} %get-tuple-element.151.views.refs_0_, bf16[8192,128]{1,0:T(8,128)(2,1)S(1)} %copy-done.1), custom_call_target="tpu_custom_call" | custom-call | flops 1000 | bytes 1000 | tf_op jit(solution)/shard_map/first_pass/pallas_call | solution.py:190
  25.8 3.0 %collective-permute-start = (f32[1,8192]{1,0:T(1,128)S(1)}, f32[1,8192]{1,0:T(1,128)S(1)}, u32[]{:S(2)}, u32[]{:S(2)}) collective-permute-start(f32[1,8192]{1,0:T(1,128)S(1)} %get-tuple-element.135), channel_id=1, source_target_pairs={{0,4},{4,0},{8,12},{12,8},{16,20},{20,16},{24,28},{28,24},{1,5},{5... | collective-permute-start | bytes 98312 | tf_op jit(solution)/shard_map/ppermute | solution.py:696
  28.8 3.5 %view_soft.4.refs_0_ = f32[1024,128]{1,0:T(8,128)S(1)} custom-call(bf16[1024,128]{1,0:T(8,128)(2,1)S(1)} %get-tuple-element.151.views.refs_0_, bf16[8192,128]{1,0:T(8,128)(2,1)S(1)} %copy-done.1), custom_call_target="tpu_custom_call" | custom-call | flops 1000 | bytes 1000 | tf_op jit(solution)/shard_map/view_soft/pallas_call | solution.py:539
  32.4 1.6 collective-permute-start.1
  34.0 2.6 %collective-permute-start.2 = (f32[1,8192]{1,0:T(1,128)S(1)}, f32[1,8192]{1,0:T(1,128)S(1)}, u32[]{:S(2)}, u32[]{:S(2)}) collective-permute-start(f32[1,8192]{1,0:T(1,128)S(1)} %add.80.refs_0_), channel_id=1, source_target_pairs={{0,16},{4,20},{8,24},{12,28},{16,0},{20,4},{24,8},{28,12},{1,17},{... | collective-permute-start | bytes 98312 | tf_op jit(solution)/shard_map/ppermute | solution.py:696
  36.8 3.5 %view_soft.5.refs_1_ = f32[1024,128]{1,0:T(8,128)S(1)} custom-call(bf16[1024,128]{1,0:T(8,128)(2,1)S(1)} %get-tuple-element.151.views.refs_0_, bf16[8192,128]{1,0:T(8,128)(2,1)S(1)} %copy-done.1), custom_call_target="tpu_custom_call" | custom-call | flops 1000 | bytes 1000 | tf_op jit(solution)/shard_map/view_soft/pallas_call | solution.py:539
  40.8 1.5 collective-permute-done.3.refs_3_
  42.3 4.1 %rowsum.2 = (f32[1,8192]{1,0:T(1,128)}, f32[1,1024]{1,0:T(1,128)S(1)}) custom-call(bf16[1024,8192]{1,0:T(8,128)(2,1)S(1)} %get-tuple-element.134.expo.refs_0_.refs_1_.refs_2_.refs_3_, f32[1,8192]{1,0:T(1,128)S(1)} %add.80.refs_0_, f32[1,8192]{1,0:T(1,128)S(1)} %collective-permute-done.1.refs_1_, f32[1,8192]{1,0:T(1,128)S(1)} %collective-permute-done.2.refs_2_, ...), custom_call_target="tpu_custom_call" | custom-call | flops 1000 | bytes 1000 | tf_op jit(solution)/shard_map/rowsum/pallas_call | solution.py:264
  46.5 1.5 collective-permute-start.5
  48.3 3.5 %view_soft.6.refs_2_ = f32[1024,128]{1,0:T(8,128)S(1)} custom-call(bf16[1024,128]{1,0:T(8,128)(2,1)S(1)} %get-tuple-element.151.views.refs_0_, bf16[8192,128]{1,0:T(8,128)(2,1)S(1)} %copy-done.1), custom_call_target="tpu_custom_call" | custom-call | flops 1000 | bytes 1000 | tf_op jit(solution)/shard_map/view_soft/pallas_call | solution.py:539
  51.9 2.2 %colsum.2 = f32[1,1,8192]{2,1,0:T(1,128)S(1)} custom-call(bf16[1024,8192]{1,0:T(8,128)(2,1)S(1)} %get-tuple-element.134.expo.refs_0_.refs_1_.refs_2_.refs_3_, f32[1,1024]{1,0:T(1,128)S(1)} %get-tuple-element.268.refs_0_), custom_call_target="tpu_custom_call" | custom-call | flops 1000 | bytes 1000 | tf_op jit(solution)/shard_map/colsum/pallas_call | solution.py:404
  56.3 3.5 %view_soft.7.refs_3_ = f32[1024,128]{1,0:T(8,128)S(1)} custom-call(bf16[1024,128]{1,0:T(8,128)(2,1)S(1)} %get-tuple-element.151.views.refs_0_, bf16[8192,128]{1,0:T(8,128)(2,1)S(1)} %copy-done.1), custom_call_target="tpu_custom_call" | custom-call | flops 1000 | bytes 1000 | tf_op jit(solution)/shard_map/view_soft/pallas_call | solution.py:539
  59.9 2.2 %collective-permute-start.13 = (f32[1,8192]{1,0:T(1,128)S(1)}, f32[1,8192]{1,0:T(1,128)S(1)}, u32[]{:S(2)}, u32[]{:S(2)}) collective-permute-start(f32[1,8192]{1,0:T(1,128)S(1)} %bitcast_add_fusion.refs_0_), channel_id=1, source_target_pairs={{0,16},{4,20},{8,24},{12,28},{16,0},{20,4},{24,8},{28,12},{1,17},{... | collective-permute-start | bytes 98312 | tf_op jit(solution)/shard_map/ppermute | solution.py:696
  62.1 2.2 %collective-permute-start.14 = (f32[1,8192]{1,0:T(1,128)S(1)}, f32[1,8192]{1,0:T(1,128)S(1)}, u32[]{:S(2)}, u32[]{:S(2)}) collective-permute-start(f32[1,8192]{1,0:T(1,128)S(1)} %bitcast_add_fusion.refs_0_), channel_id=1, source_target_pairs={{0,24},{4,28},{8,16},{12,20},{16,8},{20,12},{24,0},{28,4},{1,25},{... | collective-permute-start | bytes 98312 | tf_op jit(solution)/shard_map/ppermute | solution.py:696
  64.4 1.7 collective-permute-start.11
  66.1 1.8 collective-permute-start.9
  67.9 1.9 unit_t.2.refs_0_
  71.0 4.1 %rowsum.3 = (f32[1,8192]{1,0:T(1,128)}, f32[1,1024]{1,0:T(1,128)S(1)}) custom-call(bf16[1024,8192]{1,0:T(8,128)(2,1)S(1)} %get-tuple-element.134.expo.refs_0_.refs_1_.refs_2_.refs_3_, f32[1,8192]{1,0:T(1,128)S(1)} %bitcast_add_fusion.refs_0_, f32[1,8192]{1,0:T(1,128)S(1)} %collective-permute-done.12.refs_1_, f32[1,8192]{1,0:T(1,128)S(1)} %collective-permute-done.13.refs_2_, ...), custom_call_target="tpu_custom_call" | custom-call | flops 1000 | bytes 1000 | tf_op jit(solution)/shard_map/rowsum/pallas_call | solution.py:264
  76.9 1.9 unit_t.3.refs_8_
  80.2 2.4 %colsum.3 = f32[1,1,8192]{2,1,0:T(1,128)S(1)} custom-call(bf16[1024,8192]{1,0:T(8,128)(2,1)S(1)} %get-tuple-element.134.expo.refs_0_.refs_1_.refs_2_.refs_3_, f32[1,1024]{1,0:T(1,128)S(1)} %get-tuple-element.163.refs_0_, f32[1,1024]{1,0:T(1,128)S(1)} %collective-permute-done.15.refs_1_, f32[1,1024]{1,0:T(1,128)S(1)} %collective-permute-done.16.refs_2_, ...), custom_call_target="tpu_custom_call" | custom-call | flops 1000 | bytes 1000 | tf_op jit(solution)/shard_map/colsum/pallas_call | solution.py:404
  83.3 1.6 copy-done.2
  84.9 3.3 %proto_first.4 = (bf16[1024,2048]{1,0:T(8,128)(2,1)S(1)}, f32[1024,128]{1,0:T(8,128)S(1)}) custom-call(s32[1]{0:T(128)} %bitcast.1.place, bf16[1024,128]{1,0:T(8,128)(2,1)S(1)} %constant_dynamic-slice_fusion.protos.refs_9_, bf16[8,128,1024]{2,1,0:T(8,128)(2,1)S(1)} %bitcast.13, f32[8,1,1024]{2,1,0:T(1,128)S(1)} %constant_dynamic-update-slice_fusion.totals), custom_call_target="tpu_custom_call" | custom-call | flops 1000 | bytes 1000 | tf_op jit(solution)/shard_map/proto_first/pallas_call | solution.py:448
  90.7 2.0 %collective-permute-start.21 = (f32[1,8192]{1,0:T(1,128)S(1)}, f32[1,8192]{1,0:T(1,128)S(1)}, u32[]{:S(2)}, u32[]{:S(2)}) collective-permute-start(f32[1,8192]{1,0:T(1,128)S(1)} %add.85.refs_4_), channel_id=1, source_target_pairs={{0,24},{4,28},{8,16},{12,20},{16,8},{20,12},{24,0},{28,4},{1,25},{... | collective-permute-start | bytes 98312 | tf_op jit(solution)/shard_map/ppermute | solution.py:696
  92.7 3.3 %proto_first.5 = (bf16[1024,2048]{1,0:T(8,128)(2,1)S(1)}, f32[1024,128]{1,0:T(8,128)S(1)}) custom-call(s32[1]{0:T(128)} %bitcast.1.place, bf16[1024,128]{1,0:T(8,128)(2,1)S(1)} %constant_dynamic-slice_fusion.protos.refs_9_, bf16[8,128,1024]{2,1,0:T(8,128)(2,1)S(1)} %bitcast.14, f32[8,1,1024]{2,1,0:T(1,128)S(1)} %constant_dynamic-update-slice_fusion.totals), custom_call_target="tpu_custom_call" | custom-call | flops 1000 | bytes 1000 | tf_op jit(solution)/shard_map/proto_first/pallas_call | solution.py:448
  96.4 9.5 %rowsum_last.1 = (f32[1,8192]{1,0:T(1,128)S(1)}, f32[1,1024]{1,0:T(1,128)S(1)}, f32[1024,128]{1,0:T(8,128)S(1)}) custom-call(bf16[1024,8192]{1,0:T(8,128)(2,1)} %copy-done, bf16[1024,8192]{1,0:T(8,128)(2,1)} %copy-done, bf16[1024,8192]{1,0:T(8,128)(2,1)} %copy-done, bf16[1024,8192]{1,0:T(8,128)(2,1)} %copy-done, f32[1,8192]{1,0:T(1,128)S(1)} %add.85.refs_4_, ...), custom_call_target="tpu_custom_call" | custom-call | flops 1000 | bytes 1000 | tf_op jit(solution)/shard_map/rowsum_last/pallas_call | solution.py:323
  105.9 1.6 collective-permute-start.23
  107.8 3.3 %proto_first.6 = (bf16[1024,2048]{1,0:T(8,128)(2,1)S(1)}, f32[1024,128]{1,0:T(8,128)S(1)}) custom-call(s32[1]{0:T(128)} %bitcast.1.place, bf16[1024,128]{1,0:T(8,128)(2,1)S(1)} %constant_dynamic-slice_fusion.protos.refs_9_, bf16[8,128,1024]{2,1,0:T(8,128)(2,1)S(1)} %bitcast.15, f32[8,1,1024]{2,1,0:T(1,128)S(1)} %constant_dynamic-update-slice_fusion.totals), custom_call_target="tpu_custom_call" | custom-call | flops 1000 | bytes 1000 | tf_op jit(solution)/shard_map/proto_first/pallas_call | solution.py:448
  112.6 2.2 %view_grad.1 = bf16[1024,128]{1,0:T(8,128)(2,1)S(1)} custom-call(f32[1024,128]{1,0:T(8,128)S(1)} %get-tuple-element.209.code, f32[1,1024]{1,0:T(1,128)S(1)} %get-tuple-element.210.tot, f32[1,1024]{1,0:T(1,128)S(1)} %get-tuple-element.211.total, f32[1024,128]{1,0:T(8,128)} %copy-done.5, f32[1024,128]{1,0:T(8,128)} %copy-done.6, f32[1024,128]{1,0:T(8,128)} %copy-done.7, ...), custom_call_target="tpu_custom_call" | custom-call | flops 1000 | bytes 1000 | tf_op jit(solution)/shard_map/view_grad/pallas_call | solution.py:567
  115.1 2.5 %collective-permute-start.27 = (f32[2,1,1024]{2,1,0:T(1,128)S(1)}, f32[2,1,1024]{2,1,0:T(1,128)S(1)}, u32[]{:S(2)}, u32[]{:S(2)}) collective-permute-start(f32[2,1,1024]{2,1,0:T(1,128)S(1)} %pad_maximum_fusion.4), channel_id=1, source_target_pairs={{0,16},{4,20},{8,24},{12,28},{16,0},{20,4},{24,8},{28,12},{1,17},{... | collective-permute-start | bytes 24584 | tf_op jit(solution)/shard_map/ppermute | solution.py:696
  117.6 1.9 collective-permute-start.28
  119.5 3.3 %proto_first.7 = (bf16[1024,2048]{1,0:T(8,128)(2,1)S(1)}, f32[1024,128]{1,0:T(8,128)S(1)}) custom-call(s32[1]{0:T(128)} %bitcast.1.place, bf16[1024,128]{1,0:T(8,128)(2,1)S(1)} %constant_dynamic-slice_fusion.protos.refs_9_, bf16[8,128,1024]{2,1,0:T(8,128)(2,1)S(1)} %bitcast.16, f32[8,1,1024]{2,1,0:T(1,128)S(1)} %constant_dynamic-update-slice_fusion.totals), custom_call_target="tpu_custom_call" | custom-call | flops 1000 | bytes 1000 | tf_op jit(solution)/shard_map/proto_first/pallas_call | solution.py:448
  124.6 5.4 %proto_last.1 = bf16[1024,128]{1,0:T(8,128)(2,1)} custom-call(s32[1]{0:T(128)} %bitcast.1.place, bf16[1024,2048]{1,0:T(8,128)(2,1)S(1)} %get-tuple-element.239.refs_0_, bf16[1024,2048]{1,0:T(8,128)(2,1)S(1)} %get-tuple-element.240.refs_1_, bf16[1024,2048]{1,0:T(8,128)(2,1)S(1)} %get-tuple-element.241.refs_2_, ...), custom_call_target="tpu_custom_call" | custom-call | tf_op jit(solution)/shard_map/proto_last/pallas_call | solution.py:498
  130.8 5.9 %backward.1 = f32[8,144,128]{2,1,0:T(8,128)S(1)} custom-call(s32[1]{0:T(128)} %bitcast.turn, bf16[1024,128]{1,0:T(8,128)(2,1)S(1)} %add_convert_fusion.grad_a, bf16[1024,128]{1,0:T(8,128)(2,1)S(1)} %collective-permute-done.30.grad_b, s32[1,1024]{1,0:T(1,128)S(1)} %get-tuple-element.252.pos, f32[1024,128]{1,0:T(8,128)} %get-tuple-element.253.raw, ...), custom_call_target="tpu_custom_call" | custom-call | tf_op jit(solution)/shard_map/backward/pallas_call | solution.py:631
  138.1 6.0 %collective-permute-done.31 = bf16[4,144,128]{2,1,0:T(8,128)(2,1)S(1)} collective-permute-done((bf16[4,144,128]{2,1,0:T(8,128)(2,1)S(1)}, bf16[4,144,128]{2,1,0:T(8,128)(2,1)S(1)}, u32[]{:S(2)}, u32[]{:S(2)}) %collective-permute-start.31) | collective-permute-done | bytes 147488 | tf_op jit(solution)/shard_map/ppermute | solution.py:696
  144.6 4.1 %collective-permute-start.34 = (bf16[1,144,128]{2,1,0:T(8,128)(2,1)S(1)}, bf16[1,144,128]{2,1,0:T(8,128)(2,1)S(1)}, u32[]{:S(2)}, u32[]{:S(2)}) collective-permute-start(bf16[1,144,128]{2,1,0:T(8,128)(2,1)S(1)} %get-tuple-element.264), channel_id=1, source_target_pairs={{0,24},{4,28},{8,16},{12,20},{16,8},{20,12},{24,0},{28,4},{1,25},{... | collective-permute-start | bytes 110600 | tf_op jit(solution)/shard_map/ppermute | solution.py:696
  149.7 3.0 %collective-permute-done.34 = bf16[1,144,128]{2,1,0:T(8,128)(2,1)S(1)} collective-permute-done((bf16[1,144,128]{2,1,0:T(8,128)(2,1)S(1)}, bf16[1,144,128]{2,1,0:T(8,128)(2,1)S(1)}, u32[]{:S(2)}, u32[]{:S(2)}) %collective-permute-start.34) | collective-permute-done | bytes 36896 | tf_op jit(solution)/shard_map/ppermute | solution.py:696
  152.8 2.3 %collective-permute-start.35 = (bf16[1,144,128]{2,1,0:T(8,128)(2,1)S(1)}, bf16[1,144,128]{2,1,0:T(8,128)(2,1)S(1)}, u32[]{:S(2)}, u32[]{:S(2)}) collective-permute-start(bf16[1,144,128]{2,1,0:T(8,128)(2,1)S(1)} %get-tuple-element.260), channel_id=1, source_target_pairs={{0,8},{4,12},{8,0},{12,4},{16,24},{20,28},{24,16},{28,20},{1,9},{5... | collective-permute-start | bytes 110600 | tf_op jit(solution)/shard_map/ppermute | solution.py:696
  155.5 2.0 %collective-permute-start.37 = (bf16[1,144,128]{2,1,0:T(8,128)(2,1)S(1)}, bf16[1,144,128]{2,1,0:T(8,128)(2,1)S(1)}, u32[]{:S(2)}, u32[]{:S(2)}) collective-permute-start(bf16[1,144,128]{2,1,0:T(8,128)(2,1)S(1)} %get-tuple-element.260), channel_id=1, source_target_pairs={{0,24},{4,28},{8,16},{12,20},{16,8},{20,12},{24,0},{28,4},{1,25},{... | collective-permute-start | bytes 110600 | tf_op jit(solution)/shard_map/ppermute | solution.py:696
  157.6 2.4 %collective-permute-done.36 = bf16[1,144,128]{2,1,0:T(8,128)(2,1)S(1)} collective-permute-done((bf16[1,144,128]{2,1,0:T(8,128)(2,1)S(1)}, bf16[1,144,128]{2,1,0:T(8,128)(2,1)S(1)}, u32[]{:S(2)}, u32[]{:S(2)}) %collective-permute-start.36) | collective-permute-done | bytes 36896 | tf_op jit(solution)/shard_map/ppermute | solution.py:696
  161.3 2.0 %collective-permute-start.38 = (bf16[4,144,128]{2,1,0:T(8,128)(2,1)S(1)}, bf16[4,144,128]{2,1,0:T(8,128)(2,1)S(1)}, u32[]{:S(2)}, u32[]{:S(2)}) collective-permute-start(bf16[4,144,128]{2,1,0:T(8,128)(2,1)S(1)} %pad_maximum_fusion.1), channel_id=1, source_target_pairs={{0,4},{4,0},{8,12},{12,8},{16,20},{20,16},{24,28},{28,24},{1,5},{5... | collective-permute-start | bytes 442376 | tf_op jit(solution)/shard_map/ppermute | solution.py:696
  163.4 6.3 %collective-permute-done.38 = bf16[4,144,128]{2,1,0:T(8,128)(2,1)S(1)} collective-permute-done((bf16[4,144,128]{2,1,0:T(8,128)(2,1)S(1)}, bf16[4,144,128]{2,1,0:T(8,128)(2,1)S(1)}, u32[]{:S(2)}, u32[]{:S(2)}) %collective-permute-start.38) | collective-permute-done | bytes 147488 | tf_op jit(solution)/shard_map/ppermute | solution.py:696
  169.7 1.6 collective-permute-start.39
  171.3 5.1 %collective-permute-done.39 = bf16[1,8,144,128]{3,2,1,0:T(8,128)(2,1)S(1)} collective-permute-done((bf16[1,8,144,128]{3,2,1,0:T(8,128)(2,1)S(1)}, bf16[1,8,144,128]{3,2,1,0:T(8,128)(2,1)S(1)}, u32[]{:S(2)}, u32[]{:S(2)}) %collective-permute-start.39) | collective-permute-done | bytes 294944 | tf_op jit(solution)/shard_map/ppermute | solution.py:696
  176.7 1.9 collective-permute-done.40.refs_1_
  178.6 2.1 %unpack.1 = (f32[1024,512]{1,0:T(8,128)}, f32[512,128]{1,0:T(8,128)}) custom-call(s32[2]{0:T(128)S(1)} %pad_add_fusion.place, bf16[2,8,144,128]{3,2,1,0:T(8,128)(2,1)S(1)} %pad_maximum_fusion.refs_0_, bf16[2,8,144,128]{3,2,1,0:T(8,128)(2,1)S(1)} %collective-permute-done.40.refs_1_), custom_call_target="tpu_custom_call" | custom-call | tf_op jit(solution)/shard_map/unpack/pallas_call | solution.py:665
  180.7 3.3 %all-gather.4.cloned.1.call-done = bf16[8192,128]{1,0:T(8,128)(2,1)} async-done(((bf16[1024,128]{1,0:T(8,128)(2,1)}), bf16[8192,128]{1,0:T(8,128)(2,1)}) %all-gather.4.cloned.1.call-update) | async-done | bytes 2097168 | tf_op jit(solution)/shard_map/all_gather | solution.py:801
  184.0 3.9 %convert_element_type.51 = f32[8192,128]{1,0:T(8,128)} convert(bf16[8192,128]{1,0:T(8,128)(2,1)} %all-gather.4.cloned.1.call-done) | non-fusion elementwise | flops 1048576 | bytes 6291456 | tf_op jit(solution)/shard_map/convert_element_type | solution.py:834
  (111 shorter events, 21.4 us)
Async XLA Ops:
  7.2 7.6 %copy-start.1 = (bf16[8192,128]{1,0:T(8,128)(2,1)S(1)}, bf16[8192,128]{1,0:T(8,128)(2,1)}, u32[]{:S(2)}) copy-start(bf16[8192,128]{1,0:T(8,128)(2,1)} %protos.3) | copy-start | bytes 6291460
  7.2 75.4 %all-gather.6.cloned.1.call-start = ((), (), s32[]{:S(2)}) async-start(), calls=%async_computation.1 | async-start | bytes 2359296 | tf_op jit(solution)/shard_map/all_gather | solution.py:717
  14.7 169.3 %all-gather.4.cloned.1.call-start = ((), (), s32[]{:S(2)}) async-start(), calls=%async_computation | async-start | bytes 2359296 | tf_op jit(solution)/shard_map/all_gather | solution.py:801
  25.8 54.4 %copy-start = (bf16[1024,8192]{1,0:T(8,128)(2,1)}, bf16[1024,8192]{1,0:T(8,128)(2,1)S(1)}, u32[]{:S(2)}) copy-start(bf16[1024,8192]{1,0:T(8,128)(2,1)S(1)} %get-tuple-element.134.expo.refs_0_.refs_1_.refs_2_.refs_3_) | copy-start | bytes 50331652
  25.8 6.5 %collective-permute-start = (f32[1,8192]{1,0:T(1,128)S(1)}, f32[1,8192]{1,0:T(1,128)S(1)}, u32[]{:S(2)}, u32[]{:S(2)}) collective-permute-start(f32[1,8192]{1,0:T(1,128)S(1)} %get-tuple-element.135), channel_id=1, source_target_pairs={{0,4},{4,0},{8,12},{12,8},{16,20},{20,16},{24,28},{28,24},{1,5},{5... | collective-permute-start | bytes 98312 | tf_op jit(solution)/shard_map/ppermute | solution.py:696
  32.3 14.1 %copy-start.5 = (f32[1024,128]{1,0:T(8,128)}, f32[1024,128]{1,0:T(8,128)S(1)}, u32[]{:S(2)}) copy-start(f32[1024,128]{1,0:T(8,128)S(1)} %view_soft.4.refs_0_) | copy-start | bytes 1572868
  32.4 8.0 %collective-permute-start.1 = (f32[1,8192]{1,0:T(1,128)S(1)}, f32[1,8192]{1,0:T(1,128)S(1)}, u32[]{:S(2)}, u32[]{:S(2)}) collective-permute-start(f32[1,8192]{1,0:T(1,128)S(1)} %add.80.refs_0_), channel_id=1, source_target_pairs={{0,8},{4,12},{8,0},{12,4},{16,24},{20,28},{24,16},{28,20},{1,9},{5... | collective-permute-start | bytes 98312 | tf_op jit(solution)/shard_map/ppermute | solution.py:696
  34.0 6.8 %collective-permute-start.2 = (f32[1,8192]{1,0:T(1,128)S(1)}, f32[1,8192]{1,0:T(1,128)S(1)}, u32[]{:S(2)}, u32[]{:S(2)}) collective-permute-start(f32[1,8192]{1,0:T(1,128)S(1)} %add.80.refs_0_), channel_id=1, source_target_pairs={{0,16},{4,20},{8,24},{12,28},{16,0},{20,4},{24,8},{28,12},{1,17},{... | collective-permute-start | bytes 98312 | tf_op jit(solution)/shard_map/ppermute | solution.py:696
  36.6 5.7 %collective-permute-start.3 = (f32[1,8192]{1,0:T(1,128)S(1)}, f32[1,8192]{1,0:T(1,128)S(1)}, u32[]{:S(2)}, u32[]{:S(2)}) collective-permute-start(f32[1,8192]{1,0:T(1,128)S(1)} %add.80.refs_0_), channel_id=1, source_target_pairs={{0,24},{4,28},{8,16},{12,20},{16,8},{20,12},{24,0},{28,4},{1,25},{... | collective-permute-start | bytes 98312 | tf_op jit(solution)/shard_map/ppermute | solution.py:696
  46.4 5.5 %collective-permute-start.4 = (f32[2,1024]{1,0:T(2,128)S(1)}, f32[2,1024]{1,0:T(2,128)S(1)}, u32[]{:S(2)}, u32[]{:S(2)}) collective-permute-start(f32[2,1024]{1,0:T(2,128)S(1)} %pad_maximum_fusion.2), channel_id=1, source_target_pairs={{0,1},{1,0},{2,3},{3,2},{4,5},{5,4},{6,7},{7,6},{8,9},{9,8},{10,11... | collective-permute-start | bytes 24584 | tf_op jit(solution)/shard_map/ppermute | solution.py:696
  46.5 5.4 %collective-permute-start.5 = (f32[2,1024]{1,0:T(2,128)S(1)}, f32[2,1024]{1,0:T(2,128)S(1)}, u32[]{:S(2)}, u32[]{:S(2)}) collective-permute-start(f32[2,1024]{1,0:T(2,128)S(1)} %pad_maximum_fusion.2), channel_id=1, source_target_pairs={{0,2},{1,3},{2,0},{3,1},{4,6},{5,7},{6,4},{7,5},{8,10},{9,11},{10,... | collective-permute-start | bytes 24584 | tf_op jit(solution)/shard_map/ppermute | solution.py:696
  48.0 3.9 %collective-permute-start.6 = (f32[2,1024]{1,0:T(2,128)S(1)}, f32[2,1024]{1,0:T(2,128)S(1)}, u32[]{:S(2)}, u32[]{:S(2)}) collective-permute-start(f32[2,1024]{1,0:T(2,128)S(1)} %pad_maximum_fusion.2), channel_id=1, source_target_pairs={{0,3},{1,2},{2,1},{3,0},{4,7},{5,6},{6,5},{7,4},{8,11},{9,10},{10,... | collective-permute-start | bytes 24584 | tf_op jit(solution)/shard_map/ppermute | solution.py:696
  54.2 5.6 %collective-permute-start.8 = (f32[1,8192]{1,0:T(1,128)S(1)}, f32[1,8192]{1,0:T(1,128)S(1)}, u32[]{:S(2)}, u32[]{:S(2)}) collective-permute-start(f32[1,8192]{1,0:T(1,128)S(1)} %bitcast.20), channel_id=1, source_target_pairs={{0,4},{4,0},{8,12},{12,8},{16,20},{20,16},{24,28},{28,24},{1,5},{5... | collective-permute-start | bytes 98312 | tf_op jit(solution)/shard_map/ppermute | solution.py:696
  54.7 5.0 %collective-permute-start.7 = (f32[1,1,1024]{2,1,0:T(1,128)S(1)}, f32[1,1,1024]{2,1,0:T(1,128)S(1)}, u32[]{:S(2)}, u32[]{:S(2)}) collective-permute-start(f32[1,1,1024]{2,1,0:T(1,128)S(1)} %get-tuple-element.267), channel_id=1, source_target_pairs={{0,4},{4,0},{8,12},{12,8},{16,20},{20,16},{24,28},{28,24},{1,5},{5... | collective-permute-start | bytes 12296 | tf_op jit(solution)/shard_map/ppermute | solution.py:696
  59.7 10.0 %copy-start.8 = (f32[1024,128]{1,0:T(8,128)}, f32[1024,128]{1,0:T(8,128)S(1)}, u32[]{:S(2)}) copy-start(f32[1024,128]{1,0:T(8,128)S(1)} %view_soft.7.refs_3_) | copy-start | bytes 1572868
  59.8 6.3 %collective-permute-start.12 = (f32[1,8192]{1,0:T(1,128)S(1)}, f32[1,8192]{1,0:T(1,128)S(1)}, u32[]{:S(2)}, u32[]{:S(2)}) collective-permute-start(f32[1,8192]{1,0:T(1,128)S(1)} %bitcast_add_fusion.refs_0_), channel_id=1, source_target_pairs={{0,8},{4,12},{8,0},{12,4},{16,24},{20,28},{24,16},{28,20},{1,9},{5... | collective-permute-start | bytes 98312 | tf_op jit(solution)/shard_map/ppermute | solution.py:696
  59.9 9.8 %collective-permute-start.13 = (f32[1,8192]{1,0:T(1,128)S(1)}, f32[1,8192]{1,0:T(1,128)S(1)}, u32[]{:S(2)}, u32[]{:S(2)}) collective-permute-start(f32[1,8192]{1,0:T(1,128)S(1)} %bitcast_add_fusion.refs_0_), channel_id=1, source_target_pairs={{0,16},{4,20},{8,24},{12,28},{16,0},{20,4},{24,8},{28,12},{1,17},{... | collective-permute-start | bytes 98312 | tf_op jit(solution)/shard_map/ppermute | solution.py:696
  62.1 7.7 %collective-permute-start.14 = (f32[1,8192]{1,0:T(1,128)S(1)}, f32[1,8192]{1,0:T(1,128)S(1)}, u32[]{:S(2)}, u32[]{:S(2)}) collective-permute-start(f32[1,8192]{1,0:T(1,128)S(1)} %bitcast_add_fusion.refs_0_), channel_id=1, source_target_pairs={{0,24},{4,28},{8,16},{12,20},{16,8},{20,12},{24,0},{28,4},{1,25},{... | collective-permute-start | bytes 98312 | tf_op jit(solution)/shard_map/ppermute | solution.py:696
  64.3 6.7 %collective-permute-start.10 = (f32[2,1,1024]{2,1,0:T(1,128)S(1)}, f32[2,1,1024]{2,1,0:T(1,128)S(1)}, u32[]{:S(2)}, u32[]{:S(2)}) collective-permute-start(f32[2,1,1024]{2,1,0:T(1,128)S(1)} %pad_maximum_fusion.3), channel_id=1, source_target_pairs={{0,16},{4,20},{8,24},{12,28},{16,0},{20,4},{24,8},{28,12},{1,17},{... | collective-permute-start | bytes 24584 | tf_op jit(solution)/shard_map/ppermute | solution.py:696
  64.4 6.6 %collective-permute-start.11 = (f32[2,1,1024]{2,1,0:T(1,128)S(1)}, f32[2,1,1024]{2,1,0:T(1,128)S(1)}, u32[]{:S(2)}, u32[]{:S(2)}) collective-permute-start(f32[2,1,1024]{2,1,0:T(1,128)S(1)} %pad_maximum_fusion.3), channel_id=1, source_target_pairs={{0,24},{4,28},{8,16},{12,20},{16,8},{20,12},{24,0},{28,4},{1,25},{... | collective-permute-start | bytes 24584 | tf_op jit(solution)/shard_map/ppermute | solution.py:696
  66.1 4.9 %collective-permute-start.9 = (f32[2,1,1024]{2,1,0:T(1,128)S(1)}, f32[2,1,1024]{2,1,0:T(1,128)S(1)}, u32[]{:S(2)}, u32[]{:S(2)}) collective-permute-start(f32[2,1,1024]{2,1,0:T(1,128)S(1)} %pad_maximum_fusion.3), channel_id=1, source_target_pairs={{0,8},{4,12},{8,0},{12,4},{16,24},{20,28},{24,16},{28,20},{1,9},{5... | collective-permute-start | bytes 24584 | tf_op jit(solution)/shard_map/ppermute | solution.py:696
  75.1 5.1 %collective-permute-start.15 = (f32[1,1024]{1,0:T(1,128)S(1)}, f32[1,1024]{1,0:T(1,128)S(1)}, u32[]{:S(2)}, u32[]{:S(2)}) collective-permute-start(f32[1,1024]{1,0:T(1,128)S(1)} %get-tuple-element.163.refs_0_), channel_id=1, source_target_pairs={{0,1},{1,0},{2,3},{3,2},{4,5},{5,4},{6,7},{7,6},{8,9},{9,8},{10,11... | collective-permute-start | bytes 12296 | tf_op jit(solution)/shard_map/ppermute | solution.py:696
  75.1 5.1 %collective-permute-start.16 = (f32[1,1024]{1,0:T(1,128)S(1)}, f32[1,1024]{1,0:T(1,128)S(1)}, u32[]{:S(2)}, u32[]{:S(2)}) collective-permute-start(f32[1,1024]{1,0:T(1,128)S(1)} %get-tuple-element.163.refs_0_), channel_id=1, source_target_pairs={{0,2},{1,3},{2,0},{3,1},{4,6},{5,7},{6,4},{7,5},{8,10},{9,11},{10,... | collective-permute-start | bytes 12296 | tf_op jit(solution)/shard_map/ppermute | solution.py:696
  76.5 3.6 %collective-permute-start.17 = (f32[1,1024]{1,0:T(1,128)S(1)}, f32[1,1024]{1,0:T(1,128)S(1)}, u32[]{:S(2)}, u32[]{:S(2)}) collective-permute-start(f32[1,1024]{1,0:T(1,128)S(1)} %get-tuple-element.163.refs_0_), channel_id=1, source_target_pairs={{0,3},{1,2},{2,1},{3,0},{4,7},{5,6},{6,5},{7,4},{8,11},{9,10},{10,... | collective-permute-start | bytes 12296 | tf_op jit(solution)/shard_map/ppermute | solution.py:696
  82.6 5.6 %collective-permute-start.18 = (f32[1,8192]{1,0:T(1,128)S(1)}, f32[1,8192]{1,0:T(1,128)S(1)}, u32[]{:S(2)}, u32[]{:S(2)}) collective-permute-start(f32[1,8192]{1,0:T(1,128)S(1)} %bitcast.18), channel_id=1, source_target_pairs={{0,4},{4,0},{8,12},{12,8},{16,20},{20,16},{24,28},{28,24},{1,5},{5... | collective-permute-start | bytes 98312 | tf_op jit(solution)/shard_map/ppermute | solution.py:696
  88.2 7.7 %collective-permute-start.19 = (f32[1,8192]{1,0:T(1,128)S(1)}, f32[1,8192]{1,0:T(1,128)S(1)}, u32[]{:S(2)}, u32[]{:S(2)}) collective-permute-start(f32[1,8192]{1,0:T(1,128)S(1)} %add.85.refs_4_), channel_id=1, source_target_pairs={{0,8},{4,12},{8,0},{12,4},{16,24},{20,28},{24,16},{28,20},{1,9},{5... | collective-permute-start | bytes 98312 | tf_op jit(solution)/shard_map/ppermute | solution.py:696
  89.2 6.8 %collective-permute-start.20 = (f32[1,8192]{1,0:T(1,128)S(1)}, f32[1,8192]{1,0:T(1,128)S(1)}, u32[]{:S(2)}, u32[]{:S(2)}) collective-permute-start(f32[1,8192]{1,0:T(1,128)S(1)} %add.85.refs_4_), channel_id=1, source_target_pairs={{0,16},{4,20},{8,24},{12,28},{16,0},{20,4},{24,8},{28,12},{1,17},{... | collective-permute-start | bytes 98312 | tf_op jit(solution)/shard_map/ppermute | solution.py:696
  90.7 5.7 %collective-permute-start.21 = (f32[1,8192]{1,0:T(1,128)S(1)}, f32[1,8192]{1,0:T(1,128)S(1)}, u32[]{:S(2)}, u32[]{:S(2)}) collective-permute-start(f32[1,8192]{1,0:T(1,128)S(1)} %add.85.refs_4_), channel_id=1, source_target_pairs={{0,24},{4,28},{8,16},{12,20},{16,8},{20,12},{24,0},{28,4},{1,25},{... | collective-permute-start | bytes 98312 | tf_op jit(solution)/shard_map/ppermute | solution.py:696
  96.4 11.4 %copy-start.3 = (bf16[1024,1024]{1,0:T(8,128)(2,1)S(1)}, bf16[1024,1024]{1,0:T(8,128)(2,1)}, u32[]{:S(2)}) copy-start(bf16[1024,1024]{1,0:T(8,128)(2,1)} %all-gather.6.cloned.1.call-done) | copy-start | bytes 6291460
  105.8 5.2 %collective-permute-start.22 = (f32[1,1024]{1,0:T(1,128)S(1)}, f32[1,1024]{1,0:T(1,128)S(1)}, u32[]{:S(2)}, u32[]{:S(2)}) collective-permute-start(f32[1,1024]{1,0:T(1,128)S(1)} %get-tuple-element.194), channel_id=1, source_target_pairs={{0,1},{1,0},{2,3},{3,2},{4,5},{5,4},{6,7},{7,6},{8,9},{9,8},{10,11... | collective-permute-start | bytes 12296 | tf_op jit(solution)/shard_map/ppermute | solution.py:696
  105.9 5.1 %collective-permute-start.23 = (f32[1,1024]{1,0:T(1,128)S(1)}, f32[1,1024]{1,0:T(1,128)S(1)}, u32[]{:S(2)}, u32[]{:S(2)}) collective-permute-start(f32[1,1024]{1,0:T(1,128)S(1)} %get-tuple-element.194), channel_id=1, source_target_pairs={{0,2},{1,3},{2,0},{3,1},{4,6},{5,7},{6,4},{7,5},{8,10},{9,11},{10,... | collective-permute-start | bytes 12296 | tf_op jit(solution)/shard_map/ppermute | solution.py:696
  107.5 3.6 %collective-permute-start.24 = (f32[1,1024]{1,0:T(1,128)S(1)}, f32[1,1024]{1,0:T(1,128)S(1)}, u32[]{:S(2)}, u32[]{:S(2)}) collective-permute-start(f32[1,1024]{1,0:T(1,128)S(1)} %get-tuple-element.194), channel_id=1, source_target_pairs={{0,3},{1,2},{2,1},{3,0},{4,7},{5,6},{6,5},{7,4},{8,11},{9,10},{10,... | collective-permute-start | bytes 12296 | tf_op jit(solution)/shard_map/ppermute | solution.py:696
  111.1 3.7 %collective-permute-start.25 = (f32[1,1,1024]{2,1,0:T(1,128)S(1)}, f32[1,1,1024]{2,1,0:T(1,128)S(1)}, u32[]{:S(2)}, u32[]{:S(2)}) collective-permute-start(f32[1,1,1024]{2,1,0:T(1,128)S(1)} %bitcast.21), channel_id=1, source_target_pairs={{0,4},{4,0},{8,12},{12,8},{16,20},{20,16},{24,28},{28,24},{1,5},{5... | collective-permute-start | bytes 12296 | tf_op jit(solution)/shard_map/ppermute | solution.py:696
  114.8 8.2 %collective-permute-start.29 = (bf16[1024,128]{1,0:T(8,128)(2,1)S(1)}, bf16[1024,128]{1,0:T(8,128)(2,1)S(1)}, u32[]{:S(2)}, u32[]{:S(2)}) collective-permute-start(bf16[1024,128]{1,0:T(8,128)(2,1)S(1)} %view_grad.1), channel_id=1, source_target_pairs={{0,1},{1,0},{2,3},{3,2},{4,5},{5,4},{6,7},{7,6},{8,9},{9,8},{10,11... | collective-permute-start | bytes 786440 | tf_op jit(solution)/shard_map/ppermute | solution.py:696
  115.0 7.7 %collective-permute-start.26 = (f32[2,1,1024]{2,1,0:T(1,128)S(1)}, f32[2,1,1024]{2,1,0:T(1,128)S(1)}, u32[]{:S(2)}, u32[]{:S(2)}) collective-permute-start(f32[2,1,1024]{2,1,0:T(1,128)S(1)} %pad_maximum_fusion.4), channel_id=1, source_target_pairs={{0,8},{4,12},{8,0},{12,4},{16,24},{20,28},{24,16},{28,20},{1,9},{5... | collective-permute-start | bytes 24584 | tf_op jit(solution)/shard_map/ppermute | solution.py:696
  115.1 7.7 %collective-permute-start.27 = (f32[2,1,1024]{2,1,0:T(1,128)S(1)}, f32[2,1,1024]{2,1,0:T(1,128)S(1)}, u32[]{:S(2)}, u32[]{:S(2)}) collective-permute-start(f32[2,1,1024]{2,1,0:T(1,128)S(1)} %pad_maximum_fusion.4), channel_id=1, source_target_pairs={{0,16},{4,20},{8,24},{12,28},{16,0},{20,4},{24,8},{28,12},{1,17},{... | collective-permute-start | bytes 24584 | tf_op jit(solution)/shard_map/ppermute | solution.py:696
  117.6 5.4 %collective-permute-start.28 = (f32[2,1,1024]{2,1,0:T(1,128)S(1)}, f32[2,1,1024]{2,1,0:T(1,128)S(1)}, u32[]{:S(2)}, u32[]{:S(2)}) collective-permute-start(f32[2,1,1024]{2,1,0:T(1,128)S(1)} %pad_maximum_fusion.4), channel_id=1, source_target_pairs={{0,24},{4,28},{8,16},{12,20},{16,8},{20,12},{24,0},{28,4},{1,25},{... | collective-permute-start | bytes 24584 | tf_op jit(solution)/shard_map/ppermute | solution.py:696
  123.1 7.6 %collective-permute-start.30 = (bf16[1024,128]{1,0:T(8,128)(2,1)S(1)}, bf16[1024,128]{1,0:T(8,128)(2,1)S(1)}, u32[]{:S(2)}, u32[]{:S(2)}) collective-permute-start(bf16[1024,128]{1,0:T(8,128)(2,1)S(1)} %add_convert_fusion.grad_a), channel_id=1, source_target_pairs={{0,2},{1,3},{2,0},{3,1},{4,6},{5,7},{6,4},{7,5},{8,10},{9,11},{10,... | collective-permute-start | bytes 786440 | tf_op jit(solution)/shard_map/ppermute | solution.py:696
  136.7 7.4 %collective-permute-start.31 = (bf16[4,144,128]{2,1,0:T(8,128)(2,1)S(1)}, bf16[4,144,128]{2,1,0:T(8,128)(2,1)S(1)}, u32[]{:S(2)}, u32[]{:S(2)}) collective-permute-start(bf16[4,144,128]{2,1,0:T(8,128)(2,1)S(1)} %dynamic-slice_convert_fusion), channel_id=1, source_target_pairs={{0,4},{4,0},{8,12},{12,8},{16,20},{20,16},{24,28},{28,24},{1,5},{5... | collective-permute-start | bytes 442376 | tf_op jit(solution)/shard_map/ppermute | solution.py:696
  144.2 4.8 %collective-permute-start.32 = (bf16[1,144,128]{2,1,0:T(8,128)(2,1)S(1)}, bf16[1,144,128]{2,1,0:T(8,128)(2,1)S(1)}, u32[]{:S(2)}, u32[]{:S(2)}) collective-permute-start(bf16[1,144,128]{2,1,0:T(8,128)(2,1)S(1)} %get-tuple-element.263), channel_id=1, source_target_pairs={{0,8},{4,12},{8,0},{12,4},{16,24},{20,28},{24,16},{28,20},{1,9},{5... | collective-permute-start | bytes 110600 | tf_op jit(solution)/shard_map/ppermute | solution.py:696
  144.3 5.5 %collective-permute-start.33 = (bf16[1,144,128]{2,1,0:T(8,128)(2,1)S(1)}, bf16[1,144,128]{2,1,0:T(8,128)(2,1)S(1)}, u32[]{:S(2)}, u32[]{:S(2)}) collective-permute-start(bf16[1,144,128]{2,1,0:T(8,128)(2,1)S(1)} %get-tuple-element.265), channel_id=1, source_target_pairs={{0,16},{4,20},{8,24},{12,28},{16,0},{20,4},{24,8},{28,12},{1,17},{... | collective-permute-start | bytes 110600 | tf_op jit(solution)/shard_map/ppermute | solution.py:696
  144.6 8.2 %collective-permute-start.34 = (bf16[1,144,128]{2,1,0:T(8,128)(2,1)S(1)}, bf16[1,144,128]{2,1,0:T(8,128)(2,1)S(1)}, u32[]{:S(2)}, u32[]{:S(2)}) collective-permute-start(bf16[1,144,128]{2,1,0:T(8,128)(2,1)S(1)} %get-tuple-element.264), channel_id=1, source_target_pairs={{0,24},{4,28},{8,16},{12,20},{16,8},{20,12},{24,0},{28,4},{1,25},{... | collective-permute-start | bytes 110600 | tf_op jit(solution)/shard_map/ppermute | solution.py:696
  152.8 4.8 %collective-permute-start.35 = (bf16[1,144,128]{2,1,0:T(8,128)(2,1)S(1)}, bf16[1,144,128]{2,1,0:T(8,128)(2,1)S(1)}, u32[]{:S(2)}, u32[]{:S(2)}) collective-permute-start(bf16[1,144,128]{2,1,0:T(8,128)(2,1)S(1)} %get-tuple-element.260), channel_id=1, source_target_pairs={{0,8},{4,12},{8,0},{12,4},{16,24},{20,28},{24,16},{28,20},{1,9},{5... | collective-permute-start | bytes 110600 | tf_op jit(solution)/shard_map/ppermute | solution.py:696
  155.1 4.9 %collective-permute-start.36 = (bf16[1,144,128]{2,1,0:T(8,128)(2,1)S(1)}, bf16[1,144,128]{2,1,0:T(8,128)(2,1)S(1)}, u32[]{:S(2)}, u32[]{:S(2)}) collective-permute-start(bf16[1,144,128]{2,1,0:T(8,128)(2,1)S(1)} %get-tuple-element.260), channel_id=1, source_target_pairs={{0,16},{4,20},{8,24},{12,28},{16,0},{20,4},{24,8},{28,12},{1,17},{... | collective-permute-start | bytes 110600 | tf_op jit(solution)/shard_map/ppermute | solution.py:696
  155.5 5.8 %collective-permute-start.37 = (bf16[1,144,128]{2,1,0:T(8,128)(2,1)S(1)}, bf16[1,144,128]{2,1,0:T(8,128)(2,1)S(1)}, u32[]{:S(2)}, u32[]{:S(2)}) collective-permute-start(bf16[1,144,128]{2,1,0:T(8,128)(2,1)S(1)} %get-tuple-element.260), channel_id=1, source_target_pairs={{0,24},{4,28},{8,16},{12,20},{16,8},{20,12},{24,0},{28,4},{1,25},{... | collective-permute-start | bytes 110600 | tf_op jit(solution)/shard_map/ppermute | solution.py:696
  161.3 8.3 %collective-permute-start.38 = (bf16[4,144,128]{2,1,0:T(8,128)(2,1)S(1)}, bf16[4,144,128]{2,1,0:T(8,128)(2,1)S(1)}, u32[]{:S(2)}, u32[]{:S(2)}) collective-permute-start(bf16[4,144,128]{2,1,0:T(8,128)(2,1)S(1)} %pad_maximum_fusion.1), channel_id=1, source_target_pairs={{0,4},{4,0},{8,12},{12,8},{16,20},{20,16},{24,28},{28,24},{1,5},{5... | collective-permute-start | bytes 442376 | tf_op jit(solution)/shard_map/ppermute | solution.py:696
  169.7 6.8 %collective-permute-start.39 = (bf16[1,8,144,128]{3,2,1,0:T(8,128)(2,1)S(1)}, bf16[1,8,144,128]{3,2,1,0:T(8,128)(2,1)S(1)}, u32[]{:S(2)}, u32[]{:S(2)}) collective-permute-start(bf16[1,8,144,128]{3,2,1,0:T(8,128)(2,1)S(1)} %bitcast.23), channel_id=1, source_target_pairs={{0,2},{1,3},{2,0},{3,1},{4,6},{5,7},{6,4},{7,5},{8,10},{9,11},{10,... | collective-permute-start | bytes 884744 | tf_op jit(solution)/shard_map/ppermute | solution.py:696
  176.5 2.1 %collective-permute-start.40 = (bf16[2,8,144,128]{3,2,1,0:T(8,128)(2,1)S(1)}, bf16[2,8,144,128]{3,2,1,0:T(8,128)(2,1)S(1)}, u32[]{:S(2)}, u32[]{:S(2)}) collective-permute-start(bf16[2,8,144,128]{3,2,1,0:T(8,128)(2,1)S(1)} %pad_maximum_fusion.refs_0_), channel_id=1, source_target_pairs={{0,1},{1,0},{2,3},{3,2},{4,5},{5,4},{6,7},{7,6},{8,9},{9,8},{10,11... | collective-permute-start | bytes 1769480 | tf_op jit(solution)/shard_map/ppermute | solution.py:696
  (4 other events, 11.3 us)
Sparse Core Ops, SparseCore 0:
  14.8 58.2 all-gather.5
  130.9 53.1 all-gather.3

commit v9 on v8

--- a/solution.py
+++ b/solution.py
@@ -414,17 +414,23 @@
 
 
 def proto_first_kernel(chunk, tile, lead, place, protos, views, totals, expo, grad, *scratch):
-    weights, twice, pair, stage, soft16, acc = scratch
+    weights, twice, pair, stage, soft16, acc, near, arrived = scratch
     count = expo.shape[1] // views.shape[2]
     _, depth, rows = views.shape
     width = protos.shape[0]
+    copies = [
+        pltpu.make_async_copy(views.at[lead + n], near.at[n], arrived.at[n]) for n in range(count)
+    ]
+    for copy in copies:
+        copy.start()
     _, _, unit = unit_of(protos[...])
     pair[...] = scaled_pair(unit.astype(bf16), 1)
     for n in range(count):
-        k = lead + n
-        weights[...] = (views[k].astype(f32) * (GRAD_SCALE / totals[place[0] ^ k])).astype(bf16)
-        twice[:depth, :] = views[k]
-        twice[depth:, :] = views[k]
+        copies[n].wait()
+        total = totals[place[0] ^ (lead + n)]
+        weights[...] = (near[n].astype(f32) * (GRAD_SCALE / total)).astype(bf16)
+        twice[:depth, :] = near[n]
+        twice[depth:, :] = near[n]
         for c in range(width // chunk):
             stage[c % 2] = dot(pair[c * chunk : (c + 1) * chunk, :], twice[...])
             for start in range(0, chunk, tile):
@@ -447,7 +453,12 @@
     tile = min(16, chunk)
     return pl.pallas_call(
         functools.partial(proto_first_kernel, chunk, tile, lead),
-        in_specs=[pl.BlockSpec(memory_space=pltpu.SMEM)] + [WHOLE] * 3,
+        in_specs=[
+            pl.BlockSpec(memory_space=pltpu.SMEM),
+            WHOLE,
+            pl.BlockSpec(memory_space=pl.ANY),
+            WHOLE,
+        ],
         out_specs=[WHOLE] * 2,
         out_shape=[
             pltpu.VMEM((width, count * rows), bf16),
@@ -460,11 +471,13 @@
             pltpu.VMEM((2, chunk, rows), f32),
             pltpu.VMEM((width, rows), bf16),
             pltpu.VMEM((width, depth), f32),
+            pltpu.VMEM((count, depth, rows), bf16),
+            pltpu.SemaphoreType.DMA((count,)),
         ],
         compiler_params=params(),
         cost_estimate=SMALL,
         name="proto_first",
-    )(place, protos, views, totals)
+    )(place, protos, in_hbm(views), totals)
 
 
 def proto_last_kernel(groups, place, *refs):
@@ -670,6 +683,46 @@
         compiler_params=params(),
         name="unpack",
     )(place, *pieces)
+
+
+def widen_kernel(x, out, narrow, wide, came, went):
+    count, rows, _ = narrow.shape
+    ins = [
+        pltpu.make_async_copy(x.at[pl.ds(k * rows, rows)], narrow.at[k], came.at[k])
+        for k in range(count)
+    ]
+    outs = [
+        pltpu.make_async_copy(wide.at[k], out.at[pl.ds(k * rows, rows)], went.at[k])
+        for k in range(count)
+    ]
+    for copy in ins:
+        copy.start()
+    for k in range(count):
+        ins[k].wait()
+        wide[k] = narrow[k].astype(f32)
+        outs[k].start()
+    for copy in outs:
+        copy.wait()
+
+
+def widen(x):
+    rows, depth = x.shape
+    count = 8
+    block = rows // count
+    return pl.pallas_call(
+        widen_kernel,
+        in_specs=[pl.BlockSpec(memory_space=pl.ANY)],
+        out_specs=pl.BlockSpec(memory_space=pl.ANY),
+        out_shape=jax.ShapeDtypeStruct((rows, depth), f32),
+        scratch_shapes=[
+            pltpu.VMEM((count, block, depth), bf16),
+            pltpu.VMEM((count, block, depth), f32),
+            pltpu.SemaphoreType.DMA((count,)),
+            pltpu.SemaphoreType.DMA((count,)),
+        ],
+        compiler_params=params(),
+        name="widen",
+    )(in_hbm(x))
 
 
 def stages(size, first=1):
@@ -831,7 +884,7 @@
     grad_in, grad_out = unpack(
         order, order_b, places, pieces, (wide, hidden_n), (hidden_n, depth)
     )
-    return (grad_in, grad_out, grad_proto.astype(f32))
+    return (grad_in, grad_out, widen(grad_proto))
 
 
 def solution(mesh):

time: 195 us -> 195 us (level)
  Pallas kernels: 87 us -> 93.2 us
  other arithmetic: 4.32 us -> 0.45 us
    pallas_call x4, Pallas kernels: 13 us -> 17 us  [proto_first(): pl.pallas_call(functools.partial(proto_first_kernel, chunk, tile, lead),...]
    convert_element_type x1 -> x0, other arithmetic: 3.87 us -> none  [body(): return (grad_in, grad_out, grad_proto.astype(f32))]
    pallas_call x0 -> x1, Pallas kernels: none -> 3.12 us  [widen(): pl.pallas_call(widen_kernel, in_specs=[pl.BlockSpec(memory_space=pl.ANY)]...]
  transfers between devices with their start and end apart: 43 -> 43, of which waited for: 16 -> 14; matrix products, arithmetic and copies ran while one was open for 0% -> 0% of each run, Pallas kernels for 36% -> 38%
where the time goes in v9:
time: 195 us
  Pallas kernels  93.2 us (48%)
  starting transfers between devices  50.3 us (26%)
  waiting for transfers between devices  35 us (18%)
  between operations  14.7 us (8%)
    ppermute x41, starting transfers between devices, flipped(): return lax.ppermute(x, axis, [(i, i ^ step) for i in range(size)])  50.2 us
    ppermute x41, waiting for transfers between devices, flipped(): return lax.ppermute(x, axis, [(i, i ^ step) for i in range(size)])  31.5 us
    pallas_call x4, Pallas kernels, proto_first(): pl.pallas_call(functools.partial(proto_first_kernel, chunk, tile, lead),...  17 us
    pallas_call x4, Pallas kernels, view_soft(): pl.pallas_call(functools.partial(view_soft_body, block, min(32, chunk), l...  13.8 us
    pallas_call x1, Pallas kernels, first_pass(): pl.pallas_call(functools.partial(first_kernel, block, chunk, tile), in_sp...  11 us
    pallas_call x1, Pallas kernels, rowsum_last(): pl.pallas_call(functools.partial(rowsum_last_kernel, pieces, len(parts)),...  9.34 us
    pallas_call x2, Pallas kernels, rowsum(): pl.pallas_call(functools.partial(rowsum_kernel, len(parts)), in_specs=[WH...  7.54 us
    pallas_call x1, Pallas kernels, head(): pl.pallas_call(head_kernel, grid=(steps,), in_specs=[pl.BlockSpec((block,...  7.41 us
  transfers between devices with their start and end apart: 43, of which 14 were waited for; matrix products, arithmetic and copies ran while one was open for 0% of the time, Pallas kernels for 38%

profile of v9, /device:TPU:0, one launch (start us, length us, event | category | flops | bytes accessed | tf_op | source)
XLA Modules:
  0.0 195.2 jit_solution(1462612893642319469)
XLA Ops:
  7.2 7.4 %head.1 = (f32[1024,512]{1,0:T(8,128)}, bf16[1024,512]{1,0:T(8,128)(2,1)}, f32[1024,128]{1,0:T(8,128)}, bf16[1024,128]{1,0:T(8,128)(2,1)S(1)}, bf16[128,1024]{1,0:T(8,128)(2,1)}, /*index=5*/s32[1,1024]{1,0:T(1,128)S(1)}) custom-call(bf16[1024,1024]{1,0:T(8,128)(2,1)} %emb.3, s32[1,1024]{1,0:T(1,128)} %bitcast.25, bf16[1024,512]{1,0:T(8,128)(2,1)} %w_in.1, ...), custom_call_target="tpu_custom_call" | custom-call | tf_op jit(solution)/shard_map/head/pallas_call | solution.py:105
  14.8 11.0 %first_pass.1 = (bf16[1024,8192]{1,0:T(8,128)(2,1)S(1)}, f32[1,8192]{1,0:T(1,128)S(1)}, f32[1,1024]{1,0:T(1,128)S(1)}) custom-call(bf16[1024,128]{1,0:T(8,128)(2,1)S(1)} %get-tuple-element.151.views.refs_0_, bf16[8192,128]{1,0:T(8,128)(2,1)S(1)} %copy-done.1), custom_call_target="tpu_custom_call" | custom-call | flops 1000 | bytes 1000 | tf_op jit(solution)/shard_map/first_pass/pallas_call | solution.py:190
  25.8 3.0 %collective-permute-start = (f32[1,8192]{1,0:T(1,128)S(1)}, f32[1,8192]{1,0:T(1,128)S(1)}, u32[]{:S(2)}, u32[]{:S(2)}) collective-permute-start(f32[1,8192]{1,0:T(1,128)S(1)} %get-tuple-element.135), channel_id=1, source_target_pairs={{0,4},{4,0},{8,12},{12,8},{16,20},{20,16},{24,28},{28,24},{1,5},{5... | collective-permute-start | bytes 98312 | tf_op jit(solution)/shard_map/ppermute | solution.py:749
  28.8 3.5 %view_soft.4.refs_0_ = f32[1024,128]{1,0:T(8,128)S(1)} custom-call(bf16[1024,128]{1,0:T(8,128)(2,1)S(1)} %get-tuple-element.151.views.refs_0_, bf16[8192,128]{1,0:T(8,128)(2,1)S(1)} %copy-done.1), custom_call_target="tpu_custom_call" | custom-call | flops 1000 | bytes 1000 | tf_op jit(solution)/shard_map/view_soft/pallas_call | solution.py:552
  32.4 1.6 collective-permute-start.1
  34.0 2.6 %collective-permute-start.2 = (f32[1,8192]{1,0:T(1,128)S(1)}, f32[1,8192]{1,0:T(1,128)S(1)}, u32[]{:S(2)}, u32[]{:S(2)}) collective-permute-start(f32[1,8192]{1,0:T(1,128)S(1)} %add.80.refs_0_), channel_id=1, source_target_pairs={{0,16},{4,20},{8,24},{12,28},{16,0},{20,4},{24,8},{28,12},{1,17},{... | collective-permute-start | bytes 98312 | tf_op jit(solution)/shard_map/ppermute | solution.py:749
  36.8 3.5 %view_soft.5.refs_1_ = f32[1024,128]{1,0:T(8,128)S(1)} custom-call(bf16[1024,128]{1,0:T(8,128)(2,1)S(1)} %get-tuple-element.151.views.refs_0_, bf16[8192,128]{1,0:T(8,128)(2,1)S(1)} %copy-done.1), custom_call_target="tpu_custom_call" | custom-call | flops 1000 | bytes 1000 | tf_op jit(solution)/shard_map/view_soft/pallas_call | solution.py:552
  42.3 3.8 %rowsum.2 = (f32[1,8192]{1,0:T(1,128)}, f32[1,1024]{1,0:T(1,128)S(1)}) custom-call(bf16[1024,8192]{1,0:T(8,128)(2,1)S(1)} %get-tuple-element.134.expo.refs_0_.refs_1_.refs_2_.refs_3_, f32[1,8192]{1,0:T(1,128)S(1)} %add.80.refs_0_, f32[1,8192]{1,0:T(1,128)S(1)} %collective-permute-done.1.refs_1_, f32[1,8192]{1,0:T(1,128)S(1)} %collective-permute-done.2.refs_2_, ...), custom_call_target="tpu_custom_call" | custom-call | flops 1000 | bytes 1000 | tf_op jit(solution)/shard_map/rowsum/pallas_call | solution.py:264
  48.0 3.5 %view_soft.6.refs_2_ = f32[1024,128]{1,0:T(8,128)S(1)} custom-call(bf16[1024,128]{1,0:T(8,128)(2,1)S(1)} %get-tuple-element.151.views.refs_0_, bf16[8192,128]{1,0:T(8,128)(2,1)S(1)} %copy-done.1), custom_call_target="tpu_custom_call" | custom-call | flops 1000 | bytes 1000 | tf_op jit(solution)/shard_map/view_soft/pallas_call | solution.py:552
  51.6 2.2 %colsum.2 = f32[1,1,8192]{2,1,0:T(1,128)S(1)} custom-call(bf16[1024,8192]{1,0:T(8,128)(2,1)S(1)} %get-tuple-element.134.expo.refs_0_.refs_1_.refs_2_.refs_3_, f32[1,1024]{1,0:T(1,128)S(1)} %get-tuple-element.268.refs_0_), custom_call_target="tpu_custom_call" | custom-call | flops 1000 | bytes 1000 | tf_op jit(solution)/shard_map/colsum/pallas_call | solution.py:404
  55.9 3.5 %view_soft.7.refs_3_ = f32[1024,128]{1,0:T(8,128)S(1)} custom-call(bf16[1024,128]{1,0:T(8,128)(2,1)S(1)} %get-tuple-element.151.views.refs_0_, bf16[8192,128]{1,0:T(8,128)(2,1)S(1)} %copy-done.1), custom_call_target="tpu_custom_call" | custom-call | flops 1000 | bytes 1000 | tf_op jit(solution)/shard_map/view_soft/pallas_call | solution.py:552
  59.5 2.2 %collective-permute-start.13 = (f32[1,8192]{1,0:T(1,128)S(1)}, f32[1,8192]{1,0:T(1,128)S(1)}, u32[]{:S(2)}, u32[]{:S(2)}) collective-permute-start(f32[1,8192]{1,0:T(1,128)S(1)} %bitcast_add_fusion.refs_0_), channel_id=1, source_target_pairs={{0,16},{4,20},{8,24},{12,28},{16,0},{20,4},{24,8},{28,12},{1,17},{... | collective-permute-start | bytes 98312 | tf_op jit(solution)/shard_map/ppermute | solution.py:749
  61.7 2.2 %collective-permute-start.14 = (f32[1,8192]{1,0:T(1,128)S(1)}, f32[1,8192]{1,0:T(1,128)S(1)}, u32[]{:S(2)}, u32[]{:S(2)}) collective-permute-start(f32[1,8192]{1,0:T(1,128)S(1)} %bitcast_add_fusion.refs_0_), channel_id=1, source_target_pairs={{0,24},{4,28},{8,16},{12,20},{16,8},{20,12},{24,0},{28,4},{1,25},{... | collective-permute-start | bytes 98312 | tf_op jit(solution)/shard_map/ppermute | solution.py:749
  64.0 1.7 collective-permute-start.11
  65.7 1.8 collective-permute-start.9
  67.5 1.9 unit_t.2.refs_0_
  70.6 3.8 %rowsum.3 = (f32[1,8192]{1,0:T(1,128)}, f32[1,1024]{1,0:T(1,128)S(1)}) custom-call(bf16[1024,8192]{1,0:T(8,128)(2,1)S(1)} %get-tuple-element.134.expo.refs_0_.refs_1_.refs_2_.refs_3_, f32[1,8192]{1,0:T(1,128)S(1)} %bitcast_add_fusion.refs_0_, f32[1,8192]{1,0:T(1,128)S(1)} %collective-permute-done.12.refs_1_, f32[1,8192]{1,0:T(1,128)S(1)} %collective-permute-done.13.refs_2_, ...), custom_call_target="tpu_custom_call" | custom-call | flops 1000 | bytes 1000 | tf_op jit(solution)/shard_map/rowsum/pallas_call | solution.py:264
  76.3 1.9 unit_t.3.refs_8_
  79.5 2.4 %colsum.3 = f32[1,1,8192]{2,1,0:T(1,128)S(1)} custom-call(bf16[1024,8192]{1,0:T(8,128)(2,1)S(1)} %get-tuple-element.134.expo.refs_0_.refs_1_.refs_2_.refs_3_, f32[1,1024]{1,0:T(1,128)S(1)} %get-tuple-element.163.refs_0_, f32[1,1024]{1,0:T(1,128)S(1)} %collective-permute-done.15.refs_1_, f32[1,1024]{1,0:T(1,128)S(1)} %collective-permute-done.16.refs_2_, ...), custom_call_target="tpu_custom_call" | custom-call | flops 1000 | bytes 1000 | tf_op jit(solution)/shard_map/colsum/pallas_call | solution.py:404
  82.3 4.3 %proto_first.4 = (bf16[1024,2048]{1,0:T(8,128)(2,1)S(1)}, f32[1024,128]{1,0:T(8,128)S(1)}) custom-call(s32[1]{0:T(128)} %bitcast.1.place, bf16[1024,128]{1,0:T(8,128)(2,1)S(1)} %constant_dynamic-slice_fusion.protos.refs_9_, bf16[8,128,1024]{2,1,0:T(8,128)(2,1)} %bitcast.13, f32[8,1,1024]{2,1,0:T(1,128)S(1)} %constant_dynamic-update-slice_fusion.totals), custom_call_target="tpu_custom_call" | custom-call | flops 1000 | bytes 1000 | tf_op jit(solution)/shard_map/proto_first/pallas_call | solution.py:454
  87.8 1.8 collective-permute-start.20
  89.6 1.6 collective-permute-start.21
  91.2 4.2 %proto_first.5 = (bf16[1024,2048]{1,0:T(8,128)(2,1)S(1)}, f32[1024,128]{1,0:T(8,128)S(1)}) custom-call(s32[1]{0:T(128)} %bitcast.1.place, bf16[1024,128]{1,0:T(8,128)(2,1)S(1)} %constant_dynamic-slice_fusion.protos.refs_9_, bf16[8,128,1024]{2,1,0:T(8,128)(2,1)} %bitcast.14, f32[8,1,1024]{2,1,0:T(1,128)S(1)} %constant_dynamic-update-slice_fusion.totals), custom_call_target="tpu_custom_call" | custom-call | flops 1000 | bytes 1000 | tf_op jit(solution)/shard_map/proto_first/pallas_call | solution.py:454
  95.5 9.3 %rowsum_last.1 = (f32[1,8192]{1,0:T(1,128)S(1)}, f32[1,1024]{1,0:T(1,128)S(1)}, f32[1024,128]{1,0:T(8,128)S(1)}) custom-call(bf16[1024,8192]{1,0:T(8,128)(2,1)} %copy-done, bf16[1024,8192]{1,0:T(8,128)(2,1)} %copy-done, bf16[1024,8192]{1,0:T(8,128)(2,1)} %copy-done, bf16[1024,8192]{1,0:T(8,128)(2,1)} %copy-done, f32[1,8192]{1,0:T(1,128)S(1)} %add.85.refs_4_, ...), custom_call_target="tpu_custom_call" | custom-call | flops 1000 | bytes 1000 | tf_op jit(solution)/shard_map/rowsum_last/pallas_call | solution.py:323
  104.9 1.6 collective-permute-start.23
  106.7 4.2 %proto_first.6 = (bf16[1024,2048]{1,0:T(8,128)(2,1)S(1)}, f32[1024,128]{1,0:T(8,128)S(1)}) custom-call(s32[1]{0:T(128)} %bitcast.1.place, bf16[1024,128]{1,0:T(8,128)(2,1)S(1)} %constant_dynamic-slice_fusion.protos.refs_9_, bf16[8,128,1024]{2,1,0:T(8,128)(2,1)} %bitcast.15, f32[8,1,1024]{2,1,0:T(1,128)S(1)} %constant_dynamic-update-slice_fusion.totals), custom_call_target="tpu_custom_call" | custom-call | flops 1000 | bytes 1000 | tf_op jit(solution)/shard_map/proto_first/pallas_call | solution.py:454
  111.0 1.7 collective-permute-start.25
  112.8 2.2 %view_grad.1 = bf16[1024,128]{1,0:T(8,128)(2,1)S(1)} custom-call(f32[1024,128]{1,0:T(8,128)S(1)} %get-tuple-element.209.code, f32[1,1024]{1,0:T(1,128)S(1)} %get-tuple-element.210.tot, f32[1,1024]{1,0:T(1,128)S(1)} %get-tuple-element.211.total, f32[1024,128]{1,0:T(8,128)} %copy-done.4, f32[1024,128]{1,0:T(8,128)} %copy-done.5, f32[1024,128]{1,0:T(8,128)} %copy-done.6, ...), custom_call_target="tpu_custom_call" | custom-call | flops 1000 | bytes 1000 | tf_op jit(solution)/shard_map/view_grad/pallas_call | solution.py:580
  115.2 2.6 %collective-permute-start.27 = (f32[2,1,1024]{2,1,0:T(1,128)S(1)}, f32[2,1,1024]{2,1,0:T(1,128)S(1)}, u32[]{:S(2)}, u32[]{:S(2)}) collective-permute-start(f32[2,1,1024]{2,1,0:T(1,128)S(1)} %pad_maximum_fusion.4), channel_id=1, source_target_pairs={{0,16},{4,20},{8,24},{12,28},{16,0},{20,4},{24,8},{28,12},{1,17},{... | collective-permute-start | bytes 24584 | tf_op jit(solution)/shard_map/ppermute | solution.py:749
  117.9 1.7 collective-permute-start.28
  119.6 4.2 %proto_first.7 = (bf16[1024,2048]{1,0:T(8,128)(2,1)S(1)}, f32[1024,128]{1,0:T(8,128)S(1)}) custom-call(s32[1]{0:T(128)} %bitcast.1.place, bf16[1024,128]{1,0:T(8,128)(2,1)S(1)} %constant_dynamic-slice_fusion.protos.refs_9_, bf16[8,128,1024]{2,1,0:T(8,128)(2,1)} %bitcast.16, f32[8,1,1024]{2,1,0:T(1,128)S(1)} %constant_dynamic-update-slice_fusion.totals), custom_call_target="tpu_custom_call" | custom-call | flops 1000 | bytes 1000 | tf_op jit(solution)/shard_map/proto_first/pallas_call | solution.py:454
  124.0 1.6 collective-permute-start.30
  125.6 5.4 %proto_last.1 = bf16[1024,128]{1,0:T(8,128)(2,1)} custom-call(s32[1]{0:T(128)} %bitcast.1.place, bf16[1024,2048]{1,0:T(8,128)(2,1)S(1)} %get-tuple-element.239.refs_0_, bf16[1024,2048]{1,0:T(8,128)(2,1)S(1)} %get-tuple-element.240.refs_1_, bf16[1024,2048]{1,0:T(8,128)(2,1)S(1)} %get-tuple-element.241.refs_2_, ...), custom_call_target="tpu_custom_call" | custom-call | tf_op jit(solution)/shard_map/proto_last/pallas_call | solution.py:511
  131.9 5.9 %backward.1 = f32[8,144,128]{2,1,0:T(8,128)S(1)} custom-call(s32[1]{0:T(128)} %bitcast.turn, bf16[1024,128]{1,0:T(8,128)(2,1)S(1)} %add_convert_fusion.grad_a, bf16[1024,128]{1,0:T(8,128)(2,1)S(1)} %collective-permute-done.30.grad_b, s32[1,1024]{1,0:T(1,128)S(1)} %get-tuple-element.252.pos, f32[1024,128]{1,0:T(8,128)} %get-tuple-element.253.raw, ...), custom_call_target="tpu_custom_call" | custom-call | tf_op jit(solution)/shard_map/backward/pallas_call | solution.py:644
  139.2 5.7 %collective-permute-done.31 = bf16[4,144,128]{2,1,0:T(8,128)(2,1)S(1)} collective-permute-done((bf16[4,144,128]{2,1,0:T(8,128)(2,1)S(1)}, bf16[4,144,128]{2,1,0:T(8,128)(2,1)S(1)}, u32[]{:S(2)}, u32[]{:S(2)}) %collective-permute-start.31) | collective-permute-done | bytes 147488 | tf_op jit(solution)/shard_map/ppermute | solution.py:749
  145.8 3.6 %collective-permute-start.34 = (bf16[1,144,128]{2,1,0:T(8,128)(2,1)S(1)}, bf16[1,144,128]{2,1,0:T(8,128)(2,1)S(1)}, u32[]{:S(2)}, u32[]{:S(2)}) collective-permute-start(bf16[1,144,128]{2,1,0:T(8,128)(2,1)S(1)} %get-tuple-element.264), channel_id=1, source_target_pairs={{0,24},{4,28},{8,16},{12,20},{16,8},{20,12},{24,0},{28,4},{1,25},{... | collective-permute-start | bytes 110600 | tf_op jit(solution)/shard_map/ppermute | solution.py:749
  150.8 2.5 %collective-permute-done.34 = bf16[1,144,128]{2,1,0:T(8,128)(2,1)S(1)} collective-permute-done((bf16[1,144,128]{2,1,0:T(8,128)(2,1)S(1)}, bf16[1,144,128]{2,1,0:T(8,128)(2,1)S(1)}, u32[]{:S(2)}, u32[]{:S(2)}) %collective-permute-start.34) | collective-permute-done | bytes 36896 | tf_op jit(solution)/shard_map/ppermute | solution.py:749
  153.3 2.3 %collective-permute-start.35 = (bf16[1,144,128]{2,1,0:T(8,128)(2,1)S(1)}, bf16[1,144,128]{2,1,0:T(8,128)(2,1)S(1)}, u32[]{:S(2)}, u32[]{:S(2)}) collective-permute-start(bf16[1,144,128]{2,1,0:T(8,128)(2,1)S(1)} %get-tuple-element.260), channel_id=1, source_target_pairs={{0,8},{4,12},{8,0},{12,4},{16,24},{20,28},{24,16},{28,20},{1,9},{5... | collective-permute-start | bytes 110600 | tf_op jit(solution)/shard_map/ppermute | solution.py:749
  158.0 2.4 %collective-permute-done.36 = bf16[1,144,128]{2,1,0:T(8,128)(2,1)S(1)} collective-permute-done((bf16[1,144,128]{2,1,0:T(8,128)(2,1)S(1)}, bf16[1,144,128]{2,1,0:T(8,128)(2,1)S(1)}, u32[]{:S(2)}, u32[]{:S(2)}) %collective-permute-start.36) | collective-permute-done | bytes 36896 | tf_op jit(solution)/shard_map/ppermute | solution.py:749
  160.4 1.9 collective-permute-done.37
  162.4 1.9 collective-permute-start.38
  164.3 6.4 %collective-permute-done.38 = bf16[4,144,128]{2,1,0:T(8,128)(2,1)S(1)} collective-permute-done((bf16[4,144,128]{2,1,0:T(8,128)(2,1)S(1)}, bf16[4,144,128]{2,1,0:T(8,128)(2,1)S(1)}, u32[]{:S(2)}, u32[]{:S(2)}) %collective-permute-start.38) | collective-permute-done | bytes 147488 | tf_op jit(solution)/shard_map/ppermute | solution.py:749
  170.8 1.6 collective-permute-start.39
  172.4 5.1 %collective-permute-done.39 = bf16[1,8,144,128]{3,2,1,0:T(8,128)(2,1)S(1)} collective-permute-done((bf16[1,8,144,128]{3,2,1,0:T(8,128)(2,1)S(1)}, bf16[1,8,144,128]{3,2,1,0:T(8,128)(2,1)S(1)}, u32[]{:S(2)}, u32[]{:S(2)}) %collective-permute-start.39) | collective-permute-done | bytes 294944 | tf_op jit(solution)/shard_map/ppermute | solution.py:749
  177.8 1.9 collective-permute-done.40.refs_1_
  179.7 2.1 %unpack.1 = (f32[1024,512]{1,0:T(8,128)}, f32[512,128]{1,0:T(8,128)}) custom-call(s32[2]{0:T(128)S(1)} %pad_add_fusion.place, bf16[2,8,144,128]{3,2,1,0:T(8,128)(2,1)S(1)} %pad_maximum_fusion.refs_0_, bf16[2,8,144,128]{3,2,1,0:T(8,128)(2,1)S(1)} %collective-permute-done.40.refs_1_), custom_call_target="tpu_custom_call" | custom-call | tf_op jit(solution)/shard_map/unpack/pallas_call | solution.py:678
  181.8 3.4 %all-gather.4.cloned.1.call-done.x = bf16[8192,128]{1,0:T(8,128)(2,1)} async-done(((bf16[1024,128]{1,0:T(8,128)(2,1)}), bf16[8192,128]{1,0:T(8,128)(2,1)}) %all-gather.4.cloned.1.call-update) | async-done | bytes 2097168 | tf_op jit(solution)/shard_map/all_gather | solution.py:854
  185.2 3.1 %widen.1 = f32[8192,128]{1,0:T(8,128)} custom-call(bf16[8192,128]{1,0:T(8,128)(2,1)} %all-gather.4.cloned.1.call-done.x), custom_call_target="tpu_custom_call" | custom-call | tf_op jit(solution)/shard_map/widen/pallas_call | solution.py:712
  (109 shorter events, 20.7 us)
Async XLA Ops:
  7.2 7.6 %copy-start.1 = (bf16[8192,128]{1,0:T(8,128)(2,1)S(1)}, bf16[8192,128]{1,0:T(8,128)(2,1)}, u32[]{:S(2)}) copy-start(bf16[8192,128]{1,0:T(8,128)(2,1)} %protos.3) | copy-start | bytes 6291460
  7.2 74.7 %all-gather.6.cloned.1.call-start = ((), (), s32[]{:S(2)}) async-start(), calls=%async_computation.1 | async-start | bytes 2359296 | tf_op jit(solution)/shard_map/all_gather | solution.py:770
  14.7 170.5 %all-gather.4.cloned.1.call-start = ((), (), s32[]{:S(2)}) async-start(), calls=%async_computation | async-start | bytes 2359296 | tf_op jit(solution)/shard_map/all_gather | solution.py:854
  25.8 53.7 %copy-start = (bf16[1024,8192]{1,0:T(8,128)(2,1)}, bf16[1024,8192]{1,0:T(8,128)(2,1)S(1)}, u32[]{:S(2)}) copy-start(bf16[1024,8192]{1,0:T(8,128)(2,1)S(1)} %get-tuple-element.134.expo.refs_0_.refs_1_.refs_2_.refs_3_) | copy-start | bytes 50331652
  25.8 6.5 %collective-permute-start = (f32[1,8192]{1,0:T(1,128)S(1)}, f32[1,8192]{1,0:T(1,128)S(1)}, u32[]{:S(2)}, u32[]{:S(2)}) collective-permute-start(f32[1,8192]{1,0:T(1,128)S(1)} %get-tuple-element.135), channel_id=1, source_target_pairs={{0,4},{4,0},{8,12},{12,8},{16,20},{20,16},{24,28},{28,24},{1,5},{5... | collective-permute-start | bytes 98312 | tf_op jit(solution)/shard_map/ppermute | solution.py:749
  32.3 13.8 %copy-start.4 = (f32[1024,128]{1,0:T(8,128)}, f32[1024,128]{1,0:T(8,128)S(1)}, u32[]{:S(2)}) copy-start(f32[1024,128]{1,0:T(8,128)S(1)} %view_soft.4.refs_0_) | copy-start | bytes 1572868
  32.4 7.9 %collective-permute-start.1 = (f32[1,8192]{1,0:T(1,128)S(1)}, f32[1,8192]{1,0:T(1,128)S(1)}, u32[]{:S(2)}, u32[]{:S(2)}) collective-permute-start(f32[1,8192]{1,0:T(1,128)S(1)} %add.80.refs_0_), channel_id=1, source_target_pairs={{0,8},{4,12},{8,0},{12,4},{16,24},{20,28},{24,16},{28,20},{1,9},{5... | collective-permute-start | bytes 98312 | tf_op jit(solution)/shard_map/ppermute | solution.py:749
  34.0 6.8 %collective-permute-start.2 = (f32[1,8192]{1,0:T(1,128)S(1)}, f32[1,8192]{1,0:T(1,128)S(1)}, u32[]{:S(2)}, u32[]{:S(2)}) collective-permute-start(f32[1,8192]{1,0:T(1,128)S(1)} %add.80.refs_0_), channel_id=1, source_target_pairs={{0,16},{4,20},{8,24},{12,28},{16,0},{20,4},{24,8},{28,12},{1,17},{... | collective-permute-start | bytes 98312 | tf_op jit(solution)/shard_map/ppermute | solution.py:749
  36.6 5.7 %collective-permute-start.3 = (f32[1,8192]{1,0:T(1,128)S(1)}, f32[1,8192]{1,0:T(1,128)S(1)}, u32[]{:S(2)}, u32[]{:S(2)}) collective-permute-start(f32[1,8192]{1,0:T(1,128)S(1)} %add.80.refs_0_), channel_id=1, source_target_pairs={{0,24},{4,28},{8,16},{12,20},{16,8},{20,12},{24,0},{28,4},{1,25},{... | collective-permute-start | bytes 98312 | tf_op jit(solution)/shard_map/ppermute | solution.py:749
  46.1 5.4 %collective-permute-start.4 = (f32[2,1024]{1,0:T(2,128)S(1)}, f32[2,1024]{1,0:T(2,128)S(1)}, u32[]{:S(2)}, u32[]{:S(2)}) collective-permute-start(f32[2,1024]{1,0:T(2,128)S(1)} %pad_maximum_fusion.2), channel_id=1, source_target_pairs={{0,1},{1,0},{2,3},{3,2},{4,5},{5,4},{6,7},{7,6},{8,9},{9,8},{10,11... | collective-permute-start | bytes 24584 | tf_op jit(solution)/shard_map/ppermute | solution.py:749
  46.2 5.3 %collective-permute-start.5 = (f32[2,1024]{1,0:T(2,128)S(1)}, f32[2,1024]{1,0:T(2,128)S(1)}, u32[]{:S(2)}, u32[]{:S(2)}) collective-permute-start(f32[2,1024]{1,0:T(2,128)S(1)} %pad_maximum_fusion.2), channel_id=1, source_target_pairs={{0,2},{1,3},{2,0},{3,1},{4,6},{5,7},{6,4},{7,5},{8,10},{9,11},{10,... | collective-permute-start | bytes 24584 | tf_op jit(solution)/shard_map/ppermute | solution.py:749
  47.7 3.8 %collective-permute-start.6 = (f32[2,1024]{1,0:T(2,128)S(1)}, f32[2,1024]{1,0:T(2,128)S(1)}, u32[]{:S(2)}, u32[]{:S(2)}) collective-permute-start(f32[2,1024]{1,0:T(2,128)S(1)} %pad_maximum_fusion.2), channel_id=1, source_target_pairs={{0,3},{1,2},{2,1},{3,0},{4,7},{5,6},{6,5},{7,4},{8,11},{9,10},{10,... | collective-permute-start | bytes 24584 | tf_op jit(solution)/shard_map/ppermute | solution.py:749
  53.8 5.6 %collective-permute-start.8 = (f32[1,8192]{1,0:T(1,128)S(1)}, f32[1,8192]{1,0:T(1,128)S(1)}, u32[]{:S(2)}, u32[]{:S(2)}) collective-permute-start(f32[1,8192]{1,0:T(1,128)S(1)} %bitcast.20), channel_id=1, source_target_pairs={{0,4},{4,0},{8,12},{12,8},{16,20},{20,16},{24,28},{28,24},{1,5},{5... | collective-permute-start | bytes 98312 | tf_op jit(solution)/shard_map/ppermute | solution.py:749
  54.4 5.0 %collective-permute-start.7 = (f32[1,1,1024]{2,1,0:T(1,128)S(1)}, f32[1,1,1024]{2,1,0:T(1,128)S(1)}, u32[]{:S(2)}, u32[]{:S(2)}) collective-permute-start(f32[1,1,1024]{2,1,0:T(1,128)S(1)} %get-tuple-element.267), channel_id=1, source_target_pairs={{0,4},{4,0},{8,12},{12,8},{16,20},{20,16},{24,28},{28,24},{1,5},{5... | collective-permute-start | bytes 12296 | tf_op jit(solution)/shard_map/ppermute | solution.py:749
  59.4 10.0 %copy-start.7 = (f32[1024,128]{1,0:T(8,128)}, f32[1024,128]{1,0:T(8,128)S(1)}, u32[]{:S(2)}) copy-start(f32[1024,128]{1,0:T(8,128)S(1)} %view_soft.7.refs_3_) | copy-start | bytes 1572868
  59.4 6.2 %collective-permute-start.12 = (f32[1,8192]{1,0:T(1,128)S(1)}, f32[1,8192]{1,0:T(1,128)S(1)}, u32[]{:S(2)}, u32[]{:S(2)}) collective-permute-start(f32[1,8192]{1,0:T(1,128)S(1)} %bitcast_add_fusion.refs_0_), channel_id=1, source_target_pairs={{0,8},{4,12},{8,0},{12,4},{16,24},{20,28},{24,16},{28,20},{1,9},{5... | collective-permute-start | bytes 98312 | tf_op jit(solution)/shard_map/ppermute | solution.py:749
  59.5 9.8 %collective-permute-start.13 = (f32[1,8192]{1,0:T(1,128)S(1)}, f32[1,8192]{1,0:T(1,128)S(1)}, u32[]{:S(2)}, u32[]{:S(2)}) collective-permute-start(f32[1,8192]{1,0:T(1,128)S(1)} %bitcast_add_fusion.refs_0_), channel_id=1, source_target_pairs={{0,16},{4,20},{8,24},{12,28},{16,0},{20,4},{24,8},{28,12},{1,17},{... | collective-permute-start | bytes 98312 | tf_op jit(solution)/shard_map/ppermute | solution.py:749
  61.7 7.7 %collective-permute-start.14 = (f32[1,8192]{1,0:T(1,128)S(1)}, f32[1,8192]{1,0:T(1,128)S(1)}, u32[]{:S(2)}, u32[]{:S(2)}) collective-permute-start(f32[1,8192]{1,0:T(1,128)S(1)} %bitcast_add_fusion.refs_0_), channel_id=1, source_target_pairs={{0,24},{4,28},{8,16},{12,20},{16,8},{20,12},{24,0},{28,4},{1,25},{... | collective-permute-start | bytes 98312 | tf_op jit(solution)/shard_map/ppermute | solution.py:749
  63.9 6.7 %collective-permute-start.10 = (f32[2,1,1024]{2,1,0:T(1,128)S(1)}, f32[2,1,1024]{2,1,0:T(1,128)S(1)}, u32[]{:S(2)}, u32[]{:S(2)}) collective-permute-start(f32[2,1,1024]{2,1,0:T(1,128)S(1)} %pad_maximum_fusion.3), channel_id=1, source_target_pairs={{0,16},{4,20},{8,24},{12,28},{16,0},{20,4},{24,8},{28,12},{1,17},{... | collective-permute-start | bytes 24584 | tf_op jit(solution)/shard_map/ppermute | solution.py:749
  64.0 6.6 %collective-permute-start.11 = (f32[2,1,1024]{2,1,0:T(1,128)S(1)}, f32[2,1,1024]{2,1,0:T(1,128)S(1)}, u32[]{:S(2)}, u32[]{:S(2)}) collective-permute-start(f32[2,1,1024]{2,1,0:T(1,128)S(1)} %pad_maximum_fusion.3), channel_id=1, source_target_pairs={{0,24},{4,28},{8,16},{12,20},{16,8},{20,12},{24,0},{28,4},{1,25},{... | collective-permute-start | bytes 24584 | tf_op jit(solution)/shard_map/ppermute | solution.py:749
  65.7 4.9 %collective-permute-start.9 = (f32[2,1,1024]{2,1,0:T(1,128)S(1)}, f32[2,1,1024]{2,1,0:T(1,128)S(1)}, u32[]{:S(2)}, u32[]{:S(2)}) collective-permute-start(f32[2,1,1024]{2,1,0:T(1,128)S(1)} %pad_maximum_fusion.3), channel_id=1, source_target_pairs={{0,8},{4,12},{8,0},{12,4},{16,24},{20,28},{24,16},{28,20},{1,9},{5... | collective-permute-start | bytes 24584 | tf_op jit(solution)/shard_map/ppermute | solution.py:749
  74.4 5.1 %collective-permute-start.15 = (f32[1,1024]{1,0:T(1,128)S(1)}, f32[1,1024]{1,0:T(1,128)S(1)}, u32[]{:S(2)}, u32[]{:S(2)}) collective-permute-start(f32[1,1024]{1,0:T(1,128)S(1)} %get-tuple-element.163.refs_0_), channel_id=1, source_target_pairs={{0,1},{1,0},{2,3},{3,2},{4,5},{5,4},{6,7},{7,6},{8,9},{9,8},{10,11... | collective-permute-start | bytes 12296 | tf_op jit(solution)/shard_map/ppermute | solution.py:749
  74.4 5.1 %collective-permute-start.16 = (f32[1,1024]{1,0:T(1,128)S(1)}, f32[1,1024]{1,0:T(1,128)S(1)}, u32[]{:S(2)}, u32[]{:S(2)}) collective-permute-start(f32[1,1024]{1,0:T(1,128)S(1)} %get-tuple-element.163.refs_0_), channel_id=1, source_target_pairs={{0,2},{1,3},{2,0},{3,1},{4,6},{5,7},{6,4},{7,5},{8,10},{9,11},{10,... | collective-permute-start | bytes 12296 | tf_op jit(solution)/shard_map/ppermute | solution.py:749
  75.9 3.6 %collective-permute-start.17 = (f32[1,1024]{1,0:T(1,128)S(1)}, f32[1,1024]{1,0:T(1,128)S(1)}, u32[]{:S(2)}, u32[]{:S(2)}) collective-permute-start(f32[1,1024]{1,0:T(1,128)S(1)} %get-tuple-element.163.refs_0_), channel_id=1, source_target_pairs={{0,3},{1,2},{2,1},{3,0},{4,7},{5,6},{6,5},{7,4},{8,11},{9,10},{10,... | collective-permute-start | bytes 12296 | tf_op jit(solution)/shard_map/ppermute | solution.py:749
  81.9 4.8 %collective-permute-start.18 = (f32[1,8192]{1,0:T(1,128)S(1)}, f32[1,8192]{1,0:T(1,128)S(1)}, u32[]{:S(2)}, u32[]{:S(2)}) collective-permute-start(f32[1,8192]{1,0:T(1,128)S(1)} %bitcast.18), channel_id=1, source_target_pairs={{0,4},{4,0},{8,12},{12,8},{16,20},{20,16},{24,28},{28,24},{1,5},{5... | collective-permute-start | bytes 98312 | tf_op jit(solution)/shard_map/ppermute | solution.py:749
  86.7 8.7 %collective-permute-start.19 = (f32[1,8192]{1,0:T(1,128)S(1)}, f32[1,8192]{1,0:T(1,128)S(1)}, u32[]{:S(2)}, u32[]{:S(2)}) collective-permute-start(f32[1,8192]{1,0:T(1,128)S(1)} %add.85.refs_4_), channel_id=1, source_target_pairs={{0,8},{4,12},{8,0},{12,4},{16,24},{20,28},{24,16},{28,20},{1,9},{5... | collective-permute-start | bytes 98312 | tf_op jit(solution)/shard_map/ppermute | solution.py:749
  87.8 7.6 %collective-permute-start.20 = (f32[1,8192]{1,0:T(1,128)S(1)}, f32[1,8192]{1,0:T(1,128)S(1)}, u32[]{:S(2)}, u32[]{:S(2)}) collective-permute-start(f32[1,8192]{1,0:T(1,128)S(1)} %add.85.refs_4_), channel_id=1, source_target_pairs={{0,16},{4,20},{8,24},{12,28},{16,0},{20,4},{24,8},{28,12},{1,17},{... | collective-permute-start | bytes 98312 | tf_op jit(solution)/shard_map/ppermute | solution.py:749
  89.6 5.8 %collective-permute-start.21 = (f32[1,8192]{1,0:T(1,128)S(1)}, f32[1,8192]{1,0:T(1,128)S(1)}, u32[]{:S(2)}, u32[]{:S(2)}) collective-permute-start(f32[1,8192]{1,0:T(1,128)S(1)} %add.85.refs_4_), channel_id=1, source_target_pairs={{0,24},{4,28},{8,16},{12,20},{16,8},{20,12},{24,0},{28,4},{1,25},{... | collective-permute-start | bytes 98312 | tf_op jit(solution)/shard_map/ppermute | solution.py:749
  104.8 6.2 %collective-permute-start.22 = (f32[1,1024]{1,0:T(1,128)S(1)}, f32[1,1024]{1,0:T(1,128)S(1)}, u32[]{:S(2)}, u32[]{:S(2)}) collective-permute-start(f32[1,1024]{1,0:T(1,128)S(1)} %get-tuple-element.194), channel_id=1, source_target_pairs={{0,1},{1,0},{2,3},{3,2},{4,5},{5,4},{6,7},{7,6},{8,9},{9,8},{10,11... | collective-permute-start | bytes 12296 | tf_op jit(solution)/shard_map/ppermute | solution.py:749
  104.9 6.1 %collective-permute-start.23 = (f32[1,1024]{1,0:T(1,128)S(1)}, f32[1,1024]{1,0:T(1,128)S(1)}, u32[]{:S(2)}, u32[]{:S(2)}) collective-permute-start(f32[1,1024]{1,0:T(1,128)S(1)} %get-tuple-element.194), channel_id=1, source_target_pairs={{0,2},{1,3},{2,0},{3,1},{4,6},{5,7},{6,4},{7,5},{8,10},{9,11},{10,... | collective-permute-start | bytes 12296 | tf_op jit(solution)/shard_map/ppermute | solution.py:749
  106.5 4.5 %collective-permute-start.24 = (f32[1,1024]{1,0:T(1,128)S(1)}, f32[1,1024]{1,0:T(1,128)S(1)}, u32[]{:S(2)}, u32[]{:S(2)}) collective-permute-start(f32[1,1024]{1,0:T(1,128)S(1)} %get-tuple-element.194), channel_id=1, source_target_pairs={{0,3},{1,2},{2,1},{3,0},{4,7},{5,6},{6,5},{7,4},{8,11},{9,10},{10,... | collective-permute-start | bytes 12296 | tf_op jit(solution)/shard_map/ppermute | solution.py:749
  111.0 4.0 %collective-permute-start.25 = (f32[1,1,1024]{2,1,0:T(1,128)S(1)}, f32[1,1,1024]{2,1,0:T(1,128)S(1)}, u32[]{:S(2)}, u32[]{:S(2)}) collective-permute-start(f32[1,1,1024]{2,1,0:T(1,128)S(1)} %bitcast.21), channel_id=1, source_target_pairs={{0,4},{4,0},{8,12},{12,8},{16,20},{20,16},{24,28},{28,24},{1,5},{5... | collective-permute-start | bytes 12296 | tf_op jit(solution)/shard_map/ppermute | solution.py:749
  115.0 10.6 %copy-start.2 = (bf16[1024,1024]{1,0:T(8,128)(2,1)S(1)}, bf16[1024,1024]{1,0:T(8,128)(2,1)}, u32[]{:S(2)}) copy-start(bf16[1024,1024]{1,0:T(8,128)(2,1)} %all-gather.6.cloned.1.call-done) | copy-start | bytes 6291460
  115.0 8.9 %collective-permute-start.29 = (bf16[1024,128]{1,0:T(8,128)(2,1)S(1)}, bf16[1024,128]{1,0:T(8,128)(2,1)S(1)}, u32[]{:S(2)}, u32[]{:S(2)}) collective-permute-start(bf16[1024,128]{1,0:T(8,128)(2,1)S(1)} %view_grad.1), channel_id=1, source_target_pairs={{0,1},{1,0},{2,3},{3,2},{4,5},{5,4},{6,7},{7,6},{8,9},{9,8},{10,11... | collective-permute-start | bytes 786440 | tf_op jit(solution)/shard_map/ppermute | solution.py:749
  115.1 8.7 %collective-permute-start.26 = (f32[2,1,1024]{2,1,0:T(1,128)S(1)}, f32[2,1,1024]{2,1,0:T(1,128)S(1)}, u32[]{:S(2)}, u32[]{:S(2)}) collective-permute-start(f32[2,1,1024]{2,1,0:T(1,128)S(1)} %pad_maximum_fusion.4), channel_id=1, source_target_pairs={{0,8},{4,12},{8,0},{12,4},{16,24},{20,28},{24,16},{28,20},{1,9},{5... | collective-permute-start | bytes 24584 | tf_op jit(solution)/shard_map/ppermute | solution.py:749
  115.2 8.6 %collective-permute-start.27 = (f32[2,1,1024]{2,1,0:T(1,128)S(1)}, f32[2,1,1024]{2,1,0:T(1,128)S(1)}, u32[]{:S(2)}, u32[]{:S(2)}) collective-permute-start(f32[2,1,1024]{2,1,0:T(1,128)S(1)} %pad_maximum_fusion.4), channel_id=1, source_target_pairs={{0,16},{4,20},{8,24},{12,28},{16,0},{20,4},{24,8},{28,12},{1,17},{... | collective-permute-start | bytes 24584 | tf_op jit(solution)/shard_map/ppermute | solution.py:749
  117.9 6.0 %collective-permute-start.28 = (f32[2,1,1024]{2,1,0:T(1,128)S(1)}, f32[2,1,1024]{2,1,0:T(1,128)S(1)}, u32[]{:S(2)}, u32[]{:S(2)}) collective-permute-start(f32[2,1,1024]{2,1,0:T(1,128)S(1)} %pad_maximum_fusion.4), channel_id=1, source_target_pairs={{0,24},{4,28},{8,16},{12,20},{16,8},{20,12},{24,0},{28,4},{1,25},{... | collective-permute-start | bytes 24584 | tf_op jit(solution)/shard_map/ppermute | solution.py:749
  124.0 7.9 %collective-permute-start.30 = (bf16[1024,128]{1,0:T(8,128)(2,1)S(1)}, bf16[1024,128]{1,0:T(8,128)(2,1)S(1)}, u32[]{:S(2)}, u32[]{:S(2)}) collective-permute-start(bf16[1024,128]{1,0:T(8,128)(2,1)S(1)} %add_convert_fusion.grad_a), channel_id=1, source_target_pairs={{0,2},{1,3},{2,0},{3,1},{4,6},{5,7},{6,4},{7,5},{8,10},{9,11},{10,... | collective-permute-start | bytes 786440 | tf_op jit(solution)/shard_map/ppermute | solution.py:749
  137.8 7.0 %collective-permute-start.31 = (bf16[4,144,128]{2,1,0:T(8,128)(2,1)S(1)}, bf16[4,144,128]{2,1,0:T(8,128)(2,1)S(1)}, u32[]{:S(2)}, u32[]{:S(2)}) collective-permute-start(bf16[4,144,128]{2,1,0:T(8,128)(2,1)S(1)} %dynamic-slice_convert_fusion), channel_id=1, source_target_pairs={{0,4},{4,0},{8,12},{12,8},{16,20},{20,16},{24,28},{28,24},{1,5},{5... | collective-permute-start | bytes 442376 | tf_op jit(solution)/shard_map/ppermute | solution.py:749
  144.9 5.3 %collective-permute-start.32 = (bf16[1,144,128]{2,1,0:T(8,128)(2,1)S(1)}, bf16[1,144,128]{2,1,0:T(8,128)(2,1)S(1)}, u32[]{:S(2)}, u32[]{:S(2)}) collective-permute-start(bf16[1,144,128]{2,1,0:T(8,128)(2,1)S(1)} %get-tuple-element.263), channel_id=1, source_target_pairs={{0,8},{4,12},{8,0},{12,4},{16,24},{20,28},{24,16},{28,20},{1,9},{5... | collective-permute-start | bytes 110600 | tf_op jit(solution)/shard_map/ppermute | solution.py:749
  145.0 5.8 %collective-permute-start.33 = (bf16[1,144,128]{2,1,0:T(8,128)(2,1)S(1)}, bf16[1,144,128]{2,1,0:T(8,128)(2,1)S(1)}, u32[]{:S(2)}, u32[]{:S(2)}) collective-permute-start(bf16[1,144,128]{2,1,0:T(8,128)(2,1)S(1)} %get-tuple-element.265), channel_id=1, source_target_pairs={{0,16},{4,20},{8,24},{12,28},{16,0},{20,4},{24,8},{28,12},{1,17},{... | collective-permute-start | bytes 110600 | tf_op jit(solution)/shard_map/ppermute | solution.py:749
  145.8 7.4 %collective-permute-start.34 = (bf16[1,144,128]{2,1,0:T(8,128)(2,1)S(1)}, bf16[1,144,128]{2,1,0:T(8,128)(2,1)S(1)}, u32[]{:S(2)}, u32[]{:S(2)}) collective-permute-start(bf16[1,144,128]{2,1,0:T(8,128)(2,1)S(1)} %get-tuple-element.264), channel_id=1, source_target_pairs={{0,24},{4,28},{8,16},{12,20},{16,8},{20,12},{24,0},{28,4},{1,25},{... | collective-permute-start | bytes 110600 | tf_op jit(solution)/shard_map/ppermute | solution.py:749
  153.3 4.7 %collective-permute-start.35 = (bf16[1,144,128]{2,1,0:T(8,128)(2,1)S(1)}, bf16[1,144,128]{2,1,0:T(8,128)(2,1)S(1)}, u32[]{:S(2)}, u32[]{:S(2)}) collective-permute-start(bf16[1,144,128]{2,1,0:T(8,128)(2,1)S(1)} %get-tuple-element.260), channel_id=1, source_target_pairs={{0,8},{4,12},{8,0},{12,4},{16,24},{20,28},{24,16},{28,20},{1,9},{5... | collective-permute-start | bytes 110600 | tf_op jit(solution)/shard_map/ppermute | solution.py:749
  155.6 4.9 %collective-permute-start.36 = (bf16[1,144,128]{2,1,0:T(8,128)(2,1)S(1)}, bf16[1,144,128]{2,1,0:T(8,128)(2,1)S(1)}, u32[]{:S(2)}, u32[]{:S(2)}) collective-permute-start(bf16[1,144,128]{2,1,0:T(8,128)(2,1)S(1)} %get-tuple-element.260), channel_id=1, source_target_pairs={{0,16},{4,20},{8,24},{12,28},{16,0},{20,4},{24,8},{28,12},{1,17},{... | collective-permute-start | bytes 110600 | tf_op jit(solution)/shard_map/ppermute | solution.py:749
  156.6 5.8 %collective-permute-start.37 = (bf16[1,144,128]{2,1,0:T(8,128)(2,1)S(1)}, bf16[1,144,128]{2,1,0:T(8,128)(2,1)S(1)}, u32[]{:S(2)}, u32[]{:S(2)}) collective-permute-start(bf16[1,144,128]{2,1,0:T(8,128)(2,1)S(1)} %get-tuple-element.260), channel_id=1, source_target_pairs={{0,24},{4,28},{8,16},{12,20},{16,8},{20,12},{24,0},{28,4},{1,25},{... | collective-permute-start | bytes 110600 | tf_op jit(solution)/shard_map/ppermute | solution.py:749
  162.4 8.3 %collective-permute-start.38 = (bf16[4,144,128]{2,1,0:T(8,128)(2,1)S(1)}, bf16[4,144,128]{2,1,0:T(8,128)(2,1)S(1)}, u32[]{:S(2)}, u32[]{:S(2)}) collective-permute-start(bf16[4,144,128]{2,1,0:T(8,128)(2,1)S(1)} %pad_maximum_fusion.1), channel_id=1, source_target_pairs={{0,4},{4,0},{8,12},{12,8},{16,20},{20,16},{24,28},{28,24},{1,5},{5... | collective-permute-start | bytes 442376 | tf_op jit(solution)/shard_map/ppermute | solution.py:749
  170.8 6.8 %collective-permute-start.39 = (bf16[1,8,144,128]{3,2,1,0:T(8,128)(2,1)S(1)}, bf16[1,8,144,128]{3,2,1,0:T(8,128)(2,1)S(1)}, u32[]{:S(2)}, u32[]{:S(2)}) collective-permute-start(bf16[1,8,144,128]{3,2,1,0:T(8,128)(2,1)S(1)} %bitcast.23), channel_id=1, source_target_pairs={{0,2},{1,3},{2,0},{3,1},{4,6},{5,7},{6,4},{7,5},{8,10},{9,11},{10,... | collective-permute-start | bytes 884744 | tf_op jit(solution)/shard_map/ppermute | solution.py:749
  177.6 2.1 %collective-permute-start.40 = (bf16[2,8,144,128]{3,2,1,0:T(8,128)(2,1)S(1)}, bf16[2,8,144,128]{3,2,1,0:T(8,128)(2,1)S(1)}, u32[]{:S(2)}, u32[]{:S(2)}) collective-permute-start(bf16[2,8,144,128]{3,2,1,0:T(8,128)(2,1)S(1)} %pad_maximum_fusion.refs_0_), channel_id=1, source_target_pairs={{0,1},{1,0},{2,3},{3,2},{4,5},{5,4},{6,7},{7,6},{8,9},{9,8},{10,11... | collective-permute-start | bytes 1769480 | tf_op jit(solution)/shard_map/ppermute | solution.py:749
  (3 other events, 9.4 us)
Sparse Core Ops, SparseCore 0:
  14.8 58.0 all-gather.5
  132.0 53.1 all-gather.3

commit v10 on v9

--- a/solution.py
+++ b/solution.py
@@ -414,23 +414,17 @@
 
 
 def proto_first_kernel(chunk, tile, lead, place, protos, views, totals, expo, grad, *scratch):
-    weights, twice, pair, stage, soft16, acc, near, arrived = scratch
+    weights, twice, pair, stage, soft16, acc = scratch
     count = expo.shape[1] // views.shape[2]
     _, depth, rows = views.shape
     width = protos.shape[0]
-    copies = [
-        pltpu.make_async_copy(views.at[lead + n], near.at[n], arrived.at[n]) for n in range(count)
-    ]
-    for copy in copies:
-        copy.start()
     _, _, unit = unit_of(protos[...])
     pair[...] = scaled_pair(unit.astype(bf16), 1)
     for n in range(count):
-        copies[n].wait()
-        total = totals[place[0] ^ (lead + n)]
-        weights[...] = (near[n].astype(f32) * (GRAD_SCALE / total)).astype(bf16)
-        twice[:depth, :] = near[n]
-        twice[depth:, :] = near[n]
+        k = lead + n
+        weights[...] = (views[k].astype(f32) * (GRAD_SCALE / totals[place[0] ^ k])).astype(bf16)
+        twice[:depth, :] = views[k]
+        twice[depth:, :] = views[k]
         for c in range(width // chunk):
             stage[c % 2] = dot(pair[c * chunk : (c + 1) * chunk, :], twice[...])
             for start in range(0, chunk, tile):
@@ -453,12 +447,7 @@
     tile = min(16, chunk)
     return pl.pallas_call(
         functools.partial(proto_first_kernel, chunk, tile, lead),
-        in_specs=[
-            pl.BlockSpec(memory_space=pltpu.SMEM),
-            WHOLE,
-            pl.BlockSpec(memory_space=pl.ANY),
-            WHOLE,
-        ],
+        in_specs=[pl.BlockSpec(memory_space=pltpu.SMEM)] + [WHOLE] * 3,
         out_specs=[WHOLE] * 2,
         out_shape=[
             pltpu.VMEM((width, count * rows), bf16),
@@ -471,13 +460,11 @@
             pltpu.VMEM((2, chunk, rows), f32),
             pltpu.VMEM((width, rows), bf16),
             pltpu.VMEM((width, depth), f32),
-            pltpu.VMEM((count, depth, rows), bf16),
-            pltpu.SemaphoreType.DMA((count,)),
         ],
         compiler_params=params(),
         cost_estimate=SMALL,
         name="proto_first",
-    )(place, protos, in_hbm(views), totals)
+    )(place, protos, views, totals)
 
 
 def proto_last_kernel(groups, place, *refs):
@@ -799,18 +786,17 @@
     rounds = stages(nb)
     for n, steps in enumerate(rounds):
         others = [flipped(tot_all, "batch", nb, step) for step in steps]
-        if queue:
-            parts = trade(col, "batch", nb, steps, queue, softs)
-        else:
-            parts = trade(col, "batch", nb, steps, halves, taken)
+        parts = trade(col, "batch", nb, steps, halves, taken)
         others, parts = lax.optimization_barrier((others, parts))
         tot_all = jnp.concatenate([tot_all, *others], axis=0)
         if n < len(rounds) - 1:
             for part in parts:
                 col = col + part
     scale, row = rowsum(expo, [col, *parts])
-    halves = [None] * rest + halves
-    col = colsum(expo, summed(row, "proto", npr, halves, taken))[0]
+    queue = [None] * rest + queue
+    col = colsum(expo, summed(row, "proto", npr, queue, softs))[0]
+    for left, results in ((halves, taken), (queue, softs)):
+        results.extend(work[0](*work[1]) for work in left if work)
     unit_t = taken[-1]
 
     col, views_all = lax.optimization_barrier((col, views_all))
@@ -836,21 +822,21 @@
             grads = [(grads[0].astype(f32) + grads[1].astype(f32)).astype(bf16)]
             others[0], grads[0] = lax.optimization_barrier((others[0], grads[0]))
         if turn * 2 < npr:
-            grads = [grads[0], flipped(grads[0], "proto", npr, turn)]
             turn *= 2
+            grads = [grads[0], flipped(grads[0], "proto", npr, npr // turn)]
         total_all = jnp.concatenate([total_all, *others], axis=0)
 
     while turn * 2 < npr:
         if len(grads) > 1:
             grads = [(grads[0].astype(f32) + grads[1].astype(f32)).astype(bf16)]
-        grads = [grads[0], flipped(grads[0], "proto", npr, turn)]
         turn *= 2
+        grads = [grads[0], flipped(grads[0], "proto", npr, npr // turn)]
     if len(grads) > 1:
         grads = [(grads[0].astype(f32) + grads[1].astype(f32)).astype(bf16)]
     expos, parts = [x for x, _ in owns], [x for _, x in owns]
     queue = [(proto_last, (place, expos, parts, scale, protos_own, views_all, total_all))]
     found = []
-    grads = [grads[0], *trade(grads[0], "proto", npr, [npr // 2], queue, found)]
+    grads = [grads[0], *trade(grads[0], "proto", npr, [1], queue, found)]
     grad_proto = lax.all_gather(found[0], "batch", axis=0, tiled=True)
     both = backward(nb, npr, turn_p, *grads, pos, raw, pre, embeddings, hid, w_out)
     for steps in stages(nb):

time: 195 us -> 193 us (0.990)
  Pallas kernels: 93.2 us -> 89.3 us
  waiting for transfers between devices: 35 us -> 38.6 us
  starting transfers between devices: 50.3 us -> 47.5 us
    ppermute x41, waiting for transfers between devices: 31.5 us -> 36.8 us  [flipped(): return lax.ppermute(x, axis, [(i, i ^ step) for i in range(size)])]
    pallas_call x4, Pallas kernels: 17 us -> 13 us  [proto_first(): pl.pallas_call(functools.partial(proto_first_kernel, chunk, tile, lead),...]
    ppermute x41, starting transfers between devices: 50.2 us -> 47.4 us  [flipped(): return lax.ppermute(x, axis, [(i, i ^ step) for i in range(size)])]
  transfers between devices with their start and end apart: 43 -> 43, of which waited for: 14 -> 16; matrix products, arithmetic and copies ran while one was open for 0% -> 0% of each run, Pallas kernels for 38% -> 36%
where the time goes in v10:
time: 193 us
  Pallas kernels  89.3 us (46%)
  starting transfers between devices  47.5 us (25%)
  waiting for transfers between devices  38.6 us (20%)
  between operations  14.6 us (8%)
  local copies, waits for them, and re-layouts  2.63 us (1%)
    ppermute x41, starting transfers between devices, flipped(): return lax.ppermute(x, axis, [(i, i ^ step) for i in range(size)])  47.4 us
    ppermute x41, waiting for transfers between devices, flipped(): return lax.ppermute(x, axis, [(i, i ^ step) for i in range(size)])  36.8 us
    pallas_call x4, Pallas kernels, view_soft(): pl.pallas_call(functools.partial(view_soft_body, block, min(32, chunk), l...  13.8 us
    pallas_call x4, Pallas kernels, proto_first(): pl.pallas_call(functools.partial(proto_first_kernel, chunk, tile, lead),...  13 us
    pallas_call x1, Pallas kernels, first_pass(): pl.pallas_call(functools.partial(first_kernel, block, chunk, tile), in_sp...  11 us
    pallas_call x1, Pallas kernels, rowsum_last(): pl.pallas_call(functools.partial(rowsum_last_kernel, pieces, len(parts)),...  9.45 us
    pallas_call x2, Pallas kernels, rowsum(): pl.pallas_call(functools.partial(rowsum_kernel, len(parts)), in_specs=[WH...  7.53 us
    pallas_call x1, Pallas kernels, head(): pl.pallas_call(head_kernel, grid=(steps,), in_specs=[pl.BlockSpec((block,...  7.41 us
  transfers between devices with their start and end apart: 43, of which 16 were waited for; matrix products, arithmetic and copies ran while one was open for 0% of the time, Pallas kernels for 36%

profile of v10, /device:TPU:0, one launch (start us, length us, event | category | flops | bytes accessed | tf_op | source)
XLA Modules:
  0.0 193.1 jit_solution(16986439477015703851)
XLA Ops:
  7.2 7.4 %head.1 = (f32[1024,512]{1,0:T(8,128)}, bf16[1024,512]{1,0:T(8,128)(2,1)}, f32[1024,128]{1,0:T(8,128)}, bf16[1024,128]{1,0:T(8,128)(2,1)S(1)}, bf16[128,1024]{1,0:T(8,128)(2,1)}, /*index=5*/s32[1,1024]{1,0:T(1,128)S(1)}) custom-call(bf16[1024,1024]{1,0:T(8,128)(2,1)} %emb.3, s32[1,1024]{1,0:T(1,128)} %bitcast.25, bf16[1024,512]{1,0:T(8,128)(2,1)} %w_in.1, ...), custom_call_target="tpu_custom_call" | custom-call | tf_op jit(solution)/shard_map/head/pallas_call | solution.py:105
  14.8 11.0 %first_pass.1 = (bf16[1024,8192]{1,0:T(8,128)(2,1)S(1)}, f32[1,8192]{1,0:T(1,128)S(1)}, f32[1,1024]{1,0:T(1,128)S(1)}) custom-call(bf16[1024,128]{1,0:T(8,128)(2,1)S(1)} %get-tuple-element.164.views.refs_0_, bf16[8192,128]{1,0:T(8,128)(2,1)S(1)} %copy-done.1), custom_call_target="tpu_custom_call" | custom-call | flops 1000 | bytes 1000 | tf_op jit(solution)/shard_map/first_pass/pallas_call | solution.py:190
  25.8 3.0 %collective-permute-start = (f32[1,8192]{1,0:T(1,128)S(1)}, f32[1,8192]{1,0:T(1,128)S(1)}, u32[]{:S(2)}, u32[]{:S(2)}) collective-permute-start(f32[1,8192]{1,0:T(1,128)S(1)} %get-tuple-element.135), channel_id=1, source_target_pairs={{0,4},{4,0},{8,12},{12,8},{16,20},{20,16},{24,28},{28,24},{1,5},{5... | collective-permute-start | bytes 98312 | tf_op jit(solution)/shard_map/ppermute | solution.py:736
  28.8 3.5 %view_soft.4.refs_0_ = f32[1024,128]{1,0:T(8,128)S(1)} custom-call(bf16[1024,128]{1,0:T(8,128)(2,1)S(1)} %get-tuple-element.164.views.refs_0_, bf16[8192,128]{1,0:T(8,128)(2,1)S(1)} %copy-done.1), custom_call_target="tpu_custom_call" | custom-call | flops 1000 | bytes 1000 | tf_op jit(solution)/shard_map/view_soft/pallas_call | solution.py:539
  32.4 1.6 collective-permute-start.1
  34.0 2.6 %collective-permute-start.2 = (f32[1,8192]{1,0:T(1,128)S(1)}, f32[1,8192]{1,0:T(1,128)S(1)}, u32[]{:S(2)}, u32[]{:S(2)}) collective-permute-start(f32[1,8192]{1,0:T(1,128)S(1)} %add.80.refs_0_), channel_id=1, source_target_pairs={{0,16},{4,20},{8,24},{12,28},{16,0},{20,4},{24,8},{28,12},{1,17},{... | collective-permute-start | bytes 98312 | tf_op jit(solution)/shard_map/ppermute | solution.py:736
  36.8 3.5 %view_soft.5.refs_1_ = f32[1024,128]{1,0:T(8,128)S(1)} custom-call(bf16[1024,128]{1,0:T(8,128)(2,1)S(1)} %get-tuple-element.164.views.refs_0_, bf16[8192,128]{1,0:T(8,128)(2,1)S(1)} %copy-done.1), custom_call_target="tpu_custom_call" | custom-call | flops 1000 | bytes 1000 | tf_op jit(solution)/shard_map/view_soft/pallas_call | solution.py:539
  42.3 3.8 %rowsum.2 = (f32[1,8192]{1,0:T(1,128)}, f32[1,1024]{1,0:T(1,128)S(1)}) custom-call(bf16[1024,8192]{1,0:T(8,128)(2,1)S(1)} %get-tuple-element.134.expo.refs_0_.refs_1_.refs_2_.refs_3_, f32[1,8192]{1,0:T(1,128)S(1)} %add.80.refs_0_, f32[1,8192]{1,0:T(1,128)S(1)} %collective-permute-done.1.refs_1_, f32[1,8192]{1,0:T(1,128)S(1)} %collective-permute-done.2.refs_2_, ...), custom_call_target="tpu_custom_call" | custom-call | flops 1000 | bytes 1000 | tf_op jit(solution)/shard_map/rowsum/pallas_call | solution.py:264
  46.2 1.6 collective-permute-start.5
  48.0 3.5 %view_soft.6.refs_2_ = f32[1024,128]{1,0:T(8,128)S(1)} custom-call(bf16[1024,128]{1,0:T(8,128)(2,1)S(1)} %get-tuple-element.164.views.refs_0_, bf16[8192,128]{1,0:T(8,128)(2,1)S(1)} %copy-done.1), custom_call_target="tpu_custom_call" | custom-call | flops 1000 | bytes 1000 | tf_op jit(solution)/shard_map/view_soft/pallas_call | solution.py:539
  51.6 2.2 %colsum.2 = f32[1,1,8192]{2,1,0:T(1,128)S(1)} custom-call(bf16[1024,8192]{1,0:T(8,128)(2,1)S(1)} %get-tuple-element.134.expo.refs_0_.refs_1_.refs_2_.refs_3_, f32[1,1024]{1,0:T(1,128)S(1)} %get-tuple-element.268.refs_0_), custom_call_target="tpu_custom_call" | custom-call | flops 1000 | bytes 1000 | tf_op jit(solution)/shard_map/colsum/pallas_call | solution.py:404
  55.9 1.9 unit_t.2.refs_0_
  58.9 2.2 %collective-permute-start.13 = (f32[1,8192]{1,0:T(1,128)S(1)}, f32[1,8192]{1,0:T(1,128)S(1)}, u32[]{:S(2)}, u32[]{:S(2)}) collective-permute-start(f32[1,8192]{1,0:T(1,128)S(1)} %bitcast_add_fusion.refs_0_), channel_id=1, source_target_pairs={{0,16},{4,20},{8,24},{12,28},{16,0},{20,4},{24,8},{28,12},{1,17},{... | collective-permute-start | bytes 98312 | tf_op jit(solution)/shard_map/ppermute | solution.py:736
  61.1 2.2 %collective-permute-start.14 = (f32[1,8192]{1,0:T(1,128)S(1)}, f32[1,8192]{1,0:T(1,128)S(1)}, u32[]{:S(2)}, u32[]{:S(2)}) collective-permute-start(f32[1,8192]{1,0:T(1,128)S(1)} %bitcast_add_fusion.refs_0_), channel_id=1, source_target_pairs={{0,24},{4,28},{8,16},{12,20},{16,8},{20,12},{24,0},{28,4},{1,25},{... | collective-permute-start | bytes 98312 | tf_op jit(solution)/shard_map/ppermute | solution.py:736
  63.3 1.7 collective-permute-start.11
  65.0 1.8 collective-permute-start.9
  66.8 1.9 unit_t.3.refs_8_
  69.9 3.8 %rowsum.3 = (f32[1,8192]{1,0:T(1,128)}, f32[1,1024]{1,0:T(1,128)S(1)}) custom-call(bf16[1024,8192]{1,0:T(8,128)(2,1)S(1)} %get-tuple-element.134.expo.refs_0_.refs_1_.refs_2_.refs_3_, f32[1,8192]{1,0:T(1,128)S(1)} %bitcast_add_fusion.refs_0_, f32[1,8192]{1,0:T(1,128)S(1)} %collective-permute-done.12.refs_1_, f32[1,8192]{1,0:T(1,128)S(1)} %collective-permute-done.13.refs_2_, ...), custom_call_target="tpu_custom_call" | custom-call | flops 1000 | bytes 1000 | tf_op jit(solution)/shard_map/rowsum/pallas_call | solution.py:264
  75.6 3.5 %view_soft.7.refs_3_ = f32[1024,128]{1,0:T(8,128)S(1)} custom-call(bf16[1024,128]{1,0:T(8,128)(2,1)S(1)} %get-tuple-element.164.views.refs_0_, bf16[8192,128]{1,0:T(8,128)(2,1)S(1)} %copy-done.1), custom_call_target="tpu_custom_call" | custom-call | flops 1000 | bytes 1000 | tf_op jit(solution)/shard_map/view_soft/pallas_call | solution.py:539
  79.9 2.4 %colsum.3 = f32[1,1,8192]{2,1,0:T(1,128)S(1)} custom-call(bf16[1024,8192]{1,0:T(8,128)(2,1)S(1)} %get-tuple-element.134.expo.refs_0_.refs_1_.refs_2_.refs_3_, f32[1,1024]{1,0:T(1,128)S(1)} %get-tuple-element.163.refs_0_, f32[1,1024]{1,0:T(1,128)S(1)} %collective-permute-done.15.refs_1_, f32[1,1024]{1,0:T(1,128)S(1)} %collective-permute-done.16.refs_2_, ...), custom_call_target="tpu_custom_call" | custom-call | flops 1000 | bytes 1000 | tf_op jit(solution)/shard_map/colsum/pallas_call | solution.py:404
  82.9 1.6 copy-done.2
  84.5 3.3 %proto_first.4 = (bf16[1024,2048]{1,0:T(8,128)(2,1)S(1)}, f32[1024,128]{1,0:T(8,128)S(1)}) custom-call(s32[1]{0:T(128)} %bitcast.1.place, bf16[1024,128]{1,0:T(8,128)(2,1)S(1)} %constant_dynamic-slice_fusion.protos.refs_9_, bf16[8,128,1024]{2,1,0:T(8,128)(2,1)S(1)} %bitcast.13, f32[8,1,1024]{2,1,0:T(1,128)S(1)} %constant_dynamic-update-slice_fusion.totals), custom_call_target="tpu_custom_call" | custom-call | flops 1000 | bytes 1000 | tf_op jit(solution)/shard_map/proto_first/pallas_call | solution.py:448
  88.7 1.9 %collective-permute-start.20 = (f32[1,8192]{1,0:T(1,128)S(1)}, f32[1,8192]{1,0:T(1,128)S(1)}, u32[]{:S(2)}, u32[]{:S(2)}) collective-permute-start(f32[1,8192]{1,0:T(1,128)S(1)} %add.85.refs_4_), channel_id=1, source_target_pairs={{0,16},{4,20},{8,24},{12,28},{16,0},{20,4},{24,8},{28,12},{1,17},{... | collective-permute-start | bytes 98312 | tf_op jit(solution)/shard_map/ppermute | solution.py:736
  90.7 1.6 collective-permute-start.21
  92.2 3.3 %proto_first.5 = (bf16[1024,2048]{1,0:T(8,128)(2,1)S(1)}, f32[1024,128]{1,0:T(8,128)S(1)}) custom-call(s32[1]{0:T(128)} %bitcast.1.place, bf16[1024,128]{1,0:T(8,128)(2,1)S(1)} %constant_dynamic-slice_fusion.protos.refs_9_, bf16[8,128,1024]{2,1,0:T(8,128)(2,1)S(1)} %bitcast.14, f32[8,1,1024]{2,1,0:T(1,128)S(1)} %constant_dynamic-update-slice_fusion.totals), custom_call_target="tpu_custom_call" | custom-call | flops 1000 | bytes 1000 | tf_op jit(solution)/shard_map/proto_first/pallas_call | solution.py:448
  96.4 9.5 %rowsum_last.1 = (f32[1,8192]{1,0:T(1,128)S(1)}, f32[1,1024]{1,0:T(1,128)S(1)}, f32[1024,128]{1,0:T(8,128)S(1)}) custom-call(bf16[1024,8192]{1,0:T(8,128)(2,1)} %copy-done, bf16[1024,8192]{1,0:T(8,128)(2,1)} %copy-done, bf16[1024,8192]{1,0:T(8,128)(2,1)} %copy-done, bf16[1024,8192]{1,0:T(8,128)(2,1)} %copy-done, f32[1,8192]{1,0:T(1,128)S(1)} %add.85.refs_4_, ...), custom_call_target="tpu_custom_call" | custom-call | flops 1000 | bytes 1000 | tf_op jit(solution)/shard_map/rowsum_last/pallas_call | solution.py:323
  105.9 1.6 collective-permute-start.23
  107.8 3.3 %proto_first.6 = (bf16[1024,2048]{1,0:T(8,128)(2,1)S(1)}, f32[1024,128]{1,0:T(8,128)S(1)}) custom-call(s32[1]{0:T(128)} %bitcast.1.place, bf16[1024,128]{1,0:T(8,128)(2,1)S(1)} %constant_dynamic-slice_fusion.protos.refs_9_, bf16[8,128,1024]{2,1,0:T(8,128)(2,1)S(1)} %bitcast.15, f32[8,1,1024]{2,1,0:T(1,128)S(1)} %constant_dynamic-update-slice_fusion.totals), custom_call_target="tpu_custom_call" | custom-call | flops 1000 | bytes 1000 | tf_op jit(solution)/shard_map/proto_first/pallas_call | solution.py:448
  112.6 2.2 %view_grad.1 = bf16[1024,128]{1,0:T(8,128)(2,1)S(1)} custom-call(f32[1024,128]{1,0:T(8,128)S(1)} %get-tuple-element.209.code, f32[1,1024]{1,0:T(1,128)S(1)} %get-tuple-element.210.tot, f32[1,1024]{1,0:T(1,128)S(1)} %get-tuple-element.211.total, f32[1024,128]{1,0:T(8,128)} %copy-done.5, f32[1024,128]{1,0:T(8,128)} %copy-done.6, f32[1024,128]{1,0:T(8,128)} %copy-done.7, ...), custom_call_target="tpu_custom_call" | custom-call | flops 1000 | bytes 1000 | tf_op jit(solution)/shard_map/view_grad/pallas_call | solution.py:567
  116.5 2.2 %collective-permute-start.27 = (f32[2,1,1024]{2,1,0:T(1,128)S(1)}, f32[2,1,1024]{2,1,0:T(1,128)S(1)}, u32[]{:S(2)}, u32[]{:S(2)}) collective-permute-start(f32[2,1,1024]{2,1,0:T(1,128)S(1)} %pad_maximum_fusion.4), channel_id=1, source_target_pairs={{0,16},{4,20},{8,24},{12,28},{16,0},{20,4},{24,8},{28,12},{1,17},{... | collective-permute-start | bytes 24584 | tf_op jit(solution)/shard_map/ppermute | solution.py:736
  118.7 2.2 %collective-permute-start.28 = (f32[2,1,1024]{2,1,0:T(1,128)S(1)}, f32[2,1,1024]{2,1,0:T(1,128)S(1)}, u32[]{:S(2)}, u32[]{:S(2)}) collective-permute-start(f32[2,1,1024]{2,1,0:T(1,128)S(1)} %pad_maximum_fusion.4), channel_id=1, source_target_pairs={{0,24},{4,28},{8,16},{12,20},{16,8},{20,12},{24,0},{28,4},{1,25},{... | collective-permute-start | bytes 24584 | tf_op jit(solution)/shard_map/ppermute | solution.py:736
  120.9 3.3 %proto_first.7 = (bf16[1024,2048]{1,0:T(8,128)(2,1)S(1)}, f32[1024,128]{1,0:T(8,128)S(1)}) custom-call(s32[1]{0:T(128)} %bitcast.1.place, bf16[1024,128]{1,0:T(8,128)(2,1)S(1)} %constant_dynamic-slice_fusion.protos.refs_9_, bf16[8,128,1024]{2,1,0:T(8,128)(2,1)S(1)} %bitcast.16, f32[8,1,1024]{2,1,0:T(1,128)S(1)} %constant_dynamic-update-slice_fusion.totals), custom_call_target="tpu_custom_call" | custom-call | flops 1000 | bytes 1000 | tf_op jit(solution)/shard_map/proto_first/pallas_call | solution.py:448
  124.4 5.4 %proto_last.1 = bf16[1024,128]{1,0:T(8,128)(2,1)} custom-call(s32[1]{0:T(128)} %bitcast.1.place, bf16[1024,2048]{1,0:T(8,128)(2,1)S(1)} %get-tuple-element.239.refs_0_, bf16[1024,2048]{1,0:T(8,128)(2,1)S(1)} %get-tuple-element.240.refs_1_, bf16[1024,2048]{1,0:T(8,128)(2,1)S(1)} %get-tuple-element.241.refs_2_, ...), custom_call_target="tpu_custom_call" | custom-call | tf_op jit(solution)/shard_map/proto_last/pallas_call | solution.py:498
  129.8 5.9 %backward.1 = f32[8,144,128]{2,1,0:T(8,128)S(1)} custom-call(s32[1]{0:T(128)} %bitcast.turn, bf16[1024,128]{1,0:T(8,128)(2,1)S(1)} %add_convert_fusion.grad_a, bf16[1024,128]{1,0:T(8,128)(2,1)S(1)} %collective-permute-done.30.grad_b, s32[1,1024]{1,0:T(1,128)S(1)} %get-tuple-element.252.pos, f32[1024,128]{1,0:T(8,128)} %get-tuple-element.253.raw, ...), custom_call_target="tpu_custom_call" | custom-call | tf_op jit(solution)/shard_map/backward/pallas_call | solution.py:631
  137.2 7.7 %collective-permute-done.31 = bf16[4,144,128]{2,1,0:T(8,128)(2,1)S(1)} collective-permute-done((bf16[4,144,128]{2,1,0:T(8,128)(2,1)S(1)}, bf16[4,144,128]{2,1,0:T(8,128)(2,1)S(1)}, u32[]{:S(2)}, u32[]{:S(2)}) %collective-permute-start.31) | collective-permute-done | bytes 147488 | tf_op jit(solution)/shard_map/ppermute | solution.py:736
  145.0 1.8 collective-permute-start.33
  146.8 2.6 %collective-permute-start.34 = (bf16[1,144,128]{2,1,0:T(8,128)(2,1)S(1)}, bf16[1,144,128]{2,1,0:T(8,128)(2,1)S(1)}, u32[]{:S(2)}, u32[]{:S(2)}) collective-permute-start(bf16[1,144,128]{2,1,0:T(8,128)(2,1)S(1)} %get-tuple-element.264), channel_id=1, source_target_pairs={{0,24},{4,28},{8,16},{12,20},{16,8},{20,12},{24,0},{28,4},{1,25},{... | collective-permute-start | bytes 110600 | tf_op jit(solution)/shard_map/ppermute | solution.py:736
  149.6 3.6 %collective-permute-done.33 = bf16[1,144,128]{2,1,0:T(8,128)(2,1)S(1)} collective-permute-done((bf16[1,144,128]{2,1,0:T(8,128)(2,1)S(1)}, bf16[1,144,128]{2,1,0:T(8,128)(2,1)S(1)}, u32[]{:S(2)}, u32[]{:S(2)}) %collective-permute-start.33) | collective-permute-done | bytes 36896 | tf_op jit(solution)/shard_map/ppermute | solution.py:736
  153.4 1.6 collective-permute-start.35
  156.0 1.8 collective-permute-start.37
  157.9 2.3 %collective-permute-done.36 = bf16[1,144,128]{2,1,0:T(8,128)(2,1)S(1)} collective-permute-done((bf16[1,144,128]{2,1,0:T(8,128)(2,1)S(1)}, bf16[1,144,128]{2,1,0:T(8,128)(2,1)S(1)}, u32[]{:S(2)}, u32[]{:S(2)}) %collective-permute-start.36) | collective-permute-done | bytes 36896 | tf_op jit(solution)/shard_map/ppermute | solution.py:736
  160.2 1.8 collective-permute-done.37
  162.9 7.5 %collective-permute-done.38 = bf16[4,144,128]{2,1,0:T(8,128)(2,1)S(1)} collective-permute-done((bf16[4,144,128]{2,1,0:T(8,128)(2,1)S(1)}, bf16[4,144,128]{2,1,0:T(8,128)(2,1)S(1)}, u32[]{:S(2)}, u32[]{:S(2)}) %collective-permute-start.38) | collective-permute-done | bytes 147488 | tf_op jit(solution)/shard_map/ppermute | solution.py:736
  170.7 6.5 %collective-permute-done.39 = bf16[1,8,144,128]{3,2,1,0:T(8,128)(2,1)S(1)} collective-permute-done((bf16[1,8,144,128]{3,2,1,0:T(8,128)(2,1)S(1)}, bf16[1,8,144,128]{3,2,1,0:T(8,128)(2,1)S(1)}, u32[]{:S(2)}, u32[]{:S(2)}) %collective-permute-start.39) | collective-permute-done | bytes 294944 | tf_op jit(solution)/shard_map/ppermute | solution.py:736
  177.4 1.9 collective-permute-done.40.refs_1_
  179.3 2.1 %unpack.1 = (f32[1024,512]{1,0:T(8,128)}, f32[512,128]{1,0:T(8,128)}) custom-call(s32[2]{0:T(128)S(1)} %pad_add_fusion.place, bf16[2,8,144,128]{3,2,1,0:T(8,128)(2,1)S(1)} %pad_maximum_fusion.refs_0_, bf16[2,8,144,128]{3,2,1,0:T(8,128)(2,1)S(1)} %collective-permute-done.40.refs_1_), custom_call_target="tpu_custom_call" | custom-call | tf_op jit(solution)/shard_map/unpack/pallas_call | solution.py:665
  181.4 1.7 all-gather.4.cloned.1.call-done.x
  183.1 3.1 %widen.1 = f32[8192,128]{1,0:T(8,128)} custom-call(bf16[8192,128]{1,0:T(8,128)(2,1)} %all-gather.4.cloned.1.call-done.x), custom_call_target="tpu_custom_call" | custom-call | tf_op jit(solution)/shard_map/widen/pallas_call | solution.py:699
  (111 shorter events, 20.7 us)
Async XLA Ops:
  7.2 7.6 %copy-start.1 = (bf16[8192,128]{1,0:T(8,128)(2,1)S(1)}, bf16[8192,128]{1,0:T(8,128)(2,1)}, u32[]{:S(2)}) copy-start(bf16[8192,128]{1,0:T(8,128)(2,1)} %refs_1_.3) | copy-start | bytes 6291460
  7.2 75.1 %all-gather.6.cloned.1.call-start = ((), (), s32[]{:S(2)}) async-start(), calls=%async_computation.1 | async-start | bytes 2359296 | tf_op jit(solution)/shard_map/all_gather | solution.py:757
  14.7 168.5 %all-gather.4.cloned.1.call-start = ((), (), s32[]{:S(2)}) async-start(), calls=%async_computation | async-start | bytes 2359296 | tf_op jit(solution)/shard_map/all_gather | solution.py:840
  25.8 54.1 %copy-start = (bf16[1024,8192]{1,0:T(8,128)(2,1)}, bf16[1024,8192]{1,0:T(8,128)(2,1)S(1)}, u32[]{:S(2)}) copy-start(bf16[1024,8192]{1,0:T(8,128)(2,1)S(1)} %get-tuple-element.134.expo.refs_0_.refs_1_.refs_2_.refs_3_) | copy-start | bytes 50331652
  25.8 6.5 %collective-permute-start = (f32[1,8192]{1,0:T(1,128)S(1)}, f32[1,8192]{1,0:T(1,128)S(1)}, u32[]{:S(2)}, u32[]{:S(2)}) collective-permute-start(f32[1,8192]{1,0:T(1,128)S(1)} %get-tuple-element.135), channel_id=1, source_target_pairs={{0,4},{4,0},{8,12},{12,8},{16,20},{20,16},{24,28},{28,24},{1,5},{5... | collective-permute-start | bytes 98312 | tf_op jit(solution)/shard_map/ppermute | solution.py:736
  32.3 13.8 %copy-start.5 = (f32[1024,128]{1,0:T(8,128)}, f32[1024,128]{1,0:T(8,128)S(1)}, u32[]{:S(2)}) copy-start(f32[1024,128]{1,0:T(8,128)S(1)} %view_soft.4.refs_0_) | copy-start | bytes 1572868
  32.4 7.9 %collective-permute-start.1 = (f32[1,8192]{1,0:T(1,128)S(1)}, f32[1,8192]{1,0:T(1,128)S(1)}, u32[]{:S(2)}, u32[]{:S(2)}) collective-permute-start(f32[1,8192]{1,0:T(1,128)S(1)} %add.80.refs_0_), channel_id=1, source_target_pairs={{0,8},{4,12},{8,0},{12,4},{16,24},{20,28},{24,16},{28,20},{1,9},{5... | collective-permute-start | bytes 98312 | tf_op jit(solution)/shard_map/ppermute | solution.py:736
  34.0 6.8 %collective-permute-start.2 = (f32[1,8192]{1,0:T(1,128)S(1)}, f32[1,8192]{1,0:T(1,128)S(1)}, u32[]{:S(2)}, u32[]{:S(2)}) collective-permute-start(f32[1,8192]{1,0:T(1,128)S(1)} %add.80.refs_0_), channel_id=1, source_target_pairs={{0,16},{4,20},{8,24},{12,28},{16,0},{20,4},{24,8},{28,12},{1,17},{... | collective-permute-start | bytes 98312 | tf_op jit(solution)/shard_map/ppermute | solution.py:736
  36.6 5.7 %collective-permute-start.3 = (f32[1,8192]{1,0:T(1,128)S(1)}, f32[1,8192]{1,0:T(1,128)S(1)}, u32[]{:S(2)}, u32[]{:S(2)}) collective-permute-start(f32[1,8192]{1,0:T(1,128)S(1)} %add.80.refs_0_), channel_id=1, source_target_pairs={{0,24},{4,28},{8,16},{12,20},{16,8},{20,12},{24,0},{28,4},{1,25},{... | collective-permute-start | bytes 98312 | tf_op jit(solution)/shard_map/ppermute | solution.py:736
  40.3 5.8 %copy-start.6 = (f32[1024,128]{1,0:T(8,128)}, f32[1024,128]{1,0:T(8,128)S(1)}, u32[]{:S(2)}) copy-start(f32[1024,128]{1,0:T(8,128)S(1)} %view_soft.5.refs_1_) | copy-start | bytes 1572868
  46.1 5.4 %collective-permute-start.4 = (f32[2,1024]{1,0:T(2,128)S(1)}, f32[2,1024]{1,0:T(2,128)S(1)}, u32[]{:S(2)}, u32[]{:S(2)}) collective-permute-start(f32[2,1024]{1,0:T(2,128)S(1)} %pad_maximum_fusion.2), channel_id=1, source_target_pairs={{0,1},{1,0},{2,3},{3,2},{4,5},{5,4},{6,7},{7,6},{8,9},{9,8},{10,11... | collective-permute-start | bytes 24584 | tf_op jit(solution)/shard_map/ppermute | solution.py:736
  46.2 5.3 %collective-permute-start.5 = (f32[2,1024]{1,0:T(2,128)S(1)}, f32[2,1024]{1,0:T(2,128)S(1)}, u32[]{:S(2)}, u32[]{:S(2)}) collective-permute-start(f32[2,1024]{1,0:T(2,128)S(1)} %pad_maximum_fusion.2), channel_id=1, source_target_pairs={{0,2},{1,3},{2,0},{3,1},{4,6},{5,7},{6,4},{7,5},{8,10},{9,11},{10,... | collective-permute-start | bytes 24584 | tf_op jit(solution)/shard_map/ppermute | solution.py:736
  47.7 3.8 %collective-permute-start.6 = (f32[2,1024]{1,0:T(2,128)S(1)}, f32[2,1024]{1,0:T(2,128)S(1)}, u32[]{:S(2)}, u32[]{:S(2)}) collective-permute-start(f32[2,1024]{1,0:T(2,128)S(1)} %pad_maximum_fusion.2), channel_id=1, source_target_pairs={{0,3},{1,2},{2,1},{3,0},{4,7},{5,6},{6,5},{7,4},{8,11},{9,10},{10,... | collective-permute-start | bytes 24584 | tf_op jit(solution)/shard_map/ppermute | solution.py:736
  53.8 4.8 %collective-permute-start.8 = (f32[1,8192]{1,0:T(1,128)S(1)}, f32[1,8192]{1,0:T(1,128)S(1)}, u32[]{:S(2)}, u32[]{:S(2)}) collective-permute-start(f32[1,8192]{1,0:T(1,128)S(1)} %bitcast.20), channel_id=1, source_target_pairs={{0,4},{4,0},{8,12},{12,8},{16,20},{20,16},{24,28},{28,24},{1,5},{5... | collective-permute-start | bytes 98312 | tf_op jit(solution)/shard_map/ppermute | solution.py:736
  54.4 4.4 %collective-permute-start.7 = (f32[1,1,1024]{2,1,0:T(1,128)S(1)}, f32[1,1,1024]{2,1,0:T(1,128)S(1)}, u32[]{:S(2)}, u32[]{:S(2)}) collective-permute-start(f32[1,1,1024]{2,1,0:T(1,128)S(1)} %get-tuple-element.267), channel_id=1, source_target_pairs={{0,4},{4,0},{8,12},{12,8},{16,20},{20,16},{24,28},{28,24},{1,5},{5... | collective-permute-start | bytes 12296 | tf_op jit(solution)/shard_map/ppermute | solution.py:736
  58.8 6.2 %collective-permute-start.12 = (f32[1,8192]{1,0:T(1,128)S(1)}, f32[1,8192]{1,0:T(1,128)S(1)}, u32[]{:S(2)}, u32[]{:S(2)}) collective-permute-start(f32[1,8192]{1,0:T(1,128)S(1)} %bitcast_add_fusion.refs_0_), channel_id=1, source_target_pairs={{0,8},{4,12},{8,0},{12,4},{16,24},{20,28},{24,16},{28,20},{1,9},{5... | collective-permute-start | bytes 98312 | tf_op jit(solution)/shard_map/ppermute | solution.py:736
  58.9 9.8 %collective-permute-start.13 = (f32[1,8192]{1,0:T(1,128)S(1)}, f32[1,8192]{1,0:T(1,128)S(1)}, u32[]{:S(2)}, u32[]{:S(2)}) collective-permute-start(f32[1,8192]{1,0:T(1,128)S(1)} %bitcast_add_fusion.refs_0_), channel_id=1, source_target_pairs={{0,16},{4,20},{8,24},{12,28},{16,0},{20,4},{24,8},{28,12},{1,17},{... | collective-permute-start | bytes 98312 | tf_op jit(solution)/shard_map/ppermute | solution.py:736
  61.1 7.7 %collective-permute-start.14 = (f32[1,8192]{1,0:T(1,128)S(1)}, f32[1,8192]{1,0:T(1,128)S(1)}, u32[]{:S(2)}, u32[]{:S(2)}) collective-permute-start(f32[1,8192]{1,0:T(1,128)S(1)} %bitcast_add_fusion.refs_0_), channel_id=1, source_target_pairs={{0,24},{4,28},{8,16},{12,20},{16,8},{20,12},{24,0},{28,4},{1,25},{... | collective-permute-start | bytes 98312 | tf_op jit(solution)/shard_map/ppermute | solution.py:736
  63.3 6.7 %collective-permute-start.10 = (f32[2,1,1024]{2,1,0:T(1,128)S(1)}, f32[2,1,1024]{2,1,0:T(1,128)S(1)}, u32[]{:S(2)}, u32[]{:S(2)}) collective-permute-start(f32[2,1,1024]{2,1,0:T(1,128)S(1)} %pad_maximum_fusion.3), channel_id=1, source_target_pairs={{0,16},{4,20},{8,24},{12,28},{16,0},{20,4},{24,8},{28,12},{1,17},{... | collective-permute-start | bytes 24584 | tf_op jit(solution)/shard_map/ppermute | solution.py:736
  63.3 6.6 %collective-permute-start.11 = (f32[2,1,1024]{2,1,0:T(1,128)S(1)}, f32[2,1,1024]{2,1,0:T(1,128)S(1)}, u32[]{:S(2)}, u32[]{:S(2)}) collective-permute-start(f32[2,1,1024]{2,1,0:T(1,128)S(1)} %pad_maximum_fusion.3), channel_id=1, source_target_pairs={{0,24},{4,28},{8,16},{12,20},{16,8},{20,12},{24,0},{28,4},{1,25},{... | collective-permute-start | bytes 24584 | tf_op jit(solution)/shard_map/ppermute | solution.py:736
  65.0 4.9 %collective-permute-start.9 = (f32[2,1,1024]{2,1,0:T(1,128)S(1)}, f32[2,1,1024]{2,1,0:T(1,128)S(1)}, u32[]{:S(2)}, u32[]{:S(2)}) collective-permute-start(f32[2,1,1024]{2,1,0:T(1,128)S(1)} %pad_maximum_fusion.3), channel_id=1, source_target_pairs={{0,8},{4,12},{8,0},{12,4},{16,24},{20,28},{24,16},{28,20},{1,9},{5... | collective-permute-start | bytes 24584 | tf_op jit(solution)/shard_map/ppermute | solution.py:736
  73.7 6.1 %collective-permute-start.15 = (f32[1,1024]{1,0:T(1,128)S(1)}, f32[1,1024]{1,0:T(1,128)S(1)}, u32[]{:S(2)}, u32[]{:S(2)}) collective-permute-start(f32[1,1024]{1,0:T(1,128)S(1)} %get-tuple-element.163.refs_0_), channel_id=1, source_target_pairs={{0,1},{1,0},{2,3},{3,2},{4,5},{5,4},{6,7},{7,6},{8,9},{9,8},{10,11... | collective-permute-start | bytes 12296 | tf_op jit(solution)/shard_map/ppermute | solution.py:736
  73.7 6.1 %collective-permute-start.16 = (f32[1,1024]{1,0:T(1,128)S(1)}, f32[1,1024]{1,0:T(1,128)S(1)}, u32[]{:S(2)}, u32[]{:S(2)}) collective-permute-start(f32[1,1024]{1,0:T(1,128)S(1)} %get-tuple-element.163.refs_0_), channel_id=1, source_target_pairs={{0,2},{1,3},{2,0},{3,1},{4,6},{5,7},{6,4},{7,5},{8,10},{9,11},{10,... | collective-permute-start | bytes 12296 | tf_op jit(solution)/shard_map/ppermute | solution.py:736
  75.2 4.7 %collective-permute-start.17 = (f32[1,1024]{1,0:T(1,128)S(1)}, f32[1,1024]{1,0:T(1,128)S(1)}, u32[]{:S(2)}, u32[]{:S(2)}) collective-permute-start(f32[1,1024]{1,0:T(1,128)S(1)} %get-tuple-element.163.refs_0_), channel_id=1, source_target_pairs={{0,3},{1,2},{2,1},{3,0},{4,7},{5,6},{6,5},{7,4},{8,11},{9,10},{10,... | collective-permute-start | bytes 12296 | tf_op jit(solution)/shard_map/ppermute | solution.py:736
  82.3 5.4 %collective-permute-start.18 = (f32[1,8192]{1,0:T(1,128)S(1)}, f32[1,8192]{1,0:T(1,128)S(1)}, u32[]{:S(2)}, u32[]{:S(2)}) collective-permute-start(f32[1,8192]{1,0:T(1,128)S(1)} %bitcast.18), channel_id=1, source_target_pairs={{0,4},{4,0},{8,12},{12,8},{16,20},{20,16},{24,28},{28,24},{1,5},{5... | collective-permute-start | bytes 98312 | tf_op jit(solution)/shard_map/ppermute | solution.py:736
  87.8 7.7 %collective-permute-start.19 = (f32[1,8192]{1,0:T(1,128)S(1)}, f32[1,8192]{1,0:T(1,128)S(1)}, u32[]{:S(2)}, u32[]{:S(2)}) collective-permute-start(f32[1,8192]{1,0:T(1,128)S(1)} %add.85.refs_4_), channel_id=1, source_target_pairs={{0,8},{4,12},{8,0},{12,4},{16,24},{20,28},{24,16},{28,20},{1,9},{5... | collective-permute-start | bytes 98312 | tf_op jit(solution)/shard_map/ppermute | solution.py:736
  88.7 6.8 %collective-permute-start.20 = (f32[1,8192]{1,0:T(1,128)S(1)}, f32[1,8192]{1,0:T(1,128)S(1)}, u32[]{:S(2)}, u32[]{:S(2)}) collective-permute-start(f32[1,8192]{1,0:T(1,128)S(1)} %add.85.refs_4_), channel_id=1, source_target_pairs={{0,16},{4,20},{8,24},{12,28},{16,0},{20,4},{24,8},{28,12},{1,17},{... | collective-permute-start | bytes 98312 | tf_op jit(solution)/shard_map/ppermute | solution.py:736
  90.7 5.7 %collective-permute-start.21 = (f32[1,8192]{1,0:T(1,128)S(1)}, f32[1,8192]{1,0:T(1,128)S(1)}, u32[]{:S(2)}, u32[]{:S(2)}) collective-permute-start(f32[1,8192]{1,0:T(1,128)S(1)} %add.85.refs_4_), channel_id=1, source_target_pairs={{0,24},{4,28},{8,16},{12,20},{16,8},{20,12},{24,0},{28,4},{1,25},{... | collective-permute-start | bytes 98312 | tf_op jit(solution)/shard_map/ppermute | solution.py:736
  96.4 11.4 %copy-start.3 = (bf16[1024,1024]{1,0:T(8,128)(2,1)S(1)}, bf16[1024,1024]{1,0:T(8,128)(2,1)}, u32[]{:S(2)}) copy-start(bf16[1024,1024]{1,0:T(8,128)(2,1)} %all-gather.6.cloned.1.call-done) | copy-start | bytes 6291460
  105.8 5.2 %collective-permute-start.22 = (f32[1,1024]{1,0:T(1,128)S(1)}, f32[1,1024]{1,0:T(1,128)S(1)}, u32[]{:S(2)}, u32[]{:S(2)}) collective-permute-start(f32[1,1024]{1,0:T(1,128)S(1)} %get-tuple-element.194), channel_id=1, source_target_pairs={{0,1},{1,0},{2,3},{3,2},{4,5},{5,4},{6,7},{7,6},{8,9},{9,8},{10,11... | collective-permute-start | bytes 12296 | tf_op jit(solution)/shard_map/ppermute | solution.py:736
  105.9 5.1 %collective-permute-start.23 = (f32[1,1024]{1,0:T(1,128)S(1)}, f32[1,1024]{1,0:T(1,128)S(1)}, u32[]{:S(2)}, u32[]{:S(2)}) collective-permute-start(f32[1,1024]{1,0:T(1,128)S(1)} %get-tuple-element.194), channel_id=1, source_target_pairs={{0,2},{1,3},{2,0},{3,1},{4,6},{5,7},{6,4},{7,5},{8,10},{9,11},{10,... | collective-permute-start | bytes 12296 | tf_op jit(solution)/shard_map/ppermute | solution.py:736
  107.5 3.6 %collective-permute-start.24 = (f32[1,1024]{1,0:T(1,128)S(1)}, f32[1,1024]{1,0:T(1,128)S(1)}, u32[]{:S(2)}, u32[]{:S(2)}) collective-permute-start(f32[1,1024]{1,0:T(1,128)S(1)} %get-tuple-element.194), channel_id=1, source_target_pairs={{0,3},{1,2},{2,1},{3,0},{4,7},{5,6},{6,5},{7,4},{8,11},{9,10},{10,... | collective-permute-start | bytes 12296 | tf_op jit(solution)/shard_map/ppermute | solution.py:736
  111.1 3.8 %collective-permute-start.25 = (f32[1,1,1024]{2,1,0:T(1,128)S(1)}, f32[1,1,1024]{2,1,0:T(1,128)S(1)}, u32[]{:S(2)}, u32[]{:S(2)}) collective-permute-start(f32[1,1,1024]{2,1,0:T(1,128)S(1)} %bitcast.21), channel_id=1, source_target_pairs={{0,4},{4,0},{8,12},{12,8},{16,20},{20,16},{24,28},{28,24},{1,5},{5... | collective-permute-start | bytes 12296 | tf_op jit(solution)/shard_map/ppermute | solution.py:736
  114.9 9.3 %collective-permute-start.29 = (bf16[1024,128]{1,0:T(8,128)(2,1)S(1)}, bf16[1024,128]{1,0:T(8,128)(2,1)S(1)}, u32[]{:S(2)}, u32[]{:S(2)}) collective-permute-start(bf16[1024,128]{1,0:T(8,128)(2,1)S(1)} %view_grad.1), channel_id=1, source_target_pairs={{0,2},{1,3},{2,0},{3,1},{4,6},{5,7},{6,4},{7,5},{8,10},{9,11},{10,... | collective-permute-start | bytes 786440 | tf_op jit(solution)/shard_map/ppermute | solution.py:736
  116.4 7.7 %collective-permute-start.26 = (f32[2,1,1024]{2,1,0:T(1,128)S(1)}, f32[2,1,1024]{2,1,0:T(1,128)S(1)}, u32[]{:S(2)}, u32[]{:S(2)}) collective-permute-start(f32[2,1,1024]{2,1,0:T(1,128)S(1)} %pad_maximum_fusion.4), channel_id=1, source_target_pairs={{0,8},{4,12},{8,0},{12,4},{16,24},{20,28},{24,16},{28,20},{1,9},{5... | collective-permute-start | bytes 24584 | tf_op jit(solution)/shard_map/ppermute | solution.py:736
  116.5 7.7 %collective-permute-start.27 = (f32[2,1,1024]{2,1,0:T(1,128)S(1)}, f32[2,1,1024]{2,1,0:T(1,128)S(1)}, u32[]{:S(2)}, u32[]{:S(2)}) collective-permute-start(f32[2,1,1024]{2,1,0:T(1,128)S(1)} %pad_maximum_fusion.4), channel_id=1, source_target_pairs={{0,16},{4,20},{8,24},{12,28},{16,0},{20,4},{24,8},{28,12},{1,17},{... | collective-permute-start | bytes 24584 | tf_op jit(solution)/shard_map/ppermute | solution.py:736
  118.7 5.5 %collective-permute-start.28 = (f32[2,1,1024]{2,1,0:T(1,128)S(1)}, f32[2,1,1024]{2,1,0:T(1,128)S(1)}, u32[]{:S(2)}, u32[]{:S(2)}) collective-permute-start(f32[2,1,1024]{2,1,0:T(1,128)S(1)} %pad_maximum_fusion.4), channel_id=1, source_target_pairs={{0,24},{4,28},{8,16},{12,20},{16,8},{20,12},{24,0},{28,4},{1,25},{... | collective-permute-start | bytes 24584 | tf_op jit(solution)/shard_map/ppermute | solution.py:736
  124.3 5.5 %collective-permute-start.30 = (bf16[1024,128]{1,0:T(8,128)(2,1)S(1)}, bf16[1024,128]{1,0:T(8,128)(2,1)S(1)}, u32[]{:S(2)}, u32[]{:S(2)}) collective-permute-start(bf16[1024,128]{1,0:T(8,128)(2,1)S(1)} %add_convert_fusion.grad_a), channel_id=1, source_target_pairs={{0,1},{1,0},{2,3},{3,2},{4,5},{5,4},{6,7},{7,6},{8,9},{9,8},{10,11... | collective-permute-start | bytes 786440 | tf_op jit(solution)/shard_map/ppermute | solution.py:736
  135.8 9.1 %collective-permute-start.31 = (bf16[4,144,128]{2,1,0:T(8,128)(2,1)S(1)}, bf16[4,144,128]{2,1,0:T(8,128)(2,1)S(1)}, u32[]{:S(2)}, u32[]{:S(2)}) collective-permute-start(bf16[4,144,128]{2,1,0:T(8,128)(2,1)S(1)} %dynamic-slice_convert_fusion), channel_id=1, source_target_pairs={{0,4},{4,0},{8,12},{12,8},{16,20},{20,16},{24,28},{28,24},{1,5},{5... | collective-permute-start | bytes 442376 | tf_op jit(solution)/shard_map/ppermute | solution.py:736
  145.0 4.6 %collective-permute-start.32 = (bf16[1,144,128]{2,1,0:T(8,128)(2,1)S(1)}, bf16[1,144,128]{2,1,0:T(8,128)(2,1)S(1)}, u32[]{:S(2)}, u32[]{:S(2)}) collective-permute-start(bf16[1,144,128]{2,1,0:T(8,128)(2,1)S(1)} %get-tuple-element.263), channel_id=1, source_target_pairs={{0,8},{4,12},{8,0},{12,4},{16,24},{20,28},{24,16},{28,20},{1,9},{5... | collective-permute-start | bytes 110600 | tf_op jit(solution)/shard_map/ppermute | solution.py:736
  145.0 8.1 %collective-permute-start.33 = (bf16[1,144,128]{2,1,0:T(8,128)(2,1)S(1)}, bf16[1,144,128]{2,1,0:T(8,128)(2,1)S(1)}, u32[]{:S(2)}, u32[]{:S(2)}) collective-permute-start(bf16[1,144,128]{2,1,0:T(8,128)(2,1)S(1)} %get-tuple-element.265), channel_id=1, source_target_pairs={{0,16},{4,20},{8,24},{12,28},{16,0},{20,4},{24,8},{28,12},{1,17},{... | collective-permute-start | bytes 110600 | tf_op jit(solution)/shard_map/ppermute | solution.py:736
  146.8 6.6 %collective-permute-start.34 = (bf16[1,144,128]{2,1,0:T(8,128)(2,1)S(1)}, bf16[1,144,128]{2,1,0:T(8,128)(2,1)S(1)}, u32[]{:S(2)}, u32[]{:S(2)}) collective-permute-start(bf16[1,144,128]{2,1,0:T(8,128)(2,1)S(1)} %get-tuple-element.264), channel_id=1, source_target_pairs={{0,24},{4,28},{8,16},{12,20},{16,8},{20,12},{24,0},{28,4},{1,25},{... | collective-permute-start | bytes 110600 | tf_op jit(solution)/shard_map/ppermute | solution.py:736
  153.4 4.5 %collective-permute-start.35 = (bf16[1,144,128]{2,1,0:T(8,128)(2,1)S(1)}, bf16[1,144,128]{2,1,0:T(8,128)(2,1)S(1)}, u32[]{:S(2)}, u32[]{:S(2)}) collective-permute-start(bf16[1,144,128]{2,1,0:T(8,128)(2,1)S(1)} %get-tuple-element.260), channel_id=1, source_target_pairs={{0,8},{4,12},{8,0},{12,4},{16,24},{20,28},{24,16},{28,20},{1,9},{5... | collective-permute-start | bytes 110600 | tf_op jit(solution)/shard_map/ppermute | solution.py:736
  155.0 5.2 %collective-permute-start.36 = (bf16[1,144,128]{2,1,0:T(8,128)(2,1)S(1)}, bf16[1,144,128]{2,1,0:T(8,128)(2,1)S(1)}, u32[]{:S(2)}, u32[]{:S(2)}) collective-permute-start(bf16[1,144,128]{2,1,0:T(8,128)(2,1)S(1)} %get-tuple-element.260), channel_id=1, source_target_pairs={{0,16},{4,20},{8,24},{12,28},{16,0},{20,4},{24,8},{28,12},{1,17},{... | collective-permute-start | bytes 110600 | tf_op jit(solution)/shard_map/ppermute | solution.py:736
  156.0 6.0 %collective-permute-start.37 = (bf16[1,144,128]{2,1,0:T(8,128)(2,1)S(1)}, bf16[1,144,128]{2,1,0:T(8,128)(2,1)S(1)}, u32[]{:S(2)}, u32[]{:S(2)}) collective-permute-start(bf16[1,144,128]{2,1,0:T(8,128)(2,1)S(1)} %get-tuple-element.260), channel_id=1, source_target_pairs={{0,24},{4,28},{8,16},{12,20},{16,8},{20,12},{24,0},{28,4},{1,25},{... | collective-permute-start | bytes 110600 | tf_op jit(solution)/shard_map/ppermute | solution.py:736
  162.0 8.4 %collective-permute-start.38 = (bf16[4,144,128]{2,1,0:T(8,128)(2,1)S(1)}, bf16[4,144,128]{2,1,0:T(8,128)(2,1)S(1)}, u32[]{:S(2)}, u32[]{:S(2)}) collective-permute-start(bf16[4,144,128]{2,1,0:T(8,128)(2,1)S(1)} %pad_maximum_fusion.1), channel_id=1, source_target_pairs={{0,4},{4,0},{8,12},{12,8},{16,20},{20,16},{24,28},{28,24},{1,5},{5... | collective-permute-start | bytes 442376 | tf_op jit(solution)/shard_map/ppermute | solution.py:736
  170.4 6.8 %collective-permute-start.39 = (bf16[1,8,144,128]{3,2,1,0:T(8,128)(2,1)S(1)}, bf16[1,8,144,128]{3,2,1,0:T(8,128)(2,1)S(1)}, u32[]{:S(2)}, u32[]{:S(2)}) collective-permute-start(bf16[1,8,144,128]{3,2,1,0:T(8,128)(2,1)S(1)} %bitcast.23), channel_id=1, source_target_pairs={{0,2},{1,3},{2,0},{3,1},{4,6},{5,7},{6,4},{7,5},{8,10},{9,11},{10,... | collective-permute-start | bytes 884744 | tf_op jit(solution)/shard_map/ppermute | solution.py:736
  177.3 2.1 %collective-permute-start.40 = (bf16[2,8,144,128]{3,2,1,0:T(8,128)(2,1)S(1)}, bf16[2,8,144,128]{3,2,1,0:T(8,128)(2,1)S(1)}, u32[]{:S(2)}, u32[]{:S(2)}) collective-permute-start(bf16[2,8,144,128]{3,2,1,0:T(8,128)(2,1)S(1)} %pad_maximum_fusion.refs_0_), channel_id=1, source_target_pairs={{0,1},{1,0},{2,3},{3,2},{4,5},{5,4},{6,7},{7,6},{8,9},{9,8},{10,11... | collective-permute-start | bytes 1769480 | tf_op jit(solution)/shard_map/ppermute | solution.py:736
  (4 other events, 9.7 us)
Sparse Core Ops, SparseCore 0:
  14.8 57.7 all-gather.5
  129.9 53.1 all-gather.3

commit v11 on v10

--- a/solution.py
+++ b/solution.py
@@ -316,8 +316,8 @@
 def rowsum_last(expo, parts, unit_t):
     rows, width = expo.shape
     depth = unit_t.shape[0]
-    block = min(2048, width)
-    pieces = 4
+    block = min(1024, width)
+    pieces = 2
     deep = block // pieces
     vec = pl.BlockSpec((1, block), lambda j: (0, j))
     return pl.pallas_call(

time: 193 us -> 195 us (1.010)
  no operation moved by 1% of the time
where the time goes in v11:
time: 195 us
  Pallas kernels  91.1 us (47%)
  starting transfers between devices  47.5 us (24%)
  waiting for transfers between devices  38.6 us (20%)
  between operations  14.6 us (7%)
  local copies, waits for them, and re-layouts  2.63 us (1%)
    ppermute x41, starting transfers between devices, flipped(): return lax.ppermute(x, axis, [(i, i ^ step) for i in range(size)])  47.4 us
    ppermute x41, waiting for transfers between devices, flipped(): return lax.ppermute(x, axis, [(i, i ^ step) for i in range(size)])  36.8 us
    pallas_call x4, Pallas kernels, view_soft(): pl.pallas_call(functools.partial(view_soft_body, block, min(32, chunk), l...  13.8 us
    pallas_call x4, Pallas kernels, proto_first(): pl.pallas_call(functools.partial(proto_first_kernel, chunk, tile, lead),...  13 us
    pallas_call x1, Pallas kernels, rowsum_last(): pl.pallas_call(functools.partial(rowsum_last_kernel, pieces, len(parts)),...  11.2 us
    pallas_call x1, Pallas kernels, first_pass(): pl.pallas_call(functools.partial(first_kernel, block, chunk, tile), in_sp...  11 us
    pallas_call x2, Pallas kernels, rowsum(): pl.pallas_call(functools.partial(rowsum_kernel, len(parts)), in_specs=[WH...  7.53 us
    pallas_call x1, Pallas kernels, head(): pl.pallas_call(head_kernel, grid=(steps,), in_specs=[pl.BlockSpec((block,...  7.41 us
  transfers between devices with their start and end apart: 43, of which 16 were waited for; matrix products, arithmetic and copies ran while one was open for 0% of the time, Pallas kernels for 36%

profile of v11, /device:TPU:0, one launch (start us, length us, event | category | flops | bytes accessed | tf_op | source)
XLA Modules:
  0.0 194.8 jit_solution(17915390957113253156)
XLA Ops:
  7.2 7.4 %head.1 = (f32[1024,512]{1,0:T(8,128)}, bf16[1024,512]{1,0:T(8,128)(2,1)}, f32[1024,128]{1,0:T(8,128)}, bf16[1024,128]{1,0:T(8,128)(2,1)S(1)}, bf16[128,1024]{1,0:T(8,128)(2,1)}, /*index=5*/s32[1,1024]{1,0:T(1,128)S(1)}) custom-call(bf16[1024,1024]{1,0:T(8,128)(2,1)} %emb.3, s32[1,1024]{1,0:T(1,128)} %bitcast.25, bf16[1024,512]{1,0:T(8,128)(2,1)} %w_in.1, ...), custom_call_target="tpu_custom_call" | custom-call | tf_op jit(solution)/shard_map/head/pallas_call | solution.py:105
  14.8 11.0 %first_pass.1 = (bf16[1024,8192]{1,0:T(8,128)(2,1)S(1)}, f32[1,8192]{1,0:T(1,128)S(1)}, f32[1,1024]{1,0:T(1,128)S(1)}) custom-call(bf16[1024,128]{1,0:T(8,128)(2,1)S(1)} %get-tuple-element.164.views.refs_0_, bf16[8192,128]{1,0:T(8,128)(2,1)S(1)} %copy-done.1), custom_call_target="tpu_custom_call" | custom-call | flops 1000 | bytes 1000 | tf_op jit(solution)/shard_map/first_pass/pallas_call | solution.py:190
  25.8 3.0 %collective-permute-start = (f32[1,8192]{1,0:T(1,128)S(1)}, f32[1,8192]{1,0:T(1,128)S(1)}, u32[]{:S(2)}, u32[]{:S(2)}) collective-permute-start(f32[1,8192]{1,0:T(1,128)S(1)} %get-tuple-element.135), channel_id=1, source_target_pairs={{0,4},{4,0},{8,12},{12,8},{16,20},{20,16},{24,28},{28,24},{1,5},{5... | collective-permute-start | bytes 98312 | tf_op jit(solution)/shard_map/ppermute | solution.py:736
  28.8 3.5 %view_soft.4.refs_0_ = f32[1024,128]{1,0:T(8,128)S(1)} custom-call(bf16[1024,128]{1,0:T(8,128)(2,1)S(1)} %get-tuple-element.164.views.refs_0_, bf16[8192,128]{1,0:T(8,128)(2,1)S(1)} %copy-done.1), custom_call_target="tpu_custom_call" | custom-call | flops 1000 | bytes 1000 | tf_op jit(solution)/shard_map/view_soft/pallas_call | solution.py:539
  32.4 1.6 collective-permute-start.1
  34.0 2.6 %collective-permute-start.2 = (f32[1,8192]{1,0:T(1,128)S(1)}, f32[1,8192]{1,0:T(1,128)S(1)}, u32[]{:S(2)}, u32[]{:S(2)}) collective-permute-start(f32[1,8192]{1,0:T(1,128)S(1)} %add.80.refs_0_), channel_id=1, source_target_pairs={{0,16},{4,20},{8,24},{12,28},{16,0},{20,4},{24,8},{28,12},{1,17},{... | collective-permute-start | bytes 98312 | tf_op jit(solution)/shard_map/ppermute | solution.py:736
  36.8 3.5 %view_soft.5.refs_1_ = f32[1024,128]{1,0:T(8,128)S(1)} custom-call(bf16[1024,128]{1,0:T(8,128)(2,1)S(1)} %get-tuple-element.164.views.refs_0_, bf16[8192,128]{1,0:T(8,128)(2,1)S(1)} %copy-done.1), custom_call_target="tpu_custom_call" | custom-call | flops 1000 | bytes 1000 | tf_op jit(solution)/shard_map/view_soft/pallas_call | solution.py:539
  42.3 3.8 %rowsum.2 = (f32[1,8192]{1,0:T(1,128)}, f32[1,1024]{1,0:T(1,128)S(1)}) custom-call(bf16[1024,8192]{1,0:T(8,128)(2,1)S(1)} %get-tuple-element.134.expo.refs_0_.refs_1_, f32[1,8192]{1,0:T(1,128)S(1)} %add.80.refs_0_, f32[1,8192]{1,0:T(1,128)S(1)} %collective-permute-done.1.refs_1_, f32[1,8192]{1,0:T(1,128)S(1)} %collective-permute-done.2.refs_2_, ...), custom_call_target="tpu_custom_call" | custom-call | flops 1000 | bytes 1000 | tf_op jit(solution)/shard_map/rowsum/pallas_call | solution.py:264
  46.2 1.6 collective-permute-start.5
  48.0 3.5 %view_soft.6.refs_2_ = f32[1024,128]{1,0:T(8,128)S(1)} custom-call(bf16[1024,128]{1,0:T(8,128)(2,1)S(1)} %get-tuple-element.164.views.refs_0_, bf16[8192,128]{1,0:T(8,128)(2,1)S(1)} %copy-done.1), custom_call_target="tpu_custom_call" | custom-call | flops 1000 | bytes 1000 | tf_op jit(solution)/shard_map/view_soft/pallas_call | solution.py:539
  51.6 2.2 %colsum.2 = f32[1,1,8192]{2,1,0:T(1,128)S(1)} custom-call(bf16[1024,8192]{1,0:T(8,128)(2,1)S(1)} %get-tuple-element.134.expo.refs_0_.refs_1_, f32[1,1024]{1,0:T(1,128)S(1)} %get-tuple-element.268.refs_0_), custom_call_target="tpu_custom_call" | custom-call | flops 1000 | bytes 1000 | tf_op jit(solution)/shard_map/colsum/pallas_call | solution.py:404
  55.9 1.9 unit_t.2.refs_0_
  58.9 2.2 %collective-permute-start.13 = (f32[1,8192]{1,0:T(1,128)S(1)}, f32[1,8192]{1,0:T(1,128)S(1)}, u32[]{:S(2)}, u32[]{:S(2)}) collective-permute-start(f32[1,8192]{1,0:T(1,128)S(1)} %bitcast_add_fusion.refs_0_), channel_id=1, source_target_pairs={{0,16},{4,20},{8,24},{12,28},{16,0},{20,4},{24,8},{28,12},{1,17},{... | collective-permute-start | bytes 98312 | tf_op jit(solution)/shard_map/ppermute | solution.py:736
  61.1 2.2 %collective-permute-start.14 = (f32[1,8192]{1,0:T(1,128)S(1)}, f32[1,8192]{1,0:T(1,128)S(1)}, u32[]{:S(2)}, u32[]{:S(2)}) collective-permute-start(f32[1,8192]{1,0:T(1,128)S(1)} %bitcast_add_fusion.refs_0_), channel_id=1, source_target_pairs={{0,24},{4,28},{8,16},{12,20},{16,8},{20,12},{24,0},{28,4},{1,25},{... | collective-permute-start | bytes 98312 | tf_op jit(solution)/shard_map/ppermute | solution.py:736
  63.3 1.7 collective-permute-start.11
  65.0 1.8 collective-permute-start.9
  66.8 1.9 unit_t.3.refs_6_
  69.9 3.8 %rowsum.3 = (f32[1,8192]{1,0:T(1,128)}, f32[1,1024]{1,0:T(1,128)S(1)}) custom-call(bf16[1024,8192]{1,0:T(8,128)(2,1)S(1)} %get-tuple-element.134.expo.refs_0_.refs_1_, f32[1,8192]{1,0:T(1,128)S(1)} %bitcast_add_fusion.refs_0_, f32[1,8192]{1,0:T(1,128)S(1)} %collective-permute-done.12.refs_1_, f32[1,8192]{1,0:T(1,128)S(1)} %collective-permute-done.13.refs_2_, ...), custom_call_target="tpu_custom_call" | custom-call | flops 1000 | bytes 1000 | tf_op jit(solution)/shard_map/rowsum/pallas_call | solution.py:264
  75.6 3.5 %view_soft.7.refs_3_ = f32[1024,128]{1,0:T(8,128)S(1)} custom-call(bf16[1024,128]{1,0:T(8,128)(2,1)S(1)} %get-tuple-element.164.views.refs_0_, bf16[8192,128]{1,0:T(8,128)(2,1)S(1)} %copy-done.1), custom_call_target="tpu_custom_call" | custom-call | flops 1000 | bytes 1000 | tf_op jit(solution)/shard_map/view_soft/pallas_call | solution.py:539
  79.9 2.4 %colsum.3 = f32[1,1,8192]{2,1,0:T(1,128)S(1)} custom-call(bf16[1024,8192]{1,0:T(8,128)(2,1)S(1)} %get-tuple-element.134.expo.refs_0_.refs_1_, f32[1,1024]{1,0:T(1,128)S(1)} %get-tuple-element.163.refs_0_, f32[1,1024]{1,0:T(1,128)S(1)} %collective-permute-done.15.refs_1_, f32[1,1024]{1,0:T(1,128)S(1)} %collective-permute-done.16.refs_2_, ...), custom_call_target="tpu_custom_call" | custom-call | flops 1000 | bytes 1000 | tf_op jit(solution)/shard_map/colsum/pallas_call | solution.py:404
  82.9 1.6 copy-done.2
  84.5 3.3 %proto_first.4 = (bf16[1024,2048]{1,0:T(8,128)(2,1)S(1)}, f32[1024,128]{1,0:T(8,128)S(1)}) custom-call(s32[1]{0:T(128)} %bitcast.1.place, bf16[1024,128]{1,0:T(8,128)(2,1)S(1)} %constant_dynamic-slice_fusion.protos.refs_9_, bf16[8,128,1024]{2,1,0:T(8,128)(2,1)S(1)} %bitcast.13, f32[8,1,1024]{2,1,0:T(1,128)S(1)} %constant_dynamic-update-slice_fusion.totals), custom_call_target="tpu_custom_call" | custom-call | flops 1000 | bytes 1000 | tf_op jit(solution)/shard_map/proto_first/pallas_call | solution.py:448
  88.7 1.9 collective-permute-start.20
  90.7 1.6 collective-permute-start.21
  92.2 3.3 %proto_first.5 = (bf16[1024,2048]{1,0:T(8,128)(2,1)S(1)}, f32[1024,128]{1,0:T(8,128)S(1)}) custom-call(s32[1]{0:T(128)} %bitcast.1.place, bf16[1024,128]{1,0:T(8,128)(2,1)S(1)} %constant_dynamic-slice_fusion.protos.refs_9_, bf16[8,128,1024]{2,1,0:T(8,128)(2,1)S(1)} %bitcast.14, f32[8,1,1024]{2,1,0:T(1,128)S(1)} %constant_dynamic-update-slice_fusion.totals), custom_call_target="tpu_custom_call" | custom-call | flops 1000 | bytes 1000 | tf_op jit(solution)/shard_map/proto_first/pallas_call | solution.py:448
  96.4 11.2 %rowsum_last.1 = (f32[1,8192]{1,0:T(1,128)S(1)}, f32[1,1024]{1,0:T(1,128)S(1)}, f32[1024,128]{1,0:T(8,128)S(1)}) custom-call(bf16[1024,8192]{1,0:T(8,128)(2,1)} %copy-done, bf16[1024,8192]{1,0:T(8,128)(2,1)} %copy-done, f32[1,8192]{1,0:T(1,128)S(1)} %add.85.refs_2_, f32[1,8192]{1,0:T(1,128)S(1)} %collective-permute-done.19.refs_3_, ...), custom_call_target="tpu_custom_call" | custom-call | flops 1000 | bytes 1000 | tf_op jit(solution)/shard_map/rowsum_last/pallas_call | solution.py:323
  107.7 1.5 collective-permute-start.23
  109.5 3.3 %proto_first.6 = (bf16[1024,2048]{1,0:T(8,128)(2,1)S(1)}, f32[1024,128]{1,0:T(8,128)S(1)}) custom-call(s32[1]{0:T(128)} %bitcast.1.place, bf16[1024,128]{1,0:T(8,128)(2,1)S(1)} %constant_dynamic-slice_fusion.protos.refs_9_, bf16[8,128,1024]{2,1,0:T(8,128)(2,1)S(1)} %bitcast.15, f32[8,1,1024]{2,1,0:T(1,128)S(1)} %constant_dynamic-update-slice_fusion.totals), custom_call_target="tpu_custom_call" | custom-call | flops 1000 | bytes 1000 | tf_op jit(solution)/shard_map/proto_first/pallas_call | solution.py:448
  114.4 2.2 %view_grad.1 = bf16[1024,128]{1,0:T(8,128)(2,1)S(1)} custom-call(f32[1024,128]{1,0:T(8,128)S(1)} %get-tuple-element.209.code, f32[1,1024]{1,0:T(1,128)S(1)} %get-tuple-element.210.tot, f32[1,1024]{1,0:T(1,128)S(1)} %get-tuple-element.211.total, f32[1024,128]{1,0:T(8,128)} %copy-done.5, f32[1024,128]{1,0:T(8,128)} %copy-done.6, f32[1024,128]{1,0:T(8,128)} %copy-done.7, ...), custom_call_target="tpu_custom_call" | custom-call | flops 1000 | bytes 1000 | tf_op jit(solution)/shard_map/view_grad/pallas_call | solution.py:567
  118.2 2.2 %collective-permute-start.27 = (f32[2,1,1024]{2,1,0:T(1,128)S(1)}, f32[2,1,1024]{2,1,0:T(1,128)S(1)}, u32[]{:S(2)}, u32[]{:S(2)}) collective-permute-start(f32[2,1,1024]{2,1,0:T(1,128)S(1)} %pad_maximum_fusion.4), channel_id=1, source_target_pairs={{0,16},{4,20},{8,24},{12,28},{16,0},{20,4},{24,8},{28,12},{1,17},{... | collective-permute-start | bytes 24584 | tf_op jit(solution)/shard_map/ppermute | solution.py:736
  120.4 2.2 %collective-permute-start.28 = (f32[2,1,1024]{2,1,0:T(1,128)S(1)}, f32[2,1,1024]{2,1,0:T(1,128)S(1)}, u32[]{:S(2)}, u32[]{:S(2)}) collective-permute-start(f32[2,1,1024]{2,1,0:T(1,128)S(1)} %pad_maximum_fusion.4), channel_id=1, source_target_pairs={{0,24},{4,28},{8,16},{12,20},{16,8},{20,12},{24,0},{28,4},{1,25},{... | collective-permute-start | bytes 24584 | tf_op jit(solution)/shard_map/ppermute | solution.py:736
  122.6 3.3 %proto_first.7 = (bf16[1024,2048]{1,0:T(8,128)(2,1)S(1)}, f32[1024,128]{1,0:T(8,128)S(1)}) custom-call(s32[1]{0:T(128)} %bitcast.1.place, bf16[1024,128]{1,0:T(8,128)(2,1)S(1)} %constant_dynamic-slice_fusion.protos.refs_9_, bf16[8,128,1024]{2,1,0:T(8,128)(2,1)S(1)} %bitcast.16, f32[8,1,1024]{2,1,0:T(1,128)S(1)} %constant_dynamic-update-slice_fusion.totals), custom_call_target="tpu_custom_call" | custom-call | flops 1000 | bytes 1000 | tf_op jit(solution)/shard_map/proto_first/pallas_call | solution.py:448
  126.1 5.4 %proto_last.1 = bf16[1024,128]{1,0:T(8,128)(2,1)} custom-call(s32[1]{0:T(128)} %bitcast.1.place, bf16[1024,2048]{1,0:T(8,128)(2,1)S(1)} %get-tuple-element.239.refs_0_, bf16[1024,2048]{1,0:T(8,128)(2,1)S(1)} %get-tuple-element.240.refs_1_, bf16[1024,2048]{1,0:T(8,128)(2,1)S(1)} %get-tuple-element.241.refs_2_, ...), custom_call_target="tpu_custom_call" | custom-call | tf_op jit(solution)/shard_map/proto_last/pallas_call | solution.py:498
  131.5 5.9 %backward.1 = f32[8,144,128]{2,1,0:T(8,128)S(1)} custom-call(s32[1]{0:T(128)} %bitcast.turn, bf16[1024,128]{1,0:T(8,128)(2,1)S(1)} %add_convert_fusion.grad_a, bf16[1024,128]{1,0:T(8,128)(2,1)S(1)} %collective-permute-done.30.grad_b, s32[1,1024]{1,0:T(1,128)S(1)} %get-tuple-element.252.pos, f32[1024,128]{1,0:T(8,128)} %get-tuple-element.253.raw, ...), custom_call_target="tpu_custom_call" | custom-call | tf_op jit(solution)/shard_map/backward/pallas_call | solution.py:631
  138.9 7.7 %collective-permute-done.31 = bf16[4,144,128]{2,1,0:T(8,128)(2,1)S(1)} collective-permute-done((bf16[4,144,128]{2,1,0:T(8,128)(2,1)S(1)}, bf16[4,144,128]{2,1,0:T(8,128)(2,1)S(1)}, u32[]{:S(2)}, u32[]{:S(2)}) %collective-permute-start.31) | collective-permute-done | bytes 147488 | tf_op jit(solution)/shard_map/ppermute | solution.py:736
  146.8 1.8 collective-permute-start.33
  148.5 2.6 %collective-permute-start.34 = (bf16[1,144,128]{2,1,0:T(8,128)(2,1)S(1)}, bf16[1,144,128]{2,1,0:T(8,128)(2,1)S(1)}, u32[]{:S(2)}, u32[]{:S(2)}) collective-permute-start(bf16[1,144,128]{2,1,0:T(8,128)(2,1)S(1)} %get-tuple-element.264), channel_id=1, source_target_pairs={{0,24},{4,28},{8,16},{12,20},{16,8},{20,12},{24,0},{28,4},{1,25},{... | collective-permute-start | bytes 110600 | tf_op jit(solution)/shard_map/ppermute | solution.py:736
  151.3 3.5 %collective-permute-done.33 = bf16[1,144,128]{2,1,0:T(8,128)(2,1)S(1)} collective-permute-done((bf16[1,144,128]{2,1,0:T(8,128)(2,1)S(1)}, bf16[1,144,128]{2,1,0:T(8,128)(2,1)S(1)}, u32[]{:S(2)}, u32[]{:S(2)}) %collective-permute-start.33) | collective-permute-done | bytes 36896 | tf_op jit(solution)/shard_map/ppermute | solution.py:736
  155.1 1.6 collective-permute-start.35
  157.7 1.8 collective-permute-start.37
  159.6 2.3 %collective-permute-done.36 = bf16[1,144,128]{2,1,0:T(8,128)(2,1)S(1)} collective-permute-done((bf16[1,144,128]{2,1,0:T(8,128)(2,1)S(1)}, bf16[1,144,128]{2,1,0:T(8,128)(2,1)S(1)}, u32[]{:S(2)}, u32[]{:S(2)}) %collective-permute-start.36) | collective-permute-done | bytes 36896 | tf_op jit(solution)/shard_map/ppermute | solution.py:736
  161.9 1.8 collective-permute-done.37
  164.6 7.5 %collective-permute-done.38 = bf16[4,144,128]{2,1,0:T(8,128)(2,1)S(1)} collective-permute-done((bf16[4,144,128]{2,1,0:T(8,128)(2,1)S(1)}, bf16[4,144,128]{2,1,0:T(8,128)(2,1)S(1)}, u32[]{:S(2)}, u32[]{:S(2)}) %collective-permute-start.38) | collective-permute-done | bytes 147488 | tf_op jit(solution)/shard_map/ppermute | solution.py:736
  172.5 6.5 %collective-permute-done.39 = bf16[1,8,144,128]{3,2,1,0:T(8,128)(2,1)S(1)} collective-permute-done((bf16[1,8,144,128]{3,2,1,0:T(8,128)(2,1)S(1)}, bf16[1,8,144,128]{3,2,1,0:T(8,128)(2,1)S(1)}, u32[]{:S(2)}, u32[]{:S(2)}) %collective-permute-start.39) | collective-permute-done | bytes 294944 | tf_op jit(solution)/shard_map/ppermute | solution.py:736
  179.1 1.9 collective-permute-done.40.refs_1_
  181.1 2.1 %unpack.1 = (f32[1024,512]{1,0:T(8,128)}, f32[512,128]{1,0:T(8,128)}) custom-call(s32[2]{0:T(128)S(1)} %pad_add_fusion.place, bf16[2,8,144,128]{3,2,1,0:T(8,128)(2,1)S(1)} %pad_maximum_fusion.refs_0_, bf16[2,8,144,128]{3,2,1,0:T(8,128)(2,1)S(1)} %collective-permute-done.40.refs_1_), custom_call_target="tpu_custom_call" | custom-call | tf_op jit(solution)/shard_map/unpack/pallas_call | solution.py:665
  183.1 1.7 all-gather.4.cloned.1.call-done.x
  184.9 3.1 %widen.1 = f32[8192,128]{1,0:T(8,128)} custom-call(bf16[8192,128]{1,0:T(8,128)(2,1)} %all-gather.4.cloned.1.call-done.x), custom_call_target="tpu_custom_call" | custom-call | tf_op jit(solution)/shard_map/widen/pallas_call | solution.py:699
  (111 shorter events, 20.7 us)
Async XLA Ops:
  7.2 7.6 %copy-start.1 = (bf16[8192,128]{1,0:T(8,128)(2,1)S(1)}, bf16[8192,128]{1,0:T(8,128)(2,1)}, u32[]{:S(2)}) copy-start(bf16[8192,128]{1,0:T(8,128)(2,1)} %refs_1_.3) | copy-start | bytes 6291460
  7.2 75.1 %all-gather.6.cloned.1.call-start = ((), (), s32[]{:S(2)}) async-start(), calls=%async_computation.1 | async-start | bytes 2359296 | tf_op jit(solution)/shard_map/all_gather | solution.py:757
  14.7 170.2 %all-gather.4.cloned.1.call-start = ((), (), s32[]{:S(2)}) async-start(), calls=%async_computation | async-start | bytes 2359296 | tf_op jit(solution)/shard_map/all_gather | solution.py:840
  25.8 54.1 %copy-start = (bf16[1024,8192]{1,0:T(8,128)(2,1)}, bf16[1024,8192]{1,0:T(8,128)(2,1)S(1)}, u32[]{:S(2)}) copy-start(bf16[1024,8192]{1,0:T(8,128)(2,1)S(1)} %get-tuple-element.134.expo.refs_0_.refs_1_) | copy-start | bytes 50331652
  25.8 6.5 %collective-permute-start = (f32[1,8192]{1,0:T(1,128)S(1)}, f32[1,8192]{1,0:T(1,128)S(1)}, u32[]{:S(2)}, u32[]{:S(2)}) collective-permute-start(f32[1,8192]{1,0:T(1,128)S(1)} %get-tuple-element.135), channel_id=1, source_target_pairs={{0,4},{4,0},{8,12},{12,8},{16,20},{20,16},{24,28},{28,24},{1,5},{5... | collective-permute-start | bytes 98312 | tf_op jit(solution)/shard_map/ppermute | solution.py:736
  32.3 13.8 %copy-start.5 = (f32[1024,128]{1,0:T(8,128)}, f32[1024,128]{1,0:T(8,128)S(1)}, u32[]{:S(2)}) copy-start(f32[1024,128]{1,0:T(8,128)S(1)} %view_soft.4.refs_0_) | copy-start | bytes 1572868
  32.4 7.9 %collective-permute-start.1 = (f32[1,8192]{1,0:T(1,128)S(1)}, f32[1,8192]{1,0:T(1,128)S(1)}, u32[]{:S(2)}, u32[]{:S(2)}) collective-permute-start(f32[1,8192]{1,0:T(1,128)S(1)} %add.80.refs_0_), channel_id=1, source_target_pairs={{0,8},{4,12},{8,0},{12,4},{16,24},{20,28},{24,16},{28,20},{1,9},{5... | collective-permute-start | bytes 98312 | tf_op jit(solution)/shard_map/ppermute | solution.py:736
  34.0 6.8 %collective-permute-start.2 = (f32[1,8192]{1,0:T(1,128)S(1)}, f32[1,8192]{1,0:T(1,128)S(1)}, u32[]{:S(2)}, u32[]{:S(2)}) collective-permute-start(f32[1,8192]{1,0:T(1,128)S(1)} %add.80.refs_0_), channel_id=1, source_target_pairs={{0,16},{4,20},{8,24},{12,28},{16,0},{20,4},{24,8},{28,12},{1,17},{... | collective-permute-start | bytes 98312 | tf_op jit(solution)/shard_map/ppermute | solution.py:736
  36.6 5.7 %collective-permute-start.3 = (f32[1,8192]{1,0:T(1,128)S(1)}, f32[1,8192]{1,0:T(1,128)S(1)}, u32[]{:S(2)}, u32[]{:S(2)}) collective-permute-start(f32[1,8192]{1,0:T(1,128)S(1)} %add.80.refs_0_), channel_id=1, source_target_pairs={{0,24},{4,28},{8,16},{12,20},{16,8},{20,12},{24,0},{28,4},{1,25},{... | collective-permute-start | bytes 98312 | tf_op jit(solution)/shard_map/ppermute | solution.py:736
  40.3 5.8 %copy-start.6 = (f32[1024,128]{1,0:T(8,128)}, f32[1024,128]{1,0:T(8,128)S(1)}, u32[]{:S(2)}) copy-start(f32[1024,128]{1,0:T(8,128)S(1)} %view_soft.5.refs_1_) | copy-start | bytes 1572868
  46.1 5.4 %collective-permute-start.4 = (f32[2,1024]{1,0:T(2,128)S(1)}, f32[2,1024]{1,0:T(2,128)S(1)}, u32[]{:S(2)}, u32[]{:S(2)}) collective-permute-start(f32[2,1024]{1,0:T(2,128)S(1)} %pad_maximum_fusion.2), channel_id=1, source_target_pairs={{0,1},{1,0},{2,3},{3,2},{4,5},{5,4},{6,7},{7,6},{8,9},{9,8},{10,11... | collective-permute-start | bytes 24584 | tf_op jit(solution)/shard_map/ppermute | solution.py:736
  46.2 5.3 %collective-permute-start.5 = (f32[2,1024]{1,0:T(2,128)S(1)}, f32[2,1024]{1,0:T(2,128)S(1)}, u32[]{:S(2)}, u32[]{:S(2)}) collective-permute-start(f32[2,1024]{1,0:T(2,128)S(1)} %pad_maximum_fusion.2), channel_id=1, source_target_pairs={{0,2},{1,3},{2,0},{3,1},{4,6},{5,7},{6,4},{7,5},{8,10},{9,11},{10,... | collective-permute-start | bytes 24584 | tf_op jit(solution)/shard_map/ppermute | solution.py:736
  47.7 3.8 %collective-permute-start.6 = (f32[2,1024]{1,0:T(2,128)S(1)}, f32[2,1024]{1,0:T(2,128)S(1)}, u32[]{:S(2)}, u32[]{:S(2)}) collective-permute-start(f32[2,1024]{1,0:T(2,128)S(1)} %pad_maximum_fusion.2), channel_id=1, source_target_pairs={{0,3},{1,2},{2,1},{3,0},{4,7},{5,6},{6,5},{7,4},{8,11},{9,10},{10,... | collective-permute-start | bytes 24584 | tf_op jit(solution)/shard_map/ppermute | solution.py:736
  53.8 4.8 %collective-permute-start.8 = (f32[1,8192]{1,0:T(1,128)S(1)}, f32[1,8192]{1,0:T(1,128)S(1)}, u32[]{:S(2)}, u32[]{:S(2)}) collective-permute-start(f32[1,8192]{1,0:T(1,128)S(1)} %bitcast.20), channel_id=1, source_target_pairs={{0,4},{4,0},{8,12},{12,8},{16,20},{20,16},{24,28},{28,24},{1,5},{5... | collective-permute-start | bytes 98312 | tf_op jit(solution)/shard_map/ppermute | solution.py:736
  54.4 4.4 %collective-permute-start.7 = (f32[1,1,1024]{2,1,0:T(1,128)S(1)}, f32[1,1,1024]{2,1,0:T(1,128)S(1)}, u32[]{:S(2)}, u32[]{:S(2)}) collective-permute-start(f32[1,1,1024]{2,1,0:T(1,128)S(1)} %get-tuple-element.267), channel_id=1, source_target_pairs={{0,4},{4,0},{8,12},{12,8},{16,20},{20,16},{24,28},{28,24},{1,5},{5... | collective-permute-start | bytes 12296 | tf_op jit(solution)/shard_map/ppermute | solution.py:736
  58.8 6.2 %collective-permute-start.12 = (f32[1,8192]{1,0:T(1,128)S(1)}, f32[1,8192]{1,0:T(1,128)S(1)}, u32[]{:S(2)}, u32[]{:S(2)}) collective-permute-start(f32[1,8192]{1,0:T(1,128)S(1)} %bitcast_add_fusion.refs_0_), channel_id=1, source_target_pairs={{0,8},{4,12},{8,0},{12,4},{16,24},{20,28},{24,16},{28,20},{1,9},{5... | collective-permute-start | bytes 98312 | tf_op jit(solution)/shard_map/ppermute | solution.py:736
  58.9 9.8 %collective-permute-start.13 = (f32[1,8192]{1,0:T(1,128)S(1)}, f32[1,8192]{1,0:T(1,128)S(1)}, u32[]{:S(2)}, u32[]{:S(2)}) collective-permute-start(f32[1,8192]{1,0:T(1,128)S(1)} %bitcast_add_fusion.refs_0_), channel_id=1, source_target_pairs={{0,16},{4,20},{8,24},{12,28},{16,0},{20,4},{24,8},{28,12},{1,17},{... | collective-permute-start | bytes 98312 | tf_op jit(solution)/shard_map/ppermute | solution.py:736
  61.1 7.7 %collective-permute-start.14 = (f32[1,8192]{1,0:T(1,128)S(1)}, f32[1,8192]{1,0:T(1,128)S(1)}, u32[]{:S(2)}, u32[]{:S(2)}) collective-permute-start(f32[1,8192]{1,0:T(1,128)S(1)} %bitcast_add_fusion.refs_0_), channel_id=1, source_target_pairs={{0,24},{4,28},{8,16},{12,20},{16,8},{20,12},{24,0},{28,4},{1,25},{... | collective-permute-start | bytes 98312 | tf_op jit(solution)/shard_map/ppermute | solution.py:736
  63.3 6.7 %collective-permute-start.10 = (f32[2,1,1024]{2,1,0:T(1,128)S(1)}, f32[2,1,1024]{2,1,0:T(1,128)S(1)}, u32[]{:S(2)}, u32[]{:S(2)}) collective-permute-start(f32[2,1,1024]{2,1,0:T(1,128)S(1)} %pad_maximum_fusion.3), channel_id=1, source_target_pairs={{0,16},{4,20},{8,24},{12,28},{16,0},{20,4},{24,8},{28,12},{1,17},{... | collective-permute-start | bytes 24584 | tf_op jit(solution)/shard_map/ppermute | solution.py:736
  63.3 6.6 %collective-permute-start.11 = (f32[2,1,1024]{2,1,0:T(1,128)S(1)}, f32[2,1,1024]{2,1,0:T(1,128)S(1)}, u32[]{:S(2)}, u32[]{:S(2)}) collective-permute-start(f32[2,1,1024]{2,1,0:T(1,128)S(1)} %pad_maximum_fusion.3), channel_id=1, source_target_pairs={{0,24},{4,28},{8,16},{12,20},{16,8},{20,12},{24,0},{28,4},{1,25},{... | collective-permute-start | bytes 24584 | tf_op jit(solution)/shard_map/ppermute | solution.py:736
  65.0 4.9 %collective-permute-start.9 = (f32[2,1,1024]{2,1,0:T(1,128)S(1)}, f32[2,1,1024]{2,1,0:T(1,128)S(1)}, u32[]{:S(2)}, u32[]{:S(2)}) collective-permute-start(f32[2,1,1024]{2,1,0:T(1,128)S(1)} %pad_maximum_fusion.3), channel_id=1, source_target_pairs={{0,8},{4,12},{8,0},{12,4},{16,24},{20,28},{24,16},{28,20},{1,9},{5... | collective-permute-start | bytes 24584 | tf_op jit(solution)/shard_map/ppermute | solution.py:736
  73.7 6.1 %collective-permute-start.15 = (f32[1,1024]{1,0:T(1,128)S(1)}, f32[1,1024]{1,0:T(1,128)S(1)}, u32[]{:S(2)}, u32[]{:S(2)}) collective-permute-start(f32[1,1024]{1,0:T(1,128)S(1)} %get-tuple-element.163.refs_0_), channel_id=1, source_target_pairs={{0,1},{1,0},{2,3},{3,2},{4,5},{5,4},{6,7},{7,6},{8,9},{9,8},{10,11... | collective-permute-start | bytes 12296 | tf_op jit(solution)/shard_map/ppermute | solution.py:736
  73.7 6.1 %collective-permute-start.16 = (f32[1,1024]{1,0:T(1,128)S(1)}, f32[1,1024]{1,0:T(1,128)S(1)}, u32[]{:S(2)}, u32[]{:S(2)}) collective-permute-start(f32[1,1024]{1,0:T(1,128)S(1)} %get-tuple-element.163.refs_0_), channel_id=1, source_target_pairs={{0,2},{1,3},{2,0},{3,1},{4,6},{5,7},{6,4},{7,5},{8,10},{9,11},{10,... | collective-permute-start | bytes 12296 | tf_op jit(solution)/shard_map/ppermute | solution.py:736
  75.2 4.7 %collective-permute-start.17 = (f32[1,1024]{1,0:T(1,128)S(1)}, f32[1,1024]{1,0:T(1,128)S(1)}, u32[]{:S(2)}, u32[]{:S(2)}) collective-permute-start(f32[1,1024]{1,0:T(1,128)S(1)} %get-tuple-element.163.refs_0_), channel_id=1, source_target_pairs={{0,3},{1,2},{2,1},{3,0},{4,7},{5,6},{6,5},{7,4},{8,11},{9,10},{10,... | collective-permute-start | bytes 12296 | tf_op jit(solution)/shard_map/ppermute | solution.py:736
  82.3 5.4 %collective-permute-start.18 = (f32[1,8192]{1,0:T(1,128)S(1)}, f32[1,8192]{1,0:T(1,128)S(1)}, u32[]{:S(2)}, u32[]{:S(2)}) collective-permute-start(f32[1,8192]{1,0:T(1,128)S(1)} %bitcast.18), channel_id=1, source_target_pairs={{0,4},{4,0},{8,12},{12,8},{16,20},{20,16},{24,28},{28,24},{1,5},{5... | collective-permute-start | bytes 98312 | tf_op jit(solution)/shard_map/ppermute | solution.py:736
  87.8 7.7 %collective-permute-start.19 = (f32[1,8192]{1,0:T(1,128)S(1)}, f32[1,8192]{1,0:T(1,128)S(1)}, u32[]{:S(2)}, u32[]{:S(2)}) collective-permute-start(f32[1,8192]{1,0:T(1,128)S(1)} %add.85.refs_2_), channel_id=1, source_target_pairs={{0,8},{4,12},{8,0},{12,4},{16,24},{20,28},{24,16},{28,20},{1,9},{5... | collective-permute-start | bytes 98312 | tf_op jit(solution)/shard_map/ppermute | solution.py:736
  88.7 6.8 %collective-permute-start.20 = (f32[1,8192]{1,0:T(1,128)S(1)}, f32[1,8192]{1,0:T(1,128)S(1)}, u32[]{:S(2)}, u32[]{:S(2)}) collective-permute-start(f32[1,8192]{1,0:T(1,128)S(1)} %add.85.refs_2_), channel_id=1, source_target_pairs={{0,16},{4,20},{8,24},{12,28},{16,0},{20,4},{24,8},{28,12},{1,17},{... | collective-permute-start | bytes 98312 | tf_op jit(solution)/shard_map/ppermute | solution.py:736
  90.7 5.7 %collective-permute-start.21 = (f32[1,8192]{1,0:T(1,128)S(1)}, f32[1,8192]{1,0:T(1,128)S(1)}, u32[]{:S(2)}, u32[]{:S(2)}) collective-permute-start(f32[1,8192]{1,0:T(1,128)S(1)} %add.85.refs_2_), channel_id=1, source_target_pairs={{0,24},{4,28},{8,16},{12,20},{16,8},{20,12},{24,0},{28,4},{1,25},{... | collective-permute-start | bytes 98312 | tf_op jit(solution)/shard_map/ppermute | solution.py:736
  96.4 13.1 %copy-start.3 = (bf16[1024,1024]{1,0:T(8,128)(2,1)S(1)}, bf16[1024,1024]{1,0:T(8,128)(2,1)}, u32[]{:S(2)}) copy-start(bf16[1024,1024]{1,0:T(8,128)(2,1)} %all-gather.6.cloned.1.call-done) | copy-start | bytes 6291460
  107.6 5.2 %collective-permute-start.22 = (f32[1,1024]{1,0:T(1,128)S(1)}, f32[1,1024]{1,0:T(1,128)S(1)}, u32[]{:S(2)}, u32[]{:S(2)}) collective-permute-start(f32[1,1024]{1,0:T(1,128)S(1)} %get-tuple-element.194), channel_id=1, source_target_pairs={{0,1},{1,0},{2,3},{3,2},{4,5},{5,4},{6,7},{7,6},{8,9},{9,8},{10,11... | collective-permute-start | bytes 12296 | tf_op jit(solution)/shard_map/ppermute | solution.py:736
  107.7 5.1 %collective-permute-start.23 = (f32[1,1024]{1,0:T(1,128)S(1)}, f32[1,1024]{1,0:T(1,128)S(1)}, u32[]{:S(2)}, u32[]{:S(2)}) collective-permute-start(f32[1,1024]{1,0:T(1,128)S(1)} %get-tuple-element.194), channel_id=1, source_target_pairs={{0,2},{1,3},{2,0},{3,1},{4,6},{5,7},{6,4},{7,5},{8,10},{9,11},{10,... | collective-permute-start | bytes 12296 | tf_op jit(solution)/shard_map/ppermute | solution.py:736
  109.2 3.6 %collective-permute-start.24 = (f32[1,1024]{1,0:T(1,128)S(1)}, f32[1,1024]{1,0:T(1,128)S(1)}, u32[]{:S(2)}, u32[]{:S(2)}) collective-permute-start(f32[1,1024]{1,0:T(1,128)S(1)} %get-tuple-element.194), channel_id=1, source_target_pairs={{0,3},{1,2},{2,1},{3,0},{4,7},{5,6},{6,5},{7,4},{8,11},{9,10},{10,... | collective-permute-start | bytes 12296 | tf_op jit(solution)/shard_map/ppermute | solution.py:736
  112.8 3.8 %collective-permute-start.25 = (f32[1,1,1024]{2,1,0:T(1,128)S(1)}, f32[1,1,1024]{2,1,0:T(1,128)S(1)}, u32[]{:S(2)}, u32[]{:S(2)}) collective-permute-start(f32[1,1,1024]{2,1,0:T(1,128)S(1)} %bitcast.21), channel_id=1, source_target_pairs={{0,4},{4,0},{8,12},{12,8},{16,20},{20,16},{24,28},{28,24},{1,5},{5... | collective-permute-start | bytes 12296 | tf_op jit(solution)/shard_map/ppermute | solution.py:736
  116.6 9.3 %collective-permute-start.29 = (bf16[1024,128]{1,0:T(8,128)(2,1)S(1)}, bf16[1024,128]{1,0:T(8,128)(2,1)S(1)}, u32[]{:S(2)}, u32[]{:S(2)}) collective-permute-start(bf16[1024,128]{1,0:T(8,128)(2,1)S(1)} %view_grad.1), channel_id=1, source_target_pairs={{0,2},{1,3},{2,0},{3,1},{4,6},{5,7},{6,4},{7,5},{8,10},{9,11},{10,... | collective-permute-start | bytes 786440 | tf_op jit(solution)/shard_map/ppermute | solution.py:736
  118.2 7.7 %collective-permute-start.26 = (f32[2,1,1024]{2,1,0:T(1,128)S(1)}, f32[2,1,1024]{2,1,0:T(1,128)S(1)}, u32[]{:S(2)}, u32[]{:S(2)}) collective-permute-start(f32[2,1,1024]{2,1,0:T(1,128)S(1)} %pad_maximum_fusion.4), channel_id=1, source_target_pairs={{0,8},{4,12},{8,0},{12,4},{16,24},{20,28},{24,16},{28,20},{1,9},{5... | collective-permute-start | bytes 24584 | tf_op jit(solution)/shard_map/ppermute | solution.py:736
  118.2 7.7 %collective-permute-start.27 = (f32[2,1,1024]{2,1,0:T(1,128)S(1)}, f32[2,1,1024]{2,1,0:T(1,128)S(1)}, u32[]{:S(2)}, u32[]{:S(2)}) collective-permute-start(f32[2,1,1024]{2,1,0:T(1,128)S(1)} %pad_maximum_fusion.4), channel_id=1, source_target_pairs={{0,16},{4,20},{8,24},{12,28},{16,0},{20,4},{24,8},{28,12},{1,17},{... | collective-permute-start | bytes 24584 | tf_op jit(solution)/shard_map/ppermute | solution.py:736
  120.4 5.5 %collective-permute-start.28 = (f32[2,1,1024]{2,1,0:T(1,128)S(1)}, f32[2,1,1024]{2,1,0:T(1,128)S(1)}, u32[]{:S(2)}, u32[]{:S(2)}) collective-permute-start(f32[2,1,1024]{2,1,0:T(1,128)S(1)} %pad_maximum_fusion.4), channel_id=1, source_target_pairs={{0,24},{4,28},{8,16},{12,20},{16,8},{20,12},{24,0},{28,4},{1,25},{... | collective-permute-start | bytes 24584 | tf_op jit(solution)/shard_map/ppermute | solution.py:736
  126.0 5.5 %collective-permute-start.30 = (bf16[1024,128]{1,0:T(8,128)(2,1)S(1)}, bf16[1024,128]{1,0:T(8,128)(2,1)S(1)}, u32[]{:S(2)}, u32[]{:S(2)}) collective-permute-start(bf16[1024,128]{1,0:T(8,128)(2,1)S(1)} %add_convert_fusion.grad_a), channel_id=1, source_target_pairs={{0,1},{1,0},{2,3},{3,2},{4,5},{5,4},{6,7},{7,6},{8,9},{9,8},{10,11... | collective-permute-start | bytes 786440 | tf_op jit(solution)/shard_map/ppermute | solution.py:736
  137.5 9.1 %collective-permute-start.31 = (bf16[4,144,128]{2,1,0:T(8,128)(2,1)S(1)}, bf16[4,144,128]{2,1,0:T(8,128)(2,1)S(1)}, u32[]{:S(2)}, u32[]{:S(2)}) collective-permute-start(bf16[4,144,128]{2,1,0:T(8,128)(2,1)S(1)} %dynamic-slice_convert_fusion), channel_id=1, source_target_pairs={{0,4},{4,0},{8,12},{12,8},{16,20},{20,16},{24,28},{28,24},{1,5},{5... | collective-permute-start | bytes 442376 | tf_op jit(solution)/shard_map/ppermute | solution.py:736
  146.7 4.6 %collective-permute-start.32 = (bf16[1,144,128]{2,1,0:T(8,128)(2,1)S(1)}, bf16[1,144,128]{2,1,0:T(8,128)(2,1)S(1)}, u32[]{:S(2)}, u32[]{:S(2)}) collective-permute-start(bf16[1,144,128]{2,1,0:T(8,128)(2,1)S(1)} %get-tuple-element.263), channel_id=1, source_target_pairs={{0,8},{4,12},{8,0},{12,4},{16,24},{20,28},{24,16},{28,20},{1,9},{5... | collective-permute-start | bytes 110600 | tf_op jit(solution)/shard_map/ppermute | solution.py:736
  146.8 8.1 %collective-permute-start.33 = (bf16[1,144,128]{2,1,0:T(8,128)(2,1)S(1)}, bf16[1,144,128]{2,1,0:T(8,128)(2,1)S(1)}, u32[]{:S(2)}, u32[]{:S(2)}) collective-permute-start(bf16[1,144,128]{2,1,0:T(8,128)(2,1)S(1)} %get-tuple-element.265), channel_id=1, source_target_pairs={{0,16},{4,20},{8,24},{12,28},{16,0},{20,4},{24,8},{28,12},{1,17},{... | collective-permute-start | bytes 110600 | tf_op jit(solution)/shard_map/ppermute | solution.py:736
  148.5 6.6 %collective-permute-start.34 = (bf16[1,144,128]{2,1,0:T(8,128)(2,1)S(1)}, bf16[1,144,128]{2,1,0:T(8,128)(2,1)S(1)}, u32[]{:S(2)}, u32[]{:S(2)}) collective-permute-start(bf16[1,144,128]{2,1,0:T(8,128)(2,1)S(1)} %get-tuple-element.264), channel_id=1, source_target_pairs={{0,24},{4,28},{8,16},{12,20},{16,8},{20,12},{24,0},{28,4},{1,25},{... | collective-permute-start | bytes 110600 | tf_op jit(solution)/shard_map/ppermute | solution.py:736
  155.1 4.5 %collective-permute-start.35 = (bf16[1,144,128]{2,1,0:T(8,128)(2,1)S(1)}, bf16[1,144,128]{2,1,0:T(8,128)(2,1)S(1)}, u32[]{:S(2)}, u32[]{:S(2)}) collective-permute-start(bf16[1,144,128]{2,1,0:T(8,128)(2,1)S(1)} %get-tuple-element.260), channel_id=1, source_target_pairs={{0,8},{4,12},{8,0},{12,4},{16,24},{20,28},{24,16},{28,20},{1,9},{5... | collective-permute-start | bytes 110600 | tf_op jit(solution)/shard_map/ppermute | solution.py:736
  156.7 5.2 %collective-permute-start.36 = (bf16[1,144,128]{2,1,0:T(8,128)(2,1)S(1)}, bf16[1,144,128]{2,1,0:T(8,128)(2,1)S(1)}, u32[]{:S(2)}, u32[]{:S(2)}) collective-permute-start(bf16[1,144,128]{2,1,0:T(8,128)(2,1)S(1)} %get-tuple-element.260), channel_id=1, source_target_pairs={{0,16},{4,20},{8,24},{12,28},{16,0},{20,4},{24,8},{28,12},{1,17},{... | collective-permute-start | bytes 110600 | tf_op jit(solution)/shard_map/ppermute | solution.py:736
  157.7 6.0 %collective-permute-start.37 = (bf16[1,144,128]{2,1,0:T(8,128)(2,1)S(1)}, bf16[1,144,128]{2,1,0:T(8,128)(2,1)S(1)}, u32[]{:S(2)}, u32[]{:S(2)}) collective-permute-start(bf16[1,144,128]{2,1,0:T(8,128)(2,1)S(1)} %get-tuple-element.260), channel_id=1, source_target_pairs={{0,24},{4,28},{8,16},{12,20},{16,8},{20,12},{24,0},{28,4},{1,25},{... | collective-permute-start | bytes 110600 | tf_op jit(solution)/shard_map/ppermute | solution.py:736
  163.7 8.4 %collective-permute-start.38 = (bf16[4,144,128]{2,1,0:T(8,128)(2,1)S(1)}, bf16[4,144,128]{2,1,0:T(8,128)(2,1)S(1)}, u32[]{:S(2)}, u32[]{:S(2)}) collective-permute-start(bf16[4,144,128]{2,1,0:T(8,128)(2,1)S(1)} %pad_maximum_fusion.1), channel_id=1, source_target_pairs={{0,4},{4,0},{8,12},{12,8},{16,20},{20,16},{24,28},{28,24},{1,5},{5... | collective-permute-start | bytes 442376 | tf_op jit(solution)/shard_map/ppermute | solution.py:736
  172.1 6.8 %collective-permute-start.39 = (bf16[1,8,144,128]{3,2,1,0:T(8,128)(2,1)S(1)}, bf16[1,8,144,128]{3,2,1,0:T(8,128)(2,1)S(1)}, u32[]{:S(2)}, u32[]{:S(2)}) collective-permute-start(bf16[1,8,144,128]{3,2,1,0:T(8,128)(2,1)S(1)} %bitcast.23), channel_id=1, source_target_pairs={{0,2},{1,3},{2,0},{3,1},{4,6},{5,7},{6,4},{7,5},{8,10},{9,11},{10,... | collective-permute-start | bytes 884744 | tf_op jit(solution)/shard_map/ppermute | solution.py:736
  179.0 2.1 %collective-permute-start.40 = (bf16[2,8,144,128]{3,2,1,0:T(8,128)(2,1)S(1)}, bf16[2,8,144,128]{3,2,1,0:T(8,128)(2,1)S(1)}, u32[]{:S(2)}, u32[]{:S(2)}) collective-permute-start(bf16[2,8,144,128]{3,2,1,0:T(8,128)(2,1)S(1)} %pad_maximum_fusion.refs_0_), channel_id=1, source_target_pairs={{0,1},{1,0},{2,3},{3,2},{4,5},{5,4},{6,7},{7,6},{8,9},{9,8},{10,11... | collective-permute-start | bytes 1769480 | tf_op jit(solution)/shard_map/ppermute | solution.py:736
  (4 other events, 9.7 us)
Sparse Core Ops, SparseCore 0:
  14.8 57.7 all-gather.5
  131.7 53.1 all-gather.3
